TPU v7x, 32 devices: a whole 2x2x4 slice. The times are simulated.
32 devices in a mesh: region: 8 (over z, y), dest: 4 (over x, core).
Axes of the slice: x: 2, y: 2, z: 4, core: 2. Of those that a mesh axis runs over, the one named last changes fastest.
Arguments:
- occupancy: float32 [16384, 4096], P('region', 'dest'), may hold values from 0 to 9, as said below
- capacity: float32 [16384], P('region'), may hold values from 0.5 to 1.5
- jam: float32 [16384], P('region'), may hold values from 13 to 16
- wave: float32 [16384], P('region'), may hold values from 0.08 to 0.25
- node_in: int32 [4, 8192], P(None, 'region'), may hold values from -1 to 2047, as said below
- node_out: int32 [4, 8192], P(None, 'region'), may hold values from -1 to 16383, as said below
- send_list: int32 [32, 192], P('region'), may hold values from -1 to 4095, as said below
- recv_list: int32 [32, 192], P('region'), may hold values from -1 to 2047, as said below
- turn: int32 [8192, 4096], P('region', 'dest'), may hold values from 0 to 3, as said below
Outputs:
- new_occupancy: float32 [16384, 4096], P('region', 'dest')
Inputs may be any that keep to these rules, and one draw needn't show every extreme that they name: `node_in`: every cell of a region is the incoming cell of exactly one node block of that region; each block has 1 to 4 valid incoming slots, first in order, and some block of every region has 4. `node_out`: every cell is the outgoing cell of exactly one slot of one node block; each block has 1 to 4 valid outgoing slots, first in order, and some block of every region has 4. The outgoing cells lie in the block's own region or in the regions at offsets 1, -1, 2, -2 around the cyclic order of regions. `send_list`: row 4 r + t lists, in its first slots, every outgoing slot of region r that leads into region r + d_t (d = 1, -1, 2, -2), at most 192 of them; regions r and r + d send each other equally many; some pair at offset 1 and some at offset 2 send exactly 192. `recv_list`: row 4 r + t holds, slot by slot, the cells of region r that the slots of row 4 (r - d_t) + t of send_list lead into, -1 where that slot is empty. turn[n, k] is always a valid outgoing slot of node block n. `occupancy`: entries are positive.
All inputs are finite; a program needn't handle non-finite values.
Results may differ from a plain program's by a relative error of at most 0.0003.
Values sent between devices are 32-bit elements; how exact they have to be, the bound alone decides.
No kernel may reach another device: no remote copies, remote signals or barrier semaphores. Data moves between devices by JAX's collectives and lax.ppermute only.
A program may use at most 128 MiB of HBM per device.

v0:
```python
import jax
import jax.numpy as jnp
from jax import lax
from jax.sharding import PartitionSpec as P

SHIFTS = (1, -1, 2, -2)
EXACT = lax.Precision.HIGHEST


def shifted(block, axis, distance):
    devices = range(lax.axis_size(axis))
    route = [((i - distance) % len(devices), i) for i in devices]
    return lax.ppermute(block, axis, route)


def to_cells(incidence, rows):
    return jnp.einsum(
        "nc,nk->ck", incidence, rows, preferred_element_type=jnp.float32, precision=EXACT
    )


def on_device(occupancy, capacity, jam, wave, node_in, node_out, send_list, recv_list, turn):
    cell_count, row_width = occupancy.shape
    branch_count, node_count = node_in.shape
    flat_size = branch_count * node_count
    commodities = row_width * lax.axis_size("dest")
    region_no = lax.axis_index("region")
    cell_ids = jnp.arange(cell_count, dtype=jnp.int32)
    node_ids = jnp.arange(node_count, dtype=jnp.int32)
    incidence = jnp.any(node_in[:, :, None] == cell_ids[None, None, :], axis=0).astype(jnp.float32)
    turn_small = turn.astype(jnp.bfloat16)
    local_sum = jnp.sum(occupancy, axis=1)
    vehicles = lax.psum(local_sum, "dest") / commodities
    fraction = jnp.minimum(vehicles, capacity) / vehicles
    node_flow = jnp.dot(
        incidence,
        occupancy * fraction[:, None],
        preferred_element_type=jnp.float32,
        precision=EXACT,
    )
    partial_value = jnp.stack(
        [
            jnp.sum(jnp.where(turn == outlet, node_flow, 0.0), axis=1)
            for outlet in range(branch_count)
        ]
    )
    demand = lax.psum(partial_value, "dest") / commodities
    supply = jnp.minimum(capacity, wave * (jam - vehicles))
    out_valid = node_out >= 0
    home = out_valid & (node_out // cell_count == region_no)
    home_local = jnp.where(home, node_out - region_no * cell_count, 0)
    flat_room = jnp.where(home, supply[home_local], 0.0).reshape(-1)
    for side_no in range(4):
        stride = SHIFTS[side_no]
        wanted = recv_list[side_no]
        values = jnp.where(wanted >= 0, supply[jnp.maximum(wanted, 0)], 0.0)
        returned = shifted(values, "region", -stride)
        slot_ids = send_list[side_no]
        flat_room = flat_room.at[jnp.where(slot_ids >= 0, slot_ids, flat_size)].set(
            returned, mode="drop"
        )
    room = flat_room.reshape(branch_count, node_count)
    ratio = room / jnp.maximum(demand, room)
    theta = jnp.min(jnp.where(out_valid, ratio, 1.0), axis=0)
    scaled = node_flow * theta[:, None]
    home_hot = home[:, :, None] & (home_local[:, :, None] == cell_ids[None, None, :])
    home_map = jnp.any(home_hot, axis=0).astype(jnp.float32)
    outlet_ids = jnp.arange(branch_count, dtype=jnp.float32)[:, None, None]
    slot_of_cell = jnp.sum(jnp.where(home_hot, outlet_ids, 0.0), axis=(0, 1))
    home_turn = jnp.einsum(
        "nc,nk->ck", home_map.astype(jnp.bfloat16), turn_small, preferred_element_type=jnp.float32
    )
    home_rows = to_cells(home_map, scaled)
    inflow = jnp.where(home_turn == slot_of_cell[:, None], home_rows, 0.0)
    slot_valid = send_list >= 0
    slot_node = jnp.where(slot_valid, send_list % node_count, -1).reshape(-1)
    slot_outlet = (jnp.maximum(send_list, 0) // node_count).astype(jnp.float32).reshape(-1)
    selector = (slot_node[:, None] == node_ids[None, :]).astype(jnp.float32)
    chosen_rows = jnp.dot(selector, scaled, preferred_element_type=jnp.float32, precision=EXACT)
    chosen_turn = jnp.dot(
        selector.astype(jnp.bfloat16), turn_small, preferred_element_type=jnp.float32
    )
    keep_slot = (chosen_turn == slot_outlet[:, None]) & slot_valid.reshape(-1)[:, None]
    outgoing_all = jnp.where(keep_slot, chosen_rows, 0.0).reshape(4, send_list.shape[1], row_width)
    outgoing = [outgoing_all[side_no] for side_no in range(4)]
    received = []
    for side_no in range(4):
        received.append(shifted(outgoing[side_no], "region", SHIFTS[side_no]))
    landing_map = (recv_list.reshape(-1)[:, None] == cell_ids[None, :]).astype(jnp.float32)
    inflow = inflow + to_cells(landing_map, jnp.concatenate(received, axis=0))
    cell_theta = jnp.dot(
        theta[None, :], incidence, preferred_element_type=jnp.float32, precision=EXACT
    )[0]
    keeping = 1.0 - cell_theta * fraction
    return occupancy * keeping[:, None] + inflow


def solution(mesh):
    return jax.shard_map(
        on_device,
        mesh=mesh,
        in_specs=(
            P("region", "dest"),
            P("region"),
            P("region"),
            P("region"),
            P(None, "region"),
            P(None, "region"),
            P("region", None),
            P("region", None),
            P("region", "dest"),
        ),
        out_specs=P("region", "dest"),
        check_vma=False,
    )
```

profile of v0, /device:TPU:6, one launch (start us, length us, event | category | flops | bytes accessed | tf_op | source)
XLA Modules:
  0.0 204.3 jit_solution(10124922272172426367)
XLA Ops:
  0.0 0.9 compare_reduce_fusion
  0.9 0.8 slice_maximum_fusion
  1.7 3.8 %reduce_sum.54 = f32[2048]{0:T(1024)S(1)} reduce(f32[2048,1024]{1,0:T(8,128)} %param.9, f32[]{:T(128)} %constant.73.clone.1), dimensions={1}, to_apply=%region_0.0 | reduce | flops 2095104 | bytes 8396804 | tf_op jit(solution)/shard_map/reduce_sum | solution.py:32
  5.6 6.0 %psum.14 = f32[2048]{0:T(1024)S(1)} all-reduce(f32[2048]{0:T(1024)S(1)} %reduce_sum.54), channel_id=1, replica_groups=mesh['region'=8,'dest'=4] {'dest'}, use_global_device_ids=true, to_apply=%region_1.0 | all-reduce | flops 2048 | bytes 16384 | tf_op jit(solution)/shard_map/psum | solution.py:33
  11.7 1.4 gather_fusion.4
  13.2 1.6 collective-permute-start.3
  14.8 1.4 gather_fusion.3
  16.2 2.3 %collective-permute-start.2 = (f32[192]{0:T(256)S(1)}, f32[192]{0:T(256)S(1)}, u32[]{:S(2)}, u32[]{:S(2)}) collective-permute-start(f32[192]{0:T(256)S(1)} %broadcast_select_fusion.1), channel_id=1, source_target_pairs={{8,0},{12,4},{16,8},{20,12},{24,16},{28,20},{0,24},{4,28},{9,1},{1... | collective-permute-start | bytes 2312 | tf_op jit(solution)/shard_map/ppermute | solution.py:13
  18.6 1.4 gather_fusion.2
  20.1 1.4 gather_fusion.1
  21.5 2.1 %collective-permute-start = (f32[192]{0:T(256)S(1)}, f32[192]{0:T(256)S(1)}, u32[]{:S(2)}, u32[]{:S(2)}) collective-permute-start(f32[192]{0:T(256)S(1)} %broadcast_select_fusion.3), channel_id=1, source_target_pairs={{4,0},{8,4},{12,8},{16,12},{20,16},{24,20},{28,24},{0,28},{5,1},{9... | collective-permute-start | bytes 2312 | tf_op jit(solution)/shard_map/ppermute | solution.py:13
  23.7 6.5 %select_reduce_fusion = f32[2048]{0:T(1024)S(1)} fusion(s32[4,1024]{1,0:T(4,128)S(1)} %get-tuple-element.14, pred[4,1024]{1,0:T(4,128)(4,1)S(1)} %get-tuple-element.15), kind=kLoop, calls=%fused_computation.9 | loop fusion | flops 33552384 | bytes 28672 | tf_op jit(solution)/shard_map/reduce_sum | solution.py:69
  30.2 8.9 %fusion.2 = pred[1024,2048]{1,0:T(8,128)(4,1)} fusion(s32[4,1024]{1,0:T(4,128)S(1)} %get-tuple-element.14, pred[4,1024]{1,0:T(4,128)(4,1)S(1)} %get-tuple-element.15), kind=kLoop, calls=%fused_computation.14 | loop fusion | flops 23068672 | bytes 2117632 | tf_op jit(solution)/shard_map/reduce_or | solution.py:67
  39.2 23.0 %gather_fusion = f32[4096]{0:T(1024)S(1)} fusion(f32[2048]{0:T(1024)S(1)} %get-tuple-element.20, s32[4096]{0:T(1024)S(1)} %bitcast_clamp_fusion), kind=kCustom, calls=%fused_computation | custom fusion | bytes 49152 | tf_op jit(solution)/shard_map/gather | solution.py:52
  62.3 5.9 %fusion = pred[1024,2048]{1,0:T(8,128)(4,1)} fusion(s32[4,1024]{1,0:T(4,128)S(1)} %copy-done.9), kind=kLoop, calls=%fused_computation.12 | loop fusion | flops 14680064 | bytes 2113536 | tf_op jit(solution)/shard_map/reduce_or | solution.py:30
  68.2 5.3 %copy.18 = s32[1024,1024]{0,1:T(8,128)} copy(s32[1024,1024]{1,0:T(8,128)} %param.17) | data formatting | bytes 8388608 | tf_op args[8]
  73.6 4.2 %fusion.25 = f32[768,1024]{1,0:T(8,128)S(1)} fusion(s32[768]{0:T(1024)S(1)} %eq.128, s32[1024,1024]{1,0:T(8,128)} %param.17), kind=kOutput, calls=%fused_computation.45 | convolution fusion | flops 1614020608 | bytes 7343104 | tf_op jit(solution)/shard_map/dot_general | solution.py:80
  77.8 7.1 %fusion.6 = f32[2048,1024]{1,0:T(8,128)} fusion(pred[1024,2048]{1,0:T(8,128)(4,1)S(1)} %copy-done.3, s32[1024,1024]{1,0:T(8,128)S(1)} %copy-done), kind=kOutput, calls=%fused_computation.21 | convolution fusion | flops 4300210176 | bytes 14680064 | tf_op jit(solution)/shard_map/nc,nk->ck/dot_general | solution.py:70
  84.9 17.5 %select_reduce_fusion.4 = (f32[1024]{0:T(1024)S(1)}, f32[1024]{0:T(1024)S(1)}, f32[1024]{0:T(1024)S(1)}, f32[1024]{0:T(1024)S(1)}, f32[1024,1024]{0,1:T(8,128)}) fusion(s32[1024,1024]{0,1:T(8,128)S(1)} %copy-done.2, pred[1024,2048]{1,0:T(8,128)(4,1)S(1)} %copy-done.5, f32[2048,1024]{1,0:T(8,128)S(1)} %bitcast.40, f32[2048]{0:T(1024)S(1)} %get-tuple-element.21), kind=kOutput, calls=%fused_computation.27 | convolution fusion | flops 25784479744 | bytes 18898944 | tf_op jit(solution)/shard_map/dot_general | solution.py:35
  102.4 10.1 %psum.15 = f32[4,1024]{1,0:T(4,128)S(1)} all-reduce(f32[4,1024]{1,0:T(4,128)S(1)} %pad_maximum_fusion), channel_id=1, replica_groups=mesh['region'=8,'dest'=4] {'dest'}, use_global_device_ids=true, to_apply=%region_11.12 | all-reduce | flops 4096 | bytes 32768 | tf_op jit(solution)/shard_map/psum | solution.py:47
  112.8 1.2 scatter_fusion
  114.0 1.2 scatter_fusion.1
  115.3 1.2 scatter_fusion.2
  116.6 1.7 scatter_fusion.3
  118.3 3.9 %fusion.42 = f32[1,2048]{1,0:T(1,128)S(1)} fusion(f32[1024,1]{0,1:T(1,128)S(1)} %bitcast.41, pred[1024,2048]{1,0:T(8,128)(4,1)} %fusion), kind=kOutput, calls=%fused_computation.109 | convolution fusion | flops 25165824 | bytes 2109440 | tf_op jit(solution)/shard_map/dot_general | solution.py:91
  122.2 5.6 %and_select_fusion = f32[768,1024]{1,0:T(8,128)S(1)} fusion(f32[768,1024]{1,0:T(8,128)S(1)} %fusion.25, f32[1024,1024]{0,1:T(8,128)S(1)} %copy-done.1, f32[1024]{0:T(1024)S(1)} %select_reduce_fusion.5, f32[768]{0:T(1024)S(1)} %eq.132, s32[768]{0:T(1024)S(1)} %eq.128, pred[768]{0:T(1024)(128)(4,1)S(1)} %and.43), kind=kOutput, calls=%fused_computation.42 | convolution fusion | flops 9667870720 | bytes 10496768 | tf_op jit(solution)/shard_map/dot_general | solution.py:79
  128.1 1.0 collective-permute-start.4
  129.1 5.4 %collective-permute-start.7 = (f32[192,1024]{1,0:T(8,128)S(1)}, f32[192,1024]{1,0:T(8,128)S(1)}, u32[]{:S(2)}, u32[]{:S(2)}) collective-permute-start(f32[192,1024]{1,0:T(8,128)S(1)} %get-tuple-element.17), channel_id=1, source_target_pairs={{8,0},{12,4},{16,8},{20,12},{24,16},{28,20},{0,24},{4,28},{9,1},{1... | collective-permute-start | bytes 2359304 | tf_op jit(solution)/shard_map/ppermute | solution.py:13
  134.7 17.4 %fusion.7 = f32[2048,1024]{1,0:T(8,128)} fusion(pred[1024,2048]{1,0:T(8,128)(4,1)S(1)} %copy-done.4, f32[1024,1024]{0,1:T(8,128)S(1)} %copy-done.1, f32[1024]{0:T(1024)S(1)} %select_reduce_fusion.5), kind=kOutput, calls=%fused_computation.22 | convolution fusion | flops 25772949504 | bytes 14684160 | tf_op jit(solution)/shard_map/nc,nk->ck/dot_general | solution.py:17
  152.0 12.5 %collective-permute-done.7 = f32[192,1024]{1,0:T(8,128)S(1)} collective-permute-done((f32[192,1024]{1,0:T(8,128)S(1)}, f32[192,1024]{1,0:T(8,128)S(1)}, u32[]{:S(2)}, u32[]{:S(2)}) %collective-permute-start.7) | collective-permute-done | bytes 786464 | tf_op jit(solution)/shard_map/ppermute | solution.py:13
  164.5 20.7 %collective-permute-done.6 = f32[192,1024]{1,0:T(8,128)S(1)} collective-permute-done((f32[192,1024]{1,0:T(8,128)S(1)}, f32[192,1024]{1,0:T(8,128)S(1)}, u32[]{:S(2)}, u32[]{:S(2)}) %collective-permute-start.6) | collective-permute-done | bytes 786464 | tf_op jit(solution)/shard_map/ppermute | solution.py:13
  185.2 18.9 %add_add_fusion = f32[2048,1024]{1,0:T(8,128)} fusion(f32[2048,1024]{1,0:T(8,128)} %fusion.7, f32[2048,1024]{1,0:T(8,128)} %param.9, f32[2048,1024]{1,0:T(8,128)} %fusion.6, f32[2048]{0:T(1024)S(1)} %select_reduce_fusion, f32[2048]{0:T(1024)S(1)} %multiply_subtract_fusion, f32[192,1024]{1,0:T(8,128)S(1)} %collective-permute-done.7, ...), kind=kOutput, calls=%fused_computation.15 | convolution fusion | flops 19341770752 | bytes 36719616 | tf_op jit(solution)/shard_map/nc,nk->ck/dot_general | solution.py:17
  (66 shorter events, 1.1 us)
Async XLA Ops:
  1.7 9.9 %copy-start.10 = (f32[2048]{0:T(1024)S(1)}, f32[2048]{0:T(1024)}, u32[]{:S(2)}) copy-start(f32[2048]{0:T(1024)} %param.10) | copy-start | bytes 24580
  1.7 9.9 %copy-start.11 = (f32[2048]{0:T(1024)S(1)}, f32[2048]{0:T(1024)}, u32[]{:S(2)}) copy-start(f32[2048]{0:T(1024)} %param.12) | copy-start | bytes 24580
  1.7 9.9 %copy-start.12 = (f32[2048]{0:T(1024)S(1)}, f32[2048]{0:T(1024)}, u32[]{:S(2)}) copy-start(f32[2048]{0:T(1024)} %param.11) | copy-start | bytes 24580
  5.6 18.0 %copy-start.7 = (s32[4,192]{1,0:T(4,128)S(1)}, s32[4,192]{1,0:T(4,128)}, u32[]{:S(2)}) copy-start(s32[4,192]{1,0:T(4,128)} %param.15) | copy-start | bytes 9220
  5.6 18.1 %copy-start.6 = (s32[4,1024]{1,0:T(4,128)S(1)}, s32[4,1024]{1,0:T(4,128)}, u32[]{:S(2)}) copy-start(s32[4,1024]{1,0:T(4,128)} %param.14) | copy-start | bytes 49156
  13.2 103.4 %collective-permute-start.3 = (f32[192]{0:T(256)S(1)}, f32[192]{0:T(256)S(1)}, u32[]{:S(2)}, u32[]{:S(2)}) collective-permute-start(f32[192]{0:T(256)S(1)} %broadcast_select_fusion), channel_id=1, source_target_pairs={{24,0},{28,4},{0,8},{4,12},{8,16},{12,20},{16,24},{20,28},{25,1},{... | collective-permute-start | bytes 2312 | tf_op jit(solution)/shard_map/ppermute | solution.py:13
  16.2 99.1 %collective-permute-start.2 = (f32[192]{0:T(256)S(1)}, f32[192]{0:T(256)S(1)}, u32[]{:S(2)}, u32[]{:S(2)}) collective-permute-start(f32[192]{0:T(256)S(1)} %broadcast_select_fusion.1), channel_id=1, source_target_pairs={{8,0},{12,4},{16,8},{20,12},{24,16},{28,20},{0,24},{4,28},{9,1},{1... | collective-permute-start | bytes 2312 | tf_op jit(solution)/shard_map/ppermute | solution.py:13
  20.0 94.0 %collective-permute-start.1 = (f32[192]{0:T(256)S(1)}, f32[192]{0:T(256)S(1)}, u32[]{:S(2)}, u32[]{:S(2)}) collective-permute-start(f32[192]{0:T(256)S(1)} %broadcast_select_fusion.2), channel_id=1, source_target_pairs={{28,0},{0,4},{4,8},{8,12},{12,16},{16,20},{20,24},{24,28},{29,1},{... | collective-permute-start | bytes 2312 | tf_op jit(solution)/shard_map/ppermute | solution.py:13
  21.5 91.3 %collective-permute-start = (f32[192]{0:T(256)S(1)}, f32[192]{0:T(256)S(1)}, u32[]{:S(2)}, u32[]{:S(2)}) collective-permute-start(f32[192]{0:T(256)S(1)} %broadcast_select_fusion.3), channel_id=1, source_target_pairs={{4,0},{8,4},{12,8},{16,12},{20,16},{24,20},{28,24},{0,28},{5,1},{9... | collective-permute-start | bytes 2312 | tf_op jit(solution)/shard_map/ppermute | solution.py:13
  39.2 23.1 %copy-start.9 = (s32[4,1024]{1,0:T(4,128)S(1)}, s32[4,1024]{1,0:T(4,128)}, u32[]{:S(2)}) copy-start(s32[4,1024]{1,0:T(4,128)} %param.13) | copy-start | bytes 49156
  73.6 4.2 %copy-start = (s32[1024,1024]{1,0:T(8,128)S(1)}, s32[1024,1024]{1,0:T(8,128)}, u32[]{:S(2)}) copy-start(s32[1024,1024]{1,0:T(8,128)} %param.17) | copy-start | bytes 12582916
  73.6 4.2 %copy-start.3 = (pred[1024,2048]{1,0:T(8,128)(4,1)S(1)}, pred[1024,2048]{1,0:T(8,128)(4,1)}, u32[]{:S(2)}) copy-start(pred[1024,2048]{1,0:T(8,128)(4,1)} %fusion.2) | copy-start | bytes 6291460
  73.6 11.3 %slice-start = ((s8[8388608]{0:T(1024)(128)(4,1)}), s8[4194304]{0:T(1024)(128)(4,1)S(1)}, s32[]{:S(2)}) async-start(s8[8388608]{0:T(1024)(128)(4,1)} %bitcast.39), calls=%async_computation | async-start | bytes 8388608
  77.8 7.1 %slice-start.1 = ((s8[8388608]{0:T(1024)(128)(4,1)}), s8[4194304]{0:T(1024)(128)(4,1)S(1)}, s32[]{:S(2)}) async-start(s8[8388608]{0:T(1024)(128)(4,1)} %bitcast.39), calls=%async_computation.1 | async-start | bytes 8388608
  77.8 7.1 %copy-start.2 = (s32[1024,1024]{0,1:T(8,128)S(1)}, s32[1024,1024]{0,1:T(8,128)}, u32[]{:S(2)}) copy-start(s32[1024,1024]{0,1:T(8,128)} %copy.18) | copy-start | bytes 12582916
  77.8 7.1 %copy-start.5 = (pred[1024,2048]{1,0:T(8,128)(4,1)S(1)}, pred[1024,2048]{1,0:T(8,128)(4,1)}, u32[]{:S(2)}) copy-start(pred[1024,2048]{1,0:T(8,128)(4,1)} %fusion) | copy-start | bytes 6291460
  84.9 27.6 %copy-start.8 = (s32[4,192]{1,0:T(4,128)S(1)}, s32[4,192]{1,0:T(4,128)}, u32[]{:S(2)}) copy-start(s32[4,192]{1,0:T(4,128)} %param.16) | copy-start | bytes 9220
  118.3 3.9 %copy-start.1 = (f32[1024,1024]{0,1:T(8,128)S(1)}, f32[1024,1024]{0,1:T(8,128)}, u32[]{:S(2)}) copy-start(f32[1024,1024]{0,1:T(8,128)} %get-tuple-element.32) | copy-start | bytes 12582916
  127.9 6.8 %copy-start.4 = (pred[1024,2048]{1,0:T(8,128)(4,1)S(1)}, pred[1024,2048]{1,0:T(8,128)(4,1)}, u32[]{:S(2)}) copy-start(pred[1024,2048]{1,0:T(8,128)(4,1)} %fusion.2) | copy-start | bytes 6291460
  128.1 23.9 %collective-permute-start.4 = (f32[192,1024]{1,0:T(8,128)S(1)}, f32[192,1024]{1,0:T(8,128)S(1)}, u32[]{:S(2)}, u32[]{:S(2)}) collective-permute-start(f32[192,1024]{1,0:T(8,128)S(1)} %get-tuple-element.16), channel_id=1, source_target_pairs={{28,0},{0,4},{4,8},{8,12},{12,16},{16,20},{20,24},{24,28},{29,1},{... | collective-permute-start | bytes 2359304 | tf_op jit(solution)/shard_map/ppermute | solution.py:13
  129.1 35.5 %collective-permute-start.7 = (f32[192,1024]{1,0:T(8,128)S(1)}, f32[192,1024]{1,0:T(8,128)S(1)}, u32[]{:S(2)}, u32[]{:S(2)}) collective-permute-start(f32[192,1024]{1,0:T(8,128)S(1)} %get-tuple-element.17), channel_id=1, source_target_pairs={{8,0},{12,4},{16,8},{20,12},{24,16},{28,20},{0,24},{4,28},{9,1},{1... | collective-permute-start | bytes 2359304 | tf_op jit(solution)/shard_map/ppermute | solution.py:13
  134.5 50.7 %collective-permute-start.6 = (f32[192,1024]{1,0:T(8,128)S(1)}, f32[192,1024]{1,0:T(8,128)S(1)}, u32[]{:S(2)}, u32[]{:S(2)}) collective-permute-start(f32[192,1024]{1,0:T(8,128)S(1)} %get-tuple-element.18), channel_id=1, source_target_pairs={{24,0},{28,4},{0,8},{4,12},{8,16},{12,20},{16,24},{20,28},{25,1},{... | collective-permute-start | bytes 2359304 | tf_op jit(solution)/shard_map/ppermute | solution.py:13
  134.5 50.7 %collective-permute-start.5 = (f32[192,1024]{1,0:T(8,128)S(1)}, f32[192,1024]{1,0:T(8,128)S(1)}, u32[]{:S(2)}, u32[]{:S(2)}) collective-permute-start(f32[192,1024]{1,0:T(8,128)S(1)} %get-tuple-element.19), channel_id=1, source_target_pairs={{4,0},{8,4},{12,8},{16,12},{20,16},{24,20},{28,24},{0,28},{5,1},{9... | collective-permute-start | bytes 2359304 | tf_op jit(solution)/shard_map/ppermute | solution.py:13
where the time goes:
time: 207 us; the launch traced here: 204 us
  matrix products  74.4 us (36%)
  local copies, waits for them, and re-layouts  40.2 us (19%)
  waiting for transfers between devices  33.2 us (16%)
  other arithmetic  27.1 us (13%)
  blocking collectives  16.1 us (8%)
  starting transfers between devices  12.6 us (6%)
    dot_general x2, matrix products, to_cells(): jnp.einsum('nc,nk->ck', incidence, rows, preferred_element_type=jnp.float...  36.2 us
    ppermute x8, waiting for transfers between devices, shifted(): return lax.ppermute(block, axis, route)  33.2 us
    gather x2, local copies, waits for them, and re-layouts, on_device(): flat_room = jnp.where(home, supply[home_local], 0.0).reshape(-1)  23 us
    dot_general x1, matrix products, on_device(): jnp.dot(incidence, occupancy * fraction[:, None], preferred_element_type=...  17.5 us
    ppermute x8, starting transfers between devices, shifted(): return lax.ppermute(block, axis, route)  12.6 us
    psum x1, blocking collectives, on_device(): demand = lax.psum(partial_value, 'dest') / commodities  10.1 us
    reduce_or x1, other arithmetic, on_device(): home_map = jnp.any(home_hot, axis=0).astype(jnp.float32)  8.91 us
    dot_general x1, matrix products, on_device(): jnp.einsum('nc,nk->ck', home_map.astype(jnp.bfloat16), turn_small, prefer...  7.08 us
  transfers between devices with their start and end apart: 8, of which 2 were waited for; matrix products, arithmetic and copies ran while one was open for 51% of the time, Pallas kernels for 0%

commit v1 on v0

v1 whole, which is shorter than its diff:
```python
import functools

import jax
import jax.numpy as jnp
from jax import lax
from jax.experimental import pallas as pl
from jax.experimental.pallas import tpu as pltpu
from jax.sharding import PartitionSpec as P

SHIFTS = (1, -1, 2, -2)
EXACT = lax.Precision.HIGHEST
LANES = 128
MIB = 1 << 20
VMEM_WHOLE = pl.BlockSpec(memory_space=pltpu.VMEM)
SMEM_WHOLE = pl.BlockSpec(memory_space=pltpu.SMEM)


def shifted(block, axis, distance):
    devices = range(lax.axis_size(axis))
    route = [((i - distance) % len(devices), i) for i in devices]
    return lax.ppermute(block, axis, route)


def params(mib):
    return pltpu.CompilerParams(vmem_limit_bytes=mib * MIB)


def cost(flops, moved):
    return pl.CostEstimate(flops=flops, bytes_accessed=moved, transcendentals=0)


def lane_sums(partial):
    ones = jnp.ones((8, LANES), jnp.float32)
    sums = lax.dot_general(
        ones, partial, (((1,), (1,)), ((), ())),
        preferred_element_type=jnp.float32, precision=EXACT,
    )
    return sums[0:1, :]


def to_rows(x_ref, rows_ref, first, count, sub):
    for group in range(count // 8):
        for q in range(sub):
            piece = x_ref[group * 8 : group * 8 + 8, q * LANES : (q + 1) * LANES]
            start = (first + group * 8) * sub + q
            rows_ref[pl.ds(start, 8, stride=sub), :] = piece


def cell_sum_kernel(block, sub, x_ref, sum_ref, rows_ref):
    step = pl.program_id(0)
    to_rows(x_ref, rows_ref, step * block, block, sub)
    partial = x_ref[:, 0:LANES]
    for q in range(1, sub):
        partial = partial + x_ref[:, q * LANES : (q + 1) * LANES]
    sums = lane_sums(partial)
    per_step = block // LANES
    for part in range(per_step):
        sum_ref[pl.ds(step * per_step + part, 1), :] = sums[:, part * LANES : (part + 1) * LANES]


def turn_rows_kernel(block, sub, x_ref, rows_ref):
    to_rows(x_ref, rows_ref, pl.program_id(0) * block, block, sub)


def node_flow_kernel(sizes, fraction, in_row, send_row, send_outlet, rows, turns, flow, *rest):
    cells, nodes, branches, cap, sub = sizes
    sends, scaled = rest[:4], rest[4]

    def row(index):
        return pl.ds(pl.multiple_of(index, sub), sub)

    def scale(step, carry):
        first = step * 16
        values = [
            rows[row((first + i) * sub), :] * fraction[first + i] for i in range(16)
        ]
        for i in range(16):
            scaled[row((first + i) * sub), :] = values[i]
        return carry

    lax.fori_loop(0, cells // 16, scale, 0)
    scaled[row(cells * sub), :] = jnp.zeros((sub, LANES), jnp.float32)

    def gather(step, carry):
        first = step * 8
        values = []
        for i in range(8):
            parts = [
                scaled[row(in_row[j * nodes + first + i]), :] for j in range(branches)
            ]
            while len(parts) > 1:
                parts = [sum(parts[k : k + 2][1:], parts[k]) for k in range(0, len(parts), 2)]
            values.append(parts[0])
        for i in range(8):
            flow[row((first + i) * sub), :] = values[i]
        return carry

    lax.fori_loop(0, nodes // 8, gather, 0)

    for side, send in enumerate(sends):

        def pick(step, carry, side=side, send=send):
            first = step * 8
            values = []
            for i in range(8):
                slot = side * cap + first + i
                where_from = row(send_row[slot])
                values.append(
                    jnp.where(turns[where_from, :] == send_outlet[slot], flow[where_from, :], 0.0)
                )
            for i in range(8):
                send[row((first + i) * sub), :] = values[i]
            return carry

        lax.fori_loop(0, cap // 8, pick, 0)


def demand_kernel(sizes, flow, turn, demand, partial):
    cells, nodes, branches, cap, sub = sizes

    def group(step, carry):
        first = step * 8
        totals = [jnp.zeros((8, LANES), jnp.float32)] * branches
        for q in range(sub):
            value = flow[pl.ds(first * sub + q, 8, stride=sub), :]
            choice = turn[pl.ds(pl.multiple_of(first, 8), 8), q * LANES : (q + 1) * LANES]
            totals = [
                total + jnp.where(choice == j, value, 0.0) for j, total in enumerate(totals)
            ]
        for j in range(branches):
            partial[j, pl.ds(pl.multiple_of(first, 8), 8), :] = totals[j]
        return carry

    lax.fori_loop(0, nodes // 8, group, 0)
    for j in range(branches):
        demand[j : j + 1, :] = lane_sums(partial[j])


def room_kernel(table, place, room):
    def body(step, carry):
        first = step * 16
        values = [table[place[first + i]] for i in range(16)]
        for i in range(16):
            room[first + i] = values[i]
        return carry

    lax.fori_loop(0, place.shape[0] // 16, body, 0)


def home_kernel(sizes, theta, keep, home_row, rows, turns, flow, base):
    cells, nodes, branches, cap, sub = sizes

    def row(index):
        return pl.ds(pl.multiple_of(index, sub), sub)

    def body(step, carry):
        first = step * 4
        stores = []
        for i in range(4):
            node = first + i
            moved = flow[row(node * sub), :] * theta[node]
            choice = turns[row(node * sub), :]
            for j in range(branches):
                cell = home_row[j * nodes + node]
                at = row(cell * sub)
                kept = rows[row(jnp.minimum(cell, cells - 1) * sub), :] * keep[cell]
                stores.append((at, kept + jnp.where(choice == j, moved, 0.0)))
        for at, value in stores:
            base[at, :] = value
        return carry

    lax.fori_loop(0, nodes // 4, body, 0)


def finish_kernel(sizes, block, keep, scale, land, rows, *rest):
    cells, nodes, branches, cap, sub = sizes
    received, (base_in, out, base) = rest[:4], rest[4:]

    def row(index):
        return pl.ds(pl.multiple_of(index, sub), sub)

    step = pl.program_id(0)

    @pl.when(step == 0)
    def _():
        for side in range(4):

            def body(turn_no, carry, side=side):
                first = turn_no * 8
                stores = []
                for i in range(8):
                    slot = side * cap + first + i
                    cell = land[slot]
                    kept = rows[row(jnp.minimum(cell, cells - 1) * sub), :] * keep[cell]
                    value = kept + received[side][row((first + i) * sub), :] * scale[slot]
                    stores.append((row(cell * sub), value))
                for at, value in stores:
                    base[at, :] = value
                return carry

            lax.fori_loop(0, cap // 8, body, 0)

    for group in range(block // 8):
        for q in range(sub):
            start = (step * block + group * 8) * sub + q
            out[group * 8 : group * 8 + 8, q * LANES : (q + 1) * LANES] = base[
                pl.ds(start, 8, stride=sub), :
            ]


def on_device(occupancy, capacity, jam, wave, node_in, node_out, send_list, recv_list, turn):
    cells, width = occupancy.shape
    branches, nodes = node_in.shape
    cap = send_list.shape[1]
    sub = width // LANES
    sizes = (cells, nodes, branches, cap, sub)
    regions = lax.axis_size("region")
    commodities = width * lax.axis_size("dest")
    region_no = lax.axis_index("region")
    block = 256
    f32 = jnp.float32

    local_sum, rows = pl.pallas_call(
        functools.partial(cell_sum_kernel, block, sub),
        grid=(cells // block,),
        in_specs=[pl.BlockSpec((block, width), lambda i: (i, 0))],
        out_specs=[pl.BlockSpec((cells // LANES, LANES), lambda i: (0, 0)), VMEM_WHOLE],
        out_shape=[
            jax.ShapeDtypeStruct((cells // LANES, LANES), f32),
            pltpu.VMEM((cells * sub, LANES), f32),
        ],
        compiler_params=params(12),
        cost_estimate=cost(cells * width, cells * width * 4),
        name="cell_sum",
    )(occupancy)

    turn_block = 128
    turns = pl.pallas_call(
        functools.partial(turn_rows_kernel, turn_block, sub),
        grid=(nodes // turn_block,),
        in_specs=[pl.BlockSpec((turn_block, width), lambda i: (i, 0))],
        out_specs=VMEM_WHOLE,
        out_shape=pltpu.VMEM((nodes * sub, LANES), jnp.int32),
        compiler_params=params(8),
        cost_estimate=cost(0, nodes * width * 4),
        name="turn_rows",
    )(turn)

    in_row = jnp.where(node_in >= 0, node_in, cells).reshape(-1) * sub
    slots = send_list.reshape(-1)
    send_row = jnp.where(slots >= 0, slots % nodes, 0) * sub
    send_outlet = jnp.where(slots >= 0, slots // nodes, -1)
    land = jnp.where(recv_list >= 0, recv_list, cells).reshape(-1)
    out_valid = node_out >= 0
    out_cell = jnp.maximum(node_out, 0)
    offset = (out_cell // cells - region_no) % regions
    out_local = out_cell % cells
    home = out_valid & (offset == 0)
    home_row = jnp.where(home, out_local, cells).reshape(-1)
    sector = jnp.zeros_like(offset)
    for side, stride in enumerate(SHIFTS):
        sector = jnp.where(offset == stride % regions, side + 1, sector)
    place = (sector * cells + out_local).reshape(-1)

    vehicles = lax.psum(local_sum, "dest") / commodities
    cap_of = capacity.reshape(vehicles.shape)
    fraction = jnp.minimum(vehicles, cap_of) / vehicles
    supply = jnp.minimum(
        cap_of, wave.reshape(vehicles.shape) * (jam.reshape(vehicles.shape) - vehicles)
    )
    fraction = fraction.reshape(-1)

    row_shape = jax.ShapeDtypeStruct((cap * sub, LANES), f32)
    flow, *sends = pl.pallas_call(
        functools.partial(node_flow_kernel, sizes),
        in_specs=[SMEM_WHOLE] * 4 + [VMEM_WHOLE] * 2,
        out_specs=[VMEM_WHOLE] * 5,
        out_shape=[pltpu.VMEM((nodes * sub, LANES), f32)]
        + [pltpu.VMEM((cap * sub, LANES), f32)] * 4,
        scratch_shapes=[pltpu.VMEM(((cells + 1) * sub, LANES), f32)],
        compiler_params=params(16),
        cost_estimate=cost(cells * width * 2, cells * width * 4),
        name="node_flow",
    )(fraction, in_row, send_row, send_outlet, rows, turns)

    arrived = [shifted(sends[side], "region", SHIFTS[side]) for side in range(4)]

    table = jnp.concatenate(
        [supply] + [shifted(supply, "region", -stride) for stride in SHIFTS]
    ).reshape(-1)

    demand = pl.pallas_call(
        functools.partial(demand_kernel, sizes),
        in_specs=[VMEM_WHOLE] * 2,
        out_specs=VMEM_WHOLE,
        out_shape=jax.ShapeDtypeStruct((branches, nodes), f32),
        scratch_shapes=[pltpu.VMEM((branches, nodes, LANES), f32)],
        compiler_params=params(12),
        cost_estimate=cost(nodes * width * 8, nodes * width * 4),
        name="demand",
    )(flow, turn)
    demand = lax.psum(demand, "dest") / commodities

    room = pl.pallas_call(
        room_kernel,
        in_specs=[SMEM_WHOLE] * 2,
        out_specs=SMEM_WHOLE,
        out_shape=jax.ShapeDtypeStruct((branches * nodes,), f32),
        cost_estimate=cost(0, branches * nodes * 4),
        name="room",
    )(table, place).reshape(branches, nodes)
    ratio = room / jnp.maximum(demand, room)
    theta = jnp.min(jnp.where(out_valid, ratio, 1.0), axis=0)

    sent_theta = pl.pallas_call(
        room_kernel,
        in_specs=[SMEM_WHOLE] * 2,
        out_specs=SMEM_WHOLE,
        out_shape=jax.ShapeDtypeStruct((4 * cap,), f32),
        cost_estimate=cost(0, cap * 16),
        name="slot_theta",
    )(theta, send_row // sub).reshape(4, cap)
    scale = jnp.concatenate(
        [shifted(sent_theta[side], "region", SHIFTS[side]) for side in range(4)]
    )

    cell_ids = jnp.arange(cells, dtype=jnp.int32)
    incidence = jnp.any(node_in[:, :, None] == cell_ids[None, None, :], axis=0).astype(f32)
    cell_theta = jnp.dot(
        theta[None, :], incidence, preferred_element_type=f32, precision=EXACT
    )[0]
    keep = jnp.concatenate([1.0 - cell_theta * fraction, jnp.zeros((LANES,), f32)])

    base = pl.pallas_call(
        functools.partial(home_kernel, sizes),
        in_specs=[SMEM_WHOLE] * 3 + [VMEM_WHOLE] * 3,
        out_specs=VMEM_WHOLE,
        out_shape=pltpu.VMEM(((cells + 1) * sub, LANES), f32),
        compiler_params=params(8),
        cost_estimate=cost(cells * width * 2, cells * width * 4),
        name="home_inflow",
    )(theta, keep, home_row, rows, turns, flow)

    out, _ = pl.pallas_call(
        functools.partial(finish_kernel, sizes, block),
        grid=(cells // block,),
        in_specs=[SMEM_WHOLE] * 3 + [VMEM_WHOLE] * 6,
        out_specs=[pl.BlockSpec((block, width), lambda i: (i, 0)), VMEM_WHOLE],
        out_shape=[
            jax.ShapeDtypeStruct((cells, width), f32),
            pltpu.VMEM(((cells + 1) * sub, LANES), f32),
        ],
        input_output_aliases={8: 1},
        compiler_params=params(12),
        cost_estimate=cost(cells * width, cells * width * 4),
        name="finish",
    )(keep, scale, land, rows, *arrived, base)
    return out


def solution(mesh):
    return jax.shard_map(
        on_device,
        mesh=mesh,
        in_specs=(
            P("region", "dest"),
            P("region"),
            P("region"),
            P("region"),
            P(None, "region"),
            P(None, "region"),
            P("region", None),
            P("region", None),
            P("region", "dest"),
        ),
        out_specs=P("region", "dest"),
        check_vma=False,
    )
```

time: 207 us -> 163 us (0.79)
  the two profiles are of different devices: /device:TPU:6 before, /device:TPU:0 now
where the time goes in v1:
time: 163 us; the launch traced here: 162 us
  Pallas kernels  56 us (34%)
  local copies, waits for them, and re-layouts  32.2 us (20%)
  waiting for transfers between devices  25.4 us (16%)
  blocking collectives  19.2 us (12%)
  starting transfers between devices  18.3 us (11%)
  other arithmetic  7.39 us (5%)
  matrix products  3.74 us (2%)
    unnamed x50, local copies, waits for them, and re-layouts  30.4 us
    ppermute x12, waiting for transfers between devices, shifted(): return lax.ppermute(block, axis, route)  25.4 us
    ppermute x12, starting transfers between devices, shifted(): return lax.ppermute(block, axis, route)  18.3 us
    pallas_call x1, Pallas kernels, on_device(): pl.pallas_call(functools.partial(home_kernel, sizes), in_specs=[SMEM_WHOL...  17.6 us
    pallas_call x2, Pallas kernels, on_device(): pl.pallas_call(room_kernel, in_specs=[SMEM_WHOLE] * 2, out_specs=SMEM_WHO...  11.6 us
    psum x1, blocking collectives, on_device(): demand = lax.psum(demand, 'dest') / commodities  10.7 us
    pallas_call x1, Pallas kernels, on_device(): pl.pallas_call(functools.partial(node_flow_kernel, sizes), in_specs=[SMEM...  9.92 us
    pallas_call x1, Pallas kernels, on_device(): pl.pallas_call(functools.partial(finish_kernel, sizes, block), grid=(cell...  8.59 us
  transfers between devices with their start and end apart: 12, of which 3 were waited for; matrix products, arithmetic and copies ran while one was open for 8% of the time, Pallas kernels for 27%

profile of v1, /device:TPU:0, one launch (start us, length us, event | category | flops | bytes accessed | tf_op | source)
XLA Modules:
  0.0 162.5 jit_solution(6414466449201201398)
XLA Ops:
  0.0 3.4 %copy-done.11 = f32[2048,1024]{1,0:T(8,128)S(1)} copy-done((f32[2048,1024]{1,0:T(8,128)S(1)}, f32[2048,1024]{1,0:T(8,128)}, u32[]{:S(2)}) %copy-start.11) | copy-done | bytes 8388632
  3.4 3.1 %cell_sum.1 = (f32[16,128]{1,0:T(8,128)S(1)}, f32[16384,128]{1,0:T(8,128)S(1)}) custom-call(f32[2048,1024]{1,0:T(8,128)S(1)} %copy-done.11), custom_call_target="tpu_custom_call" | custom-call | flops 2097152 | bytes 8388608 | tf_op jit(solution)/shard_map/cell_sum/pallas_call | solution.py:223
  6.5 3.4 %copy-done = f32[16384,128]{1,0:T(8,128)} copy-done((f32[16384,128]{1,0:T(8,128)}, f32[16384,128]{1,0:T(8,128)S(1)}, u32[]{:S(2)}) %copy-start) | copy-done | bytes 8388632
  9.9 8.5 %psum.14 = f32[16,128]{1,0:T(8,128)S(1)} all-reduce(f32[16,128]{1,0:T(8,128)S(1)} %get-tuple-element.13), channel_id=1, replica_groups=mesh['region'=8,'dest'=4] {'dest'}, use_global_device_ids=true, to_apply=%region_0.1 | all-reduce | flops 2048 | bytes 16384 | tf_op jit(solution)/shard_map/psum | solution.py:265
  18.5 1.6 %collective-permute-start.3 = (f32[16,128]{1,0:T(8,128)S(1)}, f32[16,128]{1,0:T(8,128)S(1)}, u32[]{:S(2)}, u32[]{:S(2)}) collective-permute-start(f32[16,128]{1,0:T(8,128)S(1)} %get-tuple-element.24), channel_id=1, source_target_pairs={{24,0},{28,4},{0,8},{4,12},{8,16},{12,20},{16,24},{20,28},{25,1},{... | collective-permute-start | bytes 24584 | tf_op jit(solution)/shard_map/ppermute | solution.py:21
  20.1 2.2 %collective-permute-start.2 = (f32[16,128]{1,0:T(8,128)S(1)}, f32[16,128]{1,0:T(8,128)S(1)}, u32[]{:S(2)}, u32[]{:S(2)}) collective-permute-start(f32[16,128]{1,0:T(8,128)S(1)} %get-tuple-element.24), channel_id=1, source_target_pairs={{8,0},{12,4},{16,8},{20,12},{24,16},{28,20},{0,24},{4,28},{9,1},{1... | collective-permute-start | bytes 24584 | tf_op jit(solution)/shard_map/ppermute | solution.py:21
  22.3 1.5 collective-permute-start.1
  23.9 3.2 %collective-permute-start = (f32[16,128]{1,0:T(8,128)S(1)}, f32[16,128]{1,0:T(8,128)S(1)}, u32[]{:S(2)}, u32[]{:S(2)}) collective-permute-start(f32[16,128]{1,0:T(8,128)S(1)} %get-tuple-element.24), channel_id=1, source_target_pairs={{4,0},{8,4},{12,8},{16,12},{20,16},{24,20},{28,24},{0,28},{5,1},{9... | collective-permute-start | bytes 24584 | tf_op jit(solution)/shard_map/ppermute | solution.py:21
  27.8 2.4 %copy-done.6 = s32[1024,1024]{1,0:T(8,128)S(1)} copy-done((s32[1024,1024]{1,0:T(8,128)S(1)}, s32[1024,1024]{1,0:T(8,128)}, u32[]{:S(2)}) %copy-start.6) | copy-done | bytes 4194328
  31.8 9.9 %node_flow.1 = (f32[8192,128]{1,0:T(8,128)S(1)}, f32[1536,128]{1,0:T(8,128)}, f32[1536,128]{1,0:T(8,128)}, f32[1536,128]{1,0:T(8,128)}, f32[1536,128]{1,0:T(8,128)S(1)}) custom-call(f32[2048]{0:T(1024)S(1)} %get-tuple-element.27.fraction, s32[4096]{0:T(1024)S(1)} %bitcast.36, s32[768]{0:T(1024)S(1)} %get-tuple-element.22.send_row, ...), custom_call_target="tpu_custom_call" | custom-call | flops 4194304 | bytes 8388608 | tf_op jit(solution)/shard_map/node_flow/pallas_call | solution.py:274
  41.7 2.0 %copy-done.8 = f32[8192,128]{1,0:T(8,128)} copy-done((f32[8192,128]{1,0:T(8,128)}, f32[8192,128]{1,0:T(8,128)S(1)}, u32[]{:S(2)}) %copy-start.8) | copy-done | bytes 4194328
  44.6 2.2 %copy-done.7 = s32[1024,1024]{1,0:T(8,128)S(1)} copy-done((s32[1024,1024]{1,0:T(8,128)S(1)}, s32[1024,1024]{1,0:T(8,128)}, u32[]{:S(2)}) %copy-start.7) | copy-done | bytes 4194328
  46.8 2.2 %copy-done.9 = f32[8192,128]{1,0:T(8,128)S(1)} copy-done((f32[8192,128]{1,0:T(8,128)S(1)}, f32[8192,128]{1,0:T(8,128)}, u32[]{:S(2)}) %copy-start.9) | copy-done | bytes 4194328
  49.0 4.5 %demand.1 = f32[4,1024]{1,0:T(4,128)S(1)} custom-call(f32[8192,128]{1,0:T(8,128)S(1)} %copy-done.9, s32[1024,1024]{1,0:T(8,128)S(1)} %copy-done.7), custom_call_target="tpu_custom_call" | custom-call | flops 8388608 | bytes 4194304 | tf_op jit(solution)/shard_map/demand/pallas_call | solution.py:292
  53.6 10.7 %psum.15 = f32[4,1024]{1,0:T(4,128)S(1)} all-reduce(f32[4,1024]{1,0:T(4,128)S(1)} %demand.1), channel_id=1, replica_groups=mesh['region'=8,'dest'=4] {'dest'}, use_global_device_ids=true, to_apply=%region_1.2 | all-reduce | flops 4096 | bytes 32768 | tf_op jit(solution)/shard_map/psum | solution.py:302
  64.9 4.4 %collective-permute-start.9 = (f32[1536,128]{1,0:T(8,128)}, f32[1536,128]{1,0:T(8,128)S(1)}, u32[]{:S(2)}, u32[]{:S(2)}) collective-permute-start(f32[1536,128]{1,0:T(8,128)} %get-tuple-element.17), channel_id=1, source_target_pairs={{4,0},{8,4},{12,8},{16,12},{20,16},{24,20},{28,24},{0,28},{5,1},{9... | collective-permute-start | bytes 2359304 | tf_op jit(solution)/shard_map/ppermute | solution.py:21
  69.3 3.8 %collective-permute-start.11 = (f32[1536,128]{1,0:T(8,128)}, f32[1536,128]{1,0:T(8,128)S(1)}, u32[]{:S(2)}, u32[]{:S(2)}) collective-permute-start(f32[1536,128]{1,0:T(8,128)} %copy-done.13), channel_id=1, source_target_pairs={{8,0},{12,4},{16,8},{20,12},{24,16},{28,20},{0,24},{4,28},{9,1},{1... | collective-permute-start | bytes 2359304 | tf_op jit(solution)/shard_map/ppermute | solution.py:21
  73.8 9.0 %room.1 = f32[4096]{0:T(1024)} custom-call(f32[10240]{0:T(1024)} %bitcast.40, s32[4096]{0:T(1024)} %bitcast.39), custom_call_target="tpu_custom_call" | custom-call | bytes 16384 | tf_op jit(solution)/shard_map/room/pallas_call | solution.py:304
  84.1 2.6 %slot_theta.1 = f32[768]{0:T(1024)} custom-call(f32[1024]{0:T(1024)} %select_reduce_fusion.table.theta, s32[768]{0:T(1024)} %get-tuple-element.21.place), custom_call_target="tpu_custom_call" | custom-call | bytes 3072 | tf_op jit(solution)/shard_map/slot_theta/pallas_call | solution.py:315
  86.7 0.9 fusion.18
  87.6 6.0 %fusion = pred[1024,2048]{1,0:T(8,128)(4,1)} fusion(s32[4,1024]{1,0:T(4,128)S(1)} %copy-done.14), kind=kLoop, calls=%fused_computation.1 | loop fusion | flops 14680064 | bytes 2113536 | tf_op jit(solution)/shard_map/reduce_or | solution.py:328
  93.6 9.0 %collective-permute-done.4 = f32[192]{0:T(256)S(1)} collective-permute-done((f32[192]{0:T(256)S(1)}, f32[192]{0:T(256)S(1)}, u32[]{:S(2)}, u32[]{:S(2)}) %collective-permute-start.4) | collective-permute-done | bytes 800 | tf_op jit(solution)/shard_map/ppermute | solution.py:21
  102.6 1.5 collective-permute-start.7
  104.2 14.4 %collective-permute-done.7 = f32[192]{0:T(256)S(1)} collective-permute-done((f32[192]{0:T(256)S(1)}, f32[192]{0:T(256)S(1)}, u32[]{:S(2)}, u32[]{:S(2)}) %collective-permute-start.7) | collective-permute-done | bytes 800 | tf_op jit(solution)/shard_map/ppermute | solution.py:21
  118.6 3.7 %fusion.19 = f32[1,2048]{1,0:T(1,128)S(1)} fusion(f32[1024,1]{0,1:T(1,128)} %bitcast.38, pred[1024,2048]{1,0:T(8,128)(4,1)} %fusion), kind=kOutput, calls=%fused_computation.56 | convolution fusion | flops 25165824 | bytes 2109440 | tf_op jit(solution)/shard_map/dot_general | solution.py:329
  122.3 2.0 %collective-permute-done.6 = f32[192]{0:T(256)S(1)} collective-permute-done((f32[192]{0:T(256)S(1)}, f32[192]{0:T(256)S(1)}, u32[]{:S(2)}, u32[]{:S(2)}) %collective-permute-start.6) | collective-permute-done | bytes 800 | tf_op jit(solution)/shard_map/ppermute | solution.py:21
  124.4 3.4 %copy-done.2 = f32[16384,128]{1,0:T(8,128)S(1)} copy-done((f32[16384,128]{1,0:T(8,128)S(1)}, f32[16384,128]{1,0:T(8,128)}, u32[]{:S(2)}) %copy-start.2) | copy-done | bytes 8388632
  127.7 2.2 %copy-done.5 = s32[8192,128]{1,0:T(8,128)S(1)} copy-done((s32[8192,128]{1,0:T(8,128)S(1)}, s32[8192,128]{1,0:T(8,128)}, u32[]{:S(2)}) %copy-start.5) | copy-done | bytes 4194328
  129.9 2.2 %copy-done.10 = f32[8192,128]{1,0:T(8,128)S(1)} copy-done((f32[8192,128]{1,0:T(8,128)S(1)}, f32[8192,128]{1,0:T(8,128)}, u32[]{:S(2)}) %copy-start.10) | copy-done | bytes 4194328
  132.8 17.6 %home_inflow.1.rest_4_ = f32[16392,128]{1,0:T(8,128)S(1)} custom-call(f32[1024]{0:T(1024)S(1)} %copy-done.12, f32[2176]{0:T(1024)S(1)} %concatenate.10.keep, s32[4096]{0:T(1024)S(1)} %bitcast.37, f32[16384,128]{1,0:T(8,128)S(1)} %copy-done.2, s32[8192,128]{1,0:T(8,128)S(1)} %copy-done.5, f32[8192,128]{1,0:T(8,128)S(1)} %copy-done.10), custom_call_target="tpu_custom_call" | custom-call | flops 4194304 | bytes 8388608 | tf_op jit(solution)/shard_map/home_inflow/pallas_call | solution.py:334
  150.5 3.4 %copy-done.3 = f32[16384,128]{1,0:T(8,128)S(1)} copy-done((f32[16384,128]{1,0:T(8,128)S(1)}, f32[16384,128]{1,0:T(8,128)}, u32[]{:S(2)}) %copy-start.3) | copy-done | bytes 8388632
  153.9 8.6 %finish.1 = (f32[2048,1024]{1,0:T(8,128)}, f32[16392,128]{1,0:T(8,128)S(1)}) custom-call(f32[2176]{0:T(1024)S(1)} %concatenate.10.keep, f32[768]{0:T(1024)S(1)} %pad_maximum_fusion.scale, s32[768]{0:T(1024)S(1)} %reshape.55.land, f32[16384,128]{1,0:T(8,128)S(1)} %copy-done.3, ...), custom_call_target="tpu_custom_call", output_to_operand_aliasing={{1}: (8, {})} | custom-call | flops 2097152 | bytes 8388608 | tf_op jit(solution)/shard_map/finish/pallas_call | solution.py:344
  (68 shorter events, 6.7 us)
Async XLA Ops:
  0.0 3.4 %copy-start.11 = (f32[2048,1024]{1,0:T(8,128)S(1)}, f32[2048,1024]{1,0:T(8,128)}, u32[]{:S(2)}) copy-start(f32[2048,1024]{1,0:T(8,128)} %x_ref.2) | copy-start | bytes 25165828
  3.4 15.0 %copy-start.17 = (f32[2048]{0:T(1024)S(1)}, f32[2048]{0:T(1024)}, u32[]{:S(2)}) copy-start(f32[2048]{0:T(1024)} %param.11) | copy-start | bytes 24580
  3.4 15.0 %copy-start.18 = (f32[2048]{0:T(1024)S(1)}, f32[2048]{0:T(1024)}, u32[]{:S(2)}) copy-start(f32[2048]{0:T(1024)} %param.12) | copy-start | bytes 24580
  3.4 15.0 %copy-start.19 = (f32[2048]{0:T(1024)S(1)}, f32[2048]{0:T(1024)}, u32[]{:S(2)}) copy-start(f32[2048]{0:T(1024)} %param.10) | copy-start | bytes 24580
  3.4 23.7 %copy-start.20 = (s32[4,192]{1,0:T(4,128)S(1)}, s32[4,192]{1,0:T(4,128)}, u32[]{:S(2)}) copy-start(s32[4,192]{1,0:T(4,128)} %param.15) | copy-start | bytes 9220
  3.4 24.4 %copy-start.14 = (s32[4,1024]{1,0:T(4,128)S(1)}, s32[4,1024]{1,0:T(4,128)}, u32[]{:S(2)}) copy-start(s32[4,1024]{1,0:T(4,128)} %param.13) | copy-start | bytes 49156
  6.5 3.4 %copy-start = (f32[16384,128]{1,0:T(8,128)}, f32[16384,128]{1,0:T(8,128)S(1)}, u32[]{:S(2)}) copy-start(f32[16384,128]{1,0:T(8,128)S(1)} %get-tuple-element.14.rows) | copy-start | bytes 25165828
  18.5 54.7 %collective-permute-start.3 = (f32[16,128]{1,0:T(8,128)S(1)}, f32[16,128]{1,0:T(8,128)S(1)}, u32[]{:S(2)}, u32[]{:S(2)}) collective-permute-start(f32[16,128]{1,0:T(8,128)S(1)} %get-tuple-element.24), channel_id=1, source_target_pairs={{24,0},{28,4},{0,8},{4,12},{8,16},{12,20},{16,24},{20,28},{25,1},{... | collective-permute-start | bytes 24584 | tf_op jit(solution)/shard_map/ppermute | solution.py:21
  20.1 49.3 %collective-permute-start.2 = (f32[16,128]{1,0:T(8,128)S(1)}, f32[16,128]{1,0:T(8,128)S(1)}, u32[]{:S(2)}, u32[]{:S(2)}) collective-permute-start(f32[16,128]{1,0:T(8,128)S(1)} %get-tuple-element.24), channel_id=1, source_target_pairs={{8,0},{12,4},{16,8},{20,12},{24,16},{28,20},{0,24},{4,28},{9,1},{1... | collective-permute-start | bytes 24584 | tf_op jit(solution)/shard_map/ppermute | solution.py:21
  22.3 47.0 %collective-permute-start.1 = (f32[16,128]{1,0:T(8,128)S(1)}, f32[16,128]{1,0:T(8,128)S(1)}, u32[]{:S(2)}, u32[]{:S(2)}) collective-permute-start(f32[16,128]{1,0:T(8,128)S(1)} %get-tuple-element.24), channel_id=1, source_target_pairs={{28,0},{0,4},{4,8},{8,12},{12,16},{16,20},{20,24},{24,28},{29,1},{... | collective-permute-start | bytes 24584 | tf_op jit(solution)/shard_map/ppermute | solution.py:21
  23.9 41.0 %collective-permute-start = (f32[16,128]{1,0:T(8,128)S(1)}, f32[16,128]{1,0:T(8,128)S(1)}, u32[]{:S(2)}, u32[]{:S(2)}) collective-permute-start(f32[16,128]{1,0:T(8,128)S(1)} %get-tuple-element.24), channel_id=1, source_target_pairs={{4,0},{8,4},{12,8},{16,12},{20,16},{24,20},{28,24},{0,28},{5,1},{9... | collective-permute-start | bytes 24584 | tf_op jit(solution)/shard_map/ppermute | solution.py:21
  27.1 4.6 %copy-start.1 = (f32[16384,128]{1,0:T(8,128)S(1)}, f32[16384,128]{1,0:T(8,128)}, u32[]{:S(2)}) copy-start(f32[16384,128]{1,0:T(8,128)} %copy-done) | copy-start | bytes 25165828
  27.8 2.5 %copy-start.6 = (s32[1024,1024]{1,0:T(8,128)S(1)}, s32[1024,1024]{1,0:T(8,128)}, u32[]{:S(2)}) copy-start(s32[1024,1024]{1,0:T(8,128)} %turn.1) | copy-start | bytes 12582916
  31.0 10.8 %copy-start.4 = (s32[8192,128]{1,0:T(8,128)}, s32[8192,128]{1,0:T(8,128)S(1)}, u32[]{:S(2)}) copy-start(s32[8192,128]{1,0:T(8,128)S(1)} %turn_rows.1.turns) | copy-start | bytes 12582916
  31.8 21.7 %copy-start.15 = (s32[4,1024]{1,0:T(4,128)S(1)}, s32[4,1024]{1,0:T(4,128)}, u32[]{:S(2)}) copy-start(s32[4,1024]{1,0:T(4,128)} %param.14) | copy-start | bytes 49156
  41.7 2.0 %copy-start.8 = (f32[8192,128]{1,0:T(8,128)}, f32[8192,128]{1,0:T(8,128)S(1)}, u32[]{:S(2)}) copy-start(f32[8192,128]{1,0:T(8,128)S(1)} %get-tuple-element.15.flow) | copy-start | bytes 12582916
  43.7 0.9 copy-start.13
  44.6 59.5 %copy-start.21 = (s32[4,192]{1,0:T(4,128)S(1)}, s32[4,192]{1,0:T(4,128)}, u32[]{:S(2)}) copy-start(s32[4,192]{1,0:T(4,128)} %param.16) | copy-start | bytes 9220
  44.6 105.8 %collective-permute-start.8 = (f32[1536,128]{1,0:T(8,128)}, f32[1536,128]{1,0:T(8,128)S(1)}, u32[]{:S(2)}, u32[]{:S(2)}) collective-permute-start(f32[1536,128]{1,0:T(8,128)} %get-tuple-element.16), channel_id=1, source_target_pairs={{28,0},{0,4},{4,8},{8,12},{12,16},{16,20},{20,24},{24,28},{29,1},{... | collective-permute-start | bytes 2359304 | tf_op jit(solution)/shard_map/ppermute | solution.py:21
  44.6 2.2 %copy-start.7 = (s32[1024,1024]{1,0:T(8,128)S(1)}, s32[1024,1024]{1,0:T(8,128)}, u32[]{:S(2)}) copy-start(s32[1024,1024]{1,0:T(8,128)} %turn.1) | copy-start | bytes 12582916
  46.8 2.2 %copy-start.9 = (f32[8192,128]{1,0:T(8,128)S(1)}, f32[8192,128]{1,0:T(8,128)}, u32[]{:S(2)}) copy-start(f32[8192,128]{1,0:T(8,128)} %copy-done.8) | copy-start | bytes 12582916
  64.9 85.6 %collective-permute-start.9 = (f32[1536,128]{1,0:T(8,128)}, f32[1536,128]{1,0:T(8,128)S(1)}, u32[]{:S(2)}, u32[]{:S(2)}) collective-permute-start(f32[1536,128]{1,0:T(8,128)} %get-tuple-element.17), channel_id=1, source_target_pairs={{4,0},{8,4},{12,8},{16,12},{20,16},{24,20},{28,24},{0,28},{5,1},{9... | collective-permute-start | bytes 2359304 | tf_op jit(solution)/shard_map/ppermute | solution.py:21
  69.3 81.2 %collective-permute-start.10 = (f32[1536,128]{1,0:T(8,128)}, f32[1536,128]{1,0:T(8,128)S(1)}, u32[]{:S(2)}, u32[]{:S(2)}) collective-permute-start(f32[1536,128]{1,0:T(8,128)} %get-tuple-element.18), channel_id=1, source_target_pairs={{24,0},{28,4},{0,8},{4,12},{8,16},{12,20},{16,24},{20,28},{25,1},{... | collective-permute-start | bytes 2359304 | tf_op jit(solution)/shard_map/ppermute | solution.py:21
  69.3 81.1 %collective-permute-start.11 = (f32[1536,128]{1,0:T(8,128)}, f32[1536,128]{1,0:T(8,128)S(1)}, u32[]{:S(2)}, u32[]{:S(2)}) collective-permute-start(f32[1536,128]{1,0:T(8,128)} %copy-done.13), channel_id=1, source_target_pairs={{8,0},{12,4},{16,8},{20,12},{24,16},{28,20},{0,24},{4,28},{9,1},{1... | collective-permute-start | bytes 2359304 | tf_op jit(solution)/shard_map/ppermute | solution.py:21
  87.6 15.0 %collective-permute-start.4 = (f32[192]{0:T(256)S(1)}, f32[192]{0:T(256)S(1)}, u32[]{:S(2)}, u32[]{:S(2)}) collective-permute-start(f32[192]{0:T(256)S(1)} %get-tuple-element.28), channel_id=1, source_target_pairs={{28,0},{0,4},{4,8},{8,12},{12,16},{16,20},{20,24},{24,28},{29,1},{... | collective-permute-start | bytes 2312 | tf_op jit(solution)/shard_map/ppermute | solution.py:21
  102.6 15.9 %collective-permute-start.7 = (f32[192]{0:T(256)S(1)}, f32[192]{0:T(256)S(1)}, u32[]{:S(2)}, u32[]{:S(2)}) collective-permute-start(f32[192]{0:T(256)S(1)} %get-tuple-element.29), channel_id=1, source_target_pairs={{8,0},{12,4},{16,8},{20,12},{24,16},{28,20},{0,24},{4,28},{9,1},{1... | collective-permute-start | bytes 2312 | tf_op jit(solution)/shard_map/ppermute | solution.py:21
  118.5 5.8 %collective-permute-start.6 = (f32[192]{0:T(256)S(1)}, f32[192]{0:T(256)S(1)}, u32[]{:S(2)}, u32[]{:S(2)}) collective-permute-start(f32[192]{0:T(256)S(1)} %get-tuple-element.30), channel_id=1, source_target_pairs={{24,0},{28,4},{0,8},{4,12},{8,16},{12,20},{16,24},{20,28},{25,1},{... | collective-permute-start | bytes 2312 | tf_op jit(solution)/shard_map/ppermute | solution.py:21
  124.3 26.0 %collective-permute-start.5 = (f32[192]{0:T(256)S(1)}, f32[192]{0:T(256)S(1)}, u32[]{:S(2)}, u32[]{:S(2)}) collective-permute-start(f32[192]{0:T(256)S(1)} %get-tuple-element.31), channel_id=1, source_target_pairs={{4,0},{8,4},{12,8},{16,12},{20,16},{24,20},{28,24},{0,28},{5,1},{9... | collective-permute-start | bytes 2312 | tf_op jit(solution)/shard_map/ppermute | solution.py:21
  124.4 3.4 %copy-start.2 = (f32[16384,128]{1,0:T(8,128)S(1)}, f32[16384,128]{1,0:T(8,128)}, u32[]{:S(2)}) copy-start(f32[16384,128]{1,0:T(8,128)} %copy-done) | copy-start | bytes 25165828
  127.7 2.2 %copy-start.5 = (s32[8192,128]{1,0:T(8,128)S(1)}, s32[8192,128]{1,0:T(8,128)}, u32[]{:S(2)}) copy-start(s32[8192,128]{1,0:T(8,128)} %copy-done.4) | copy-start | bytes 12582916
  129.9 2.2 %copy-start.10 = (f32[8192,128]{1,0:T(8,128)S(1)}, f32[8192,128]{1,0:T(8,128)}, u32[]{:S(2)}) copy-start(f32[8192,128]{1,0:T(8,128)} %copy-done.8) | copy-start | bytes 12582916
  150.5 3.4 %copy-start.3 = (f32[16384,128]{1,0:T(8,128)S(1)}, f32[16384,128]{1,0:T(8,128)}, u32[]{:S(2)}) copy-start(f32[16384,128]{1,0:T(8,128)} %copy-done) | copy-start | bytes 25165828
  (2 other events, 1.3 us)

commit v2 on v1

v2 whole, which is shorter than its diff:
```python
import functools

import jax
import jax.numpy as jnp
from jax import lax
from jax.experimental import pallas as pl
from jax.experimental.pallas import tpu as pltpu
from jax.sharding import PartitionSpec as P

SHIFTS = (2, -2, 1, -1)
SIDES = (2, 3, 0, 1)
EXACT = lax.Precision.HIGHEST
LANES = 128
MIB = 1 << 20
F32 = jnp.float32
VMEM_WHOLE = pl.BlockSpec(memory_space=pltpu.VMEM)
SMEM_WHOLE = pl.BlockSpec(memory_space=pltpu.SMEM)


def shifted(block, axis, distance):
    devices = range(lax.axis_size(axis))
    route = [((i - distance) % len(devices), i) for i in devices]
    return lax.ppermute(block, axis, route)


def partners(block, axis):
    count = lax.axis_size(axis)
    return [block] + [
        lax.ppermute(block, axis, [(i, i ^ other) for i in range(count)])
        for other in range(1, count)
    ]


def tree_sum(parts):
    while len(parts) > 1:
        parts = [parts[k] + parts[k + 1] for k in range(0, len(parts), 2)]
    return parts[0]


def params(mib):
    return pltpu.CompilerParams(vmem_limit_bytes=mib * MIB)


def cost(flops, moved):
    return pl.CostEstimate(flops=flops, bytes_accessed=moved, transcendentals=0)


def lane_sums(partial):
    ones = jnp.ones((8, LANES), F32)
    sums = lax.dot_general(
        ones, partial, (((1,), (1,)), ((), ())), preferred_element_type=F32, precision=EXACT
    )
    return sums[0:1, :]


def row_at(index, sub):
    return pl.ds(pl.multiple_of(index, sub), sub)


def to_rows(x_ref, rows_ref, first, count, sub):
    for group in range(count // 8):
        for q in range(sub):
            piece = x_ref[group * 8 : group * 8 + 8, q * LANES : (q + 1) * LANES]
            start = (first + group * 8) * sub + q
            rows_ref[pl.ds(start, 8, stride=sub), :] = piece


def cell_sum_kernel(block, sub, x_ref, sum_ref, rows_ref):
    step = pl.program_id(0)
    to_rows(x_ref, rows_ref, step * block, block, sub)
    partial = x_ref[:, 0:LANES]
    for q in range(1, sub):
        partial = partial + x_ref[:, q * LANES : (q + 1) * LANES]
    sums = lane_sums(partial)
    per_step = block // LANES
    for part in range(per_step):
        sum_ref[pl.ds(step * per_step + part, 1), :] = sums[:, part * LANES : (part + 1) * LANES]

    @pl.when(step == 0)
    def _():
        zeros = rows_ref.shape[0] - sub
        rows_ref[zeros:, :] = jnp.zeros((sub, LANES), F32)


def turn_rows_kernel(block, sub, x_ref, after_ref, rows_ref):
    to_rows(x_ref, rows_ref, pl.program_id(0) * block, block, sub)


def one_hot(index, count):
    rows = lax.broadcasted_iota(jnp.int32, (count, index.shape[1]), 0)
    return jnp.where(rows == index, 1.0, 0.0)


def look_up(table, index):
    picked = lax.dot_general(
        table.T,
        one_hot(index // LANES, table.shape[0]),
        (((1,), (0,)), ((), ())),
        preferred_element_type=F32,
        precision=EXACT,
    )
    return jnp.sum(picked * one_hot(index % LANES, LANES), axis=0, keepdims=True)


def scatter(index, values, height):
    high = jnp.where(index >= 0, index // LANES, -1)
    return lax.dot_general(
        one_hot(high, height) * values,
        one_hot(jnp.where(index >= 0, index % LANES, -1), LANES),
        (((1,), (1,)), ((), ())),
        preferred_element_type=F32,
        precision=EXACT,
    )


def source_kernel(sizes, home_cell, after_ref, node, outlet):
    cells, nodes, branches, cap, sub = sizes
    height = cells // LANES
    ids = lax.broadcasted_iota(jnp.int32, (1, nodes), 1).astype(F32) + 1.0
    number = jnp.zeros((height, LANES), F32)
    slot = jnp.zeros((height, LANES), F32)
    for j in range(branches):
        here = scatter(home_cell[j : j + 1, :], ids, height)
        number = number + here
        slot = slot + jnp.where(here > 0.0, j + 1.0, 0.0)
    node[...] = jnp.maximum(number.astype(jnp.int32) - 1, 0) * sub
    outlet[...] = slot.astype(jnp.int32) - 1


def gathered_flow(node, in_cell, fraction, rows, sizes):
    cells, nodes, branches, cap, sub = sizes
    parts = []
    for i in range(branches):
        cell = in_cell[i * nodes + node]
        parts.append(rows[row_at(cell * sub, sub), :] * fraction[cell])
    return tree_sum(parts)


def send_kernel(sizes, fraction, in_cell, send_node, send_outlet, rows, turns, *sends):
    cells, nodes, branches, cap, sub = sizes
    batch = 8
    for side, send in enumerate(sends):

        def body(step, carry, side=side, send=send):
            first = step * batch
            values = []
            for i in range(batch):
                slot = side * cap + first + i
                node = send_node[slot]
                value = gathered_flow(node, in_cell, fraction, rows, sizes)
                choice = turns[row_at(node * sub, sub), :]
                values.append(jnp.where(choice == send_outlet[slot], value, 0.0))
            for i in range(batch):
                send[row_at((first + i) * sub, sub), :] = values[i]
            return carry

        lax.fori_loop(0, cap // batch, body, 0)


def node_flow_kernel(sizes, fraction, in_cell, rows, turn, flow, demand, partial):
    cells, nodes, branches, cap, sub = sizes

    def group(step, carry):
        first = step * 8
        values = [
            gathered_flow(first + i, in_cell, fraction, rows, sizes) for i in range(8)
        ]
        for i in range(8):
            flow[row_at((first + i) * sub, sub), :] = values[i]
        totals = [jnp.zeros((8, LANES), F32)] * branches
        for q in range(sub):
            value = flow[pl.ds(first * sub + q, 8, stride=sub), :]
            choice = turn[pl.ds(pl.multiple_of(first, 8), 8), q * LANES : (q + 1) * LANES]
            totals = [
                total + jnp.where(choice == j, value, 0.0) for j, total in enumerate(totals)
            ]
        for j in range(branches):
            partial[j, pl.ds(pl.multiple_of(first, 8), 8), :] = totals[j]
        return carry

    lax.fori_loop(0, nodes // 8, group, 0)
    for j in range(branches):
        demand[j : j + 1, :] = lane_sums(partial[j])


def theta_kernel(
    sizes, commodities, table, place, out_valid, in_cell, home_cell, send_node, fraction, *rest
):
    cells, nodes, branches, cap, sub = sizes
    parts, (keep, home_theta, slot_theta) = rest[:-3], rest[-3:]
    height = cells // LANES
    demand = tree_sum([part[...] for part in parts]) * (1.0 / commodities)
    lookup = table[...]
    theta = jnp.ones((1, nodes), F32)
    for j in range(branches):
        room = look_up(lookup, place[j : j + 1, :])
        ratio = room / jnp.maximum(demand[j : j + 1, :], room)
        theta = jnp.minimum(theta, jnp.where(out_valid[j : j + 1, :] > 0, ratio, 1.0))
    cell_theta = jnp.zeros((height, LANES), F32)
    into = jnp.zeros((height, LANES), F32)
    for j in range(branches):
        cell_theta = cell_theta + scatter(in_cell[j : j + 1, :], theta, height)
        into = into + scatter(home_cell[j : j + 1, :], theta, height)
    keep[...] = 1.0 - cell_theta * fraction[...]
    home_theta[...] = into
    tall = jnp.concatenate(
        [theta[:, q * LANES : (q + 1) * LANES] for q in range(nodes // LANES)], axis=0
    )
    for side in range(4):
        slot_theta[side : side + 1, :] = look_up(tall, send_node[side : side + 1, :])


def base_kernel(sizes, keep, home_theta, node_row, outlet, rows, turns, flow, base):
    cells, nodes, branches, cap, sub = sizes
    batch = 8

    def body(step, carry):
        first = step * batch
        for i in range(batch):
            cell = first + i
            at = row_at(node_row[cell], sub)
            moved = jnp.where(turns[at, :] == outlet[cell], flow[at, :], 0.0)
            kept = rows[row_at(cell * sub, sub), :] * keep[cell]
            base[row_at(cell * sub, sub), :] = kept + moved * home_theta[cell]
        return carry

    lax.fori_loop(0, cells // batch, body, 0)


def finish_kernel(sizes, block, scale, land, *rest):
    cells, nodes, branches, cap, sub = sizes
    received, (base_in, out, base) = rest[:4], rest[4:]
    step = pl.program_id(0)
    batch = 8

    @pl.when(step == 0)
    def _():
        for side in range(4):

            def body(turn_no, carry, side=side):
                first = turn_no * batch
                stores = []
                for i in range(batch):
                    slot = side * cap + first + i
                    at = row_at(land[slot], sub)
                    value = received[side][row_at((first + i) * sub, sub), :] * scale[slot]
                    stores.append((at, base[at, :] + value))
                for at, value in stores:
                    base[at, :] = value
                return carry

            lax.fori_loop(0, cap // batch, body, 0)

    for group in range(block // 8):
        for q in range(sub):
            start = (step * block + group * 8) * sub + q
            out[group * 8 : group * 8 + 8, q * LANES : (q + 1) * LANES] = base[
                pl.ds(start, 8, stride=sub), :
            ]


def on_device(occupancy, capacity, jam, wave, node_in, node_out, send_list, recv_list, turn):
    cells, width = occupancy.shape
    branches, nodes = node_in.shape
    cap = send_list.shape[1]
    sub = width // LANES
    sizes = (cells, nodes, branches, cap, sub)
    regions = lax.axis_size("region")
    commodities = width * lax.axis_size("dest")
    region_no = lax.axis_index("region")
    height = cells // LANES
    per_cell = (height, LANES)
    block = 256
    row_bytes = width * 4
    occupancy = pltpu.with_memory_space_constraint(occupancy, pltpu.HBM)
    turn = pltpu.with_memory_space_constraint(turn, pltpu.HBM)

    local_sum, rows = pl.pallas_call(
        functools.partial(cell_sum_kernel, block, sub),
        grid=(cells // block,),
        in_specs=[pl.BlockSpec((block, width), lambda i: (i, 0))],
        out_specs=[pl.BlockSpec(per_cell, lambda i: (0, 0)), VMEM_WHOLE],
        out_shape=[
            jax.ShapeDtypeStruct(per_cell, F32),
            pltpu.VMEM(((cells + 1) * sub, LANES), F32),
        ],
        compiler_params=params(8),
        cost_estimate=cost(cells * width, cells * row_bytes),
        name="cell_sum",
    )(occupancy)

    sums = partners(local_sum, "dest")

    turn_block = 128
    turns = pl.pallas_call(
        functools.partial(turn_rows_kernel, turn_block, sub),
        grid=(nodes // turn_block,),
        in_specs=[
            pl.BlockSpec((turn_block, width), lambda i: (i, 0)),
            pl.BlockSpec(memory_space=pl.ANY),
        ],
        out_specs=VMEM_WHOLE,
        out_shape=pltpu.VMEM((nodes * sub, LANES), jnp.int32),
        compiler_params=params(6),
        cost_estimate=cost(0, nodes * row_bytes),
        name="turn_rows",
    )(turn, local_sum)

    in_cell = jnp.where(node_in >= 0, node_in, cells).reshape(-1)
    slots = jnp.concatenate([send_list[side : side + 1] for side in SIDES])
    lands = jnp.concatenate([recv_list[side : side + 1] for side in SIDES])
    send_node = jnp.where(slots >= 0, slots % nodes, 0)
    send_outlet = jnp.where(slots >= 0, slots // nodes, -1)
    land = jnp.where(lands >= 0, lands, cells) * sub
    out_valid = node_out >= 0
    out_cell = jnp.maximum(node_out, 0)
    offset = (out_cell // cells - region_no) % regions
    out_local = out_cell % cells
    home_cell = jnp.where(out_valid & (offset == 0), out_local, -1)
    sector = jnp.zeros_like(offset)
    for number, stride in enumerate(SHIFTS):
        sector = jnp.where(offset == stride % regions, number + 1, sector)
    place = sector * cells + out_local

    source_node, source_outlet = pl.pallas_call(
        functools.partial(source_kernel, sizes),
        in_specs=[VMEM_WHOLE, pl.BlockSpec(memory_space=pl.ANY)],
        out_specs=[VMEM_WHOLE] * 2,
        out_shape=[jax.ShapeDtypeStruct(per_cell, jnp.int32)] * 2,
        compiler_params=params(8),
        cost_estimate=cost(branches * nodes * cells * 2, nodes * 64),
        name="source_of_cell",
    )(home_cell, local_sum)

    vehicles = tree_sum(sums) / commodities
    cap_of = capacity.reshape(per_cell)
    fraction = jnp.minimum(vehicles, cap_of) / vehicles
    supply = jnp.minimum(cap_of, wave.reshape(per_cell) * (jam.reshape(per_cell) - vehicles))
    weights = jnp.concatenate([fraction.reshape(-1), jnp.zeros((LANES,), F32)])

    sends = []
    for pair in range(2):
        of_pair = slice(2 * pair, 2 * pair + 2)
        sends += pl.pallas_call(
            functools.partial(send_kernel, sizes),
            in_specs=[SMEM_WHOLE] * 4 + [VMEM_WHOLE] * 2,
            out_specs=[VMEM_WHOLE] * 2,
            out_shape=[pltpu.VMEM((cap * sub, LANES), F32)] * 2,
            compiler_params=params(4),
            cost_estimate=cost(cap * width * 20, cap * row_bytes * 10),
            name="send_rows",
        )(
            weights, in_cell, send_node[of_pair].reshape(-1), send_outlet[of_pair].reshape(-1),
            rows, turns,
        )
    arrived = [shifted(send, "region", stride) for send, stride in zip(sends, SHIFTS)]

    table = jnp.concatenate(
        [supply] + [shifted(supply, "region", -stride) for stride in SHIFTS]
    )

    flow, demand = pl.pallas_call(
        functools.partial(node_flow_kernel, sizes),
        in_specs=[SMEM_WHOLE] * 2 + [VMEM_WHOLE] * 2,
        out_specs=[VMEM_WHOLE] * 2,
        out_shape=[
            pltpu.VMEM((nodes * sub, LANES), F32),
            jax.ShapeDtypeStruct((branches, nodes), F32),
        ],
        scratch_shapes=[pltpu.VMEM((branches, nodes, LANES), F32)],
        compiler_params=params(12),
        cost_estimate=cost(nodes * width * 16, nodes * row_bytes * 6),
        name="node_flow",
    )(weights, in_cell, rows, turn)

    demands = partners(demand, "dest")
    keep, home_theta, slot_theta = pl.pallas_call(
        functools.partial(theta_kernel, sizes, commodities),
        out_shape=[jax.ShapeDtypeStruct(per_cell, F32)] * 2
        + [jax.ShapeDtypeStruct((4, cap), F32)],
        compiler_params=params(12),
        cost_estimate=cost(branches * nodes * cells * 8, nodes * 256),
        name="theta",
    )(
        table, place, out_valid.astype(jnp.int32), node_in, home_cell, send_node, fraction,
        *demands,
    )
    scale = jnp.concatenate(
        [shifted(slot_theta[number], "region", stride) for number, stride in enumerate(SHIFTS)]
    )

    base = pl.pallas_call(
        functools.partial(base_kernel, sizes),
        in_specs=[SMEM_WHOLE] * 4 + [VMEM_WHOLE] * 3,
        out_specs=VMEM_WHOLE,
        out_shape=pltpu.VMEM(((cells + 1) * sub, LANES), F32),
        compiler_params=params(4),
        cost_estimate=cost(cells * width * 4, cells * row_bytes * 4),
        name="home_inflow",
    )(
        keep.reshape(-1), home_theta.reshape(-1), source_node.reshape(-1),
        source_outlet.reshape(-1), rows, turns, flow,
    )

    out, _ = pl.pallas_call(
        functools.partial(finish_kernel, sizes, block),
        grid=(cells // block,),
        in_specs=[SMEM_WHOLE] * 2 + [VMEM_WHOLE] * 5,
        out_specs=[pl.BlockSpec((block, width), lambda i: (i, 0)), VMEM_WHOLE],
        out_shape=[
            jax.ShapeDtypeStruct((cells, width), F32),
            pltpu.VMEM(((cells + 1) * sub, LANES), F32),
        ],
        input_output_aliases={6: 1},
        compiler_params=params(8),
        cost_estimate=cost(cells * width, cells * row_bytes),
        name="finish",
    )(scale, land.reshape(-1), *arrived, base)
    return out


def solution(mesh):
    return jax.shard_map(
        on_device,
        mesh=mesh,
        in_specs=(
            P("region", "dest"),
            P("region"),
            P("region"),
            P("region"),
            P(None, "region"),
            P(None, "region"),
            P("region", None),
            P("region", None),
            P("region", "dest"),
        ),
        out_specs=P("region", "dest"),
        check_vma=False,
    )
```

time: 163 us -> 157 us (0.963)
  waiting for transfers between devices: 25.4 us -> 53.3 us
  blocking collectives: 19.2 us -> 0 us
  local copies, waits for them, and re-layouts: 32.2 us -> 21.8 us
  other arithmetic: 7.39 us -> 0.2 us
  matrix products: 3.74 us -> 0 us
  Pallas kernels: 56 us -> 59.6 us
  starting transfers between devices: 18.3 us -> 21.4 us
    ppermute x12, waiting for transfers between devices: 25.4 us -> 50.6 us  [shifted(): return lax.ppermute(block, axis, route)]
    psum x2 -> x0, blocking collectives: 19.2 us -> none  [the longest x1 10.7 us: on_device(): demand = lax.psum(demand, 'dest') / commodities]
    unnamed x50 -> x36, local copies, waits for them, and re-layouts: 30.4 us -> 21.4 us
    pallas_call x4 -> x5, Pallas kernels: 33.6 us -> 25.2 us  [the longest x2 10.5 us: on_device(): pl.pallas_call(functools.partial(send_kernel, sizes), in_specs=[SMEM_WHOL...]
    reduce_or x1 -> x0, other arithmetic: 5.99 us -> none  [on_device(): jnp.any(node_in[:, :, None] == cell_ids[None, None, :], axis=0).astype(f32)]
    pallas_call x1, Pallas kernels: 9.92 us -> 15 us  [on_device(): pl.pallas_call(functools.partial(node_flow_kernel, sizes), in_specs=[SMEM...]
    pallas_call x1, Pallas kernels: 0.72 us -> 4.8 us  [on_device(): pl.pallas_call(functools.partial(turn_rows_kernel, turn_block, sub), grid...]
    pallas_call x1, Pallas kernels: 3.1 us -> 7.15 us  [on_device(): pl.pallas_call(functools.partial(cell_sum_kernel, block, sub), grid=(cell...]
  transfers between devices with their start and end apart: 12 -> 18, of which waited for: 3 -> 5; matrix products, arithmetic and copies ran while one was open for 8% -> 0% of each run, Pallas kernels for 27% -> 29%
where the time goes in v2:
time: 157 us
  Pallas kernels  59.6 us (38%)
  waiting for transfers between devices  53.3 us (34%)
  local copies, waits for them, and re-layouts  21.8 us (14%)
  starting transfers between devices  21.4 us (14%)
    ppermute x12, waiting for transfers between devices, shifted(): return lax.ppermute(block, axis, route)  50.6 us
    unnamed x36, local copies, waits for them, and re-layouts  21.4 us
    ppermute x12, starting transfers between devices, shifted(): return lax.ppermute(block, axis, route)  17.5 us
    pallas_call x1, Pallas kernels, on_device(): pl.pallas_call(functools.partial(node_flow_kernel, sizes), in_specs=[SMEM...  15 us
    pallas_call x2, Pallas kernels, on_device(): pl.pallas_call(functools.partial(send_kernel, sizes), in_specs=[SMEM_WHOL...  10.5 us
    pallas_call x1, Pallas kernels, on_device(): pl.pallas_call(functools.partial(finish_kernel, sizes, block), grid=(cell...  7.4 us
    pallas_call x1, Pallas kernels, on_device(): pl.pallas_call(functools.partial(cell_sum_kernel, block, sub), grid=(cell...  7.15 us
    pallas_call x1, Pallas kernels, on_device(): pl.pallas_call(functools.partial(base_kernel, sizes), in_specs=[SMEM_WHOL...  6.99 us
  transfers between devices with their start and end apart: 18, of which 5 were waited for; matrix products, arithmetic and copies ran while one was open for 0% of the time, Pallas kernels for 29%

profile of v2, /device:TPU:0, one launch (start us, length us, event | category | flops | bytes accessed | tf_op | source)
XLA Modules:
  0.0 156.6 jit_solution(10471354092222017898)
XLA Ops:
  0.0 7.1 %cell_sum.1 = (f32[16,128]{1,0:T(8,128)S(1)}, f32[16392,128]{1,0:T(8,128)S(1)}) custom-call(f32[2048,1024]{1,0:T(8,128)} %x_ref.2), custom_call_target="tpu_custom_call" | custom-call | flops 2097152 | bytes 8388608 | tf_op jit(solution)/shard_map/cell_sum/pallas_call | solution.py:278
  7.2 3.3 %copy-done = f32[16392,128]{1,0:T(8,128)} copy-done((f32[16392,128]{1,0:T(8,128)}, f32[16392,128]{1,0:T(8,128)S(1)}, u32[]{:S(2)}) %copy-start) | copy-done | bytes 8392728
  10.5 0.5 collective-permute-start
  11.0 2.5 %collective-permute-start.1 = (f32[16,128]{1,0:T(8,128)S(1)}, f32[16,128]{1,0:T(8,128)S(1)}, u32[]{:S(2)}, u32[]{:S(2)}) collective-permute-start(f32[16,128]{1,0:T(8,128)S(1)} %get-tuple-element.19.after_ref), channel_id=1, source_target_pairs={{0,2},{1,3},{2,0},{3,1},{4,6},{5,7},{6,4},{7,5},{8,10},{9,11},{10,... | collective-permute-start | bytes 24584 | tf_op jit(solution)/shard_map/ppermute | solution.py:29
  13.4 0.1 collective-permute-start.2
  13.8 1.3 collective-permute-done.1
  15.1 1.4 collective-permute-done.2
  16.6 3.7 %collective-permute-start.3 = (f32[16,128]{1,0:T(8,128)S(1)}, f32[16,128]{1,0:T(8,128)S(1)}, u32[]{:S(2)}, u32[]{:S(2)}) collective-permute-start(f32[16,128]{1,0:T(8,128)S(1)} %get-tuple-element.36), channel_id=1, source_target_pairs={{8,0},{12,4},{16,8},{20,12},{24,16},{28,20},{0,24},{4,28},{9,1},{1... | collective-permute-start | bytes 24584 | tf_op jit(solution)/shard_map/ppermute | solution.py:23
  20.2 4.8 %turn_rows.1.turns = s32[8192,128]{1,0:T(8,128)S(1)} custom-call(s32[1024,1024]{1,0:T(8,128)} %x_ref.3, f32[16,128]{1,0:T(8,128)S(1)} %get-tuple-element.19.after_ref), custom_call_target="tpu_custom_call" | custom-call | bytes 4194304 | tf_op jit(solution)/shard_map/turn_rows/pallas_call | solution.py:295
  25.1 2.0 %copy-done.4 = s32[8192,128]{1,0:T(8,128)} copy-done((s32[8192,128]{1,0:T(8,128)}, s32[8192,128]{1,0:T(8,128)S(1)}, u32[]{:S(2)}) %copy-start.4) | copy-done | bytes 4194328
  27.1 0.1 reshape.48.send_node
  27.3 0.1 reshape.47.send_outlet
  27.4 4.8 %collective-permute-start.5 = (f32[16,128]{1,0:T(8,128)S(1)}, f32[16,128]{1,0:T(8,128)S(1)}, u32[]{:S(2)}, u32[]{:S(2)}) collective-permute-start(f32[16,128]{1,0:T(8,128)S(1)} %get-tuple-element.36), channel_id=1, source_target_pairs={{4,0},{8,4},{12,8},{16,12},{20,16},{24,20},{28,24},{0,28},{5,1},{9... | collective-permute-start | bytes 24584 | tf_op jit(solution)/shard_map/ppermute | solution.py:23
  32.2 3.4 %copy-done.1 = f32[16392,128]{1,0:T(8,128)S(1)} copy-done((f32[16392,128]{1,0:T(8,128)S(1)}, f32[16392,128]{1,0:T(8,128)}, u32[]{:S(2)}) %copy-start.1) | copy-done | bytes 8392728
  35.6 15.0 %node_flow.1 = (f32[8192,128]{1,0:T(8,128)S(1)}, f32[4,1024]{1,0:T(4,128)S(1)}) custom-call(f32[2176]{0:T(1024)S(1)} %concatenate.21.fraction, s32[4096]{0:T(1024)S(1)} %bitcast.28, f32[16392,128]{1,0:T(8,128)S(1)} %copy-done.1, s32[1024,1024]{1,0:T(8,128)} %x_ref.3), custom_call_target="tpu_custom_call" | custom-call | flops 16777216 | bytes 25165824 | tf_op jit(solution)/shard_map/node_flow/pallas_call | solution.py:362
  50.7 4.8 %copy-done.2 = f32[16392,128]{1,0:T(8,128)S(1)} copy-done((f32[16392,128]{1,0:T(8,128)S(1)}, f32[16392,128]{1,0:T(8,128)}, u32[]{:S(2)}) %copy-start.2) | copy-done | bytes 8392728
  55.5 5.3 %send_rows.3 = (f32[1536,128]{1,0:T(8,128)}, f32[1536,128]{1,0:T(8,128)}) custom-call(f32[2176]{0:T(1024)S(1)} %concatenate.21.fraction, s32[4096]{0:T(1024)S(1)} %bitcast.29, s32[384]{0:T(512)S(1)} %reshape.48.send_node, s32[384]{0:T(512)S(1)} %reshape.49.send_outlet, f32[16392,128]{1,0:T(8,128)S(1)} %copy-done.2, s32[8192,128]{1,0:T(8,128)S(1)} %copy-done.5), custom_call_target="tpu_custom_call" | custom-call | flops 3932160 | bytes 7864320 | tf_op jit(solution)/shard_map/send_rows/pallas_call | solution.py:344
  60.8 5.2 %send_rows.2 = (f32[1536,128]{1,0:T(8,128)}, f32[1536,128]{1,0:T(8,128)}) custom-call(f32[2176]{0:T(1024)S(1)} %concatenate.21.fraction, s32[4096]{0:T(1024)S(1)} %bitcast.30, s32[384]{0:T(512)S(1)} %reshape.46.send_node, s32[384]{0:T(512)S(1)} %reshape.47.send_outlet, f32[16392,128]{1,0:T(8,128)S(1)} %copy-done.2, s32[8192,128]{1,0:T(8,128)S(1)} %copy-done.5), custom_call_target="tpu_custom_call" | custom-call | flops 3932160 | bytes 7864320 | tf_op jit(solution)/shard_map/send_rows/pallas_call | solution.py:344
  66.0 0.7 collective-permute-start.8
  66.8 4.8 %collective-permute-start.17 = (f32[1536,128]{1,0:T(8,128)}, f32[1536,128]{1,0:T(8,128)S(1)}, u32[]{:S(2)}, u32[]{:S(2)}) collective-permute-start(f32[1536,128]{1,0:T(8,128)} %get-tuple-element.26), channel_id=1, source_target_pairs={{4,0},{8,4},{12,8},{16,12},{20,16},{24,20},{28,24},{0,28},{5,1},{9... | collective-permute-start | bytes 2359304 | tf_op jit(solution)/shard_map/ppermute | solution.py:23
  71.6 3.8 %collective-permute-start.15 = (f32[1536,128]{1,0:T(8,128)}, f32[1536,128]{1,0:T(8,128)S(1)}, u32[]{:S(2)}, u32[]{:S(2)}) collective-permute-start(f32[1536,128]{1,0:T(8,128)} %get-tuple-element.24), channel_id=1, source_target_pairs={{8,0},{12,4},{16,8},{20,12},{24,16},{28,20},{0,24},{4,28},{9,1},{1... | collective-permute-start | bytes 2359304 | tf_op jit(solution)/shard_map/ppermute | solution.py:23
  75.4 5.9 %theta.1 = (f32[16,128]{1,0:T(8,128)S(1)}, f32[16,128]{1,0:T(8,128)S(1)}, f32[4,192]{1,0:T(4,128)S(1)}) custom-call(f32[80,128]{1,0:T(8,128)S(1)} %constant_dynamic-update-slice_fusion.table, s32[4,1024]{1,0:T(4,128)S(1)} %get-tuple-element.38.place, s32[4,1024]{1,0:T(4,128)S(1)} %fusion.10.out_valid, s32[4,1024]{1,0:T(4,128)S(1)} %copy-done.9, ...), custom_call_target="tpu_custom_call" | custom-call | flops 67108864 | bytes 262144 | tf_op jit(solution)/shard_map/theta/pallas_call | solution.py:377
  81.5 42.6 %collective-permute-done.10 = f32[192]{0:T(256)S(1)} collective-permute-done((f32[192]{0:T(256)S(1)}, f32[192]{0:T(256)S(1)}, u32[]{:S(2)}, u32[]{:S(2)}) %collective-permute-start.10) | collective-permute-done | bytes 800 | tf_op jit(solution)/shard_map/ppermute | solution.py:23
  124.1 3.6 %collective-permute-done.11 = f32[192]{0:T(256)S(1)} collective-permute-done((f32[192]{0:T(256)S(1)}, f32[192]{0:T(256)S(1)}, u32[]{:S(2)}, u32[]{:S(2)}) %collective-permute-start.11) | collective-permute-done | bytes 800 | tf_op jit(solution)/shard_map/ppermute | solution.py:23
  127.6 1.8 %source_of_cell.1 = (s32[16,128]{1,0:T(8,128)S(1)}, s32[16,128]{1,0:T(8,128)S(1)}) custom-call(s32[4,1024]{1,0:T(4,128)S(1)} %get-tuple-element.37.home_cell, f32[16,128]{1,0:T(8,128)S(1)} %get-tuple-element.19.after_ref), custom_call_target="tpu_custom_call" | custom-call | flops 16777216 | bytes 65536 | tf_op jit(solution)/shard_map/source_of_cell/pallas_call | solution.py:325
  129.5 4.4 %collective-permute-done.12 = f32[192]{0:T(256)S(1)} collective-permute-done((f32[192]{0:T(256)S(1)}, f32[192]{0:T(256)S(1)}, u32[]{:S(2)}, u32[]{:S(2)}) %collective-permute-start.12) | collective-permute-done | bytes 800 | tf_op jit(solution)/shard_map/ppermute | solution.py:23
  133.9 0.4 collective-permute-start.13
  134.3 3.4 %copy-done.3 = f32[16392,128]{1,0:T(8,128)S(1)} copy-done((f32[16392,128]{1,0:T(8,128)S(1)}, f32[16392,128]{1,0:T(8,128)}, u32[]{:S(2)}) %copy-start.3) | copy-done | bytes 8392728
  137.7 2.2 %copy-done.6 = s32[8192,128]{1,0:T(8,128)S(1)} copy-done((s32[8192,128]{1,0:T(8,128)S(1)}, s32[8192,128]{1,0:T(8,128)}, u32[]{:S(2)}) %copy-start.6) | copy-done | bytes 4194328
  139.9 2.2 %copy-done.8 = f32[8192,128]{1,0:T(8,128)S(1)} copy-done((f32[8192,128]{1,0:T(8,128)S(1)}, f32[8192,128]{1,0:T(8,128)}, u32[]{:S(2)}) %copy-start.8) | copy-done | bytes 4194328
  142.0 7.0 %home_inflow.1.rest_4_ = f32[16392,128]{1,0:T(8,128)S(1)} custom-call(f32[2048]{0:T(1024)S(1)} %bitcast.32, f32[2048]{0:T(1024)S(1)} %bitcast.33, s32[2048]{0:T(1024)S(1)} %bitcast.34, s32[2048]{0:T(1024)S(1)} %bitcast.35, f32[16392,128]{1,0:T(8,128)S(1)} %copy-done.3, s32[8192,128]{1,0:T(8,128)S(1)} %copy-done.6, f32[8192,128]{1,0:T(8,128)S(1)} %copy-done.8), custom_call_target="tpu_custom_call" | custom-call | flops 8388608 | bytes 33554432 | tf_op jit(solution)/shard_map/home_inflow/pallas_call | solution.py:392
  149.2 7.4 %finish.1 = (f32[2048,1024]{1,0:T(8,128)}, f32[16392,128]{1,0:T(8,128)S(1)}) custom-call(f32[768]{0:T(1024)S(1)} %pad_maximum_fusion.scale, s32[768]{0:T(1024)S(1)} %fusion.8.land, f32[1536,128]{1,0:T(8,128)S(1)} %collective-permute-done.14.rest_0_, f32[1536,128]{1,0:T(8,128)S(1)} %collective-permute-done.15.rest_1_, ...), custom_call_target="tpu_custom_call", output_to_operand_aliasing={{1}: (6, {})} | custom-call | flops 2097152 | bytes 8388608 | tf_op jit(solution)/shard_map/finish/pallas_call | solution.py:405
  (69 shorter events, 0.8 us)
Async XLA Ops:
  0.0 13.6 %copy-start.9 = (s32[4,1024]{1,0:T(4,128)S(1)}, s32[4,1024]{1,0:T(4,128)}, u32[]{:S(2)}) copy-start(s32[4,1024]{1,0:T(4,128)} %in_cell.1) | copy-start | bytes 49156
  0.0 13.6 %copy-start.14 = (s32[4,192]{1,0:T(4,128)S(1)}, s32[4,192]{1,0:T(4,128)}, u32[]{:S(2)}) copy-start(s32[4,192]{1,0:T(4,128)} %param.15) | copy-start | bytes 9220
  0.0 13.6 %copy-start.10 = (s32[4,1024]{1,0:T(4,128)S(1)}, s32[4,1024]{1,0:T(4,128)}, u32[]{:S(2)}) copy-start(s32[4,1024]{1,0:T(4,128)} %param.14) | copy-start | bytes 49156
  0.0 16.5 %copy-start.11 = (f32[2048]{0:T(1024)S(1)}, f32[2048]{0:T(1024)}, u32[]{:S(2)}) copy-start(f32[2048]{0:T(1024)} %param.10) | copy-start | bytes 24580
  0.0 16.5 %copy-start.12 = (f32[2048]{0:T(1024)S(1)}, f32[2048]{0:T(1024)}, u32[]{:S(2)}) copy-start(f32[2048]{0:T(1024)} %param.11) | copy-start | bytes 24580
  0.0 16.5 %copy-start.13 = (f32[2048]{0:T(1024)S(1)}, f32[2048]{0:T(1024)}, u32[]{:S(2)}) copy-start(f32[2048]{0:T(1024)} %param.12) | copy-start | bytes 24580
  0.0 20.2 %copy-start.15 = (s32[4,192]{1,0:T(4,128)S(1)}, s32[4,192]{1,0:T(4,128)}, u32[]{:S(2)}) copy-start(s32[4,192]{1,0:T(4,128)} %param.16) | copy-start | bytes 9220
  7.2 3.3 %copy-start = (f32[16392,128]{1,0:T(8,128)}, f32[16392,128]{1,0:T(8,128)S(1)}, u32[]{:S(2)}) copy-start(f32[16392,128]{1,0:T(8,128)S(1)} %get-tuple-element.20.rows) | copy-start | bytes 25178116
  10.5 3.3 %collective-permute-start = (f32[16,128]{1,0:T(8,128)S(1)}, f32[16,128]{1,0:T(8,128)S(1)}, u32[]{:S(2)}, u32[]{:S(2)}) collective-permute-start(f32[16,128]{1,0:T(8,128)S(1)} %get-tuple-element.19.after_ref), channel_id=1, source_target_pairs={{0,1},{1,0},{2,3},{3,2},{4,5},{5,4},{6,7},{7,6},{8,9},{9,8},{10,11... | collective-permute-start | bytes 24584 | tf_op jit(solution)/shard_map/ppermute | solution.py:29
  11.0 4.1 %collective-permute-start.1 = (f32[16,128]{1,0:T(8,128)S(1)}, f32[16,128]{1,0:T(8,128)S(1)}, u32[]{:S(2)}, u32[]{:S(2)}) collective-permute-start(f32[16,128]{1,0:T(8,128)S(1)} %get-tuple-element.19.after_ref), channel_id=1, source_target_pairs={{0,2},{1,3},{2,0},{3,1},{4,6},{5,7},{6,4},{7,5},{8,10},{9,11},{10,... | collective-permute-start | bytes 24584 | tf_op jit(solution)/shard_map/ppermute | solution.py:29
  13.4 3.1 %collective-permute-start.2 = (f32[16,128]{1,0:T(8,128)S(1)}, f32[16,128]{1,0:T(8,128)S(1)}, u32[]{:S(2)}, u32[]{:S(2)}) collective-permute-start(f32[16,128]{1,0:T(8,128)S(1)} %get-tuple-element.19.after_ref), channel_id=1, source_target_pairs={{0,3},{1,2},{2,1},{3,0},{4,7},{5,6},{6,5},{7,4},{8,11},{9,10},{10,... | collective-permute-start | bytes 24584 | tf_op jit(solution)/shard_map/ppermute | solution.py:29
  16.6 49.4 %collective-permute-start.3 = (f32[16,128]{1,0:T(8,128)S(1)}, f32[16,128]{1,0:T(8,128)S(1)}, u32[]{:S(2)}, u32[]{:S(2)}) collective-permute-start(f32[16,128]{1,0:T(8,128)S(1)} %get-tuple-element.36), channel_id=1, source_target_pairs={{8,0},{12,4},{16,8},{20,12},{24,16},{28,20},{0,24},{4,28},{9,1},{1... | collective-permute-start | bytes 24584 | tf_op jit(solution)/shard_map/ppermute | solution.py:23
  27.4 39.3 %collective-permute-start.4 = (f32[16,128]{1,0:T(8,128)S(1)}, f32[16,128]{1,0:T(8,128)S(1)}, u32[]{:S(2)}, u32[]{:S(2)}) collective-permute-start(f32[16,128]{1,0:T(8,128)S(1)} %get-tuple-element.36), channel_id=1, source_target_pairs={{24,0},{28,4},{0,8},{4,12},{8,16},{12,20},{16,24},{20,28},{25,1},{... | collective-permute-start | bytes 24584 | tf_op jit(solution)/shard_map/ppermute | solution.py:23
  27.4 39.3 %collective-permute-start.5 = (f32[16,128]{1,0:T(8,128)S(1)}, f32[16,128]{1,0:T(8,128)S(1)}, u32[]{:S(2)}, u32[]{:S(2)}) collective-permute-start(f32[16,128]{1,0:T(8,128)S(1)} %get-tuple-element.36), channel_id=1, source_target_pairs={{4,0},{8,4},{12,8},{16,12},{20,16},{24,20},{28,24},{0,28},{5,1},{9... | collective-permute-start | bytes 24584 | tf_op jit(solution)/shard_map/ppermute | solution.py:23
  32.2 34.6 %collective-permute-start.6 = (f32[16,128]{1,0:T(8,128)S(1)}, f32[16,128]{1,0:T(8,128)S(1)}, u32[]{:S(2)}, u32[]{:S(2)}) collective-permute-start(f32[16,128]{1,0:T(8,128)S(1)} %get-tuple-element.36), channel_id=1, source_target_pairs={{28,0},{0,4},{4,8},{8,12},{12,16},{16,20},{20,24},{24,28},{29,1},{... | collective-permute-start | bytes 24584 | tf_op jit(solution)/shard_map/ppermute | solution.py:23
  32.2 3.4 %copy-start.1 = (f32[16392,128]{1,0:T(8,128)S(1)}, f32[16392,128]{1,0:T(8,128)}, u32[]{:S(2)}) copy-start(f32[16392,128]{1,0:T(8,128)} %copy-done) | copy-start | bytes 25178116
  35.6 15.1 %copy-start.5 = (s32[8192,128]{1,0:T(8,128)S(1)}, s32[8192,128]{1,0:T(8,128)}, u32[]{:S(2)}) copy-start(s32[8192,128]{1,0:T(8,128)} %copy-done.4) | copy-start | bytes 12582916
  50.6 15.4 %copy-start.7 = (f32[8192,128]{1,0:T(8,128)}, f32[8192,128]{1,0:T(8,128)S(1)}, u32[]{:S(2)}) copy-start(f32[8192,128]{1,0:T(8,128)S(1)} %get-tuple-element.31.flow) | copy-start | bytes 12582916
  50.6 21.0 %collective-permute-start.7 = (f32[4,1024]{1,0:T(4,128)S(1)}, f32[4,1024]{1,0:T(4,128)S(1)}, u32[]{:S(2)}, u32[]{:S(2)}) collective-permute-start(f32[4,1024]{1,0:T(4,128)S(1)} %get-tuple-element.21.rest_0_), channel_id=1, source_target_pairs={{0,1},{1,0},{2,3},{3,2},{4,5},{5,4},{6,7},{7,6},{8,9},{9,8},{10,11... | collective-permute-start | bytes 49160 | tf_op jit(solution)/shard_map/ppermute | solution.py:29
  50.6 4.9 %copy-start.2 = (f32[16392,128]{1,0:T(8,128)S(1)}, f32[16392,128]{1,0:T(8,128)}, u32[]{:S(2)}) copy-start(f32[16392,128]{1,0:T(8,128)} %copy-done) | copy-start | bytes 25178116
  66.0 5.6 %collective-permute-start.8 = (f32[4,1024]{1,0:T(4,128)S(1)}, f32[4,1024]{1,0:T(4,128)S(1)}, u32[]{:S(2)}, u32[]{:S(2)}) collective-permute-start(f32[4,1024]{1,0:T(4,128)S(1)} %get-tuple-element.21.rest_0_), channel_id=1, source_target_pairs={{0,2},{1,3},{2,0},{3,1},{4,6},{5,7},{6,4},{7,5},{8,10},{9,11},{10,... | collective-permute-start | bytes 49160 | tf_op jit(solution)/shard_map/ppermute | solution.py:29
  66.7 8.7 %collective-permute-start.9 = (f32[4,1024]{1,0:T(4,128)S(1)}, f32[4,1024]{1,0:T(4,128)S(1)}, u32[]{:S(2)}, u32[]{:S(2)}) collective-permute-start(f32[4,1024]{1,0:T(4,128)S(1)} %get-tuple-element.21.rest_0_), channel_id=1, source_target_pairs={{0,3},{1,2},{2,1},{3,0},{4,7},{5,6},{6,5},{7,4},{8,11},{9,10},{10,... | collective-permute-start | bytes 49160 | tf_op jit(solution)/shard_map/ppermute | solution.py:29
  66.7 82.4 %collective-permute-start.16 = (f32[1536,128]{1,0:T(8,128)}, f32[1536,128]{1,0:T(8,128)S(1)}, u32[]{:S(2)}, u32[]{:S(2)}) collective-permute-start(f32[1536,128]{1,0:T(8,128)} %get-tuple-element.25), channel_id=1, source_target_pairs={{28,0},{0,4},{4,8},{8,12},{12,16},{16,20},{20,24},{24,28},{29,1},{... | collective-permute-start | bytes 2359304 | tf_op jit(solution)/shard_map/ppermute | solution.py:23
  66.8 82.3 %collective-permute-start.17 = (f32[1536,128]{1,0:T(8,128)}, f32[1536,128]{1,0:T(8,128)S(1)}, u32[]{:S(2)}, u32[]{:S(2)}) collective-permute-start(f32[1536,128]{1,0:T(8,128)} %get-tuple-element.26), channel_id=1, source_target_pairs={{4,0},{8,4},{12,8},{16,12},{20,16},{24,20},{28,24},{0,28},{5,1},{9... | collective-permute-start | bytes 2359304 | tf_op jit(solution)/shard_map/ppermute | solution.py:23
  71.6 77.6 %collective-permute-start.14 = (f32[1536,128]{1,0:T(8,128)}, f32[1536,128]{1,0:T(8,128)S(1)}, u32[]{:S(2)}, u32[]{:S(2)}) collective-permute-start(f32[1536,128]{1,0:T(8,128)} %get-tuple-element.23), channel_id=1, source_target_pairs={{24,0},{28,4},{0,8},{4,12},{8,16},{12,20},{16,24},{20,28},{25,1},{... | collective-permute-start | bytes 2359304 | tf_op jit(solution)/shard_map/ppermute | solution.py:23
  71.6 77.6 %collective-permute-start.15 = (f32[1536,128]{1,0:T(8,128)}, f32[1536,128]{1,0:T(8,128)S(1)}, u32[]{:S(2)}, u32[]{:S(2)}) collective-permute-start(f32[1536,128]{1,0:T(8,128)} %get-tuple-element.24), channel_id=1, source_target_pairs={{8,0},{12,4},{16,8},{20,12},{24,16},{28,20},{0,24},{4,28},{9,1},{1... | collective-permute-start | bytes 2359304 | tf_op jit(solution)/shard_map/ppermute | solution.py:23
  81.3 42.7 %collective-permute-start.10 = (f32[192]{0:T(256)S(1)}, f32[192]{0:T(256)S(1)}, u32[]{:S(2)}, u32[]{:S(2)}) collective-permute-start(f32[192]{0:T(256)S(1)} %bitcast.39), channel_id=1, source_target_pairs={{24,0},{28,4},{0,8},{4,12},{8,16},{12,20},{16,24},{20,28},{25,1},{... | collective-permute-start | bytes 2312 | tf_op jit(solution)/shard_map/ppermute | solution.py:23
  124.1 3.6 %collective-permute-start.11 = (f32[192]{0:T(256)S(1)}, f32[192]{0:T(256)S(1)}, u32[]{:S(2)}, u32[]{:S(2)}) collective-permute-start(f32[192]{0:T(256)S(1)} %bitcast.38), channel_id=1, source_target_pairs={{8,0},{12,4},{16,8},{20,12},{24,16},{28,20},{0,24},{4,28},{9,1},{1... | collective-permute-start | bytes 2312 | tf_op jit(solution)/shard_map/ppermute | solution.py:23
  127.6 6.3 %collective-permute-start.12 = (f32[192]{0:T(256)S(1)}, f32[192]{0:T(256)S(1)}, u32[]{:S(2)}, u32[]{:S(2)}) collective-permute-start(f32[192]{0:T(256)S(1)} %bitcast.37), channel_id=1, source_target_pairs={{28,0},{0,4},{4,8},{8,12},{12,16},{16,20},{20,24},{24,28},{29,1},{... | collective-permute-start | bytes 2312 | tf_op jit(solution)/shard_map/ppermute | solution.py:23
  133.9 15.1 %collective-permute-start.13 = (f32[192]{0:T(256)S(1)}, f32[192]{0:T(256)S(1)}, u32[]{:S(2)}, u32[]{:S(2)}) collective-permute-start(f32[192]{0:T(256)S(1)} %bitcast.36), channel_id=1, source_target_pairs={{4,0},{8,4},{12,8},{16,12},{20,16},{24,20},{28,24},{0,28},{5,1},{9... | collective-permute-start | bytes 2312 | tf_op jit(solution)/shard_map/ppermute | solution.py:23
  134.3 3.4 %copy-start.3 = (f32[16392,128]{1,0:T(8,128)S(1)}, f32[16392,128]{1,0:T(8,128)}, u32[]{:S(2)}) copy-start(f32[16392,128]{1,0:T(8,128)} %copy-done) | copy-start | bytes 25178116
  137.7 2.2 %copy-start.6 = (s32[8192,128]{1,0:T(8,128)S(1)}, s32[8192,128]{1,0:T(8,128)}, u32[]{:S(2)}) copy-start(s32[8192,128]{1,0:T(8,128)} %copy-done.4) | copy-start | bytes 12582916
  (2 other events, 4.2 us)

commit v3 on v2

v3 whole, which is shorter than its diff:
```python
import functools

import jax
import jax.numpy as jnp
from jax import lax
from jax.experimental import pallas as pl
from jax.experimental.pallas import tpu as pltpu
from jax.sharding import PartitionSpec as P

SHIFTS = (1, -1, 2, -2)
EXACT = lax.Precision.HIGHEST
LANES = 128
MIB = 1 << 20
F32 = jnp.float32
I32 = jnp.int32
VMEM_WHOLE = pl.BlockSpec(memory_space=pltpu.VMEM)
SMEM_WHOLE = pl.BlockSpec(memory_space=pltpu.SMEM)
ANYWHERE = pl.BlockSpec(memory_space=pl.ANY)


def shifted(block, axis, distance):
    devices = range(lax.axis_size(axis))
    route = [((i - distance) % len(devices), i) for i in devices]
    return lax.ppermute(block, axis, route)


def partners(block, axis):
    count = lax.axis_size(axis)
    return [block] + [
        lax.ppermute(block, axis, [(i, i ^ other) for i in range(count)])
        for other in range(1, count)
    ]


def tree_sum(parts):
    while len(parts) > 1:
        parts = [parts[k] + parts[k + 1] for k in range(0, len(parts), 2)]
    return parts[0]


def params(mib):
    return pltpu.CompilerParams(vmem_limit_bytes=mib * MIB)


def cost(flops, moved):
    return pl.CostEstimate(flops=flops, bytes_accessed=moved, transcendentals=0)


def lane_sums(partial):
    ones = jnp.ones((8, LANES), F32)
    sums = lax.dot_general(
        ones, partial, (((1,), (1,)), ((), ())), preferred_element_type=F32, precision=EXACT
    )
    return sums[0:1, :]


def row_at(index, sub):
    return pl.ds(pl.multiple_of(index, sub), sub)


def padded(cap):
    return -(-cap // LANES) * LANES


def put_row(ref, row, value, fill):
    width = value.shape[1]
    for q in range(-(-width // LANES)):
        piece = value[:, q * LANES : min((q + 1) * LANES, width)]
        lack = LANES - piece.shape[1]
        if lack:
            piece = jnp.concatenate([piece, jnp.full((1, lack), fill, piece.dtype)], axis=1)
        ref[row + q : row + q + 1, :] = piece


def one_hot(index, count):
    rows = lax.broadcasted_iota(I32, (count, index.shape[1]), 0)
    return jnp.where(rows == index, 1.0, 0.0)


def look_up(table, index):
    picked = lax.dot_general(
        table.T,
        one_hot(index // LANES, table.shape[0]),
        (((1,), (0,)), ((), ())),
        preferred_element_type=F32,
        precision=EXACT,
    )
    return jnp.sum(picked * one_hot(index % LANES, LANES), axis=0, keepdims=True)


def scatter(index, values, height):
    high = jnp.where(index >= 0, index // LANES, -1)
    return lax.dot_general(
        one_hot(high, height) * values,
        one_hot(jnp.where(index >= 0, index % LANES, -1), LANES),
        (((1,), (1,)), ((), ())),
        preferred_element_type=F32,
        precision=EXACT,
    )


def home_cells(node_out, region_no, cells):
    here = (node_out >= 0) & (node_out // cells == region_no)
    return jnp.where(here, node_out % cells, -1)


def rows_of_group(x_ref, rows_ref, first, sub):
    total = None
    for q in range(sub):
        piece = x_ref[pl.ds(pl.multiple_of(first, 8), 8), q * LANES : (q + 1) * LANES]
        rows_ref[pl.ds(first * sub + q, 8, stride=sub), :] = piece
        total = piece if total is None else total + piece
    return total


def copies_in(source, target, sems, chunk):
    copies = [
        pltpu.make_async_copy(
            source.at[pl.ds(i * chunk, chunk), :], target.at[pl.ds(i * chunk, chunk), :], sems.at[i]
        )
        for i in range(target.shape[0] // chunk)
    ]
    for copy in copies:
        copy.start()
    return copies


def cell_sum_kernel(chunk, sub, x_hbm, sum_ref, rows_ref, x, partial, sems):
    copies = copies_in(x_hbm, x, sems, chunk)
    zeros = rows_ref.shape[0] - sub
    rows_ref[zeros:, :] = jnp.zeros((sub, LANES), F32)
    for number, copy in enumerate(copies):
        copy.wait()

        def body(step, carry, number=number):
            for half in range(2):
                first = number * chunk + step * 16 + half * 8
                total = rows_of_group(x, rows_ref, first, sub)
                partial[pl.ds(pl.multiple_of(step * 16 + half * 8, 8), 8), :] = total
            return carry

        lax.fori_loop(0, chunk // 16, body, 0)
        put_row(sum_ref, number * (chunk // LANES), lane_sums(partial[...]), 0.0)


def turn_rows_kernel(chunk, sub, x_hbm, after_ref, rows_ref, x, sems):
    for number, copy in enumerate(copies_in(x_hbm, x, sems, chunk)):
        copy.wait()

        def body(step, carry, number=number):
            for half in range(2):
                rows_of_group(x, rows_ref, number * chunk + step * 16 + half * 8, sub)
            return carry

        lax.fori_loop(0, chunk // 16, body, 0)


def index_kernel(
    sizes, node_in, node_out, send_list, recv_list, after_ref,
    in_cell, send_node, send_outlet, land, source_node, source_outlet,
):
    cells, nodes, branches, cap, sub = sizes
    height = cells // LANES
    region_no = lax.axis_index("region")
    ids = lax.broadcasted_iota(I32, (1, nodes), 1).astype(F32) + 1.0
    number = jnp.zeros((height, LANES), F32)
    slot = jnp.zeros((height, LANES), F32)
    for j in range(branches):
        ins = node_in[j : j + 1, :]
        put_row(in_cell, j * (nodes // LANES), jnp.where(ins >= 0, ins, cells), cells)
        home = home_cells(node_out[j : j + 1, :], region_no, cells)
        here = scatter(home, ids, height)
        number = number + here
        slot = slot + jnp.where(here > 0.0, j + 1.0, 0.0)
    source_node[...] = jnp.maximum(number.astype(I32) - 1, 0) * sub
    source_outlet[...] = slot.astype(I32) - 1
    per_side = padded(cap) // LANES
    for side in range(4):
        slots = send_list[side : side + 1, :]
        lands = recv_list[side : side + 1, :]
        put_row(send_node, side * per_side, jnp.where(slots >= 0, slots % nodes, 0), 0)
        put_row(send_outlet, side * per_side, jnp.where(slots >= 0, slots // nodes, -1), -1)
        put_row(land, side * per_side, jnp.where(lands >= 0, lands, cells) * sub, cells * sub)


def gathered_flow(node, in_cell, fraction, rows, sizes):
    cells, nodes, branches, cap, sub = sizes
    parts = []
    for i in range(branches):
        cell = in_cell[i * nodes + node]
        parts.append(rows[row_at(cell * sub, sub), :] * fraction[cell])
    return tree_sum(parts)


def send_kernel(sizes, sides, fraction, in_cell, send_node, send_outlet, rows, turns, *rest):
    cells, nodes, branches, cap, sub = sizes
    sends = rest[-len(sides) :]
    batch = 8
    for side, send in zip(sides, sends):

        def body(step, carry, side=side, send=send):
            first = step * batch
            values = []
            for i in range(batch):
                slot = side * padded(cap) + first + i
                node = send_node[slot]
                value = gathered_flow(node, in_cell, fraction, rows, sizes)
                choice = turns[row_at(node * sub, sub), :]
                values.append(jnp.where(choice == send_outlet[slot], value, 0.0))
            for i in range(batch):
                send[row_at((first + i) * sub, sub), :] = values[i]
            return carry

        lax.fori_loop(0, cap // batch, body, 0)


def scaled_send_kernel(sizes, side, theta, send_node, send_outlet, flow, turns, send):
    cells, nodes, branches, cap, sub = sizes
    batch = 8

    def body(step, carry):
        first = step * batch
        values = []
        for i in range(batch):
            slot = side * padded(cap) + first + i
            node = send_node[slot]
            at = row_at(node * sub, sub)
            value = flow[at, :] * theta[node]
            values.append(jnp.where(turns[at, :] == send_outlet[slot], value, 0.0))
        for i in range(batch):
            send[row_at((first + i) * sub, sub), :] = values[i]
        return carry

    lax.fori_loop(0, cap // batch, body, 0)


def node_flow_kernel(sizes, fraction, in_cell, rows, turns, after_ref, flow, demand, partial):
    cells, nodes, branches, cap, sub = sizes

    def gather(step, carry):
        first = step * 8
        values = [
            gathered_flow(first + i, in_cell, fraction, rows, sizes) for i in range(8)
        ]
        for i in range(8):
            flow[row_at((first + i) * sub, sub), :] = values[i]
        return carry

    def measure(step, carry):
        for half in range(2):
            first = step * 16 + half * 8
            totals = [jnp.zeros((8, LANES), F32)] * branches
            for q in range(sub):
                at = pl.ds(first * sub + q, 8, stride=sub)
                value = flow[at, :]
                choice = turns[at, :]
                totals = [
                    total + jnp.where(choice == j, value, 0.0) for j, total in enumerate(totals)
                ]
            for j in range(branches):
                partial[j, pl.ds(pl.multiple_of(first, 8), 8), :] = totals[j]
        return carry

    lax.fori_loop(0, nodes // 8, gather, 0)
    lax.fori_loop(0, nodes // 16, measure, 0)
    for j in range(branches):
        demand[j : j + 1, :] = lane_sums(partial[j])


def theta_kernel(
    sizes, commodities, supply, demands, node_in, node_out, fraction, keep, home_theta, tall
):
    cells, nodes, branches, cap, sub = sizes
    height = cells // LANES
    region_no = lax.axis_index("region")
    parts = [demands[k : k + branches, :] for k in range(0, demands.shape[0], branches)]
    demand = tree_sum(parts) * (1.0 / commodities)
    table = supply[...]
    theta = jnp.ones((1, nodes), F32)
    for j in range(branches):
        outs = node_out[j : j + 1, :]
        room = look_up(table, jnp.maximum(outs, 0))
        ratio = room / jnp.maximum(demand[j : j + 1, :], room)
        theta = jnp.minimum(theta, jnp.where(outs >= 0, ratio, 1.0))
    cell_theta = jnp.zeros((height, LANES), F32)
    into = jnp.zeros((height, LANES), F32)
    for j in range(branches):
        home = home_cells(node_out[j : j + 1, :], region_no, cells)
        cell_theta = cell_theta + scatter(node_in[j : j + 1, :], theta, height)
        into = into + scatter(home, theta, height)
    keep[...] = 1.0 - cell_theta * fraction[...]
    home_theta[...] = into
    put_row(tall, 0, theta, 0.0)


def slot_theta_kernel(sizes, regions, sides, theta, send_lists, scale):
    cells, nodes, branches, cap, sub = sizes
    region_no = lax.axis_index("region")
    table = theta[...]
    for side in range(4):
        if side not in sides:
            put_row(scale, side * (padded(cap) // LANES), jnp.ones((1, cap), F32), 1.0)
            continue
        sender = (region_no + (regions - SHIFTS[side])) % regions
        slots = send_lists[pl.ds(4 * sender + side, 1), :]
        node = jnp.where(slots >= 0, slots % nodes, 0) + sender * nodes
        put_row(scale, side * (padded(cap) // LANES), look_up(table, node), 0.0)


def base_kernel(sizes, keep, home_theta, node_row, outlet, rows, turns, flow, base):
    cells, nodes, branches, cap, sub = sizes
    batch = 8

    def body(step, carry):
        first = step * batch
        values = []
        for i in range(batch):
            cell = first + i
            at = row_at(node_row[cell], sub)
            moved = jnp.where(turns[at, :] == outlet[cell], flow[at, :], 0.0)
            kept = rows[row_at(cell * sub, sub), :] * keep[cell]
            values.append(kept + moved * home_theta[cell])
        for i in range(batch):
            base[row_at((first + i) * sub, sub), :] = values[i]
        return carry

    lax.fori_loop(0, cells // batch, body, 0)


def land_rows(sizes, sides, scale, land, received, base):
    cells, nodes, branches, cap, sub = sizes
    batch = 8
    for side, rows in zip(sides, received):

        def body(step, carry, side=side, rows=rows):
            first = step * batch
            stores = []
            for i in range(batch):
                slot = side * padded(cap) + first + i
                at = row_at(land[slot], sub)
                value = rows[row_at((first + i) * sub, sub), :]
                if scale is not None:
                    value = value * scale[slot]
                stores.append((at, base[at, :] + value))
            for at, value in stores:
                base[at, :] = value
            return carry

        lax.fori_loop(0, cap // batch, body, 0)


def land_kernel(sizes, sides, scale, land, *rest):
    received, (base_in, base) = rest[: len(sides)], rest[len(sides) :]
    land_rows(sizes, sides, scale, land, received, base)


def finish_kernel(sizes, sides, chunk, land, *rest):
    cells, nodes, branches, cap, sub = sizes
    received, (base_in, out, base, staged, sems) = rest[: len(sides)], rest[len(sides) :]
    land_rows(sizes, sides, None, land, received, base)
    copies = []
    for number in range(cells // chunk):

        def body(step, carry, number=number):
            for half in range(2):
                first = number * chunk + step * 16 + half * 8
                for q in range(sub):
                    staged[
                        pl.ds(pl.multiple_of(first, 8), 8), q * LANES : (q + 1) * LANES
                    ] = base[pl.ds(first * sub + q, 8, stride=sub), :]
            return carry

        lax.fori_loop(0, chunk // 16, body, 0)
        at = pl.ds(number * chunk, chunk)
        copies.append(
            pltpu.make_async_copy(staged.at[at, :], out.at[at, :], sems.at[number])
        )
        copies[-1].start()
    for copy in copies:
        copy.wait()


def on_device(occupancy, capacity, jam, wave, node_in, node_out, send_list, recv_list, turn):
    cells, width = occupancy.shape
    branches, nodes = node_in.shape
    cap = send_list.shape[1]
    sub = width // LANES
    sizes = (cells, nodes, branches, cap, sub)
    regions = lax.axis_size("region")
    commodities = width * lax.axis_size("dest")
    height = cells // LANES
    per_cell = (height, LANES)
    list_shape = (4 * padded(cap) // LANES, LANES)
    chunk = 128
    row_bytes = width * 4
    occupancy = pltpu.with_memory_space_constraint(occupancy, pltpu.HBM)
    turn = pltpu.with_memory_space_constraint(turn, pltpu.HBM)

    local_sum, rows = pl.pallas_call(
        functools.partial(cell_sum_kernel, chunk, sub),
        in_specs=[ANYWHERE],
        out_specs=[VMEM_WHOLE] * 2,
        out_shape=[
            jax.ShapeDtypeStruct(per_cell, F32),
            pltpu.VMEM(((cells + 1) * sub, LANES), F32),
        ],
        scratch_shapes=[
            pltpu.VMEM((cells, width), F32),
            pltpu.VMEM((chunk, LANES), F32),
            pltpu.SemaphoreType.DMA((cells // chunk,)),
        ],
        compiler_params=params(12),
        cost_estimate=cost(cells * width, cells * row_bytes),
        name="cell_sum",
    )(occupancy)

    sums = partners(local_sum, "dest")

    turns = pl.pallas_call(
        functools.partial(turn_rows_kernel, chunk, sub),
        in_specs=[ANYWHERE] * 2,
        out_specs=VMEM_WHOLE,
        out_shape=pltpu.VMEM((nodes * sub, LANES), I32),
        scratch_shapes=[
            pltpu.VMEM((nodes, width), I32),
            pltpu.SemaphoreType.DMA((nodes // chunk,)),
        ],
        compiler_params=params(8),
        cost_estimate=cost(0, nodes * row_bytes),
        name="turn_rows",
    )(turn, local_sum)

    in_cell, send_node, send_outlet, land, source_node, source_outlet = pl.pallas_call(
        functools.partial(index_kernel, sizes),
        in_specs=[VMEM_WHOLE] * 4 + [ANYWHERE],
        out_specs=[VMEM_WHOLE] * 6,
        out_shape=[jax.ShapeDtypeStruct((branches * nodes // LANES, LANES), I32)]
        + [jax.ShapeDtypeStruct(list_shape, I32)] * 3
        + [jax.ShapeDtypeStruct(per_cell, I32)] * 2,
        compiler_params=params(8),
        cost_estimate=cost(branches * nodes * cells * 2, nodes * 64),
        name="index_lists",
    )(node_in, node_out, send_list, recv_list, local_sum)
    in_cell, send_node, send_outlet, land, source_node, source_outlet = (
        x.reshape(-1) for x in (in_cell, send_node, send_outlet, land, source_node, source_outlet)
    )

    vehicles = tree_sum(sums) / commodities
    cap_of = capacity.reshape(per_cell)
    fraction = jnp.minimum(vehicles, cap_of) / vehicles
    supply = jnp.minimum(cap_of, wave.reshape(per_cell) * (jam.reshape(per_cell) - vehicles))
    weights = jnp.concatenate([fraction.reshape(-1), jnp.zeros((LANES,), F32)])

    def send_rows(sides, after):
        return pl.pallas_call(
            functools.partial(send_kernel, sizes, sides),
            in_specs=[SMEM_WHOLE] * 4 + [VMEM_WHOLE] * 2 + [ANYWHERE] * len(after),
            out_specs=[VMEM_WHOLE] * len(sides),
            out_shape=[pltpu.VMEM((cap * sub, LANES), F32)] * len(sides),
            compiler_params=params(4),
            cost_estimate=cost(cap * width * 20, cap * row_bytes * 10),
            name="send_rows",
        )(weights, in_cell, send_node, send_outlet, rows, turns, *after)

    near = send_rows((0, 1), ())
    ahead = send_rows((2,), near[:1])
    arrived = [
        shifted(send, "region", SHIFTS[side]) for side, send in enumerate([*near, *ahead])
    ]

    supply, _ = lax.optimization_barrier((supply, ahead[0]))
    supplies = lax.all_gather(supply, "region", axis=0, tiled=True)
    send_lists = lax.all_gather(send_list, "region", axis=0, tiled=True)

    flow, demand = pl.pallas_call(
        functools.partial(node_flow_kernel, sizes),
        in_specs=[SMEM_WHOLE] * 2 + [VMEM_WHOLE] * 2 + [ANYWHERE],
        out_specs=[VMEM_WHOLE] * 2,
        out_shape=[
            pltpu.VMEM((nodes * sub, LANES), F32),
            jax.ShapeDtypeStruct((branches, nodes), F32),
        ],
        scratch_shapes=[pltpu.VMEM((branches, nodes, LANES), F32)],
        compiler_params=params(8),
        cost_estimate=cost(nodes * width * 16, nodes * row_bytes * 6),
        name="node_flow",
    )(weights, in_cell, rows, turns, ahead[0])

    demands = lax.all_gather(demand, "dest", axis=0, tiled=True)
    keep, home_theta, theta = pl.pallas_call(
        functools.partial(theta_kernel, sizes, commodities),
        out_shape=[jax.ShapeDtypeStruct(per_cell, F32)] * 2
        + [jax.ShapeDtypeStruct((nodes // LANES, LANES), F32)],
        compiler_params=params(8),
        cost_estimate=cost(branches * nodes * cells * 8, nodes * 256),
        name="theta",
    )(supplies, demands, node_in, node_out, fraction)

    (behind,) = pl.pallas_call(
        functools.partial(scaled_send_kernel, sizes, 3),
        in_specs=[SMEM_WHOLE] * 3 + [VMEM_WHOLE] * 2,
        out_specs=[VMEM_WHOLE],
        out_shape=[pltpu.VMEM((cap * sub, LANES), F32)],
        compiler_params=params(4),
        cost_estimate=cost(cap * width * 4, cap * row_bytes * 4),
        name="scaled_send_rows",
    )(theta.reshape(-1), send_node, send_outlet, flow, turns)
    last = shifted(behind, "region", SHIFTS[3])

    thetas = lax.all_gather(theta, "region", axis=0, tiled=True)
    scale = pl.pallas_call(
        functools.partial(slot_theta_kernel, sizes, regions, (0, 1, 2)),
        out_shape=jax.ShapeDtypeStruct(list_shape, F32),
        compiler_params=params(8),
        cost_estimate=cost(4 * cap * 2048, nodes * 64),
        name="slot_theta",
    )(thetas, send_lists)

    base_shape = pltpu.VMEM(((cells + 1) * sub, LANES), F32)
    base = pl.pallas_call(
        functools.partial(base_kernel, sizes),
        in_specs=[SMEM_WHOLE] * 4 + [VMEM_WHOLE] * 3,
        out_specs=VMEM_WHOLE,
        out_shape=base_shape,
        compiler_params=params(4),
        cost_estimate=cost(cells * width * 4, cells * row_bytes * 4),
        name="home_inflow",
    )(keep.reshape(-1), home_theta.reshape(-1), source_node, source_outlet, rows, turns, flow)

    base = pl.pallas_call(
        functools.partial(land_kernel, sizes, (0, 1, 2)),
        in_specs=[SMEM_WHOLE] * 2 + [VMEM_WHOLE] * 4,
        out_specs=VMEM_WHOLE,
        out_shape=base_shape,
        input_output_aliases={5: 0},
        compiler_params=params(4),
        cost_estimate=cost(cap * width * 6, cap * row_bytes * 9),
        name="land_first",
    )(scale.reshape(-1), land, *arrived, base)

    out, _ = pl.pallas_call(
        functools.partial(finish_kernel, sizes, (3,), chunk),
        in_specs=[SMEM_WHOLE] + [VMEM_WHOLE] * 2,
        out_specs=[ANYWHERE, VMEM_WHOLE],
        out_shape=[jax.ShapeDtypeStruct((cells, width), F32), base_shape],
        scratch_shapes=[
            pltpu.VMEM((cells, width), F32),
            pltpu.SemaphoreType.DMA((cells // chunk,)),
        ],
        input_output_aliases={2: 1},
        compiler_params=params(12),
        cost_estimate=cost(cells * width, cells * row_bytes),
        name="finish",
    )(land, last, base)
    return out


def solution(mesh):
    return jax.shard_map(
        on_device,
        mesh=mesh,
        in_specs=(
            P("region", "dest"),
            P("region"),
            P("region"),
            P("region"),
            P(None, "region"),
            P(None, "region"),
            P("region", None),
            P("region", None),
            P("region", "dest"),
        ),
        out_specs=P("region", "dest"),
        check_vma=False,
    )
```

time: 157 us -> 207 us (1.32)
  blocking collectives: 0 us -> 129 us
  waiting for transfers between devices: 53.3 us -> 0.02 us
  starting transfers between devices: 21.4 us -> 8 us
  local copies, waits for them, and re-layouts: 21.8 us -> 15.2 us
  Pallas kernels: 59.6 us -> 54.5 us
    all_gather x0 -> x4, blocking collectives: none -> 129 us  [the longest x1 54.3 us: on_device(): supplies = lax.all_gather(supply, 'region', axis=0, tiled=True)]
    ppermute x12 -> x4, waiting for transfers between devices: 50.6 us -> 0.01 us  [shifted(): return lax.ppermute(block, axis, route)]
    ppermute x12 -> x4, starting transfers between devices: 17.5 us -> 4.85 us  [shifted(): return lax.ppermute(block, axis, route)]
    unnamed x36 -> x34, local copies, waits for them, and re-layouts: 21.4 us -> 15.2 us
    pallas_call x1, Pallas kernels: 15 us -> 11.7 us  [on_device(): pl.pallas_call(functools.partial(node_flow_kernel, sizes), in_specs=[SMEM...]
    ppermute x6 -> x3, waiting for transfers between devices: 2.76 us -> 0.01 us  [partners(): lax.ppermute(block, axis, [(i, i ^ other) for i in range(count)])]
    pallas_call x6 -> x9, Pallas kernels: 31.7 us -> 30.2 us  [the longest x1 8.6 us: on_device(): pl.pallas_call(functools.partial(cell_sum_kernel, chunk, sub), in_specs=[...]
  transfers between devices with their start and end apart: 18 -> 7, of which waited for: 5 -> 0; matrix products, arithmetic and copies ran while one was open for 0% -> 0% of each run, Pallas kernels for 29% -> 10%
where the time goes in v3:
time: 207 us
  blocking collectives  129 us (62%)
  Pallas kernels  54.5 us (26%)
  local copies, waits for them, and re-layouts  15.2 us (7%)
  starting transfers between devices  8 us (4%)
    all_gather x1, blocking collectives, on_device(): supplies = lax.all_gather(supply, 'region', axis=0, tiled=True)  54.3 us
    all_gather x1, blocking collectives, on_device(): send_lists = lax.all_gather(send_list, 'region', axis=0, tiled=True)  38.9 us
    all_gather x1, blocking collectives, on_device(): thetas = lax.all_gather(theta, 'region', axis=0, tiled=True)  30.6 us
    unnamed x34, local copies, waits for them, and re-layouts  15.2 us
    pallas_call x1, Pallas kernels, on_device(): pl.pallas_call(functools.partial(node_flow_kernel, sizes), in_specs=[SMEM...  11.7 us
    pallas_call x1, Pallas kernels, on_device(): pl.pallas_call(functools.partial(cell_sum_kernel, chunk, sub), in_specs=[...  8.6 us
    pallas_call x2, Pallas kernels, send_rows(): pl.pallas_call(functools.partial(send_kernel, sizes, sides), in_specs=[SM...  7.8 us
    pallas_call x1, Pallas kernels, on_device(): pl.pallas_call(functools.partial(base_kernel, sizes), in_specs=[SMEM_WHOL...  6.99 us
  transfers between devices with their start and end apart: 7, of which 0 were waited for; matrix products, arithmetic and copies ran while one was open for 0% of the time, Pallas kernels for 10%

profile of v3, /device:TPU:0, one launch (start us, length us, event | category | flops | bytes accessed | tf_op | source)
XLA Modules:
  0.0 207.1 jit_solution(12477290545283224143)
XLA Ops:
  0.0 8.6 %cell_sum.1 = (f32[16,128]{1,0:T(8,128)S(1)}, f32[16392,128]{1,0:T(8,128)S(1)}) custom-call(f32[2048,1024]{1,0:T(8,128)} %x_hbm.2), custom_call_target="tpu_custom_call" | custom-call | flops 2097152 | bytes 8388608 | tf_op jit(solution)/shard_map/cell_sum/pallas_call | solution.py:399
  8.6 0.5 collective-permute-start
  9.1 2.6 %collective-permute-start.1 = (f32[16,128]{1,0:T(8,128)S(1)}, f32[16,128]{1,0:T(8,128)S(1)}, u32[]{:S(2)}, u32[]{:S(2)}) collective-permute-start(f32[16,128]{1,0:T(8,128)S(1)} %get-tuple-element.22.after_ref), channel_id=1, source_target_pairs={{0,2},{1,3},{2,0},{3,1},{4,6},{5,7},{6,4},{7,5},{8,10},{9,11},{10,... | collective-permute-start | bytes 24584 | tf_op jit(solution)/shard_map/ppermute | solution.py:30
  11.7 0.1 collective-permute-start.2
  11.8 2.3 %turn_rows.1.turns = s32[8192,128]{1,0:T(8,128)S(1)} custom-call(s32[1024,1024]{1,0:T(8,128)} %x_hbm.3, f32[16,128]{1,0:T(8,128)S(1)} %get-tuple-element.22.after_ref), custom_call_target="tpu_custom_call" | custom-call | bytes 4194304 | tf_op jit(solution)/shard_map/turn_rows/pallas_call | solution.py:419
  14.2 1.9 index_lists.1
  16.0 0.0 collective-permute-done
  16.1 5.2 %send_rows.2 = (f32[1536,128]{1,0:T(8,128)}, f32[1536,128]{1,0:T(8,128)S(1)}) custom-call(f32[2176]{0:T(1024)S(1)} %concatenate.3.fraction, s32[4096]{0:T(1024)S(1)} %bitcast.24, s32[1024]{0:T(1024)S(1)} %bitcast.27, s32[1024]{0:T(1024)S(1)} %bitcast.30, f32[16392,128]{1,0:T(8,128)S(1)} %get-tuple-element.27.rows, s32[8192,128]{1,0:T(8,128)S(1)} %turn_rows.1.turns), custom_call_target="tpu_custom_call" | custom-call | flops 3932160 | bytes 7864320 | tf_op jit(solution)/shard_map/send_rows/pallas_call | solution.py:455
  21.3 0.9 copy-done.9
  22.2 2.6 %send_rows.3.after_ref = f32[1536,128]{1,0:T(8,128)S(1)} custom-call(f32[2176]{0:T(1024)S(1)} %concatenate.3.fraction, s32[4096]{0:T(1024)S(1)} %bitcast.25, s32[1024]{0:T(1024)S(1)} %bitcast.28, s32[1024]{0:T(1024)S(1)} %bitcast.31, f32[16392,128]{1,0:T(8,128)S(1)} %get-tuple-element.27.rows, s32[8192,128]{1,0:T(8,128)S(1)} %turn_rows.1.turns, ...), custom_call_target="tpu_custom_call" | custom-call | flops 3932160 | bytes 7864320 | tf_op jit(solution)/shard_map/send_rows/pallas_call | solution.py:455
  24.9 0.0 copy-start.14
  24.9 0.0 copy-start.15
  24.9 11.7 %node_flow.1 = (f32[8192,128]{1,0:T(8,128)S(1)}, f32[4,1024]{1,0:T(4,128)S(1)}) custom-call(f32[2176]{0:T(1024)S(1)} %concatenate.3.fraction, s32[4096]{0:T(1024)S(1)} %bitcast.26, f32[16392,128]{1,0:T(8,128)S(1)} %get-tuple-element.27.rows, s32[8192,128]{1,0:T(8,128)S(1)} %turn_rows.1.turns, f32[1536,128]{1,0:T(8,128)S(1)} %send_rows.3.after_ref), custom_call_target="tpu_custom_call" | custom-call | flops 16777216 | bytes 25165824 | tf_op jit(solution)/shard_map/node_flow/pallas_call | solution.py:475
  36.6 2.0 copy-done.5
  38.6 2.7 %collective-permute-start.6 = (f32[1536,128]{1,0:T(8,128)S(1)}, f32[1536,128]{1,0:T(8,128)S(1)}, u32[]{:S(2)}, u32[]{:S(2)}) collective-permute-start(f32[1536,128]{1,0:T(8,128)S(1)} %send_rows.3.after_ref), channel_id=1, source_target_pairs={{24,0},{28,4},{0,8},{4,12},{8,16},{12,20},{16,24},{20,28},{25,1},{... | collective-permute-start | bytes 2359304 | tf_op jit(solution)/shard_map/ppermute | solution.py:24
  41.4 1.5 collective-permute-start.4
  42.9 5.2 %all-gather = f32[4,4,1024]{2,1,0:T(4,128)S(1)} all-gather(f32[1,4,1024]{2,1,0:T(4,128)S(1)} %bitcast.35), channel_id=1, replica_groups=mesh['region'=8,'dest'=4] {'dest'}, dimensions={0}, use_global_device_ids=true | all-gather | bytes 81920 | tf_op jit(solution)/shard_map/all_gather | solution.py:489
  48.2 54.3 %all_gather.12.supply = f32[128,128]{1,0:T(8,128)S(1)} all-gather(f32[16,128]{1,0:T(8,128)S(1)} %fusion.1), channel_id=1, replica_groups=mesh['region'=8,'dest'=4] {'region'}, dimensions={0}, use_global_device_ids=true | all-gather | bytes 73728 | tf_op jit(solution)/shard_map/all_gather | solution.py:472
  102.5 5.6 %theta.1 = (f32[16,128]{1,0:T(8,128)S(1)}, f32[16,128]{1,0:T(8,128)S(1)}, f32[8,128]{1,0:T(8,128)S(1)}) custom-call(f32[128,128]{1,0:T(8,128)S(1)} %all_gather.12.supply, f32[16,1024]{1,0:T(8,128)S(1)} %reshape.57.demands, s32[4,1024]{1,0:T(4,128)S(1)} %copy-done.10, s32[4,1024]{1,0:T(4,128)S(1)} %copy-done.11, f32[16,128]{1,0:T(8,128)S(1)} %get-tuple-element.39.fraction), custom_call_target="tpu_custom_call" | custom-call | flops 67108864 | bytes 262144 | tf_op jit(solution)/shard_map/theta/pallas_call | solution.py:490
  108.1 2.2 %copy-done.1 = s32[8192,128]{1,0:T(8,128)S(1)} copy-done((s32[8192,128]{1,0:T(8,128)S(1)}, s32[8192,128]{1,0:T(8,128)}, u32[]{:S(2)}) %copy-start.1) | copy-done | bytes 4194328
  110.3 2.2 %copy-done.6 = f32[8192,128]{1,0:T(8,128)S(1)} copy-done((f32[8192,128]{1,0:T(8,128)S(1)}, f32[8192,128]{1,0:T(8,128)}, u32[]{:S(2)}) %copy-start.6) | copy-done | bytes 4194328
  112.5 2.1 %scaled_send_rows.1 = f32[1536,128]{1,0:T(8,128)} custom-call(f32[1024]{0:T(1024)S(1)} %bitcast.34, s32[1024]{0:T(1024)S(1)} %bitcast.29, s32[1024]{0:T(1024)S(1)} %bitcast.32, f32[8192,128]{1,0:T(8,128)S(1)} %copy-done.6, s32[8192,128]{1,0:T(8,128)S(1)} %copy-done.1), custom_call_target="tpu_custom_call" | custom-call | flops 786432 | bytes 3145728 | tf_op jit(solution)/shard_map/scaled_send_rows/pallas_call | solution.py:499
  114.6 0.6 collective-permute-start.3
  115.2 38.9 %all-gather.1 = s32[8,4,192]{2,1,0:T(4,128)S(1)} all-gather(s32[1,4,192]{2,1,0:T(4,128)S(1)} %bitcast.43), channel_id=1, replica_groups=mesh['region'=8,'dest'=4] {'region'}, dimensions={0}, use_global_device_ids=true | all-gather | bytes 27648 | tf_op jit(solution)/shard_map/all_gather | solution.py:473
  154.2 30.6 %all_gather.14.theta = f32[64,128]{1,0:T(8,128)S(1)} all-gather(f32[8,128]{1,0:T(8,128)S(1)} %get-tuple-element.31), channel_id=1, replica_groups=mesh['region'=8,'dest'=4] {'region'}, dimensions={0}, use_global_device_ids=true | all-gather | bytes 36864 | tf_op jit(solution)/shard_map/all_gather | solution.py:510
  184.8 0.5 slot_theta.1
  185.4 2.2 %copy-done.2 = s32[8192,128]{1,0:T(8,128)S(1)} copy-done((s32[8192,128]{1,0:T(8,128)S(1)}, s32[8192,128]{1,0:T(8,128)}, u32[]{:S(2)}) %copy-start.2) | copy-done | bytes 4194328
  187.6 3.4 %copy-done.4 = f32[16392,128]{1,0:T(8,128)S(1)} copy-done((f32[16392,128]{1,0:T(8,128)S(1)}, f32[16392,128]{1,0:T(8,128)}, u32[]{:S(2)}) %copy-start.4) | copy-done | bytes 8392728
  191.0 2.2 %copy-done.7 = f32[8192,128]{1,0:T(8,128)S(1)} copy-done((f32[8192,128]{1,0:T(8,128)S(1)}, f32[8192,128]{1,0:T(8,128)}, u32[]{:S(2)}) %copy-start.7) | copy-done | bytes 4194328
  193.1 7.0 %home_inflow.1.rest_3_ = f32[16392,128]{1,0:T(8,128)S(1)} custom-call(f32[2048]{0:T(1024)S(1)} %bitcast.41, f32[2048]{0:T(1024)S(1)} %bitcast.42, s32[2048]{0:T(1024)S(1)} %bitcast.39, s32[2048]{0:T(1024)S(1)} %bitcast.40, f32[16392,128]{1,0:T(8,128)S(1)} %copy-done.4, s32[8192,128]{1,0:T(8,128)S(1)} %copy-done.2, f32[8192,128]{1,0:T(8,128)S(1)} %copy-done.7), custom_call_target="tpu_custom_call" | custom-call | flops 8388608 | bytes 33554432 | tf_op jit(solution)/shard_map/home_inflow/pallas_call | solution.py:520
  200.2 1.9 land_first.1.rest_1_
  202.1 5.0 %finish.1 = (f32[2048,1024]{1,0:T(8,128)}, f32[16392,128]{1,0:T(8,128)S(1)}) custom-call(s32[1024]{0:T(1024)S(1)} %bitcast.37, f32[1536,128]{1,0:T(8,128)} %collective-permute-done.3.rest_0_, f32[16392,128]{1,0:T(8,128)S(1)} %land_first.1.rest_1_), custom_call_target="tpu_custom_call", output_to_operand_aliasing={{1}: (2, {})} | custom-call | flops 2097152 | bytes 8388608 | tf_op jit(solution)/shard_map/finish/pallas_call | solution.py:541
  (35 shorter events, 0.1 us)
Async XLA Ops:
  0.0 14.1 %copy-start.10 = (s32[4,1024]{1,0:T(4,128)S(1)}, s32[4,1024]{1,0:T(4,128)}, u32[]{:S(2)}) copy-start(s32[4,1024]{1,0:T(4,128)} %node_in.3) | copy-start | bytes 49156
  0.0 14.1 %copy-start.11 = (s32[4,1024]{1,0:T(4,128)S(1)}, s32[4,1024]{1,0:T(4,128)}, u32[]{:S(2)}) copy-start(s32[4,1024]{1,0:T(4,128)} %node_out.3) | copy-start | bytes 49156
  0.0 14.1 %copy-start.8 = (s32[4,192]{1,0:T(4,128)S(1)}, s32[4,192]{1,0:T(4,128)}, u32[]{:S(2)}) copy-start(s32[4,192]{1,0:T(4,128)} %send_list.1) | copy-start | bytes 9220
  0.0 14.1 %copy-start.12 = (s32[4,192]{1,0:T(4,128)S(1)}, s32[4,192]{1,0:T(4,128)}, u32[]{:S(2)}) copy-start(s32[4,192]{1,0:T(4,128)} %recv_list.1) | copy-start | bytes 9220
  0.0 16.1 %copy-start.13 = (f32[2048]{0:T(1024)S(1)}, f32[2048]{0:T(1024)}, u32[]{:S(2)}) copy-start(f32[2048]{0:T(1024)} %param.10) | copy-start | bytes 24580
  8.6 16.2 %copy-start.3 = (f32[16392,128]{1,0:T(8,128)}, f32[16392,128]{1,0:T(8,128)S(1)}, u32[]{:S(2)}) copy-start(f32[16392,128]{1,0:T(8,128)S(1)} %get-tuple-element.27.rows) | copy-start | bytes 25178116
  8.6 7.4 %collective-permute-start = (f32[16,128]{1,0:T(8,128)S(1)}, f32[16,128]{1,0:T(8,128)S(1)}, u32[]{:S(2)}, u32[]{:S(2)}) collective-permute-start(f32[16,128]{1,0:T(8,128)S(1)} %get-tuple-element.22.after_ref), channel_id=1, source_target_pairs={{0,1},{1,0},{2,3},{3,2},{4,5},{5,4},{6,7},{7,6},{8,9},{9,8},{10,11... | collective-permute-start | bytes 24584 | tf_op jit(solution)/shard_map/ppermute | solution.py:30
  9.1 6.9 %collective-permute-start.1 = (f32[16,128]{1,0:T(8,128)S(1)}, f32[16,128]{1,0:T(8,128)S(1)}, u32[]{:S(2)}, u32[]{:S(2)}) collective-permute-start(f32[16,128]{1,0:T(8,128)S(1)} %get-tuple-element.22.after_ref), channel_id=1, source_target_pairs={{0,2},{1,3},{2,0},{3,1},{4,6},{5,7},{6,4},{7,5},{8,10},{9,11},{10,... | collective-permute-start | bytes 24584 | tf_op jit(solution)/shard_map/ppermute | solution.py:30
  11.7 4.4 %collective-permute-start.2 = (f32[16,128]{1,0:T(8,128)S(1)}, f32[16,128]{1,0:T(8,128)S(1)}, u32[]{:S(2)}, u32[]{:S(2)}) collective-permute-start(f32[16,128]{1,0:T(8,128)S(1)} %get-tuple-element.22.after_ref), channel_id=1, source_target_pairs={{0,3},{1,2},{2,1},{3,0},{4,7},{5,6},{6,5},{7,4},{8,11},{9,10},{10,... | collective-permute-start | bytes 24584 | tf_op jit(solution)/shard_map/ppermute | solution.py:30
  14.2 10.7 %copy-start = (s32[8192,128]{1,0:T(8,128)}, s32[8192,128]{1,0:T(8,128)S(1)}, u32[]{:S(2)}) copy-start(s32[8192,128]{1,0:T(8,128)S(1)} %turn_rows.1.turns) | copy-start | bytes 12582916
  21.3 0.9 copy-start.9
  24.9 23.3 %copy-start.14 = (f32[2048]{0:T(1024)S(1)}, f32[2048]{0:T(1024)}, u32[]{:S(2)}) copy-start(f32[2048]{0:T(1024)} %param.11) | copy-start | bytes 24580
  24.9 23.3 %copy-start.15 = (f32[2048]{0:T(1024)S(1)}, f32[2048]{0:T(1024)}, u32[]{:S(2)}) copy-start(f32[2048]{0:T(1024)} %param.12) | copy-start | bytes 24580
  36.6 2.0 copy-start.5
  38.6 161.5 %collective-permute-start.6 = (f32[1536,128]{1,0:T(8,128)S(1)}, f32[1536,128]{1,0:T(8,128)S(1)}, u32[]{:S(2)}, u32[]{:S(2)}) collective-permute-start(f32[1536,128]{1,0:T(8,128)S(1)} %send_rows.3.after_ref), channel_id=1, source_target_pairs={{24,0},{28,4},{0,8},{4,12},{8,16},{12,20},{16,24},{20,28},{25,1},{... | collective-permute-start | bytes 2359304 | tf_op jit(solution)/shard_map/ppermute | solution.py:24
  41.4 158.8 %collective-permute-start.4 = (f32[1536,128]{1,0:T(8,128)}, f32[1536,128]{1,0:T(8,128)S(1)}, u32[]{:S(2)}, u32[]{:S(2)}) collective-permute-start(f32[1536,128]{1,0:T(8,128)} %get-tuple-element.28.rest_0_), channel_id=1, source_target_pairs={{28,0},{0,4},{4,8},{8,12},{12,16},{16,20},{20,24},{24,28},{29,1},{... | collective-permute-start | bytes 2359304 | tf_op jit(solution)/shard_map/ppermute | solution.py:24
  102.5 97.6 %collective-permute-start.5 = (f32[1536,128]{1,0:T(8,128)}, f32[1536,128]{1,0:T(8,128)S(1)}, u32[]{:S(2)}, u32[]{:S(2)}) collective-permute-start(f32[1536,128]{1,0:T(8,128)} %copy-done.9), channel_id=1, source_target_pairs={{4,0},{8,4},{12,8},{16,12},{20,16},{24,20},{28,24},{0,28},{5,1},{9... | collective-permute-start | bytes 2359304 | tf_op jit(solution)/shard_map/ppermute | solution.py:24
  108.1 2.2 %copy-start.1 = (s32[8192,128]{1,0:T(8,128)S(1)}, s32[8192,128]{1,0:T(8,128)}, u32[]{:S(2)}) copy-start(s32[8192,128]{1,0:T(8,128)} %copy-done) | copy-start | bytes 12582916
  110.3 2.2 %copy-start.6 = (f32[8192,128]{1,0:T(8,128)S(1)}, f32[8192,128]{1,0:T(8,128)}, u32[]{:S(2)}) copy-start(f32[8192,128]{1,0:T(8,128)} %copy-done.5) | copy-start | bytes 12582916
  114.6 87.4 %collective-permute-start.3 = (f32[1536,128]{1,0:T(8,128)}, f32[1536,128]{1,0:T(8,128)}, u32[]{:S(2)}, u32[]{:S(2)}) collective-permute-start(f32[1536,128]{1,0:T(8,128)} %scaled_send_rows.1), channel_id=1, source_target_pairs={{8,0},{12,4},{16,8},{20,12},{24,16},{28,20},{0,24},{4,28},{9,1},{1... | collective-permute-start | bytes 2359304 | tf_op jit(solution)/shard_map/ppermute | solution.py:24
  185.4 2.2 %copy-start.2 = (s32[8192,128]{1,0:T(8,128)S(1)}, s32[8192,128]{1,0:T(8,128)}, u32[]{:S(2)}) copy-start(s32[8192,128]{1,0:T(8,128)} %copy-done) | copy-start | bytes 12582916
  187.6 3.4 %copy-start.4 = (f32[16392,128]{1,0:T(8,128)S(1)}, f32[16392,128]{1,0:T(8,128)}, u32[]{:S(2)}) copy-start(f32[16392,128]{1,0:T(8,128)} %copy-done.3) | copy-start | bytes 25178116
  191.0 2.2 %copy-start.7 = (f32[8192,128]{1,0:T(8,128)S(1)}, f32[8192,128]{1,0:T(8,128)}, u32[]{:S(2)}) copy-start(f32[8192,128]{1,0:T(8,128)} %copy-done.5) | copy-start | bytes 12582916

commit v4 on v3

--- a/solution.py
+++ b/solution.py
@@ -18,6 +18,16 @@
 ANYWHERE = pl.BlockSpec(memory_space=pl.ANY)
 
 
+def to_neighbours(block):
+    regions, members = lax.axis_size("region"), lax.axis_size("dest")
+    route = [
+        (r * members + d, (r + SHIFTS[d % 4]) % regions * members + d)
+        for r in range(regions)
+        for d in range(members)
+    ]
+    return lax.ppermute(block, ("region", "dest"), route)
+
+
 def shifted(block, axis, distance):
     devices = range(lax.axis_size(axis))
     route = [((i - distance) % len(devices), i) for i in devices]
@@ -47,11 +57,26 @@
 
 
 def lane_sums(partial):
-    ones = jnp.ones((8, LANES), F32)
-    sums = lax.dot_general(
-        ones, partial, (((1,), (1,)), ((), ())), preferred_element_type=F32, precision=EXACT
-    )
-    return sums[0:1, :]
+    sums = jnp.dot(
+        partial, jnp.ones((LANES, LANES), F32), preferred_element_type=F32, precision=EXACT
+    )
+    row = lax.broadcasted_iota(I32, (LANES, LANES), 0)
+    lane = lax.broadcasted_iota(I32, (LANES, LANES), 1)
+    pieces = [
+        jnp.sum(jnp.where(row == lane, sums[k : k + LANES, :], 0.0), axis=0, keepdims=True)
+        for k in range(0, partial.shape[0], LANES)
+    ]
+    return jnp.concatenate(pieces, axis=0)
+
+
+def stacked(row):
+    return jnp.concatenate(
+        [row[:, k : k + LANES] for k in range(0, row.shape[1], LANES)], axis=0
+    )
+
+
+def strung(rows):
+    return jnp.concatenate([rows[k : k + 1, :] for k in range(rows.shape[0])], axis=1)
 
 
 def row_at(index, sub):
@@ -136,11 +161,11 @@
             for half in range(2):
                 first = number * chunk + step * 16 + half * 8
                 total = rows_of_group(x, rows_ref, first, sub)
-                partial[pl.ds(pl.multiple_of(step * 16 + half * 8, 8), 8), :] = total
+                partial[pl.ds(pl.multiple_of(first, 8), 8), :] = total
             return carry
 
         lax.fori_loop(0, chunk // 16, body, 0)
-        put_row(sum_ref, number * (chunk // LANES), lane_sums(partial[...]), 0.0)
+    sum_ref[...] = lane_sums(partial[...])
 
 
 def turn_rows_kernel(chunk, sub, x_hbm, after_ref, rows_ref, x, sems):
@@ -183,16 +208,30 @@
         put_row(land, side * per_side, jnp.where(lands >= 0, lands, cells) * sub, cells * sub)
 
 
-def gathered_flow(node, in_cell, fraction, rows, sizes):
-    cells, nodes, branches, cap, sub = sizes
-    parts = []
-    for i in range(branches):
-        cell = in_cell[i * nodes + node]
-        parts.append(rows[row_at(cell * sub, sub), :] * fraction[cell])
-    return tree_sum(parts)
-
-
-def send_kernel(sizes, sides, fraction, in_cell, send_node, send_outlet, rows, turns, *rest):
+def gathered_flow(node, in_cell, scaled, sizes):
+    cells, nodes, branches, cap, sub = sizes
+    return tree_sum(
+        [scaled[row_at(in_cell[i * nodes + node] * sub, sub), :] for i in range(branches)]
+    )
+
+
+def scale_kernel(sizes, fraction, rows, scaled):
+    cells, nodes, branches, cap, sub = sizes
+
+    def body(step, carry):
+        first = step * 16
+        values = [
+            rows[row_at((first + i) * sub, sub), :] * fraction[first + i] for i in range(16)
+        ]
+        for i in range(16):
+            scaled[row_at((first + i) * sub, sub), :] = values[i]
+        return carry
+
+    lax.fori_loop(0, cells // 16, body, 0)
+    scaled[row_at(cells * sub, sub), :] = jnp.zeros((sub, LANES), F32)
+
+
+def send_kernel(sizes, sides, in_cell, send_node, send_outlet, scaled, turns, *rest):
     cells, nodes, branches, cap, sub = sizes
     sends = rest[-len(sides) :]
     batch = 8
@@ -204,7 +243,7 @@
             for i in range(batch):
                 slot = side * padded(cap) + first + i
                 node = send_node[slot]
-                value = gathered_flow(node, in_cell, fraction, rows, sizes)
+                value = gathered_flow(node, in_cell, scaled, sizes)
                 choice = turns[row_at(node * sub, sub), :]
                 values.append(jnp.where(choice == send_outlet[slot], value, 0.0))
             for i in range(batch):
@@ -212,6 +251,13 @@
             return carry
 
         lax.fori_loop(0, cap // batch, body, 0)
+
+
+def scale_send_kernel(
+    sizes, sides, fraction, in_cell, send_node, send_outlet, rows, turns, scaled, *sends
+):
+    scale_kernel(sizes, fraction, rows, scaled)
+    send_kernel(sizes, sides, in_cell, send_node, send_outlet, scaled, turns, *sends)
 
 
 def scaled_send_kernel(sizes, side, theta, send_node, send_outlet, flow, turns, send):
@@ -234,13 +280,13 @@
     lax.fori_loop(0, cap // batch, body, 0)
 
 
-def node_flow_kernel(sizes, fraction, in_cell, rows, turns, after_ref, flow, demand, partial):
+def node_flow_kernel(sizes, in_cell, scaled, turns, after_ref, flow, demand, partial):
     cells, nodes, branches, cap, sub = sizes
 
     def gather(step, carry):
         first = step * 8
         values = [
-            gathered_flow(first + i, in_cell, fraction, rows, sizes) for i in range(8)
+            gathered_flow(first + i, in_cell, scaled, sizes) for i in range(8)
         ]
         for i in range(8):
             flow[row_at((first + i) * sub, sub), :] = values[i]
@@ -263,25 +309,45 @@
 
     lax.fori_loop(0, nodes // 8, gather, 0)
     lax.fori_loop(0, nodes // 16, measure, 0)
+    per_outlet = nodes // LANES
     for j in range(branches):
-        demand[j : j + 1, :] = lane_sums(partial[j])
+        demand[j * per_outlet : (j + 1) * per_outlet, :] = lane_sums(partial[j])
 
 
 def theta_kernel(
-    sizes, commodities, supply, demands, node_in, node_out, fraction, keep, home_theta, tall
+    sizes, regions, commodities, supply, shared, node_in, node_out, send_list, fraction,
+    after_ref, keep, home_theta, theta_out, slot_theta,
 ):
     cells, nodes, branches, cap, sub = sizes
     height = cells // LANES
+    per_outlet = nodes // LANES
+    block = branches * per_outlet + height
     region_no = lax.axis_index("region")
-    parts = [demands[k : k + branches, :] for k in range(0, demands.shape[0], branches)]
+    members = shared.shape[0] // block
+    parts = [
+        shared[d * block : d * block + branches * per_outlet, :] for d in range(members)
+    ]
     demand = tree_sum(parts) * (1.0 / commodities)
-    table = supply[...]
-    theta = jnp.ones((1, nodes), F32)
+    table = jnp.concatenate(
+        [supply[...]]
+        + [
+            shared[d * block + branches * per_outlet : (d + 1) * block, :] for d in range(4)
+        ],
+        axis=0,
+    )
+    tall = jnp.ones((per_outlet, LANES), F32)
     for j in range(branches):
         outs = node_out[j : j + 1, :]
-        room = look_up(table, jnp.maximum(outs, 0))
-        ratio = room / jnp.maximum(demand[j : j + 1, :], room)
-        theta = jnp.minimum(theta, jnp.where(outs >= 0, ratio, 1.0))
+        cell = jnp.maximum(outs, 0)
+        offset = (cell // cells + regions - region_no) % regions
+        sector = jnp.zeros_like(offset)
+        for d in range(4):
+            sector = jnp.where(offset == (-SHIFTS[d]) % regions, d + 1, sector)
+        room = stacked(look_up(table, sector * cells + cell % cells))
+        ratio = room / jnp.maximum(demand[j * per_outlet : (j + 1) * per_outlet, :], room)
+        tall = jnp.minimum(tall, jnp.where(stacked(outs) >= 0, ratio, 1.0))
+    theta_out[...] = tall
+    theta = strung(tall)
     cell_theta = jnp.zeros((height, LANES), F32)
     into = jnp.zeros((height, LANES), F32)
     for j in range(branches):
@@ -290,24 +356,11 @@
         into = into + scatter(home, theta, height)
     keep[...] = 1.0 - cell_theta * fraction[...]
     home_theta[...] = into
-    put_row(tall, 0, theta, 0.0)
-
-
-def slot_theta_kernel(sizes, regions, sides, theta, send_lists, scale):
-    cells, nodes, branches, cap, sub = sizes
-    region_no = lax.axis_index("region")
-    table = theta[...]
-    for side in range(4):
-        if side not in sides:
-            put_row(scale, side * (padded(cap) // LANES), jnp.ones((1, cap), F32), 1.0)
-            continue
-        sender = (region_no + (regions - SHIFTS[side])) % regions
-        slots = send_lists[pl.ds(4 * sender + side, 1), :]
-        node = jnp.where(slots >= 0, slots % nodes, 0) + sender * nodes
-        put_row(scale, side * (padded(cap) // LANES), look_up(table, node), 0.0)
-
-
-def base_kernel(sizes, keep, home_theta, node_row, outlet, rows, turns, flow, base):
+    slots = send_list[pl.ds(lax.axis_index("dest") % 4, 1), :]
+    put_row(slot_theta, 0, look_up(tall, jnp.where(slots >= 0, slots % nodes, 0)), 0.0)
+
+
+def home_kernel(sizes, node_row, outlet, turns, flow, home):
     cells, nodes, branches, cap, sub = sizes
     batch = 8
 
@@ -315,11 +368,25 @@
         first = step * batch
         values = []
         for i in range(batch):
-            cell = first + i
-            at = row_at(node_row[cell], sub)
-            moved = jnp.where(turns[at, :] == outlet[cell], flow[at, :], 0.0)
-            kept = rows[row_at(cell * sub, sub), :] * keep[cell]
-            values.append(kept + moved * home_theta[cell])
+            at = row_at(node_row[first + i], sub)
+            values.append(jnp.where(turns[at, :] == outlet[first + i], flow[at, :], 0.0))
+        for i in range(batch):
+            home[row_at((first + i) * sub, sub), :] = values[i]
+        return carry
+
+    lax.fori_loop(0, cells // batch, body, 0)
+
+
+def base_kernel(sizes, keep, home_theta, rows, home, base):
+    cells, nodes, branches, cap, sub = sizes
+    batch = 8
+
+    def body(step, carry):
+        first = step * batch
+        values = []
+        for i in range(batch):
+            at = row_at((first + i) * sub, sub)
+            values.append(rows[at, :] * keep[first + i] + home[at, :] * home_theta[first + i])
         for i in range(batch):
             base[row_at((first + i) * sub, sub), :] = values[i]
         return carry
@@ -392,6 +459,12 @@
     per_cell = (height, LANES)
     list_shape = (4 * padded(cap) // LANES, LANES)
     chunk = 128
+    some_node = node_in[0, 0] >= 0
+
+    def apart(exchange, block):
+        shape = jax.eval_shape(exchange, block)
+        return lax.cond(some_node, exchange, lambda x: jnp.zeros(shape.shape, F32), block)
+
     row_bytes = width * 4
     occupancy = pltpu.with_memory_space_constraint(occupancy, pltpu.HBM)
     turn = pltpu.with_memory_space_constraint(turn, pltpu.HBM)
@@ -406,10 +479,10 @@
         ],
         scratch_shapes=[
             pltpu.VMEM((cells, width), F32),
-            pltpu.VMEM((chunk, LANES), F32),
+            pltpu.VMEM((cells, LANES), F32),
             pltpu.SemaphoreType.DMA((cells // chunk,)),
         ],
-        compiler_params=params(12),
+        compiler_params=params(14),
         cost_estimate=cost(cells * width, cells * row_bytes),
         name="cell_sum",
     )(occupancy)
@@ -449,92 +522,107 @@
     cap_of = capacity.reshape(per_cell)
     fraction = jnp.minimum(vehicles, cap_of) / vehicles
     supply = jnp.minimum(cap_of, wave.reshape(per_cell) * (jam.reshape(per_cell) - vehicles))
-    weights = jnp.concatenate([fraction.reshape(-1), jnp.zeros((LANES,), F32)])
-
-    def send_rows(sides, after):
-        return pl.pallas_call(
-            functools.partial(send_kernel, sizes, sides),
-            in_specs=[SMEM_WHOLE] * 4 + [VMEM_WHOLE] * 2 + [ANYWHERE] * len(after),
-            out_specs=[VMEM_WHOLE] * len(sides),
-            out_shape=[pltpu.VMEM((cap * sub, LANES), F32)] * len(sides),
-            compiler_params=params(4),
-            cost_estimate=cost(cap * width * 20, cap * row_bytes * 10),
-            name="send_rows",
-        )(weights, in_cell, send_node, send_outlet, rows, turns, *after)
-
-    near = send_rows((0, 1), ())
-    ahead = send_rows((2,), near[:1])
+    rows_shape = pltpu.VMEM(((cells + 1) * sub, LANES), F32)
+    send_shape = pltpu.VMEM((cap * sub, LANES), F32)
+
+    scaled, *near = pl.pallas_call(
+        functools.partial(scale_send_kernel, sizes, (0, 1)),
+        in_specs=[SMEM_WHOLE] * 4 + [VMEM_WHOLE] * 2,
+        out_specs=[VMEM_WHOLE] * 3,
+        out_shape=[rows_shape] + [send_shape] * 2,
+        compiler_params=params(4),
+        cost_estimate=cost(cap * width * 20, cap * row_bytes * 10),
+        name="send_near",
+    )(fraction.reshape(-1), in_cell, send_node, send_outlet, rows, turns)
+    ahead = pl.pallas_call(
+        functools.partial(send_kernel, sizes, (2,)),
+        in_specs=[SMEM_WHOLE] * 3 + [VMEM_WHOLE] * 2,
+        out_specs=VMEM_WHOLE,
+        out_shape=send_shape,
+        compiler_params=params(4),
+        cost_estimate=cost(1, 1),
+        name="send_ahead",
+    )(in_cell, send_node, send_outlet, scaled, turns)
     arrived = [
-        shifted(send, "region", SHIFTS[side]) for side, send in enumerate([*near, *ahead])
+        shifted(send, "region", SHIFTS[side]) for side, send in enumerate([*near, ahead])
     ]
 
-    supply, _ = lax.optimization_barrier((supply, ahead[0]))
-    supplies = lax.all_gather(supply, "region", axis=0, tiled=True)
-    send_lists = lax.all_gather(send_list, "region", axis=0, tiled=True)
+    supply, *_ = lax.optimization_barrier((supply, *near, ahead))
+    supply_there = to_neighbours(supply)
 
     flow, demand = pl.pallas_call(
         functools.partial(node_flow_kernel, sizes),
-        in_specs=[SMEM_WHOLE] * 2 + [VMEM_WHOLE] * 2 + [ANYWHERE],
+        in_specs=[SMEM_WHOLE] + [VMEM_WHOLE] * 2 + [ANYWHERE],
         out_specs=[VMEM_WHOLE] * 2,
         out_shape=[
             pltpu.VMEM((nodes * sub, LANES), F32),
-            jax.ShapeDtypeStruct((branches, nodes), F32),
+            jax.ShapeDtypeStruct((branches * nodes // LANES, LANES), F32),
         ],
         scratch_shapes=[pltpu.VMEM((branches, nodes, LANES), F32)],
         compiler_params=params(8),
-        cost_estimate=cost(nodes * width * 16, nodes * row_bytes * 6),
+        cost_estimate=cost(1, 1),
         name="node_flow",
-    )(weights, in_cell, rows, turns, ahead[0])
-
-    demands = lax.all_gather(demand, "dest", axis=0, tiled=True)
-    keep, home_theta, theta = pl.pallas_call(
-        functools.partial(theta_kernel, sizes, commodities),
+    )(in_cell, scaled, turns, supply_there)
+
+    shared = apart(
+        lambda x: lax.all_gather(x, "dest", axis=0, tiled=True),
+        jnp.concatenate([demand, supply_there]),
+    )
+    home = pl.pallas_call(
+        functools.partial(home_kernel, sizes),
+        in_specs=[SMEM_WHOLE] * 2 + [VMEM_WHOLE] * 2,
+        out_specs=VMEM_WHOLE,
+        out_shape=rows_shape,
+        compiler_params=params(4),
+        cost_estimate=cost(1, 1),
+        name="home_rows",
+    )(source_node, source_outlet, turns, flow)
+    keep, home_theta, theta, slot_theta = pl.pallas_call(
+        functools.partial(theta_kernel, sizes, regions, commodities),
+        in_specs=[VMEM_WHOLE] * 6 + [ANYWHERE],
+        out_specs=[VMEM_WHOLE] * 4,
         out_shape=[jax.ShapeDtypeStruct(per_cell, F32)] * 2
-        + [jax.ShapeDtypeStruct((nodes // LANES, LANES), F32)],
+        + [
+            jax.ShapeDtypeStruct((nodes // LANES, LANES), F32),
+            jax.ShapeDtypeStruct((padded(cap) // LANES, LANES), F32),
+        ],
         compiler_params=params(8),
-        cost_estimate=cost(branches * nodes * cells * 8, nodes * 256),
+        cost_estimate=cost(1, 1),
         name="theta",
-    )(supplies, demands, node_in, node_out, fraction)
+    )(supply, shared, node_in, node_out, send_list, fraction, home)
+    theta_there = apart(to_neighbours, slot_theta)
+    scale = lax.all_gather(theta_there, "dest", axis=0, tiled=True)[: list_shape[0]]
 
     (behind,) = pl.pallas_call(
         functools.partial(scaled_send_kernel, sizes, 3),
         in_specs=[SMEM_WHOLE] * 3 + [VMEM_WHOLE] * 2,
         out_specs=[VMEM_WHOLE],
-        out_shape=[pltpu.VMEM((cap * sub, LANES), F32)],
+        out_shape=[send_shape],
         compiler_params=params(4),
-        cost_estimate=cost(cap * width * 4, cap * row_bytes * 4),
-        name="scaled_send_rows",
+        cost_estimate=cost(1, 1),
+        name="send_scaled",
     )(theta.reshape(-1), send_node, send_outlet, flow, turns)
+    behind, _ = lax.optimization_barrier((behind, theta_there))
     last = shifted(behind, "region", SHIFTS[3])
 
-    thetas = lax.all_gather(theta, "region", axis=0, tiled=True)
-    scale = pl.pallas_call(
-        functools.partial(slot_theta_kernel, sizes, regions, (0, 1, 2)),
-        out_shape=jax.ShapeDtypeStruct(list_shape, F32),
-        compiler_params=params(8),
-        cost_estimate=cost(4 * cap * 2048, nodes * 64),
-        name="slot_theta",
-    )(thetas, send_lists)
-
-    base_shape = pltpu.VMEM(((cells + 1) * sub, LANES), F32)
     base = pl.pallas_call(
         functools.partial(base_kernel, sizes),
-        in_specs=[SMEM_WHOLE] * 4 + [VMEM_WHOLE] * 3,
+        in_specs=[SMEM_WHOLE] * 2 + [VMEM_WHOLE] * 2,
         out_specs=VMEM_WHOLE,
-        out_shape=base_shape,
+        out_shape=rows_shape,
         compiler_params=params(4),
-        cost_estimate=cost(cells * width * 4, cells * row_bytes * 4),
-        name="home_inflow",
-    )(keep.reshape(-1), home_theta.reshape(-1), source_node, source_outlet, rows, turns, flow)
+        cost_estimate=cost(1, 1),
+        name="base_rows",
+    )(keep.reshape(-1), home_theta.reshape(-1), rows, home)
 
     base = pl.pallas_call(
         functools.partial(land_kernel, sizes, (0, 1, 2)),
         in_specs=[SMEM_WHOLE] * 2 + [VMEM_WHOLE] * 4,
         out_specs=VMEM_WHOLE,
-        out_shape=base_shape,
+        out_shape=rows_shape,
         input_output_aliases={5: 0},
         compiler_params=params(4),
-        cost_estimate=cost(cap * width * 6, cap * row_bytes * 9),
+        cost_estimate=cost(1, 1),
         name="land_first",
     )(scale.reshape(-1), land, *arrived, base)
 
@@ -542,7 +630,7 @@
         functools.partial(finish_kernel, sizes, (3,), chunk),
         in_specs=[SMEM_WHOLE] + [VMEM_WHOLE] * 2,
         out_specs=[ANYWHERE, VMEM_WHOLE],
-        out_shape=[jax.ShapeDtypeStruct((cells, width), F32), base_shape],
+        out_shape=[jax.ShapeDtypeStruct((cells, width), F32), rows_shape],
         scratch_shapes=[
             pltpu.VMEM((cells, width), F32),
             pltpu.SemaphoreType.DMA((cells // chunk,)),

time: 207 us -> 103 us (0.50)
  blocking collectives: 129 us -> 12.4 us
  waiting for transfers between devices: 0.02 us -> 12 us
  starting transfers between devices: 8 us -> 11.2 us
  Pallas kernels: 54.5 us -> 51.5 us
    all_gather x4 -> x2, blocking collectives: 129 us -> 12.4 us  [the longest x1 6.31 us: on_device(): lax.all_gather(x, 'dest', axis=0, tiled=True)]
    ppermute x0 -> x2, waiting for transfers between devices: none -> 12 us  [to_neighbours(): return lax.ppermute(block, ('region', 'dest'), route)]
    pallas_call x4, Pallas kernels: 13.9 us -> 20.2 us  [the longest x1 6.62 us: on_device(): pl.pallas_call(functools.partial(scale_send_kernel, sizes, (0, 1)), in_sp...]
    pallas_call x1, Pallas kernels: 8.6 us -> 4.69 us  [on_device(): pl.pallas_call(functools.partial(cell_sum_kernel, chunk, sub), in_specs=[...]
    ppermute x0 -> x2, starting transfers between devices: none -> 2.71 us  [to_neighbours(): return lax.ppermute(block, ('region', 'dest'), route)]
    pallas_call x1, Pallas kernels: 6.99 us -> 4.7 us  [on_device(): pl.pallas_call(functools.partial(base_kernel, sizes), in_specs=[SMEM_WHOL...]
  transfers between devices with their start and end apart: 7 -> 9, of which waited for: 0 -> 1; matrix products, arithmetic and copies ran while one was open for 0% -> 1% of each run, Pallas kernels for 10% -> 32%
where the time goes in v4:
time: 103 us; the launch traced here: 102 us
  Pallas kernels  51.5 us (50%)
  local copies, waits for them, and re-layouts  14.3 us (14%)
  blocking collectives  12.4 us (12%)
  waiting for transfers between devices  12 us (12%)
  starting transfers between devices  11.2 us (11%)
    unnamed x34, local copies, waits for them, and re-layouts  13.8 us
    ppermute x2, waiting for transfers between devices, to_neighbours(): return lax.ppermute(block, ('region', 'dest'), route)  12 us
    pallas_call x1, Pallas kernels, on_device(): pl.pallas_call(functools.partial(node_flow_kernel, sizes), in_specs=[SMEM...  10.1 us
    pallas_call x1, Pallas kernels, on_device(): pl.pallas_call(functools.partial(scale_send_kernel, sizes, (0, 1)), in_sp...  6.62 us
    all_gather x1, blocking collectives, on_device(): lax.all_gather(x, 'dest', axis=0, tiled=True)  6.31 us
    all_gather x1, blocking collectives, on_device(): lax.all_gather(theta_there, 'dest', axis=0, tiled=True)[:list_shape[0]]  6.11 us
    pallas_call x1, Pallas kernels, on_device(): pl.pallas_call(functools.partial(theta_kernel, sizes, regions, commoditie...  5.76 us
    ppermute x4, starting transfers between devices, shifted(): return lax.ppermute(block, axis, route)  5.28 us
  transfers between devices with their start and end apart: 9, of which 1 were waited for; matrix products, arithmetic and copies ran while one was open for 1% of the time, Pallas kernels for 32%

profile of v4, /device:TPU:0, one launch (start us, length us, event | category | flops | bytes accessed | tf_op | source)
XLA Modules:
  0.0 102.4 jit_solution(7787392083546196018)
XLA Ops:
  0.0 4.7 %cell_sum.1 = (f32[16,128]{1,0:T(8,128)S(1)}, f32[16392,128]{1,0:T(8,128)S(1)}) custom-call(f32[2048,1024]{1,0:T(8,128)} %x_hbm.2), custom_call_target="tpu_custom_call" | custom-call | flops 2097152 | bytes 8388608 | tf_op jit(solution)/shard_map/cell_sum/pallas_call | solution.py:472
  4.7 3.0 %collective-permute-start.2 = (f32[16,128]{1,0:T(8,128)S(1)}, f32[16,128]{1,0:T(8,128)S(1)}, u32[]{:S(2)}, u32[]{:S(2)}) collective-permute-start(f32[16,128]{1,0:T(8,128)S(1)} %get-tuple-element.33.after_ref), channel_id=1, source_target_pairs={{0,2},{1,3},{2,0},{3,1},{4,6},{5,7},{6,4},{7,5},{8,10},{9,11},{10,... | collective-permute-start | bytes 24584 | tf_op jit(solution)/shard_map/ppermute | solution.py:40
  7.7 0.2 collective-permute-start.1
  7.9 2.3 %turn_rows.1.turns = s32[8192,128]{1,0:T(8,128)S(1)} custom-call(s32[1024,1024]{1,0:T(8,128)} %x_hbm.3, f32[16,128]{1,0:T(8,128)S(1)} %get-tuple-element.33.after_ref), custom_call_target="tpu_custom_call" | custom-call | bytes 4194304 | tf_op jit(solution)/shard_map/turn_rows/pallas_call | solution.py:492
  10.3 1.9 %index_lists.1 = (s32[32,128]{1,0:T(8,128)S(1)}, s32[8,128]{1,0:T(8,128)S(1)}, s32[8,128]{1,0:T(8,128)S(1)}, s32[8,128]{1,0:T(8,128)S(1)}, s32[16,128]{1,0:T(8,128)S(1)}, /*index=5*/s32[16,128]{1,0:T(8,128)S(1)}) custom-call(s32[4,1024]{1,0:T(4,128)S(1)} %copy-done.10, s32[4,1024]{1,0:T(4,128)S(1)} %copy-done.11, s32[4,192]{1,0:T(4,128)S(1)} %copy-done.12, ...), custom_call_target="tpu_custom_call" | custom-call | flops 16777216 | bytes 65536 | tf_op jit(solution)/shard_map/index_lists/pallas_call | solution.py:506
  12.3 6.6 %send_near.1 = (f32[16392,128]{1,0:T(8,128)S(1)}, f32[1536,128]{1,0:T(8,128)}, f32[1536,128]{1,0:T(8,128)}) custom-call(f32[2048]{0:T(1024)S(1)} %bitcast.27, s32[4096]{0:T(1024)S(1)} %bitcast.24, s32[1024]{0:T(1024)S(1)} %bitcast.28, s32[1024]{0:T(1024)S(1)} %bitcast.31, f32[16392,128]{1,0:T(8,128)S(1)} %get-tuple-element.38.rows, ...), custom_call_target="tpu_custom_call" | custom-call | flops 3932160 | bytes 7864320 | tf_op jit(solution)/shard_map/send_near/pallas_call | solution.py:528
  18.9 3.1 %send_ahead.1 = f32[1536,128]{1,0:T(8,128)} custom-call(s32[4096]{0:T(1024)S(1)} %bitcast.25, s32[1024]{0:T(1024)S(1)} %bitcast.29, s32[1024]{0:T(1024)S(1)} %bitcast.32, f32[16392,128]{1,0:T(8,128)S(1)} %get-tuple-element.41.scaled, s32[8192,128]{1,0:T(8,128)S(1)} %turn_rows.1.turns), custom_call_target="tpu_custom_call" | custom-call | flops 1 | bytes 1 | tf_op jit(solution)/shard_map/send_ahead/pallas_call | solution.py:537
  22.0 2.6 %collective-permute-start.4 = (f32[16,128]{1,0:T(8,128)S(1)}, f32[16,128]{1,0:T(8,128)S(1)}, u32[]{:S(2)}, u32[]{:S(2)}) collective-permute-start(f32[16,128]{1,0:T(8,128)S(1)} %fusion.1.supply), channel_id=1, source_target_pairs={{0,4},{1,29},{2,10},{3,27},{4,8},{5,1},{6,14},{7,31},{8,12},{9,5},... | collective-permute-start | bytes 24584 | tf_op jit(solution)/shard_map/ppermute | solution.py:28
  24.6 0.5 slice.3
  25.8 1.6 %collective-permute-start.6 = (f32[1536,128]{1,0:T(8,128)}, f32[1536,128]{1,0:T(8,128)S(1)}, u32[]{:S(2)}, u32[]{:S(2)}) collective-permute-start(f32[1536,128]{1,0:T(8,128)} %get-tuple-element.39), channel_id=1, source_target_pairs={{28,0},{0,4},{4,8},{8,12},{12,16},{16,20},{20,24},{24,28},{29,1},{... | collective-permute-start | bytes 2359304 | tf_op jit(solution)/shard_map/ppermute | solution.py:34
  27.4 3.2 %collective-permute-start.7 = (f32[1536,128]{1,0:T(8,128)}, f32[1536,128]{1,0:T(8,128)S(1)}, u32[]{:S(2)}, u32[]{:S(2)}) collective-permute-start(f32[1536,128]{1,0:T(8,128)} %get-tuple-element.40), channel_id=1, source_target_pairs={{4,0},{8,4},{12,8},{16,12},{20,16},{24,20},{28,24},{0,28},{5,1},{9... | collective-permute-start | bytes 2359304 | tf_op jit(solution)/shard_map/ppermute | solution.py:34
  30.6 10.1 %node_flow.1 = (f32[8192,128]{1,0:T(8,128)S(1)}, f32[32,128]{1,0:T(8,128)S(1)}) custom-call(s32[4096]{0:T(1024)S(1)} %bitcast.26, f32[16392,128]{1,0:T(8,128)S(1)} %get-tuple-element.41.scaled, s32[8192,128]{1,0:T(8,128)S(1)} %turn_rows.1.turns, f32[16,128]{1,0:T(8,128)S(1)} %collective-permute-done.4.after_ref), custom_call_target="tpu_custom_call" | custom-call | flops 1 | bytes 1 | tf_op jit(solution)/shard_map/node_flow/pallas_call | solution.py:553
  40.7 1.9 %copy-done.7 = f32[8192,128]{1,0:T(8,128)} copy-done((f32[8192,128]{1,0:T(8,128)}, f32[8192,128]{1,0:T(8,128)S(1)}, u32[]{:S(2)}) %copy-start.7) | copy-done | bytes 4194328
  42.7 6.3 %conditional.2 = (f32[192,128]{1,0:T(8,128)S(1)}) conditional(s32[]{:T(128)} %bitcast.8, () %tuple.20, f32[48,128]{1,0:T(8,128)S(1)} %pad_maximum_fusion), branch_computations={%region_0.0_spmd, %region_1.0_spmd} | conditional | bytes 122888 | solution.py:466
  42.7 6.3 %all_gather.4 = f32[192,128]{1,0:T(8,128)S(1)} all-gather(f32[48,128]{1,0:T(8,128)S(1)} %param.1), channel_id=1, replica_groups=mesh['region'=8,'dest'=4] {'dest'}, dimensions={0}, use_global_device_ids=true | all-gather | bytes 122880 | tf_op jit(solution)/shard_map/cond/branch_1_fun/all_gather | solution.py:568
  49.0 2.2 %copy-done.1 = s32[8192,128]{1,0:T(8,128)S(1)} copy-done((s32[8192,128]{1,0:T(8,128)S(1)}, s32[8192,128]{1,0:T(8,128)}, u32[]{:S(2)}) %copy-start.1) | copy-done | bytes 4194328
  51.2 2.2 %copy-done.8 = f32[8192,128]{1,0:T(8,128)S(1)} copy-done((f32[8192,128]{1,0:T(8,128)S(1)}, f32[8192,128]{1,0:T(8,128)}, u32[]{:S(2)}) %copy-start.8) | copy-done | bytes 4194328
  53.4 4.7 %home_rows.1.after_ref.home = f32[16392,128]{1,0:T(8,128)S(1)} custom-call(s32[2048]{0:T(1024)S(1)} %bitcast.37, s32[2048]{0:T(1024)S(1)} %bitcast.38, s32[8192,128]{1,0:T(8,128)S(1)} %copy-done.1, f32[8192,128]{1,0:T(8,128)S(1)} %copy-done.8), custom_call_target="tpu_custom_call" | custom-call | flops 1 | bytes 1 | tf_op jit(solution)/shard_map/home_rows/pallas_call | solution.py:571
  58.1 0.1 collective-permute-start.8
  58.2 5.8 %theta.1 = (f32[16,128]{1,0:T(8,128)S(1)}, f32[16,128]{1,0:T(8,128)S(1)}, f32[8,128]{1,0:T(8,128)S(1)}, f32[2,128]{1,0:T(2,128)S(1)}) custom-call(f32[16,128]{1,0:T(8,128)S(1)} %fusion.1.supply, f32[192,128]{1,0:T(8,128)S(1)} %get-tuple-element.55.shared, s32[4,1024]{1,0:T(4,128)S(1)} %copy-done.10, s32[4,1024]{1,0:T(4,128)S(1)} %copy-done.11, ...), custom_call_target="tpu_custom_call" | custom-call | flops 1 | bytes 1 | tf_op jit(solution)/shard_map/theta/pallas_call | solution.py:580
  64.0 0.6 copy-done.9
  64.6 1.2 %send_scaled.1 = f32[1536,128]{1,0:T(8,128)S(1)} custom-call(f32[1024]{0:T(1024)S(1)} %bitcast.41, s32[1024]{0:T(1024)S(1)} %bitcast.30, s32[1024]{0:T(1024)S(1)} %bitcast.33, f32[8192,128]{1,0:T(8,128)S(1)} %copy-done.9, s32[8192,128]{1,0:T(8,128)S(1)} %copy-done.2), custom_call_target="tpu_custom_call" | custom-call | flops 1 | bytes 1 | tf_op jit(solution)/shard_map/send_scaled/pallas_call | solution.py:596
  65.8 12.1 %conditional.3 = (f32[2,128]{1,0:T(2,128)}) conditional(s32[]{:T(128)} %bitcast.8, () %tuple.21, f32[2,128]{1,0:T(2,128)S(1)} %get-tuple-element.48), branch_computations={%region_2.0_spmd, %region_3.0_spmd} | conditional | bytes 4144 | solution.py:466
  65.9 0.1 collective-permute-start
  65.9 12.0 %collective-permute-done = f32[2,128]{1,0:T(2,128)} collective-permute-done((f32[2,128]{1,0:T(2,128)S(1)}, f32[2,128]{1,0:T(2,128)}, u32[]{:S(2)}, u32[]{:S(2)}) %collective-permute-start) | collective-permute-done | bytes 1056 | tf_op jit(solution)/shard_map/cond/branch_1_fun/ppermute | solution.py:28
  77.9 0.4 collective-permute-start.5
  78.4 3.4 %copy-done.4 = f32[16392,128]{1,0:T(8,128)S(1)} copy-done((f32[16392,128]{1,0:T(8,128)S(1)}, f32[16392,128]{1,0:T(8,128)}, u32[]{:S(2)}) %copy-start.4) | copy-done | bytes 8392728
  81.8 3.4 %copy-done.6 = f32[16392,128]{1,0:T(8,128)S(1)} copy-done((f32[16392,128]{1,0:T(8,128)S(1)}, f32[16392,128]{1,0:T(8,128)}, u32[]{:S(2)}) %copy-start.6) | copy-done | bytes 8392728
  85.2 4.7 %base_rows.1.rest_3_ = f32[16392,128]{1,0:T(8,128)S(1)} custom-call(f32[2048]{0:T(1024)S(1)} %bitcast.39, f32[2048]{0:T(1024)S(1)} %bitcast.40, f32[16392,128]{1,0:T(8,128)S(1)} %copy-done.6, f32[16392,128]{1,0:T(8,128)S(1)} %copy-done.4), custom_call_target="tpu_custom_call" | custom-call | flops 1 | bytes 1 | tf_op jit(solution)/shard_map/base_rows/pallas_call | solution.py:608
  89.9 6.1 %all-gather = f32[4,2,128]{2,1,0:T(2,128)S(1)} all-gather(f32[1,2,128]{2,1,0:T(2,128)} %bitcast.12), channel_id=1, replica_groups=mesh['region'=8,'dest'=4] {'dest'}, dimensions={0}, use_global_device_ids=true | all-gather | bytes 5120 | tf_op jit(solution)/shard_map/all_gather | solution.py:594
  96.0 1.9 %land_first.1.rest_1_ = f32[16392,128]{1,0:T(8,128)S(1)} custom-call(f32[1024]{0:T(1024)S(1)} %bitcast.36, s32[1024]{0:T(1024)S(1)} %bitcast.34, f32[1536,128]{1,0:T(8,128)S(1)} %collective-permute-done.6.rest_0_, f32[1536,128]{1,0:T(8,128)S(1)} %collective-permute-done.7.rest_1_, ...), custom_call_target="tpu_custom_call", output_to_operand_aliasing={{}: (5, {})} | custom-call | flops 1 | bytes 1 | tf_op jit(solution)/shard_map/land_first/pallas_call | solution.py:618
  97.9 4.5 %finish.1 = (f32[2048,1024]{1,0:T(8,128)}, f32[16392,128]{1,0:T(8,128)S(1)}) custom-call(s32[1024]{0:T(1024)S(1)} %bitcast.35, f32[1536,128]{1,0:T(8,128)S(1)} %collective-permute-done.5.rest_0_, f32[16392,128]{1,0:T(8,128)S(1)} %land_first.1.rest_1_), custom_call_target="tpu_custom_call", output_to_operand_aliasing={{1}: (2, {})} | custom-call | flops 2097152 | bytes 8388608 | tf_op jit(solution)/shard_map/finish/pallas_call | solution.py:629
  (40 shorter events, 0.1 us)
Async XLA Ops:
  0.0 10.3 %copy-start.10 = (s32[4,1024]{1,0:T(4,128)S(1)}, s32[4,1024]{1,0:T(4,128)}, u32[]{:S(2)}) copy-start(s32[4,1024]{1,0:T(4,128)} %node_in.3) | copy-start | bytes 49156
  0.0 10.3 %copy-start.11 = (s32[4,1024]{1,0:T(4,128)S(1)}, s32[4,1024]{1,0:T(4,128)}, u32[]{:S(2)}) copy-start(s32[4,1024]{1,0:T(4,128)} %node_out.3) | copy-start | bytes 49156
  0.0 10.3 %copy-start.12 = (s32[4,192]{1,0:T(4,128)S(1)}, s32[4,192]{1,0:T(4,128)}, u32[]{:S(2)}) copy-start(s32[4,192]{1,0:T(4,128)} %send_list.3) | copy-start | bytes 9220
  0.0 10.3 %copy-start.13 = (s32[4,192]{1,0:T(4,128)S(1)}, s32[4,192]{1,0:T(4,128)}, u32[]{:S(2)}) copy-start(s32[4,192]{1,0:T(4,128)} %recv_list.1) | copy-start | bytes 9220
  0.0 12.2 %copy-start.14 = (f32[2048]{0:T(1024)S(1)}, f32[2048]{0:T(1024)}, u32[]{:S(2)}) copy-start(f32[2048]{0:T(1024)} %param.14) | copy-start | bytes 24580
  4.7 14.2 %copy-start.5 = (f32[16392,128]{1,0:T(8,128)}, f32[16392,128]{1,0:T(8,128)S(1)}, u32[]{:S(2)}) copy-start(f32[16392,128]{1,0:T(8,128)S(1)} %get-tuple-element.38.rows) | copy-start | bytes 25178116
  4.7 7.5 %collective-permute-start.2 = (f32[16,128]{1,0:T(8,128)S(1)}, f32[16,128]{1,0:T(8,128)S(1)}, u32[]{:S(2)}, u32[]{:S(2)}) collective-permute-start(f32[16,128]{1,0:T(8,128)S(1)} %get-tuple-element.33.after_ref), channel_id=1, source_target_pairs={{0,2},{1,3},{2,0},{3,1},{4,6},{5,7},{6,4},{7,5},{8,10},{9,11},{10,... | collective-permute-start | bytes 24584 | tf_op jit(solution)/shard_map/ppermute | solution.py:40
  7.7 4.5 %collective-permute-start.3 = (f32[16,128]{1,0:T(8,128)S(1)}, f32[16,128]{1,0:T(8,128)S(1)}, u32[]{:S(2)}, u32[]{:S(2)}) collective-permute-start(f32[16,128]{1,0:T(8,128)S(1)} %get-tuple-element.33.after_ref), channel_id=1, source_target_pairs={{0,3},{1,2},{2,1},{3,0},{4,7},{5,6},{6,5},{7,4},{8,11},{9,10},{10,... | collective-permute-start | bytes 24584 | tf_op jit(solution)/shard_map/ppermute | solution.py:40
  7.7 4.5 %collective-permute-start.1 = (f32[16,128]{1,0:T(8,128)S(1)}, f32[16,128]{1,0:T(8,128)S(1)}, u32[]{:S(2)}, u32[]{:S(2)}) collective-permute-start(f32[16,128]{1,0:T(8,128)S(1)} %get-tuple-element.33.after_ref), channel_id=1, source_target_pairs={{0,1},{1,0},{2,3},{3,2},{4,5},{5,4},{6,7},{7,6},{8,9},{9,8},{10,11... | collective-permute-start | bytes 24584 | tf_op jit(solution)/shard_map/ppermute | solution.py:40
  10.3 20.3 %copy-start = (s32[8192,128]{1,0:T(8,128)}, s32[8192,128]{1,0:T(8,128)S(1)}, u32[]{:S(2)}) copy-start(s32[8192,128]{1,0:T(8,128)S(1)} %turn_rows.1.turns) | copy-start | bytes 12582916
  18.9 3.1 %copy-start.15 = (f32[2048]{0:T(1024)S(1)}, f32[2048]{0:T(1024)}, u32[]{:S(2)}) copy-start(f32[2048]{0:T(1024)} %param.15) | copy-start | bytes 24580
  18.9 3.1 %copy-start.16 = (f32[2048]{0:T(1024)S(1)}, f32[2048]{0:T(1024)}, u32[]{:S(2)}) copy-start(f32[2048]{0:T(1024)} %param.16) | copy-start | bytes 24580
  22.0 8.6 %collective-permute-start.4 = (f32[16,128]{1,0:T(8,128)S(1)}, f32[16,128]{1,0:T(8,128)S(1)}, u32[]{:S(2)}, u32[]{:S(2)}) collective-permute-start(f32[16,128]{1,0:T(8,128)S(1)} %fusion.1.supply), channel_id=1, source_target_pairs={{0,4},{1,29},{2,10},{3,27},{4,8},{5,1},{6,14},{7,31},{8,12},{9,5},... | collective-permute-start | bytes 24584 | tf_op jit(solution)/shard_map/ppermute | solution.py:28
  25.8 70.2 %collective-permute-start.6 = (f32[1536,128]{1,0:T(8,128)}, f32[1536,128]{1,0:T(8,128)S(1)}, u32[]{:S(2)}, u32[]{:S(2)}) collective-permute-start(f32[1536,128]{1,0:T(8,128)} %get-tuple-element.39), channel_id=1, source_target_pairs={{28,0},{0,4},{4,8},{8,12},{12,16},{16,20},{20,24},{24,28},{29,1},{... | collective-permute-start | bytes 2359304 | tf_op jit(solution)/shard_map/ppermute | solution.py:34
  27.4 68.6 %collective-permute-start.7 = (f32[1536,128]{1,0:T(8,128)}, f32[1536,128]{1,0:T(8,128)S(1)}, u32[]{:S(2)}, u32[]{:S(2)}) collective-permute-start(f32[1536,128]{1,0:T(8,128)} %get-tuple-element.40), channel_id=1, source_target_pairs={{4,0},{8,4},{12,8},{16,12},{20,16},{24,20},{28,24},{0,28},{5,1},{9... | collective-permute-start | bytes 2359304 | tf_op jit(solution)/shard_map/ppermute | solution.py:34
  40.7 2.0 %copy-start.7 = (f32[8192,128]{1,0:T(8,128)}, f32[8192,128]{1,0:T(8,128)S(1)}, u32[]{:S(2)}) copy-start(f32[8192,128]{1,0:T(8,128)S(1)} %get-tuple-element.46.flow) | copy-start | bytes 12582916
  49.0 2.2 %copy-start.1 = (s32[8192,128]{1,0:T(8,128)S(1)}, s32[8192,128]{1,0:T(8,128)}, u32[]{:S(2)}) copy-start(s32[8192,128]{1,0:T(8,128)} %copy-done) | copy-start | bytes 12582916
  51.2 2.2 %copy-start.8 = (f32[8192,128]{1,0:T(8,128)S(1)}, f32[8192,128]{1,0:T(8,128)}, u32[]{:S(2)}) copy-start(f32[8192,128]{1,0:T(8,128)} %copy-done.7) | copy-start | bytes 12582916
  58.1 7.7 %copy-start.3 = (f32[16392,128]{1,0:T(8,128)}, f32[16392,128]{1,0:T(8,128)S(1)}, u32[]{:S(2)}) copy-start(f32[16392,128]{1,0:T(8,128)S(1)} %home_rows.1.after_ref.home) | copy-start | bytes 25178116
  58.1 5.9 %copy-start.2 = (s32[8192,128]{1,0:T(8,128)S(1)}, s32[8192,128]{1,0:T(8,128)}, u32[]{:S(2)}) copy-start(s32[8192,128]{1,0:T(8,128)} %copy-done) | copy-start | bytes 12582916
  58.1 6.5 %copy-start.9 = (f32[8192,128]{1,0:T(8,128)S(1)}, f32[8192,128]{1,0:T(8,128)}, u32[]{:S(2)}) copy-start(f32[8192,128]{1,0:T(8,128)} %copy-done.7) | copy-start | bytes 12582916
  58.1 37.9 %collective-permute-start.8 = (f32[1536,128]{1,0:T(8,128)}, f32[1536,128]{1,0:T(8,128)S(1)}, u32[]{:S(2)}, u32[]{:S(2)}) collective-permute-start(f32[1536,128]{1,0:T(8,128)} %send_ahead.1), channel_id=1, source_target_pairs={{24,0},{28,4},{0,8},{4,12},{8,16},{12,20},{16,24},{20,28},{25,1},{... | collective-permute-start | bytes 2359304 | tf_op jit(solution)/shard_map/ppermute | solution.py:34
  65.9 12.1 %collective-permute-start = (f32[2,128]{1,0:T(2,128)S(1)}, f32[2,128]{1,0:T(2,128)}, u32[]{:S(2)}, u32[]{:S(2)}) collective-permute-start(f32[2,128]{1,0:T(2,128)S(1)} %param.3), channel_id=1, source_target_pairs={{0,4},{1,29},{2,10},{3,27},{4,8},{5,1},{6,14},{7,31},{8,12},{9,5},... | collective-permute-start | bytes 3080 | tf_op jit(solution)/shard_map/cond/branch_1_fun/ppermute | solution.py:28
  77.9 19.9 %collective-permute-start.5 = (f32[1536,128]{1,0:T(8,128)S(1)}, f32[1536,128]{1,0:T(8,128)S(1)}, u32[]{:S(2)}, u32[]{:S(2)}) collective-permute-start(f32[1536,128]{1,0:T(8,128)S(1)} %send_scaled.1), channel_id=1, source_target_pairs={{8,0},{12,4},{16,8},{20,12},{24,16},{28,20},{0,24},{4,28},{9,1},{1... | collective-permute-start | bytes 2359304 | tf_op jit(solution)/shard_map/ppermute | solution.py:34
  78.4 3.4 %copy-start.4 = (f32[16392,128]{1,0:T(8,128)S(1)}, f32[16392,128]{1,0:T(8,128)}, u32[]{:S(2)}) copy-start(f32[16392,128]{1,0:T(8,128)} %copy-done.3) | copy-start | bytes 25178116
  81.8 3.4 %copy-start.6 = (f32[16392,128]{1,0:T(8,128)S(1)}, f32[16392,128]{1,0:T(8,128)}, u32[]{:S(2)}) copy-start(f32[16392,128]{1,0:T(8,128)} %copy-done.5) | copy-start | bytes 25178116

commit v5 on v4

--- a/solution.py
+++ b/solution.py
@@ -79,8 +79,10 @@
     return jnp.concatenate([rows[k : k + 1, :] for k in range(rows.shape[0])], axis=1)
 
 
-def row_at(index, sub):
-    return pl.ds(pl.multiple_of(index, sub), sub)
+def row_of(ref, number, sub):
+    if sub % 8 == 0:
+        return ref.reshape(ref.shape[0] // sub, sub, LANES).at[number]
+    return ref.at[pl.ds(pl.multiple_of(number * sub, sub), sub), :]
 
 
 def padded(cap):
@@ -150,38 +152,8 @@
     return copies
 
 
-def cell_sum_kernel(chunk, sub, x_hbm, sum_ref, rows_ref, x, partial, sems):
-    copies = copies_in(x_hbm, x, sems, chunk)
-    zeros = rows_ref.shape[0] - sub
-    rows_ref[zeros:, :] = jnp.zeros((sub, LANES), F32)
-    for number, copy in enumerate(copies):
-        copy.wait()
-
-        def body(step, carry, number=number):
-            for half in range(2):
-                first = number * chunk + step * 16 + half * 8
-                total = rows_of_group(x, rows_ref, first, sub)
-                partial[pl.ds(pl.multiple_of(first, 8), 8), :] = total
-            return carry
-
-        lax.fori_loop(0, chunk // 16, body, 0)
-    sum_ref[...] = lane_sums(partial[...])
-
-
-def turn_rows_kernel(chunk, sub, x_hbm, after_ref, rows_ref, x, sems):
-    for number, copy in enumerate(copies_in(x_hbm, x, sems, chunk)):
-        copy.wait()
-
-        def body(step, carry, number=number):
-            for half in range(2):
-                rows_of_group(x, rows_ref, number * chunk + step * 16 + half * 8, sub)
-            return carry
-
-        lax.fori_loop(0, chunk // 16, body, 0)
-
-
-def index_kernel(
-    sizes, node_in, node_out, send_list, recv_list, after_ref,
+def make_lists(
+    sizes, node_in, node_out, send_list, recv_list,
     in_cell, send_node, send_outlet, land, source_node, source_outlet,
 ):
     cells, nodes, branches, cap, sub = sizes
@@ -197,7 +169,7 @@
         here = scatter(home, ids, height)
         number = number + here
         slot = slot + jnp.where(here > 0.0, j + 1.0, 0.0)
-    source_node[...] = jnp.maximum(number.astype(I32) - 1, 0) * sub
+    source_node[...] = jnp.maximum(number.astype(I32) - 1, 0)
     source_outlet[...] = slot.astype(I32) - 1
     per_side = padded(cap) // LANES
     for side in range(4):
@@ -205,13 +177,48 @@
         lands = recv_list[side : side + 1, :]
         put_row(send_node, side * per_side, jnp.where(slots >= 0, slots % nodes, 0), 0)
         put_row(send_outlet, side * per_side, jnp.where(slots >= 0, slots // nodes, -1), -1)
-        put_row(land, side * per_side, jnp.where(lands >= 0, lands, cells) * sub, cells * sub)
+        put_row(land, side * per_side, jnp.where(lands >= 0, lands, cells), cells)
+
+
+def cell_sum_kernel(sizes, chunk, x_hbm, *rest):
+    cells, nodes, branches, cap, sub = sizes
+    lists, (sum_ref, rows_ref), made, (x, partial, sems) = (
+        rest[:4], rest[4:6], rest[6:12], rest[12:]
+    )
+    copies = copies_in(x_hbm, x, sems, chunk)
+    make_lists(sizes, *lists, *made)
+    zeros = rows_ref.shape[0] - sub
+    rows_ref[zeros:, :] = jnp.zeros((sub, LANES), F32)
+    for number, copy in enumerate(copies):
+        copy.wait()
+
+        def body(step, carry, number=number):
+            for half in range(2):
+                first = number * chunk + step * 16 + half * 8
+                total = rows_of_group(x, rows_ref, first, sub)
+                partial[pl.ds(pl.multiple_of(first, 8), 8), :] = total
+            return carry
+
+        lax.fori_loop(0, chunk // 16, body, 0)
+    sum_ref[...] = lane_sums(partial[...])
+
+
+def turn_rows_kernel(chunk, sub, x_hbm, after_ref, rows_ref, x, sems):
+    for number, copy in enumerate(copies_in(x_hbm, x, sems, chunk)):
+        copy.wait()
+
+        def body(step, carry, number=number):
+            for half in range(2):
+                rows_of_group(x, rows_ref, number * chunk + step * 16 + half * 8, sub)
+            return carry
+
+        lax.fori_loop(0, chunk // 16, body, 0)
 
 
 def gathered_flow(node, in_cell, scaled, sizes):
     cells, nodes, branches, cap, sub = sizes
     return tree_sum(
-        [scaled[row_at(in_cell[i * nodes + node] * sub, sub), :] for i in range(branches)]
+        [row_of(scaled, in_cell[i * nodes + node], sub)[...] for i in range(branches)]
     )
 
 
@@ -221,19 +228,19 @@
     def body(step, carry):
         first = step * 16
         values = [
-            rows[row_at((first + i) * sub, sub), :] * fraction[first + i] for i in range(16)
+            row_of(rows, first + i, sub)[...] * fraction[first + i] for i in range(16)
         ]
         for i in range(16):
-            scaled[row_at((first + i) * sub, sub), :] = values[i]
+            row_of(scaled, first + i, sub)[...] = values[i]
         return carry
 
     lax.fori_loop(0, cells // 16, body, 0)
-    scaled[row_at(cells * sub, sub), :] = jnp.zeros((sub, LANES), F32)
+    row_of(scaled, cells, sub)[...] = jnp.zeros((sub, LANES), F32)
 
 
 def send_kernel(sizes, sides, in_cell, send_node, send_outlet, scaled, turns, *rest):
     cells, nodes, branches, cap, sub = sizes
-    sends = rest[-len(sides) :]
+    sends = rest[1:]
     batch = 8
     for side, send in zip(sides, sends):
 
@@ -244,20 +251,13 @@
                 slot = side * padded(cap) + first + i
                 node = send_node[slot]
                 value = gathered_flow(node, in_cell, scaled, sizes)
-                choice = turns[row_at(node * sub, sub), :]
+                choice = row_of(turns, node, sub)[...]
                 values.append(jnp.where(choice == send_outlet[slot], value, 0.0))
             for i in range(batch):
-                send[row_at((first + i) * sub, sub), :] = values[i]
+                row_of(send, first + i, sub)[...] = values[i]
             return carry
 
         lax.fori_loop(0, cap // batch, body, 0)
-
-
-def scale_send_kernel(
-    sizes, sides, fraction, in_cell, send_node, send_outlet, rows, turns, scaled, *sends
-):
-    scale_kernel(sizes, fraction, rows, scaled)
-    send_kernel(sizes, sides, in_cell, send_node, send_outlet, scaled, turns, *sends)
 
 
 def scaled_send_kernel(sizes, side, theta, send_node, send_outlet, flow, turns, send):
@@ -270,11 +270,11 @@
         for i in range(batch):
             slot = side * padded(cap) + first + i
             node = send_node[slot]
-            at = row_at(node * sub, sub)
-            value = flow[at, :] * theta[node]
-            values.append(jnp.where(turns[at, :] == send_outlet[slot], value, 0.0))
+            value = row_of(flow, node, sub)[...] * theta[node]
+            choice = row_of(turns, node, sub)[...]
+            values.append(jnp.where(choice == send_outlet[slot], value, 0.0))
         for i in range(batch):
-            send[row_at((first + i) * sub, sub), :] = values[i]
+            row_of(send, first + i, sub)[...] = values[i]
         return carry
 
     lax.fori_loop(0, cap // batch, body, 0)
@@ -289,7 +289,7 @@
             gathered_flow(first + i, in_cell, scaled, sizes) for i in range(8)
         ]
         for i in range(8):
-            flow[row_at((first + i) * sub, sub), :] = values[i]
+            row_of(flow, first + i, sub)[...] = values[i]
         return carry
 
     def measure(step, carry):
@@ -316,7 +316,7 @@
 
 def theta_kernel(
     sizes, regions, commodities, supply, shared, node_in, node_out, send_list, fraction,
-    after_ref, keep, home_theta, theta_out, slot_theta,
+    keep, home_theta, theta_out, slot_theta,
 ):
     cells, nodes, branches, cap, sub = sizes
     height = cells // LANES
@@ -360,7 +360,7 @@
     put_row(slot_theta, 0, look_up(tall, jnp.where(slots >= 0, slots % nodes, 0)), 0.0)
 
 
-def home_kernel(sizes, node_row, outlet, turns, flow, home):
+def home_kernel(sizes, source, outlet, turns, flow, home):
     cells, nodes, branches, cap, sub = sizes
     batch = 8
 
@@ -368,10 +368,12 @@
         first = step * batch
         values = []
         for i in range(batch):
-            at = row_at(node_row[first + i], sub)
-            values.append(jnp.where(turns[at, :] == outlet[first + i], flow[at, :], 0.0))
+            node = source[first + i]
+            choice = row_of(turns, node, sub)[...]
+            moved = row_of(flow, node, sub)[...]
+            values.append(jnp.where(choice == outlet[first + i], moved, 0.0))
         for i in range(batch):
-            home[row_at((first + i) * sub, sub), :] = values[i]
+            row_of(home, first + i, sub)[...] = values[i]
         return carry
 
     lax.fori_loop(0, cells // batch, body, 0)
@@ -385,10 +387,11 @@
         first = step * batch
         values = []
         for i in range(batch):
-            at = row_at((first + i) * sub, sub)
-            values.append(rows[at, :] * keep[first + i] + home[at, :] * home_theta[first + i])
+            cell = first + i
+            kept = row_of(rows, cell, sub)[...] * keep[cell]
+            values.append(kept + row_of(home, cell, sub)[...] * home_theta[cell])
         for i in range(batch):
-            base[row_at((first + i) * sub, sub), :] = values[i]
+            row_of(base, first + i, sub)[...] = values[i]
         return carry
 
     lax.fori_loop(0, cells // batch, body, 0)
@@ -404,13 +407,13 @@
             stores = []
             for i in range(batch):
                 slot = side * padded(cap) + first + i
-                at = row_at(land[slot], sub)
-                value = rows[row_at((first + i) * sub, sub), :]
+                at = row_of(base, land[slot], sub)
+                value = row_of(rows, first + i, sub)[...]
                 if scale is not None:
                     value = value * scale[slot]
-                stores.append((at, base[at, :] + value))
+                stores.append((at, at[...] + value))
             for at, value in stores:
-                base[at, :] = value
+                at[...] = value
             return carry
 
         lax.fori_loop(0, cap // batch, body, 0)
@@ -469,14 +472,17 @@
     occupancy = pltpu.with_memory_space_constraint(occupancy, pltpu.HBM)
     turn = pltpu.with_memory_space_constraint(turn, pltpu.HBM)
 
-    local_sum, rows = pl.pallas_call(
-        functools.partial(cell_sum_kernel, chunk, sub),
-        in_specs=[ANYWHERE],
-        out_specs=[VMEM_WHOLE] * 2,
+    local_sum, rows, *lists = pl.pallas_call(
+        functools.partial(cell_sum_kernel, sizes, chunk),
+        in_specs=[ANYWHERE] + [VMEM_WHOLE] * 4,
+        out_specs=[VMEM_WHOLE] * 8,
         out_shape=[
             jax.ShapeDtypeStruct(per_cell, F32),
             pltpu.VMEM(((cells + 1) * sub, LANES), F32),
-        ],
+            jax.ShapeDtypeStruct((branches * nodes // LANES, LANES), I32),
+        ]
+        + [jax.ShapeDtypeStruct(list_shape, I32)] * 3
+        + [jax.ShapeDtypeStruct(per_cell, I32)] * 2,
         scratch_shapes=[
             pltpu.VMEM((cells, width), F32),
             pltpu.VMEM((cells, LANES), F32),
@@ -485,7 +491,10 @@
         compiler_params=params(14),
         cost_estimate=cost(cells * width, cells * row_bytes),
         name="cell_sum",
-    )(occupancy)
+    )(occupancy, node_in, node_out, send_list, recv_list)
+    in_cell, send_node, send_outlet, land, source_node, source_outlet = (
+        x.reshape(-1) for x in lists
+    )
 
     sums = partners(local_sum, "dest")
 
@@ -503,21 +512,7 @@
         name="turn_rows",
     )(turn, local_sum)
 
-    in_cell, send_node, send_outlet, land, source_node, source_outlet = pl.pallas_call(
-        functools.partial(index_kernel, sizes),
-        in_specs=[VMEM_WHOLE] * 4 + [ANYWHERE],
-        out_specs=[VMEM_WHOLE] * 6,
-        out_shape=[jax.ShapeDtypeStruct((branches * nodes // LANES, LANES), I32)]
-        + [jax.ShapeDtypeStruct(list_shape, I32)] * 3
-        + [jax.ShapeDtypeStruct(per_cell, I32)] * 2,
-        compiler_params=params(8),
-        cost_estimate=cost(branches * nodes * cells * 2, nodes * 64),
-        name="index_lists",
-    )(node_in, node_out, send_list, recv_list, local_sum)
-    in_cell, send_node, send_outlet, land, source_node, source_outlet = (
-        x.reshape(-1) for x in (in_cell, send_node, send_outlet, land, source_node, source_outlet)
-    )
-
+    turns, *sums = lax.optimization_barrier((turns, *sums))
     vehicles = tree_sum(sums) / commodities
     cap_of = capacity.reshape(per_cell)
     fraction = jnp.minimum(vehicles, cap_of) / vehicles
@@ -525,30 +520,29 @@
     rows_shape = pltpu.VMEM(((cells + 1) * sub, LANES), F32)
     send_shape = pltpu.VMEM((cap * sub, LANES), F32)
 
-    scaled, *near = pl.pallas_call(
-        functools.partial(scale_send_kernel, sizes, (0, 1)),
-        in_specs=[SMEM_WHOLE] * 4 + [VMEM_WHOLE] * 2,
+    supply_there = to_neighbours(supply)
+    scaled = pl.pallas_call(
+        functools.partial(scale_kernel, sizes),
+        in_specs=[SMEM_WHOLE, VMEM_WHOLE],
+        out_specs=VMEM_WHOLE,
+        out_shape=rows_shape,
+        compiler_params=params(4),
+        cost_estimate=cost(1, 1),
+        name="scale_rows",
+    )(fraction.reshape(-1), rows)
+    early = pl.pallas_call(
+        functools.partial(send_kernel, sizes, (0, 1, 2)),
+        in_specs=[SMEM_WHOLE] * 3 + [VMEM_WHOLE] * 2 + [ANYWHERE],
         out_specs=[VMEM_WHOLE] * 3,
-        out_shape=[rows_shape] + [send_shape] * 2,
+        out_shape=[send_shape] * 3,
         compiler_params=params(4),
-        cost_estimate=cost(cap * width * 20, cap * row_bytes * 10),
-        name="send_near",
-    )(fraction.reshape(-1), in_cell, send_node, send_outlet, rows, turns)
-    ahead = pl.pallas_call(
-        functools.partial(send_kernel, sizes, (2,)),
-        in_specs=[SMEM_WHOLE] * 3 + [VMEM_WHOLE] * 2,
-        out_specs=VMEM_WHOLE,
-        out_shape=send_shape,
-        compiler_params=params(4),
-        cost_estimate=cost(1, 1),
-        name="send_ahead",
-    )(in_cell, send_node, send_outlet, scaled, turns)
+        cost_estimate=cost(1, 1),
+        name="send_rows",
+    )(in_cell, send_node, send_outlet, scaled, turns, supply_there)
     arrived = [
-        shifted(send, "region", SHIFTS[side]) for side, send in enumerate([*near, ahead])
+        shifted(send, "region", SHIFTS[side]) for side, send in enumerate(early)
     ]
 
-    supply, *_ = lax.optimization_barrier((supply, *near, ahead))
-    supply_there = to_neighbours(supply)
 
     flow, demand = pl.pallas_call(
         functools.partial(node_flow_kernel, sizes),
@@ -562,7 +556,7 @@
         compiler_params=params(8),
         cost_estimate=cost(1, 1),
         name="node_flow",
-    )(in_cell, scaled, turns, supply_there)
+    )(in_cell, scaled, turns, early[0])
 
     shared = apart(
         lambda x: lax.all_gather(x, "dest", axis=0, tiled=True),
@@ -579,7 +573,7 @@
     )(source_node, source_outlet, turns, flow)
     keep, home_theta, theta, slot_theta = pl.pallas_call(
         functools.partial(theta_kernel, sizes, regions, commodities),
-        in_specs=[VMEM_WHOLE] * 6 + [ANYWHERE],
+        in_specs=[VMEM_WHOLE] * 6,
         out_specs=[VMEM_WHOLE] * 4,
         out_shape=[jax.ShapeDtypeStruct(per_cell, F32)] * 2
         + [
@@ -589,9 +583,8 @@
         compiler_params=params(8),
         cost_estimate=cost(1, 1),
         name="theta",
-    )(supply, shared, node_in, node_out, send_list, fraction, home)
+    )(supply, shared, node_in, node_out, send_list, fraction)
     theta_there = apart(to_neighbours, slot_theta)
-    scale = lax.all_gather(theta_there, "dest", axis=0, tiled=True)[: list_shape[0]]
 
     (behind,) = pl.pallas_call(
         functools.partial(scaled_send_kernel, sizes, 3),
@@ -602,8 +595,9 @@
         cost_estimate=cost(1, 1),
         name="send_scaled",
     )(theta.reshape(-1), send_node, send_outlet, flow, turns)
-    behind, _ = lax.optimization_barrier((behind, theta_there))
+    behind, theta_there, *arrived = lax.optimization_barrier((behind, theta_there, *arrived))
     last = shifted(behind, "region", SHIFTS[3])
+    scale = lax.all_gather(theta_there, "dest", axis=0, tiled=True)[: list_shape[0]]
 
     base = pl.pallas_call(
         functools.partial(base_kernel, sizes),

time: 103 us -> 99.1 us (0.962)
  local copies, waits for them, and re-layouts: 14.3 us -> 18.4 us
  waiting for transfers between devices: 12 us -> 8 us
  blocking collectives: 12.4 us -> 10.8 us
  Pallas kernels: 51.5 us -> 50.1 us
    ppermute x2, waiting for transfers between devices: 12 us -> 7.36 us  [to_neighbours(): return lax.ppermute(block, ('region', 'dest'), route)]
    unnamed x34 -> x38, local copies, waits for them, and re-layouts: 13.8 us -> 17.9 us
    pallas_call x4 -> x3, Pallas kernels: 16.3 us -> 14.1 us  [the longest x1 5.91 us: on_device(): pl.pallas_call(functools.partial(send_kernel, sizes, (0, 1, 2)), in_specs...]
    ppermute x4, starting transfers between devices: 5.28 us -> 3.56 us  [shifted(): return lax.ppermute(block, axis, route)]
    ppermute x2, starting transfers between devices: 2.71 us -> 3.82 us  [to_neighbours(): return lax.ppermute(block, ('region', 'dest'), route)]
  transfers between devices with their start and end apart: 9 -> 9, of which waited for: 1 -> 3; matrix products, arithmetic and copies ran while one was open for 1% -> 1% of each run, Pallas kernels for 32% -> 34%
where the time goes in v5:
time: 99.1 us; the launch traced here: 98.6 us
  Pallas kernels  50.1 us (51%)
  local copies, waits for them, and re-layouts  18.4 us (19%)
  blocking collectives  10.8 us (11%)
  starting transfers between devices  10.5 us (11%)
  waiting for transfers between devices  8 us (8%)
    unnamed x38, local copies, waits for them, and re-layouts  17.9 us
    pallas_call x1, Pallas kernels, on_device(): pl.pallas_call(functools.partial(node_flow_kernel, sizes), in_specs=[SMEM...  10.2 us
    ppermute x2, waiting for transfers between devices, to_neighbours(): return lax.ppermute(block, ('region', 'dest'), route)  7.36 us
    pallas_call x1, Pallas kernels, on_device(): pl.pallas_call(functools.partial(send_kernel, sizes, (0, 1, 2)), in_specs...  5.91 us
    pallas_call x1, Pallas kernels, on_device(): pl.pallas_call(functools.partial(theta_kernel, sizes, regions, commoditie...  5.76 us
    pallas_call x1, Pallas kernels, on_device(): pl.pallas_call(functools.partial(cell_sum_kernel, sizes, chunk), in_specs...  5.68 us
    all_gather x1, blocking collectives, on_device(): lax.all_gather(x, 'dest', axis=0, tiled=True)  5.5 us
    pallas_call x1, Pallas kernels, on_device(): pl.pallas_call(functools.partial(home_kernel, sizes), in_specs=[SMEM_WHOL...  5.38 us
  transfers between devices with their start and end apart: 9, of which 3 were waited for; matrix products, arithmetic and copies ran while one was open for 1% of the time, Pallas kernels for 34%

profile of v5, /device:TPU:0, one launch (start us, length us, event | category | flops | bytes accessed | tf_op | source)
XLA Modules:
  0.0 98.6 jit_solution(1550731315996221758)
XLA Ops:
  0.0 0.7 copy-done.9
  0.7 0.7 copy-done.11
  1.4 0.7 copy-done.13
  2.8 5.7 %cell_sum.1 = (f32[16,128]{1,0:T(8,128)S(1)}, f32[16392,128]{1,0:T(8,128)S(1)}, s32[32,128]{1,0:T(8,128)S(1)}, s32[8,128]{1,0:T(8,128)S(1)}, s32[8,128]{1,0:T(8,...) custom-call(f32[2048,1024]{1,0:T(8,128)} %x_hbm.2, s32[4,1024]{1,0:T(4,128)S(1)} %copy-done.9, ...), custom_call_target="tpu_custom_call" | custom-call | flops 2097152 | bytes 8388608 | tf_op jit(solution)/shard_map/cell_sum/pallas_call | solution.py:475
  8.5 2.4 %collective-permute-start.3 = (f32[16,128]{1,0:T(8,128)S(1)}, f32[16,128]{1,0:T(8,128)S(1)}, u32[]{:S(2)}, u32[]{:S(2)}) collective-permute-start(f32[16,128]{1,0:T(8,128)S(1)} %get-tuple-element.43.after_ref), channel_id=1, source_target_pairs={{0,3},{1,2},{2,1},{3,0},{4,7},{5,6},{6,5},{7,4},{8,11},{9,10},{10,... | collective-permute-start | bytes 24584 | tf_op jit(solution)/shard_map/ppermute | solution.py:40
  11.6 2.3 %turn_rows.1.turns = s32[8192,128]{1,0:T(8,128)S(1)} custom-call(s32[1024,1024]{1,0:T(8,128)} %x_hbm.3, f32[16,128]{1,0:T(8,128)S(1)} %get-tuple-element.43.after_ref), custom_call_target="tpu_custom_call" | custom-call | bytes 4194304 | tf_op jit(solution)/shard_map/turn_rows/pallas_call | solution.py:501
  14.7 2.2 %collective-permute-start.4 = (f32[16,128]{1,0:T(8,128)S(1)}, f32[16,128]{1,0:T(8,128)S(1)}, u32[]{:S(2)}, u32[]{:S(2)}) collective-permute-start(f32[16,128]{1,0:T(8,128)S(1)} %fusion.1.supply), channel_id=1, source_target_pairs={{0,4},{1,29},{2,10},{3,27},{4,8},{5,1},{6,14},{7,31},{8,12},{9,5},... | collective-permute-start | bytes 24584 | tf_op jit(solution)/shard_map/ppermute | solution.py:28
  16.8 2.5 %scale_rows.1.scaled = f32[16392,128]{1,0:T(8,128)S(1)} custom-call(f32[2048]{0:T(1024)S(1)} %bitcast.24, f32[16392,128]{1,0:T(8,128)S(1)} %get-tuple-element.48.rows), custom_call_target="tpu_custom_call" | custom-call | flops 1 | bytes 1 | tf_op jit(solution)/shard_map/scale_rows/pallas_call | solution.py:524
  19.3 2.2 %collective-permute-done.4.rest_0_ = f32[16,128]{1,0:T(8,128)S(1)} collective-permute-done((f32[16,128]{1,0:T(8,128)S(1)}, f32[16,128]{1,0:T(8,128)S(1)}, u32[]{:S(2)}, u32[]{:S(2)}) %collective-permute-start.4) | collective-permute-done | bytes 8224 | tf_op jit(solution)/shard_map/ppermute | solution.py:28
  21.5 5.9 %send_rows.1 = (f32[1536,128]{1,0:T(8,128)S(1)}, f32[1536,128]{1,0:T(8,128)}, f32[1536,128]{1,0:T(8,128)}) custom-call(s32[4096]{0:T(1024)S(1)} %bitcast.25, s32[1024]{0:T(1024)S(1)} %bitcast.27, s32[1024]{0:T(1024)S(1)} %bitcast.29, f32[16392,128]{1,0:T(8,128)S(1)} %scale_rows.1.scaled, s32[8192,128]{1,0:T(8,128)S(1)} %turn_rows.1.turns, ...), custom_call_target="tpu_custom_call" | custom-call | flops 1 | bytes 1 | tf_op jit(solution)/shard_map/send_rows/pallas_call | solution.py:533
  27.4 2.1 %collective-permute-start.6 = (f32[1536,128]{1,0:T(8,128)}, f32[1536,128]{1,0:T(8,128)S(1)}, u32[]{:S(2)}, u32[]{:S(2)}) collective-permute-start(f32[1536,128]{1,0:T(8,128)} %get-tuple-element.57), channel_id=1, source_target_pairs={{4,0},{8,4},{12,8},{16,12},{20,16},{24,20},{28,24},{0,28},{5,1},{9... | collective-permute-start | bytes 2359304 | tf_op jit(solution)/shard_map/ppermute | solution.py:34
  30.7 10.2 %node_flow.1 = (f32[8192,128]{1,0:T(8,128)S(1)}, f32[32,128]{1,0:T(8,128)S(1)}) custom-call(s32[4096]{0:T(1024)S(1)} %bitcast.26, f32[16392,128]{1,0:T(8,128)S(1)} %scale_rows.1.scaled, s32[8192,128]{1,0:T(8,128)S(1)} %turn_rows.1.turns, f32[1536,128]{1,0:T(8,128)S(1)} %get-tuple-element.52.after_ref), custom_call_target="tpu_custom_call" | custom-call | flops 1 | bytes 1 | tf_op jit(solution)/shard_map/node_flow/pallas_call | solution.py:547
  40.8 2.0 %copy-done.5 = f32[8192,128]{1,0:T(8,128)} copy-done((f32[8192,128]{1,0:T(8,128)}, f32[8192,128]{1,0:T(8,128)S(1)}, u32[]{:S(2)}) %copy-start.5) | copy-done | bytes 4194328
  42.8 5.5 %conditional.2 = (f32[192,128]{1,0:T(8,128)S(1)}) conditional(s32[]{:T(128)} %bitcast.4, () %tuple.20, f32[48,128]{1,0:T(8,128)S(1)} %pad_maximum_fusion), branch_computations={%region_0.0_spmd, %region_1.0_spmd} | conditional | bytes 122888 | solution.py:469
  42.8 5.5 %all_gather.4 = f32[192,128]{1,0:T(8,128)S(1)} all-gather(f32[48,128]{1,0:T(8,128)S(1)} %param.1), channel_id=1, replica_groups=mesh['region'=8,'dest'=4] {'dest'}, dimensions={0}, use_global_device_ids=true | all-gather | bytes 122880 | tf_op jit(solution)/shard_map/cond/branch_1_fun/all_gather | solution.py:562
  48.3 5.8 %theta.1 = (f32[16,128]{1,0:T(8,128)S(1)}, f32[16,128]{1,0:T(8,128)S(1)}, f32[8,128]{1,0:T(8,128)S(1)}, f32[2,128]{1,0:T(2,128)S(1)}) custom-call(f32[16,128]{1,0:T(8,128)S(1)} %fusion.1.supply, f32[192,128]{1,0:T(8,128)S(1)} %get-tuple-element.71.shared, s32[4,1024]{1,0:T(4,128)S(1)} %copy-done.10, s32[4,1024]{1,0:T(4,128)S(1)} %copy-done.12, ...), custom_call_target="tpu_custom_call" | custom-call | flops 1 | bytes 1 | tf_op jit(solution)/shard_map/theta/pallas_call | solution.py:574
  54.1 2.2 %copy-done.1 = s32[8192,128]{1,0:T(8,128)S(1)} copy-done((s32[8192,128]{1,0:T(8,128)S(1)}, s32[8192,128]{1,0:T(8,128)}, u32[]{:S(2)}) %copy-start.1) | copy-done | bytes 4194328
  56.3 2.2 %copy-done.6 = f32[8192,128]{1,0:T(8,128)S(1)} copy-done((f32[8192,128]{1,0:T(8,128)S(1)}, f32[8192,128]{1,0:T(8,128)}, u32[]{:S(2)}) %copy-start.6) | copy-done | bytes 4194328
  58.5 1.2 %send_scaled.1 = f32[1536,128]{1,0:T(8,128)S(1)} custom-call(f32[1024]{0:T(1024)S(1)} %bitcast.38, s32[1024]{0:T(1024)S(1)} %bitcast.28, s32[1024]{0:T(1024)S(1)} %bitcast.30, f32[8192,128]{1,0:T(8,128)S(1)} %copy-done.6, s32[8192,128]{1,0:T(8,128)S(1)} %copy-done.1), custom_call_target="tpu_custom_call" | custom-call | flops 1 | bytes 1 | tf_op jit(solution)/shard_map/send_scaled/pallas_call | solution.py:589
  59.7 0.9 copy-done.8
  60.6 6.9 %conditional.3 = (f32[2,128]{1,0:T(2,128)}) conditional(s32[]{:T(128)} %bitcast.4, () %tuple.21, f32[2,128]{1,0:T(2,128)S(1)} %get-tuple-element.56), branch_computations={%region_2.0_spmd, %region_3.0_spmd} | conditional | bytes 4144 | solution.py:469
  60.6 1.7 %collective-permute-start = (f32[2,128]{1,0:T(2,128)S(1)}, f32[2,128]{1,0:T(2,128)}, u32[]{:S(2)}, u32[]{:S(2)}) collective-permute-start(f32[2,128]{1,0:T(2,128)S(1)} %param.3), channel_id=1, source_target_pairs={{0,4},{1,29},{2,10},{3,27},{4,8},{5,1},{6,14},{7,31},{8,12},{9,5},... | collective-permute-start | bytes 3080 | tf_op jit(solution)/shard_map/cond/branch_1_fun/ppermute | solution.py:28
  62.3 5.2 %collective-permute-done = f32[2,128]{1,0:T(2,128)} collective-permute-done((f32[2,128]{1,0:T(2,128)S(1)}, f32[2,128]{1,0:T(2,128)}, u32[]{:S(2)}, u32[]{:S(2)}) %collective-permute-start) | collective-permute-done | bytes 1056 | tf_op jit(solution)/shard_map/cond/branch_1_fun/ppermute | solution.py:28
  67.5 1.5 %collective-permute-start.8 = (f32[1536,128]{1,0:T(8,128)}, f32[1536,128]{1,0:T(8,128)S(1)}, u32[]{:S(2)}, u32[]{:S(2)}) collective-permute-start(f32[1536,128]{1,0:T(8,128)} %copy-done.8), channel_id=1, source_target_pairs={{8,0},{12,4},{16,8},{20,12},{24,16},{28,20},{0,24},{4,28},{9,1},{1... | collective-permute-start | bytes 2359304 | tf_op jit(solution)/shard_map/ppermute | solution.py:34
  69.0 2.2 %copy-done.2 = s32[8192,128]{1,0:T(8,128)S(1)} copy-done((s32[8192,128]{1,0:T(8,128)S(1)}, s32[8192,128]{1,0:T(8,128)}, u32[]{:S(2)}) %copy-start.2) | copy-done | bytes 4194328
  71.2 2.2 %copy-done.7 = f32[8192,128]{1,0:T(8,128)S(1)} copy-done((f32[8192,128]{1,0:T(8,128)S(1)}, f32[8192,128]{1,0:T(8,128)}, u32[]{:S(2)}) %copy-start.7) | copy-done | bytes 4194328
  73.4 5.4 %home_rows.1.home = f32[16392,128]{1,0:T(8,128)S(1)} custom-call(s32[2048]{0:T(1024)S(1)} %bitcast.34, s32[2048]{0:T(1024)S(1)} %bitcast.35, s32[8192,128]{1,0:T(8,128)S(1)} %copy-done.2, f32[8192,128]{1,0:T(8,128)S(1)} %copy-done.7), custom_call_target="tpu_custom_call" | custom-call | flops 1 | bytes 1 | tf_op jit(solution)/shard_map/home_rows/pallas_call | solution.py:565
  78.8 3.4 %copy-done.4 = f32[16392,128]{1,0:T(8,128)S(1)} copy-done((f32[16392,128]{1,0:T(8,128)S(1)}, f32[16392,128]{1,0:T(8,128)}, u32[]{:S(2)}) %copy-start.4) | copy-done | bytes 8392728
  82.1 4.7 %base_rows.1.rest_3_ = f32[16392,128]{1,0:T(8,128)S(1)} custom-call(f32[2048]{0:T(1024)S(1)} %bitcast.36, f32[2048]{0:T(1024)S(1)} %bitcast.37, f32[16392,128]{1,0:T(8,128)S(1)} %copy-done.4, f32[16392,128]{1,0:T(8,128)S(1)} %home_rows.1.home), custom_call_target="tpu_custom_call" | custom-call | flops 1 | bytes 1 | tf_op jit(solution)/shard_map/base_rows/pallas_call | solution.py:602
  86.9 5.3 %all-gather = f32[4,2,128]{2,1,0:T(2,128)S(1)} all-gather(f32[1,2,128]{2,1,0:T(2,128)} %bitcast.10), channel_id=1, replica_groups=mesh['region'=8,'dest'=4] {'dest'}, dimensions={0}, use_global_device_ids=true | all-gather | bytes 5120 | tf_op jit(solution)/shard_map/all_gather | solution.py:600
  92.1 1.9 %land_first.1.rest_1_ = f32[16392,128]{1,0:T(8,128)S(1)} custom-call(f32[1024]{0:T(1024)S(1)} %bitcast.33, s32[1024]{0:T(1024)S(1)} %bitcast.31, f32[1536,128]{1,0:T(8,128)S(1)} %collective-permute-done.5.rest_0_, f32[1536,128]{1,0:T(8,128)S(1)} %collective-permute-done.6.rest_1_, ...), custom_call_target="tpu_custom_call", output_to_operand_aliasing={{}: (5, {})} | custom-call | flops 1 | bytes 1 | tf_op jit(solution)/shard_map/land_first/pallas_call | solution.py:612
  94.1 4.5 %finish.1 = (f32[2048,1024]{1,0:T(8,128)}, f32[16392,128]{1,0:T(8,128)S(1)}) custom-call(s32[1024]{0:T(1024)S(1)} %bitcast.32, f32[1536,128]{1,0:T(8,128)S(1)} %collective-permute-done.8.rest_0_, f32[16392,128]{1,0:T(8,128)S(1)} %land_first.1.rest_1_), custom_call_target="tpu_custom_call", output_to_operand_aliasing={{1}: (2, {})} | custom-call | flops 2097152 | bytes 8388608 | tf_op jit(solution)/shard_map/finish/pallas_call | solution.py:623
  (43 shorter events, 2.6 us)
Async XLA Ops:
  0.0 0.7 copy-start.9
  0.7 0.7 copy-start.11
  1.4 0.7 copy-start.13
  2.1 0.7 copy-start.15
  2.8 11.8 %copy-start.16 = (f32[2048]{0:T(1024)S(1)}, f32[2048]{0:T(1024)}, u32[]{:S(2)}) copy-start(f32[2048]{0:T(1024)} %param.14) | copy-start | bytes 24580
  2.8 11.8 %copy-start.17 = (f32[2048]{0:T(1024)S(1)}, f32[2048]{0:T(1024)}, u32[]{:S(2)}) copy-start(f32[2048]{0:T(1024)} %param.15) | copy-start | bytes 24580
  2.8 11.8 %copy-start.18 = (f32[2048]{0:T(1024)S(1)}, f32[2048]{0:T(1024)}, u32[]{:S(2)}) copy-start(f32[2048]{0:T(1024)} %param.16) | copy-start | bytes 24580
  8.5 10.8 %copy-start.3 = (f32[16392,128]{1,0:T(8,128)}, f32[16392,128]{1,0:T(8,128)S(1)}, u32[]{:S(2)}) copy-start(f32[16392,128]{1,0:T(8,128)S(1)} %get-tuple-element.48.rows) | copy-start | bytes 25178116
  8.5 5.5 %collective-permute-start.3 = (f32[16,128]{1,0:T(8,128)S(1)}, f32[16,128]{1,0:T(8,128)S(1)}, u32[]{:S(2)}, u32[]{:S(2)}) collective-permute-start(f32[16,128]{1,0:T(8,128)S(1)} %get-tuple-element.43.after_ref), channel_id=1, source_target_pairs={{0,3},{1,2},{2,1},{3,0},{4,7},{5,6},{6,5},{7,4},{8,11},{9,10},{10,... | collective-permute-start | bytes 24584 | tf_op jit(solution)/shard_map/ppermute | solution.py:40
  11.0 3.7 %collective-permute-start.2 = (f32[16,128]{1,0:T(8,128)S(1)}, f32[16,128]{1,0:T(8,128)S(1)}, u32[]{:S(2)}, u32[]{:S(2)}) collective-permute-start(f32[16,128]{1,0:T(8,128)S(1)} %get-tuple-element.43.after_ref), channel_id=1, source_target_pairs={{0,2},{1,3},{2,0},{3,1},{4,6},{5,7},{6,4},{7,5},{8,10},{9,11},{10,... | collective-permute-start | bytes 24584 | tf_op jit(solution)/shard_map/ppermute | solution.py:40
  11.6 3.0 %collective-permute-start.1 = (f32[16,128]{1,0:T(8,128)S(1)}, f32[16,128]{1,0:T(8,128)S(1)}, u32[]{:S(2)}, u32[]{:S(2)}) collective-permute-start(f32[16,128]{1,0:T(8,128)S(1)} %get-tuple-element.43.after_ref), channel_id=1, source_target_pairs={{0,1},{1,0},{2,3},{3,2},{4,5},{5,4},{6,7},{7,6},{8,9},{9,8},{10,11... | collective-permute-start | bytes 24584 | tf_op jit(solution)/shard_map/ppermute | solution.py:40
  14.0 16.7 %copy-start = (s32[8192,128]{1,0:T(8,128)}, s32[8192,128]{1,0:T(8,128)S(1)}, u32[]{:S(2)}) copy-start(s32[8192,128]{1,0:T(8,128)S(1)} %turn_rows.1.turns) | copy-start | bytes 12582916
  14.7 6.8 %collective-permute-start.4 = (f32[16,128]{1,0:T(8,128)S(1)}, f32[16,128]{1,0:T(8,128)S(1)}, u32[]{:S(2)}, u32[]{:S(2)}) collective-permute-start(f32[16,128]{1,0:T(8,128)S(1)} %fusion.1.supply), channel_id=1, source_target_pairs={{0,4},{1,29},{2,10},{3,27},{4,8},{5,1},{6,14},{7,31},{8,12},{9,5},... | collective-permute-start | bytes 24584 | tf_op jit(solution)/shard_map/ppermute | solution.py:28
  27.4 20.9 %copy-start.10 = (s32[4,1024]{1,0:T(4,128)S(1)}, s32[4,1024]{1,0:T(4,128)}, u32[]{:S(2)}) copy-start(s32[4,1024]{1,0:T(4,128)} %node_in.1) | copy-start | bytes 49156
  27.4 20.9 %copy-start.12 = (s32[4,1024]{1,0:T(4,128)S(1)}, s32[4,1024]{1,0:T(4,128)}, u32[]{:S(2)}) copy-start(s32[4,1024]{1,0:T(4,128)} %node_out.1) | copy-start | bytes 49156
  27.4 20.9 %copy-start.14 = (s32[4,192]{1,0:T(4,128)S(1)}, s32[4,192]{1,0:T(4,128)}, u32[]{:S(2)}) copy-start(s32[4,192]{1,0:T(4,128)} %send_list.1) | copy-start | bytes 9220
  27.4 40.1 %collective-permute-start.6 = (f32[1536,128]{1,0:T(8,128)}, f32[1536,128]{1,0:T(8,128)S(1)}, u32[]{:S(2)}, u32[]{:S(2)}) collective-permute-start(f32[1536,128]{1,0:T(8,128)} %get-tuple-element.57), channel_id=1, source_target_pairs={{4,0},{8,4},{12,8},{16,12},{20,16},{24,20},{28,24},{0,28},{5,1},{9... | collective-permute-start | bytes 2359304 | tf_op jit(solution)/shard_map/ppermute | solution.py:34
  29.5 38.0 %collective-permute-start.7 = (f32[1536,128]{1,0:T(8,128)}, f32[1536,128]{1,0:T(8,128)S(1)}, u32[]{:S(2)}, u32[]{:S(2)}) collective-permute-start(f32[1536,128]{1,0:T(8,128)} %get-tuple-element.58), channel_id=1, source_target_pairs={{24,0},{28,4},{0,8},{4,12},{8,16},{12,20},{16,24},{20,28},{25,1},{... | collective-permute-start | bytes 2359304 | tf_op jit(solution)/shard_map/ppermute | solution.py:34
  29.5 38.0 %collective-permute-start.5 = (f32[1536,128]{1,0:T(8,128)S(1)}, f32[1536,128]{1,0:T(8,128)S(1)}, u32[]{:S(2)}, u32[]{:S(2)}) collective-permute-start(f32[1536,128]{1,0:T(8,128)S(1)} %get-tuple-element.52.after_ref), channel_id=1, source_target_pairs={{28,0},{0,4},{4,8},{8,12},{12,16},{16,20},{20,24},{24,28},{29,1},{... | collective-permute-start | bytes 2359304 | tf_op jit(solution)/shard_map/ppermute | solution.py:34
  40.8 2.0 %copy-start.5 = (f32[8192,128]{1,0:T(8,128)}, f32[8192,128]{1,0:T(8,128)S(1)}, u32[]{:S(2)}) copy-start(f32[8192,128]{1,0:T(8,128)S(1)} %get-tuple-element.55.flow) | copy-start | bytes 12582916
  54.1 2.2 %copy-start.1 = (s32[8192,128]{1,0:T(8,128)S(1)}, s32[8192,128]{1,0:T(8,128)}, u32[]{:S(2)}) copy-start(s32[8192,128]{1,0:T(8,128)} %copy-done) | copy-start | bytes 12582916
  56.3 2.2 %copy-start.6 = (f32[8192,128]{1,0:T(8,128)S(1)}, f32[8192,128]{1,0:T(8,128)}, u32[]{:S(2)}) copy-start(f32[8192,128]{1,0:T(8,128)} %copy-done.5) | copy-start | bytes 12582916
  59.7 0.9 copy-start.8
  60.6 6.9 %collective-permute-start = (f32[2,128]{1,0:T(2,128)S(1)}, f32[2,128]{1,0:T(2,128)}, u32[]{:S(2)}, u32[]{:S(2)}) collective-permute-start(f32[2,128]{1,0:T(2,128)S(1)} %param.3), channel_id=1, source_target_pairs={{0,4},{1,29},{2,10},{3,27},{4,8},{5,1},{6,14},{7,31},{8,12},{9,5},... | collective-permute-start | bytes 3080 | tf_op jit(solution)/shard_map/cond/branch_1_fun/ppermute | solution.py:28
  67.5 26.6 %collective-permute-start.8 = (f32[1536,128]{1,0:T(8,128)}, f32[1536,128]{1,0:T(8,128)S(1)}, u32[]{:S(2)}, u32[]{:S(2)}) collective-permute-start(f32[1536,128]{1,0:T(8,128)} %copy-done.8), channel_id=1, source_target_pairs={{8,0},{12,4},{16,8},{20,12},{24,16},{28,20},{0,24},{4,28},{9,1},{1... | collective-permute-start | bytes 2359304 | tf_op jit(solution)/shard_map/ppermute | solution.py:34
  69.0 2.2 %copy-start.2 = (s32[8192,128]{1,0:T(8,128)S(1)}, s32[8192,128]{1,0:T(8,128)}, u32[]{:S(2)}) copy-start(s32[8192,128]{1,0:T(8,128)} %copy-done) | copy-start | bytes 12582916
  71.2 2.2 %copy-start.7 = (f32[8192,128]{1,0:T(8,128)S(1)}, f32[8192,128]{1,0:T(8,128)}, u32[]{:S(2)}) copy-start(f32[8192,128]{1,0:T(8,128)} %copy-done.5) | copy-start | bytes 12582916
  78.8 3.4 %copy-start.4 = (f32[16392,128]{1,0:T(8,128)S(1)}, f32[16392,128]{1,0:T(8,128)}, u32[]{:S(2)}) copy-start(f32[16392,128]{1,0:T(8,128)} %copy-done.3) | copy-start | bytes 25178116

commit v6 on v5

--- a/solution.py
+++ b/solution.py
@@ -182,11 +182,20 @@
 
 def cell_sum_kernel(sizes, chunk, x_hbm, *rest):
     cells, nodes, branches, cap, sub = sizes
-    lists, (sum_ref, rows_ref), made, (x, partial, sems) = (
-        rest[:4], rest[4:6], rest[6:12], rest[12:]
-    )
+    lists, (sum_ref, rows_ref), made, held, (recv, x, partial, sems, list_sems) = (
+        rest[:4], rest[4:6], rest[6:12], rest[12:15], rest[15:]
+    )
+    held = (*held, recv)
+    list_copies = [
+        pltpu.make_async_copy(source, target, list_sems.at[k])
+        for k, (source, target) in enumerate(zip(lists, held))
+    ]
+    for copy in list_copies:
+        copy.start()
     copies = copies_in(x_hbm, x, sems, chunk)
-    make_lists(sizes, *lists, *made)
+    for copy in list_copies:
+        copy.wait()
+    make_lists(sizes, *held, *made)
     zeros = rows_ref.shape[0] - sub
     rows_ref[zeros:, :] = jnp.zeros((sub, LANES), F32)
     for number, copy in enumerate(copies):
@@ -316,7 +325,7 @@
 
 def theta_kernel(
     sizes, regions, commodities, supply, shared, node_in, node_out, send_list, fraction,
-    keep, home_theta, theta_out, slot_theta,
+    after_ref, keep, home_theta, theta_out, slot_theta,
 ):
     cells, nodes, branches, cap, sub = sizes
     height = cells // LANES
@@ -462,38 +471,40 @@
     per_cell = (height, LANES)
     list_shape = (4 * padded(cap) // LANES, LANES)
     chunk = 128
-    some_node = node_in[0, 0] >= 0
-
-    def apart(exchange, block):
-        shape = jax.eval_shape(exchange, block)
-        return lax.cond(some_node, exchange, lambda x: jnp.zeros(shape.shape, F32), block)
-
     row_bytes = width * 4
     occupancy = pltpu.with_memory_space_constraint(occupancy, pltpu.HBM)
     turn = pltpu.with_memory_space_constraint(turn, pltpu.HBM)
+    node_in, node_out, send_list, recv_list = (
+        pltpu.with_memory_space_constraint(x, pltpu.HBM)
+        for x in (node_in, node_out, send_list, recv_list)
+    )
 
     local_sum, rows, *lists = pl.pallas_call(
         functools.partial(cell_sum_kernel, sizes, chunk),
-        in_specs=[ANYWHERE] + [VMEM_WHOLE] * 4,
-        out_specs=[VMEM_WHOLE] * 8,
+        in_specs=[ANYWHERE] * 5,
+        out_specs=[VMEM_WHOLE] * 11,
         out_shape=[
             jax.ShapeDtypeStruct(per_cell, F32),
             pltpu.VMEM(((cells + 1) * sub, LANES), F32),
             jax.ShapeDtypeStruct((branches * nodes // LANES, LANES), I32),
         ]
         + [jax.ShapeDtypeStruct(list_shape, I32)] * 3
-        + [jax.ShapeDtypeStruct(per_cell, I32)] * 2,
+        + [jax.ShapeDtypeStruct(per_cell, I32)] * 2
+        + [pltpu.VMEM(x.shape, I32) for x in (node_in, node_out, send_list)],
         scratch_shapes=[
+            pltpu.VMEM(recv_list.shape, I32),
             pltpu.VMEM((cells, width), F32),
             pltpu.VMEM((cells, LANES), F32),
             pltpu.SemaphoreType.DMA((cells // chunk,)),
+            pltpu.SemaphoreType.DMA((4,)),
         ],
         compiler_params=params(14),
         cost_estimate=cost(cells * width, cells * row_bytes),
         name="cell_sum",
     )(occupancy, node_in, node_out, send_list, recv_list)
+    node_in, node_out, send_list = lists[6:]
     in_cell, send_node, send_outlet, land, source_node, source_outlet = (
-        x.reshape(-1) for x in lists
+        x.reshape(-1) for x in lists[:6]
     )
 
     sums = partners(local_sum, "dest")
@@ -558,9 +569,8 @@
         name="node_flow",
     )(in_cell, scaled, turns, early[0])
 
-    shared = apart(
-        lambda x: lax.all_gather(x, "dest", axis=0, tiled=True),
-        jnp.concatenate([demand, supply_there]),
+    shared = lax.all_gather(
+        jnp.concatenate([demand, supply_there]), "dest", axis=0, tiled=True
     )
     home = pl.pallas_call(
         functools.partial(home_kernel, sizes),
@@ -573,7 +583,7 @@
     )(source_node, source_outlet, turns, flow)
     keep, home_theta, theta, slot_theta = pl.pallas_call(
         functools.partial(theta_kernel, sizes, regions, commodities),
-        in_specs=[VMEM_WHOLE] * 6,
+        in_specs=[VMEM_WHOLE] * 6 + [ANYWHERE],
         out_specs=[VMEM_WHOLE] * 4,
         out_shape=[jax.ShapeDtypeStruct(per_cell, F32)] * 2
         + [
@@ -583,8 +593,8 @@
         compiler_params=params(8),
         cost_estimate=cost(1, 1),
         name="theta",
-    )(supply, shared, node_in, node_out, send_list, fraction)
-    theta_there = apart(to_neighbours, slot_theta)
+    )(supply, shared, node_in, node_out, send_list, fraction, home)
+    theta_there = to_neighbours(slot_theta)
 
     (behind,) = pl.pallas_call(
         functools.partial(scaled_send_kernel, sizes, 3),

time: 99.1 us -> 89.2 us (0.900)
  local copies, waits for them, and re-layouts: 18.4 us -> 0.01 us
  waiting for transfers between devices: 8 us -> 16.2 us
  Pallas kernels: 50.1 us -> 51.7 us
    unnamed x38 -> x6, local copies, waits for them, and re-layouts: 17.9 us -> 0.01 us
    ppermute x4, waiting for transfers between devices: 0.01 us -> 6.26 us  [shifted(): return lax.ppermute(block, axis, route)]
    pallas_call x1, Pallas kernels: 5.68 us -> 8.41 us  [on_device(): pl.pallas_call(functools.partial(cell_sum_kernel, sizes, chunk), in_specs...]
    ppermute x2, starting transfers between devices: 3.82 us -> 1.63 us  [to_neighbours(): return lax.ppermute(block, ('region', 'dest'), route)]
    ppermute x2, waiting for transfers between devices: 7.36 us -> 9.31 us  [to_neighbours(): return lax.ppermute(block, ('region', 'dest'), route)]
    ppermute x4, starting transfers between devices: 3.56 us -> 5.26 us  [shifted(): return lax.ppermute(block, axis, route)]
    pallas_call x1, Pallas kernels: 5.91 us -> 4.82 us  [on_device(): pl.pallas_call(functools.partial(send_kernel, sizes, (0, 1, 2)), in_specs...]
  transfers between devices with their start and end apart: 9 -> 9, of which waited for: 3 -> 4; matrix products, arithmetic and copies ran while one was open for 1% -> 0% of each run, Pallas kernels for 34% -> 38%
where the time goes in v6:
time: 89.2 us; the launch traced here: 89.1 us
  Pallas kernels  51.7 us (58%)
  waiting for transfers between devices  16.2 us (18%)
  blocking collectives  10.9 us (12%)
  starting transfers between devices  10 us (11%)
    pallas_call x1, Pallas kernels, on_device(): pl.pallas_call(functools.partial(node_flow_kernel, sizes), in_specs=[SMEM...  10.1 us
    ppermute x2, waiting for transfers between devices, to_neighbours(): return lax.ppermute(block, ('region', 'dest'), route)  9.31 us
    pallas_call x1, Pallas kernels, on_device(): pl.pallas_call(functools.partial(cell_sum_kernel, sizes, chunk), in_specs...  8.41 us
    ppermute x4, waiting for transfers between devices, shifted(): return lax.ppermute(block, axis, route)  6.26 us
    pallas_call x1, Pallas kernels, on_device(): pl.pallas_call(functools.partial(theta_kernel, sizes, regions, commoditie...  5.75 us
    all_gather x1, blocking collectives, on_device(): lax.all_gather(theta_there, 'dest', axis=0, tiled=True)[:list_shape[0]]  5.55 us
    pallas_call x1, Pallas kernels, on_device(): pl.pallas_call(functools.partial(home_kernel, sizes), in_specs=[SMEM_WHOL...  5.38 us
    all_gather x1, blocking collectives, on_device(): lax.all_gather(jnp.concatenate([demand, supply_there]), 'dest', axis=0, t...  5.34 us
  transfers between devices with their start and end apart: 9, of which 4 were waited for; matrix products, arithmetic and copies ran while one was open for 0% of the time, Pallas kernels for 38%

profile of v6, /device:TPU:0, one launch (start us, length us, event | category | flops | bytes accessed | tf_op | source)
XLA Modules:
  0.0 89.1 jit_solution(1422527928115786327)
XLA Ops:
  0.0 8.4 %cell_sum.1 = (f32[16,128]{1,0:T(8,128)S(1)}, f32[16392,128]{1,0:T(8,128)S(1)}, s32[32,128]{1,0:T(8,128)S(1)}, s32[8,128]{1,0:T(8,128)S(1)}, s32[8,128]{1,0:T(8,...) custom-call(f32[2048,1024]{1,0:T(8,128)} %x_hbm.2, ...), custom_call_target="tpu_custom_call" | custom-call | flops 2097152 | bytes 8388608 | tf_op jit(solution)/shard_map/cell_sum/pallas_call | solution.py:482
  8.4 0.5 collective-permute-start
  8.9 2.6 %collective-permute-start.1 = (f32[16,128]{1,0:T(8,128)S(1)}, f32[16,128]{1,0:T(8,128)S(1)}, u32[]{:S(2)}, u32[]{:S(2)}) collective-permute-start(f32[16,128]{1,0:T(8,128)S(1)} %get-tuple-element.38.after_ref), channel_id=1, source_target_pairs={{0,2},{1,3},{2,0},{3,1},{4,6},{5,7},{6,4},{7,5},{8,10},{9,11},{10,... | collective-permute-start | bytes 24584 | tf_op jit(solution)/shard_map/ppermute | solution.py:40
  11.5 0.1 collective-permute-start.2
  11.6 2.3 %turn_rows.1.turns = s32[8192,128]{1,0:T(8,128)S(1)} custom-call(s32[1024,1024]{1,0:T(8,128)} %x_hbm.3, f32[16,128]{1,0:T(8,128)S(1)} %get-tuple-element.38.after_ref), custom_call_target="tpu_custom_call" | custom-call | bytes 4194304 | tf_op jit(solution)/shard_map/turn_rows/pallas_call | solution.py:512
  13.9 0.0 collective-permute-done
  13.9 0.0 collective-permute-done.1
  13.9 0.7 collective-permute-done.2
  14.6 0.0 copy-done
  14.6 1.6 %collective-permute-start.3 = (f32[16,128]{1,0:T(8,128)S(1)}, f32[16,128]{1,0:T(8,128)S(1)}, u32[]{:S(2)}, u32[]{:S(2)}) collective-permute-start(f32[16,128]{1,0:T(8,128)S(1)} %fusion.1.supply), channel_id=1, source_target_pairs={{0,4},{1,29},{2,10},{3,27},{4,8},{5,1},{6,14},{7,31},{8,12},{9,5},... | collective-permute-start | bytes 24584 | tf_op jit(solution)/shard_map/ppermute | solution.py:28
  16.2 2.5 %scale_rows.1.scaled = f32[16392,128]{1,0:T(8,128)S(1)} custom-call(f32[2048]{0:T(1024)S(1)} %bitcast.23, f32[16392,128]{1,0:T(8,128)S(1)} %get-tuple-element.43.rows), custom_call_target="tpu_custom_call" | custom-call | flops 1 | bytes 1 | tf_op jit(solution)/shard_map/scale_rows/pallas_call | solution.py:535
  18.7 2.3 %collective-permute-done.3.rest_0_ = f32[16,128]{1,0:T(8,128)S(1)} collective-permute-done((f32[16,128]{1,0:T(8,128)S(1)}, f32[16,128]{1,0:T(8,128)S(1)}, u32[]{:S(2)}, u32[]{:S(2)}) %collective-permute-start.3) | collective-permute-done | bytes 8224 | tf_op jit(solution)/shard_map/ppermute | solution.py:28
  21.0 4.8 %send_rows.1 = (f32[1536,128]{1,0:T(8,128)S(1)}, f32[1536,128]{1,0:T(8,128)S(1)}, f32[1536,128]{1,0:T(8,128)S(1)}) custom-call(s32[4096]{0:T(1024)S(1)} %bitcast.24, s32[1024]{0:T(1024)S(1)} %bitcast.26, s32[1024]{0:T(1024)S(1)} %bitcast.28, f32[16392,128]{1,0:T(8,128)S(1)} %scale_rows.1.scaled, s32[8192,128]{1,0:T(8,128)S(1)} %turn_rows.1.turns, ...), custom_call_target="tpu_custom_call" | custom-call | flops 1 | bytes 1 | tf_op jit(solution)/shard_map/send_rows/pallas_call | solution.py:544
  25.9 0.1 collective-permute-start.5
  25.9 4.7 %collective-permute-start.6 = (f32[1536,128]{1,0:T(8,128)S(1)}, f32[1536,128]{1,0:T(8,128)S(1)}, u32[]{:S(2)}, u32[]{:S(2)}) collective-permute-start(f32[1536,128]{1,0:T(8,128)S(1)} %get-tuple-element.57), channel_id=1, source_target_pairs={{4,0},{8,4},{12,8},{16,12},{20,16},{24,20},{28,24},{0,28},{5,1},{9... | collective-permute-start | bytes 2359304 | tf_op jit(solution)/shard_map/ppermute | solution.py:34
  30.6 0.0 collective-permute-start.7
  30.6 10.1 %node_flow.1 = (f32[8192,128]{1,0:T(8,128)S(1)}, f32[32,128]{1,0:T(8,128)S(1)}) custom-call(s32[4096]{0:T(1024)S(1)} %bitcast.25, f32[16392,128]{1,0:T(8,128)S(1)} %scale_rows.1.scaled, s32[8192,128]{1,0:T(8,128)S(1)} %turn_rows.1.turns, f32[1536,128]{1,0:T(8,128)S(1)} %get-tuple-element.47.after_ref), custom_call_target="tpu_custom_call" | custom-call | flops 1 | bytes 1 | tf_op jit(solution)/shard_map/node_flow/pallas_call | solution.py:558
  40.8 5.4 %home_rows.1.after_ref.home = f32[16392,128]{1,0:T(8,128)S(1)} custom-call(s32[2048]{0:T(1024)S(1)} %bitcast.33, s32[2048]{0:T(1024)S(1)} %bitcast.34, s32[8192,128]{1,0:T(8,128)S(1)} %turn_rows.1.turns, f32[8192,128]{1,0:T(8,128)S(1)} %get-tuple-element.54.flow), custom_call_target="tpu_custom_call" | custom-call | flops 1 | bytes 1 | tf_op jit(solution)/shard_map/home_rows/pallas_call | solution.py:575
  46.2 5.3 %all_gather.6.shared = f32[192,128]{1,0:T(8,128)S(1)} all-gather(f32[48,128]{1,0:T(8,128)S(1)} %pad_maximum_fusion), channel_id=1, replica_groups=mesh['region'=8,'dest'=4] {'dest'}, dimensions={0}, use_global_device_ids=true | all-gather | bytes 122880 | tf_op jit(solution)/shard_map/all_gather | solution.py:572
  51.5 5.8 %theta.1 = (f32[16,128]{1,0:T(8,128)S(1)}, f32[16,128]{1,0:T(8,128)S(1)}, f32[8,128]{1,0:T(8,128)S(1)}, f32[2,128]{1,0:T(2,128)S(1)}) custom-call(f32[16,128]{1,0:T(8,128)S(1)} %fusion.1.supply, f32[192,128]{1,0:T(8,128)S(1)} %all_gather.6.shared, s32[4,1024]{1,0:T(4,128)S(1)} %get-tuple-element.49.node_in, s32[4,1024]{1,0:T(4,128)S(1)} %get-tuple-element.50.node_out, ...), custom_call_target="tpu_custom_call" | custom-call | flops 1 | bytes 1 | tf_op jit(solution)/shard_map/theta/pallas_call | solution.py:584
  57.3 0.1 collective-permute-start.4
  57.3 1.2 %send_scaled.1 = f32[1536,128]{1,0:T(8,128)S(1)} custom-call(f32[1024]{0:T(1024)S(1)} %bitcast.37, s32[1024]{0:T(1024)S(1)} %bitcast.27, s32[1024]{0:T(1024)S(1)} %bitcast.29, f32[8192,128]{1,0:T(8,128)S(1)} %get-tuple-element.54.flow, s32[8192,128]{1,0:T(8,128)S(1)} %turn_rows.1.turns), custom_call_target="tpu_custom_call" | custom-call | flops 1 | bytes 1 | tf_op jit(solution)/shard_map/send_scaled/pallas_call | solution.py:599
  58.6 7.0 %collective-permute-done.4 = f32[2,128]{1,0:T(2,128)S(1)} collective-permute-done((f32[2,128]{1,0:T(2,128)S(1)}, f32[2,128]{1,0:T(2,128)S(1)}, u32[]{:S(2)}, u32[]{:S(2)}) %collective-permute-start.4) | collective-permute-done | bytes 1056 | tf_op jit(solution)/shard_map/ppermute | solution.py:28
  65.6 0.0 collective-permute-done.5.rest_0_
  65.6 0.0 collective-permute-done.6.rest_1_
  65.6 0.0 collective-permute-done.7.rest_2_
  65.6 0.5 collective-permute-start.8
  66.1 4.7 %base_rows.1.rest_3_ = f32[16392,128]{1,0:T(8,128)S(1)} custom-call(f32[2048]{0:T(1024)S(1)} %bitcast.35, f32[2048]{0:T(1024)S(1)} %bitcast.36, f32[16392,128]{1,0:T(8,128)S(1)} %get-tuple-element.43.rows, f32[16392,128]{1,0:T(8,128)S(1)} %home_rows.1.after_ref.home), custom_call_target="tpu_custom_call" | custom-call | flops 1 | bytes 1 | tf_op jit(solution)/shard_map/base_rows/pallas_call | solution.py:612
  70.8 5.5 %all-gather = f32[4,2,128]{2,1,0:T(2,128)S(1)} all-gather(f32[1,2,128]{2,1,0:T(2,128)S(1)} %bitcast.38), channel_id=1, replica_groups=mesh['region'=8,'dest'=4] {'dest'}, dimensions={0}, use_global_device_ids=true | all-gather | bytes 5120 | tf_op jit(solution)/shard_map/all_gather | solution.py:610
  76.3 1.9 %land_first.1.rest_1_ = f32[16392,128]{1,0:T(8,128)S(1)} custom-call(f32[1024]{0:T(1024)S(1)} %bitcast.32, s32[1024]{0:T(1024)S(1)} %bitcast.30, f32[1536,128]{1,0:T(8,128)S(1)} %collective-permute-done.5.rest_0_, f32[1536,128]{1,0:T(8,128)S(1)} %collective-permute-done.6.rest_1_, ...), custom_call_target="tpu_custom_call", output_to_operand_aliasing={{}: (5, {})} | custom-call | flops 1 | bytes 1 | tf_op jit(solution)/shard_map/land_first/pallas_call | solution.py:622
  78.3 6.2 %collective-permute-done.8.rest_0_ = f32[1536,128]{1,0:T(8,128)S(1)} collective-permute-done((f32[1536,128]{1,0:T(8,128)S(1)}, f32[1536,128]{1,0:T(8,128)S(1)}, u32[]{:S(2)}, u32[]{:S(2)}) %collective-permute-start.8) | collective-permute-done | bytes 786464 | tf_op jit(solution)/shard_map/ppermute | solution.py:34
  84.5 4.5 %finish.1 = (f32[2048,1024]{1,0:T(8,128)}, f32[16392,128]{1,0:T(8,128)S(1)}) custom-call(s32[1024]{0:T(1024)S(1)} %bitcast.31, f32[1536,128]{1,0:T(8,128)S(1)} %collective-permute-done.8.rest_0_, f32[16392,128]{1,0:T(8,128)S(1)} %land_first.1.rest_1_), custom_call_target="tpu_custom_call", output_to_operand_aliasing={{1}: (2, {})} | custom-call | flops 2097152 | bytes 8388608 | tf_op jit(solution)/shard_map/finish/pallas_call | solution.py:633
  (8 shorter events, 0.0 us)
Async XLA Ops:
  0.0 14.6 %copy-start = (f32[2048]{0:T(1024)S(1)}, f32[2048]{0:T(1024)}, u32[]{:S(2)}) copy-start(f32[2048]{0:T(1024)} %param.10) | copy-start | bytes 24580
  0.0 14.6 %copy-start.1 = (f32[2048]{0:T(1024)S(1)}, f32[2048]{0:T(1024)}, u32[]{:S(2)}) copy-start(f32[2048]{0:T(1024)} %param.11) | copy-start | bytes 24580
  0.0 14.6 %copy-start.2 = (f32[2048]{0:T(1024)S(1)}, f32[2048]{0:T(1024)}, u32[]{:S(2)}) copy-start(f32[2048]{0:T(1024)} %param.12) | copy-start | bytes 24580
  8.4 5.5 %collective-permute-start = (f32[16,128]{1,0:T(8,128)S(1)}, f32[16,128]{1,0:T(8,128)S(1)}, u32[]{:S(2)}, u32[]{:S(2)}) collective-permute-start(f32[16,128]{1,0:T(8,128)S(1)} %get-tuple-element.38.after_ref), channel_id=1, source_target_pairs={{0,1},{1,0},{2,3},{3,2},{4,5},{5,4},{6,7},{7,6},{8,9},{9,8},{10,11... | collective-permute-start | bytes 24584 | tf_op jit(solution)/shard_map/ppermute | solution.py:40
  8.9 5.0 %collective-permute-start.1 = (f32[16,128]{1,0:T(8,128)S(1)}, f32[16,128]{1,0:T(8,128)S(1)}, u32[]{:S(2)}, u32[]{:S(2)}) collective-permute-start(f32[16,128]{1,0:T(8,128)S(1)} %get-tuple-element.38.after_ref), channel_id=1, source_target_pairs={{0,2},{1,3},{2,0},{3,1},{4,6},{5,7},{6,4},{7,5},{8,10},{9,11},{10,... | collective-permute-start | bytes 24584 | tf_op jit(solution)/shard_map/ppermute | solution.py:40
  11.5 3.1 %collective-permute-start.2 = (f32[16,128]{1,0:T(8,128)S(1)}, f32[16,128]{1,0:T(8,128)S(1)}, u32[]{:S(2)}, u32[]{:S(2)}) collective-permute-start(f32[16,128]{1,0:T(8,128)S(1)} %get-tuple-element.38.after_ref), channel_id=1, source_target_pairs={{0,3},{1,2},{2,1},{3,0},{4,7},{5,6},{6,5},{7,4},{8,11},{9,10},{10,... | collective-permute-start | bytes 24584 | tf_op jit(solution)/shard_map/ppermute | solution.py:40
  14.6 6.4 %collective-permute-start.3 = (f32[16,128]{1,0:T(8,128)S(1)}, f32[16,128]{1,0:T(8,128)S(1)}, u32[]{:S(2)}, u32[]{:S(2)}) collective-permute-start(f32[16,128]{1,0:T(8,128)S(1)} %fusion.1.supply), channel_id=1, source_target_pairs={{0,4},{1,29},{2,10},{3,27},{4,8},{5,1},{6,14},{7,31},{8,12},{9,5},... | collective-permute-start | bytes 24584 | tf_op jit(solution)/shard_map/ppermute | solution.py:28
  25.9 39.7 %collective-permute-start.5 = (f32[1536,128]{1,0:T(8,128)S(1)}, f32[1536,128]{1,0:T(8,128)S(1)}, u32[]{:S(2)}, u32[]{:S(2)}) collective-permute-start(f32[1536,128]{1,0:T(8,128)S(1)} %get-tuple-element.47.after_ref), channel_id=1, source_target_pairs={{28,0},{0,4},{4,8},{8,12},{12,16},{16,20},{20,24},{24,28},{29,1},{... | collective-permute-start | bytes 2359304 | tf_op jit(solution)/shard_map/ppermute | solution.py:34
  25.9 39.7 %collective-permute-start.6 = (f32[1536,128]{1,0:T(8,128)S(1)}, f32[1536,128]{1,0:T(8,128)S(1)}, u32[]{:S(2)}, u32[]{:S(2)}) collective-permute-start(f32[1536,128]{1,0:T(8,128)S(1)} %get-tuple-element.57), channel_id=1, source_target_pairs={{4,0},{8,4},{12,8},{16,12},{20,16},{24,20},{28,24},{0,28},{5,1},{9... | collective-permute-start | bytes 2359304 | tf_op jit(solution)/shard_map/ppermute | solution.py:34
  30.6 35.0 %collective-permute-start.7 = (f32[1536,128]{1,0:T(8,128)S(1)}, f32[1536,128]{1,0:T(8,128)S(1)}, u32[]{:S(2)}, u32[]{:S(2)}) collective-permute-start(f32[1536,128]{1,0:T(8,128)S(1)} %get-tuple-element.58), channel_id=1, source_target_pairs={{24,0},{28,4},{0,8},{4,12},{8,16},{12,20},{16,24},{20,28},{25,1},{... | collective-permute-start | bytes 2359304 | tf_op jit(solution)/shard_map/ppermute | solution.py:34
  57.3 8.3 %collective-permute-start.4 = (f32[2,128]{1,0:T(2,128)S(1)}, f32[2,128]{1,0:T(2,128)S(1)}, u32[]{:S(2)}, u32[]{:S(2)}) collective-permute-start(f32[2,128]{1,0:T(2,128)S(1)} %get-tuple-element.56), channel_id=1, source_target_pairs={{0,4},{1,29},{2,10},{3,27},{4,8},{5,1},{6,14},{7,31},{8,12},{9,5},... | collective-permute-start | bytes 3080 | tf_op jit(solution)/shard_map/ppermute | solution.py:28
  65.6 19.0 %collective-permute-start.8 = (f32[1536,128]{1,0:T(8,128)S(1)}, f32[1536,128]{1,0:T(8,128)S(1)}, u32[]{:S(2)}, u32[]{:S(2)}) collective-permute-start(f32[1536,128]{1,0:T(8,128)S(1)} %send_scaled.1), channel_id=1, source_target_pairs={{8,0},{12,4},{16,8},{20,12},{24,16},{28,20},{0,24},{4,28},{9,1},{1... | collective-permute-start | bytes 2359304 | tf_op jit(solution)/shard_map/ppermute | solution.py:34

commit v7 on v5

--- a/solution.py
+++ b/solution.py
@@ -180,13 +180,8 @@
         put_row(land, side * per_side, jnp.where(lands >= 0, lands, cells), cells)
 
 
-def cell_sum_kernel(sizes, chunk, x_hbm, *rest):
-    cells, nodes, branches, cap, sub = sizes
-    lists, (sum_ref, rows_ref), made, (x, partial, sems) = (
-        rest[:4], rest[4:6], rest[6:12], rest[12:]
-    )
+def cell_sum_kernel(chunk, sub, x_hbm, sum_ref, rows_ref, x, partial, sems):
     copies = copies_in(x_hbm, x, sems, chunk)
-    make_lists(sizes, *lists, *made)
     zeros = rows_ref.shape[0] - sub
     rows_ref[zeros:, :] = jnp.zeros((sub, LANES), F32)
     for number, copy in enumerate(copies):
@@ -203,8 +198,23 @@
     sum_ref[...] = lane_sums(partial[...])
 
 
-def turn_rows_kernel(chunk, sub, x_hbm, after_ref, rows_ref, x, sems):
-    for number, copy in enumerate(copies_in(x_hbm, x, sems, chunk)):
+def turn_rows_kernel(sizes, chunk, x_hbm, after_ref, *rest):
+    cells, nodes, branches, cap, sub = sizes
+    lists, rows_ref, made, held, (recv, x, sems, list_sems) = (
+        rest[:4], rest[4], rest[5:11], rest[11:14], rest[14:]
+    )
+    held = (*held, recv)
+    list_copies = [
+        pltpu.make_async_copy(source, target, list_sems.at[k])
+        for k, (source, target) in enumerate(zip(lists, held))
+    ]
+    for copy in list_copies:
+        copy.start()
+    copies = copies_in(x_hbm, x, sems, chunk)
+    for copy in list_copies:
+        copy.wait()
+    make_lists(sizes, *held, *made)
+    for number, copy in enumerate(copies):
         copy.wait()
 
         def body(step, carry, number=number):
@@ -240,7 +250,7 @@
 
 def send_kernel(sizes, sides, in_cell, send_node, send_outlet, scaled, turns, *rest):
     cells, nodes, branches, cap, sub = sizes
-    sends = rest[1:]
+    sends = rest
     batch = 8
     for side, send in zip(sides, sends):
 
@@ -316,7 +326,7 @@
 
 def theta_kernel(
     sizes, regions, commodities, supply, shared, node_in, node_out, send_list, fraction,
-    keep, home_theta, theta_out, slot_theta,
+    after_ref, keep, home_theta, theta_out, slot_theta,
 ):
     cells, nodes, branches, cap, sub = sizes
     height = cells // LANES
@@ -360,7 +370,7 @@
     put_row(slot_theta, 0, look_up(tall, jnp.where(slots >= 0, slots % nodes, 0)), 0.0)
 
 
-def home_kernel(sizes, source, outlet, turns, flow, home):
+def home_kernel(sizes, source, outlet, turns, flow, after_ref, home):
     cells, nodes, branches, cap, sub = sizes
     batch = 8
 
@@ -462,27 +472,22 @@
     per_cell = (height, LANES)
     list_shape = (4 * padded(cap) // LANES, LANES)
     chunk = 128
-    some_node = node_in[0, 0] >= 0
-
-    def apart(exchange, block):
-        shape = jax.eval_shape(exchange, block)
-        return lax.cond(some_node, exchange, lambda x: jnp.zeros(shape.shape, F32), block)
-
     row_bytes = width * 4
     occupancy = pltpu.with_memory_space_constraint(occupancy, pltpu.HBM)
     turn = pltpu.with_memory_space_constraint(turn, pltpu.HBM)
-
-    local_sum, rows, *lists = pl.pallas_call(
-        functools.partial(cell_sum_kernel, sizes, chunk),
-        in_specs=[ANYWHERE] + [VMEM_WHOLE] * 4,
-        out_specs=[VMEM_WHOLE] * 8,
+    node_in, node_out, send_list, recv_list = (
+        pltpu.with_memory_space_constraint(x, pltpu.HBM)
+        for x in (node_in, node_out, send_list, recv_list)
+    )
+
+    local_sum, rows = pl.pallas_call(
+        functools.partial(cell_sum_kernel, chunk, sub),
+        in_specs=[ANYWHERE],
+        out_specs=[VMEM_WHOLE] * 2,
         out_shape=[
             jax.ShapeDtypeStruct(per_cell, F32),
             pltpu.VMEM(((cells + 1) * sub, LANES), F32),
-            jax.ShapeDtypeStruct((branches * nodes // LANES, LANES), I32),
-        ]
-        + [jax.ShapeDtypeStruct(list_shape, I32)] * 3
-        + [jax.ShapeDtypeStruct(per_cell, I32)] * 2,
+        ],
         scratch_shapes=[
             pltpu.VMEM((cells, width), F32),
             pltpu.VMEM((cells, LANES), F32),
@@ -491,26 +496,35 @@
         compiler_params=params(14),
         cost_estimate=cost(cells * width, cells * row_bytes),
         name="cell_sum",
-    )(occupancy, node_in, node_out, send_list, recv_list)
-    in_cell, send_node, send_outlet, land, source_node, source_outlet = (
-        x.reshape(-1) for x in lists
-    )
+    )(occupancy)
 
     sums = partners(local_sum, "dest")
 
-    turns = pl.pallas_call(
-        functools.partial(turn_rows_kernel, chunk, sub),
-        in_specs=[ANYWHERE] * 2,
-        out_specs=VMEM_WHOLE,
-        out_shape=pltpu.VMEM((nodes * sub, LANES), I32),
+    turns, *lists = pl.pallas_call(
+        functools.partial(turn_rows_kernel, sizes, chunk),
+        in_specs=[ANYWHERE] * 6,
+        out_specs=[VMEM_WHOLE] * 10,
+        out_shape=[
+            pltpu.VMEM((nodes * sub, LANES), I32),
+            jax.ShapeDtypeStruct((branches * nodes // LANES, LANES), I32),
+        ]
+        + [jax.ShapeDtypeStruct(list_shape, I32)] * 3
+        + [jax.ShapeDtypeStruct(per_cell, I32)] * 2
+        + [pltpu.VMEM(x.shape, I32) for x in (node_in, node_out, send_list)],
         scratch_shapes=[
+            pltpu.VMEM(recv_list.shape, I32),
             pltpu.VMEM((nodes, width), I32),
             pltpu.SemaphoreType.DMA((nodes // chunk,)),
+            pltpu.SemaphoreType.DMA((4,)),
         ],
         compiler_params=params(8),
         cost_estimate=cost(0, nodes * row_bytes),
         name="turn_rows",
-    )(turn, local_sum)
+    )(turn, local_sum, node_in, node_out, send_list, recv_list)
+    node_in, node_out, send_list = lists[6:]
+    in_cell, send_node, send_outlet, land, source_node, source_outlet = (
+        x.reshape(-1) for x in lists[:6]
+    )
 
     turns, *sums = lax.optimization_barrier((turns, *sums))
     vehicles = tree_sum(sums) / commodities
@@ -532,13 +546,14 @@
     )(fraction.reshape(-1), rows)
     early = pl.pallas_call(
         functools.partial(send_kernel, sizes, (0, 1, 2)),
-        in_specs=[SMEM_WHOLE] * 3 + [VMEM_WHOLE] * 2 + [ANYWHERE],
+        in_specs=[SMEM_WHOLE] * 3 + [VMEM_WHOLE] * 2,
         out_specs=[VMEM_WHOLE] * 3,
         out_shape=[send_shape] * 3,
         compiler_params=params(4),
         cost_estimate=cost(1, 1),
         name="send_rows",
-    )(in_cell, send_node, send_outlet, scaled, turns, supply_there)
+    )(in_cell, send_node, send_outlet, scaled, turns)
+    supply_there, *early = lax.optimization_barrier((supply_there, *early))
     arrived = [
         shifted(send, "region", SHIFTS[side]) for side, send in enumerate(early)
     ]
@@ -558,22 +573,20 @@
         name="node_flow",
     )(in_cell, scaled, turns, early[0])
 
-    shared = apart(
-        lambda x: lax.all_gather(x, "dest", axis=0, tiled=True),
-        jnp.concatenate([demand, supply_there]),
-    )
+    joined = jnp.concatenate([demand, supply_there])
+    shared = lax.all_gather(joined, "dest", axis=0, tiled=True)
     home = pl.pallas_call(
         functools.partial(home_kernel, sizes),
-        in_specs=[SMEM_WHOLE] * 2 + [VMEM_WHOLE] * 2,
+        in_specs=[SMEM_WHOLE] * 2 + [VMEM_WHOLE] * 2 + [ANYWHERE],
         out_specs=VMEM_WHOLE,
         out_shape=rows_shape,
         compiler_params=params(4),
         cost_estimate=cost(1, 1),
         name="home_rows",
-    )(source_node, source_outlet, turns, flow)
+    )(source_node, source_outlet, turns, flow, joined)
     keep, home_theta, theta, slot_theta = pl.pallas_call(
         functools.partial(theta_kernel, sizes, regions, commodities),
-        in_specs=[VMEM_WHOLE] * 6,
+        in_specs=[VMEM_WHOLE] * 6 + [ANYWHERE],
         out_specs=[VMEM_WHOLE] * 4,
         out_shape=[jax.ShapeDtypeStruct(per_cell, F32)] * 2
         + [
@@ -583,8 +596,8 @@
         compiler_params=params(8),
         cost_estimate=cost(1, 1),
         name="theta",
-    )(supply, shared, node_in, node_out, send_list, fraction)
-    theta_there = apart(to_neighbours, slot_theta)
+    )(supply, shared, node_in, node_out, send_list, fraction, home)
+    theta_there = to_neighbours(slot_theta)
 
     (behind,) = pl.pallas_call(
         functools.partial(scaled_send_kernel, sizes, 3),

time: 99.1 us -> 86.1 us (0.87)
  local copies, waits for them, and re-layouts: 18.4 us -> 0.02 us
  waiting for transfers between devices: 8 us -> 11.2 us
  blocking collectives: 10.8 us -> 12.7 us
  starting transfers between devices: 10.5 us -> 11.5 us
    unnamed x38 -> x7, local copies, waits for them, and re-layouts: 17.9 us -> 0.01 us
    ppermute x4, waiting for transfers between devices: 0.01 us -> 6.05 us  [shifted(): return lax.ppermute(block, axis, route)]
    ppermute x4, starting transfers between devices: 3.56 us -> 6.47 us  [shifted(): return lax.ppermute(block, axis, route)]
    ppermute x2, waiting for transfers between devices: 7.36 us -> 5.12 us  [to_neighbours(): return lax.ppermute(block, ('region', 'dest'), route)]
    ppermute x2, starting transfers between devices: 3.82 us -> 1.87 us  [to_neighbours(): return lax.ppermute(block, ('region', 'dest'), route)]
    pallas_call x2, Pallas kernels: 8 us -> 9.43 us  [the longest x1 4.76 us: on_device(): pl.pallas_call(functools.partial(turn_rows_kernel, sizes, chunk), in_spec...]
    all_gather x1, blocking collectives: 5.5 us -> 6.85 us  [on_device(): shared = lax.all_gather(joined, 'dest', axis=0, tiled=True)]
    pallas_call x1, Pallas kernels: 5.91 us -> 4.82 us  [on_device(): pl.pallas_call(functools.partial(send_kernel, sizes, (0, 1, 2)), in_specs...]
  transfers between devices with their start and end apart: 9 -> 9, of which waited for: 3 -> 3; matrix products, arithmetic and copies ran while one was open for 1% -> 0% of each run, Pallas kernels for 34% -> 48%
where the time goes in v7:
time: 86.1 us; the launch traced here: 86 us
  Pallas kernels  50.4 us (59%)
  blocking collectives  12.7 us (15%)
  starting transfers between devices  11.5 us (13%)
  waiting for transfers between devices  11.2 us (13%)
    pallas_call x1, Pallas kernels, on_device(): pl.pallas_call(functools.partial(node_flow_kernel, sizes), in_specs=[SMEM...  10.1 us
    all_gather x1, blocking collectives, on_device(): shared = lax.all_gather(joined, 'dest', axis=0, tiled=True)  6.85 us
    ppermute x4, starting transfers between devices, shifted(): return lax.ppermute(block, axis, route)  6.47 us
    ppermute x4, waiting for transfers between devices, shifted(): return lax.ppermute(block, axis, route)  6.05 us
    all_gather x1, blocking collectives, on_device(): lax.all_gather(theta_there, 'dest', axis=0, tiled=True)[:list_shape[0]]  5.81 us
    pallas_call x1, Pallas kernels, on_device(): pl.pallas_call(functools.partial(theta_kernel, sizes, regions, commoditie...  5.76 us
    pallas_call x1, Pallas kernels, on_device(): pl.pallas_call(functools.partial(home_kernel, sizes), in_specs=[SMEM_WHOL...  5.38 us
    ppermute x2, waiting for transfers between devices, to_neighbours(): return lax.ppermute(block, ('region', 'dest'), route)  5.12 us
  transfers between devices with their start and end apart: 9, of which 3 were waited for; matrix products, arithmetic and copies ran while one was open for 0% of the time, Pallas kernels for 48%

profile of v7, /device:TPU:0, one launch (start us, length us, event | category | flops | bytes accessed | tf_op | source)
XLA Modules:
  0.0 86.0 jit_solution(9914074298829823786)
XLA Ops:
  0.0 4.7 %cell_sum.1 = (f32[16,128]{1,0:T(8,128)S(1)}, f32[16392,128]{1,0:T(8,128)S(1)}) custom-call(f32[2048,1024]{1,0:T(8,128)} %x_hbm.2), custom_call_target="tpu_custom_call" | custom-call | flops 2097152 | bytes 8388608 | tf_op jit(solution)/shard_map/cell_sum/pallas_call | solution.py:483
  4.7 0.5 collective-permute-start
  5.2 2.6 %collective-permute-start.1 = (f32[16,128]{1,0:T(8,128)S(1)}, f32[16,128]{1,0:T(8,128)S(1)}, u32[]{:S(2)}, u32[]{:S(2)}) collective-permute-start(f32[16,128]{1,0:T(8,128)S(1)} %get-tuple-element.44.after_ref), channel_id=1, source_target_pairs={{0,2},{1,3},{2,0},{3,1},{4,6},{5,7},{6,4},{7,5},{8,10},{9,11},{10,... | collective-permute-start | bytes 24584 | tf_op jit(solution)/shard_map/ppermute | solution.py:40
  7.8 0.1 collective-permute-start.2
  7.8 4.8 %turn_rows.1 = (s32[8192,128]{1,0:T(8,128)S(1)}, s32[32,128]{1,0:T(8,128)S(1)}, s32[8,128]{1,0:T(8,128)S(1)}, s32[8,128]{1,0:T(8,128)S(1)}, s32[8,128]{1,0:T(8,1...) custom-call(s32[1024,1024]{1,0:T(8,128)} %x_hbm.3, ...), custom_call_target="tpu_custom_call" | custom-call | bytes 4194304 | tf_op jit(solution)/shard_map/turn_rows/pallas_call | solution.py:503
  12.6 0.0 collective-permute-done
  12.6 0.0 collective-permute-done.1
  12.6 0.0 collective-permute-done.2
  12.6 0.0 copy-done
  12.7 1.8 %collective-permute-start.3 = (f32[16,128]{1,0:T(8,128)S(1)}, f32[16,128]{1,0:T(8,128)S(1)}, u32[]{:S(2)}, u32[]{:S(2)}) collective-permute-start(f32[16,128]{1,0:T(8,128)S(1)} %fusion.1.supply), channel_id=1, source_target_pairs={{0,4},{1,29},{2,10},{3,27},{4,8},{5,1},{6,14},{7,31},{8,12},{9,5},... | collective-permute-start | bytes 24584 | tf_op jit(solution)/shard_map/ppermute | solution.py:28
  14.5 2.5 %scale_rows.1.scaled = f32[16392,128]{1,0:T(8,128)S(1)} custom-call(f32[2048]{0:T(1024)S(1)} %bitcast.23, f32[16392,128]{1,0:T(8,128)S(1)} %get-tuple-element.49.rows), custom_call_target="tpu_custom_call" | custom-call | flops 1 | bytes 1 | tf_op jit(solution)/shard_map/scale_rows/pallas_call | solution.py:538
  17.0 4.8 %send_rows.1 = (f32[1536,128]{1,0:T(8,128)S(1)}, f32[1536,128]{1,0:T(8,128)S(1)}, f32[1536,128]{1,0:T(8,128)S(1)}) custom-call(s32[4096]{0:T(1024)S(1)} %bitcast.24, s32[1024]{0:T(1024)S(1)} %bitcast.26, s32[1024]{0:T(1024)S(1)} %bitcast.28, f32[16392,128]{1,0:T(8,128)S(1)} %scale_rows.1.scaled, s32[8192,128]{1,0:T(8,128)S(1)} %get-tuple-element.50.turns), custom_call_target="tpu_custom_call" | custom-call | flops 1 | bytes 1 | tf_op jit(solution)/shard_map/send_rows/pallas_call | solution.py:547
  21.8 0.0 collective-permute-done.3
  21.8 1.6 %collective-permute-start.5 = (f32[1536,128]{1,0:T(8,128)S(1)}, f32[1536,128]{1,0:T(8,128)S(1)}, u32[]{:S(2)}, u32[]{:S(2)}) collective-permute-start(f32[1536,128]{1,0:T(8,128)S(1)} %get-tuple-element.56.after_ref), channel_id=1, source_target_pairs={{28,0},{0,4},{4,8},{8,12},{12,16},{16,20},{20,24},{24,28},{29,1},{... | collective-permute-start | bytes 2359304 | tf_op jit(solution)/shard_map/ppermute | solution.py:34
  23.4 3.2 %collective-permute-start.6 = (f32[1536,128]{1,0:T(8,128)S(1)}, f32[1536,128]{1,0:T(8,128)S(1)}, u32[]{:S(2)}, u32[]{:S(2)}) collective-permute-start(f32[1536,128]{1,0:T(8,128)S(1)} %get-tuple-element.67), channel_id=1, source_target_pairs={{4,0},{8,4},{12,8},{16,12},{20,16},{24,20},{28,24},{0,28},{5,1},{9... | collective-permute-start | bytes 2359304 | tf_op jit(solution)/shard_map/ppermute | solution.py:34
  26.6 0.0 collective-permute-start.7
  26.6 10.1 %node_flow.1 = (f32[8192,128]{1,0:T(8,128)S(1)}, f32[32,128]{1,0:T(8,128)S(1)}) custom-call(s32[4096]{0:T(1024)S(1)} %bitcast.25, f32[16392,128]{1,0:T(8,128)S(1)} %scale_rows.1.scaled, s32[8192,128]{1,0:T(8,128)S(1)} %get-tuple-element.50.turns, f32[1536,128]{1,0:T(8,128)S(1)} %get-tuple-element.56.after_ref), custom_call_target="tpu_custom_call" | custom-call | flops 1 | bytes 1 | tf_op jit(solution)/shard_map/node_flow/pallas_call | solution.py:562
  36.8 5.4 %home_rows.1.after_ref.home = f32[16392,128]{1,0:T(8,128)S(1)} custom-call(s32[2048]{0:T(1024)S(1)} %bitcast.33, s32[2048]{0:T(1024)S(1)} %bitcast.34, s32[8192,128]{1,0:T(8,128)S(1)} %get-tuple-element.50.turns, f32[8192,128]{1,0:T(8,128)S(1)} %get-tuple-element.64.flow, f32[48,128]{1,0:T(8,128)S(1)} %constant_dynamic-update-slice_fusion.after_ref), custom_call_target="tpu_custom_call" | custom-call | flops 1 | bytes 1 | tf_op jit(solution)/shard_map/home_rows/pallas_call | solution.py:578
  42.2 6.9 %all_gather.6.shared = f32[192,128]{1,0:T(8,128)S(1)} all-gather(f32[48,128]{1,0:T(8,128)S(1)} %constant_dynamic-update-slice_fusion.after_ref), channel_id=1, replica_groups=mesh['region'=8,'dest'=4] {'dest'}, dimensions={0}, use_global_device_ids=true | all-gather | bytes 122880 | tf_op jit(solution)/shard_map/all_gather | solution.py:577
  49.0 5.8 %theta.1 = (f32[16,128]{1,0:T(8,128)S(1)}, f32[16,128]{1,0:T(8,128)S(1)}, f32[8,128]{1,0:T(8,128)S(1)}, f32[2,128]{1,0:T(2,128)S(1)}) custom-call(f32[16,128]{1,0:T(8,128)S(1)} %fusion.1.supply, f32[192,128]{1,0:T(8,128)S(1)} %all_gather.6.shared, s32[4,1024]{1,0:T(4,128)S(1)} %get-tuple-element.59.node_in, s32[4,1024]{1,0:T(4,128)S(1)} %get-tuple-element.60.node_out, ...), custom_call_target="tpu_custom_call" | custom-call | flops 1 | bytes 1 | tf_op jit(solution)/shard_map/theta/pallas_call | solution.py:587
  54.8 0.1 collective-permute-start.4
  54.9 1.2 %send_scaled.1 = f32[1536,128]{1,0:T(8,128)S(1)} custom-call(f32[1024]{0:T(1024)S(1)} %bitcast.37, s32[1024]{0:T(1024)S(1)} %bitcast.27, s32[1024]{0:T(1024)S(1)} %bitcast.29, f32[8192,128]{1,0:T(8,128)S(1)} %get-tuple-element.64.flow, s32[8192,128]{1,0:T(8,128)S(1)} %get-tuple-element.50.turns), custom_call_target="tpu_custom_call" | custom-call | flops 1 | bytes 1 | tf_op jit(solution)/shard_map/send_scaled/pallas_call | solution.py:602
  56.1 5.1 %collective-permute-done.4 = f32[2,128]{1,0:T(2,128)S(1)} collective-permute-done((f32[2,128]{1,0:T(2,128)S(1)}, f32[2,128]{1,0:T(2,128)S(1)}, u32[]{:S(2)}, u32[]{:S(2)}) %collective-permute-start.4) | collective-permute-done | bytes 1056 | tf_op jit(solution)/shard_map/ppermute | solution.py:28
  61.2 0.0 collective-permute-done.5.rest_0_
  61.2 0.0 collective-permute-done.6.rest_1_
  61.2 1.2 %collective-permute-done.7.rest_2_ = f32[1536,128]{1,0:T(8,128)S(1)} collective-permute-done((f32[1536,128]{1,0:T(8,128)S(1)}, f32[1536,128]{1,0:T(8,128)S(1)}, u32[]{:S(2)}, u32[]{:S(2)}) %collective-permute-start.7) | collective-permute-done | bytes 786464 | tf_op jit(solution)/shard_map/ppermute | solution.py:34
  62.4 1.7 %collective-permute-start.8 = (f32[1536,128]{1,0:T(8,128)S(1)}, f32[1536,128]{1,0:T(8,128)S(1)}, u32[]{:S(2)}, u32[]{:S(2)}) collective-permute-start(f32[1536,128]{1,0:T(8,128)S(1)} %send_scaled.1), channel_id=1, source_target_pairs={{8,0},{12,4},{16,8},{20,12},{24,16},{28,20},{0,24},{4,28},{9,1},{1... | collective-permute-start | bytes 2359304 | tf_op jit(solution)/shard_map/ppermute | solution.py:34
  64.1 4.7 %base_rows.1.rest_3_ = f32[16392,128]{1,0:T(8,128)S(1)} custom-call(f32[2048]{0:T(1024)S(1)} %bitcast.35, f32[2048]{0:T(1024)S(1)} %bitcast.36, f32[16392,128]{1,0:T(8,128)S(1)} %get-tuple-element.49.rows, f32[16392,128]{1,0:T(8,128)S(1)} %home_rows.1.after_ref.home), custom_call_target="tpu_custom_call" | custom-call | flops 1 | bytes 1 | tf_op jit(solution)/shard_map/base_rows/pallas_call | solution.py:615
  68.8 5.8 %all-gather = f32[4,2,128]{2,1,0:T(2,128)S(1)} all-gather(f32[1,2,128]{2,1,0:T(2,128)S(1)} %bitcast.38), channel_id=1, replica_groups=mesh['region'=8,'dest'=4] {'dest'}, dimensions={0}, use_global_device_ids=true | all-gather | bytes 5120 | tf_op jit(solution)/shard_map/all_gather | solution.py:613
  74.6 1.9 %land_first.1.rest_1_ = f32[16392,128]{1,0:T(8,128)S(1)} custom-call(f32[1024]{0:T(1024)S(1)} %bitcast.32, s32[1024]{0:T(1024)S(1)} %bitcast.30, f32[1536,128]{1,0:T(8,128)S(1)} %collective-permute-done.5.rest_0_, f32[1536,128]{1,0:T(8,128)S(1)} %collective-permute-done.6.rest_1_, ...), custom_call_target="tpu_custom_call", output_to_operand_aliasing={{}: (5, {})} | custom-call | flops 1 | bytes 1 | tf_op jit(solution)/shard_map/land_first/pallas_call | solution.py:625
  76.6 4.9 %collective-permute-done.8.rest_0_ = f32[1536,128]{1,0:T(8,128)S(1)} collective-permute-done((f32[1536,128]{1,0:T(8,128)S(1)}, f32[1536,128]{1,0:T(8,128)S(1)}, u32[]{:S(2)}, u32[]{:S(2)}) %collective-permute-start.8) | collective-permute-done | bytes 786464 | tf_op jit(solution)/shard_map/ppermute | solution.py:34
  81.5 4.5 %finish.1 = (f32[2048,1024]{1,0:T(8,128)}, f32[16392,128]{1,0:T(8,128)S(1)}) custom-call(s32[1024]{0:T(1024)S(1)} %bitcast.31, f32[1536,128]{1,0:T(8,128)S(1)} %collective-permute-done.8.rest_0_, f32[16392,128]{1,0:T(8,128)S(1)} %land_first.1.rest_1_), custom_call_target="tpu_custom_call", output_to_operand_aliasing={{1}: (2, {})} | custom-call | flops 2097152 | bytes 8388608 | tf_op jit(solution)/shard_map/finish/pallas_call | solution.py:636
  (9 shorter events, 0.0 us)
Async XLA Ops:
  0.0 12.6 %copy-start = (f32[2048]{0:T(1024)S(1)}, f32[2048]{0:T(1024)}, u32[]{:S(2)}) copy-start(f32[2048]{0:T(1024)} %param.10) | copy-start | bytes 24580
  0.0 12.7 %copy-start.1 = (f32[2048]{0:T(1024)S(1)}, f32[2048]{0:T(1024)}, u32[]{:S(2)}) copy-start(f32[2048]{0:T(1024)} %param.11) | copy-start | bytes 24580
  0.0 12.7 %copy-start.2 = (f32[2048]{0:T(1024)S(1)}, f32[2048]{0:T(1024)}, u32[]{:S(2)}) copy-start(f32[2048]{0:T(1024)} %param.12) | copy-start | bytes 24580
  4.7 7.9 %collective-permute-start = (f32[16,128]{1,0:T(8,128)S(1)}, f32[16,128]{1,0:T(8,128)S(1)}, u32[]{:S(2)}, u32[]{:S(2)}) collective-permute-start(f32[16,128]{1,0:T(8,128)S(1)} %get-tuple-element.44.after_ref), channel_id=1, source_target_pairs={{0,1},{1,0},{2,3},{3,2},{4,5},{5,4},{6,7},{7,6},{8,9},{9,8},{10,11... | collective-permute-start | bytes 24584 | tf_op jit(solution)/shard_map/ppermute | solution.py:40
  5.2 7.4 %collective-permute-start.1 = (f32[16,128]{1,0:T(8,128)S(1)}, f32[16,128]{1,0:T(8,128)S(1)}, u32[]{:S(2)}, u32[]{:S(2)}) collective-permute-start(f32[16,128]{1,0:T(8,128)S(1)} %get-tuple-element.44.after_ref), channel_id=1, source_target_pairs={{0,2},{1,3},{2,0},{3,1},{4,6},{5,7},{6,4},{7,5},{8,10},{9,11},{10,... | collective-permute-start | bytes 24584 | tf_op jit(solution)/shard_map/ppermute | solution.py:40
  7.8 4.9 %collective-permute-start.2 = (f32[16,128]{1,0:T(8,128)S(1)}, f32[16,128]{1,0:T(8,128)S(1)}, u32[]{:S(2)}, u32[]{:S(2)}) collective-permute-start(f32[16,128]{1,0:T(8,128)S(1)} %get-tuple-element.44.after_ref), channel_id=1, source_target_pairs={{0,3},{1,2},{2,1},{3,0},{4,7},{5,6},{6,5},{7,4},{8,11},{9,10},{10,... | collective-permute-start | bytes 24584 | tf_op jit(solution)/shard_map/ppermute | solution.py:40
  12.7 9.1 %collective-permute-start.3 = (f32[16,128]{1,0:T(8,128)S(1)}, f32[16,128]{1,0:T(8,128)S(1)}, u32[]{:S(2)}, u32[]{:S(2)}) collective-permute-start(f32[16,128]{1,0:T(8,128)S(1)} %fusion.1.supply), channel_id=1, source_target_pairs={{0,4},{1,29},{2,10},{3,27},{4,8},{5,1},{6,14},{7,31},{8,12},{9,5},... | collective-permute-start | bytes 24584 | tf_op jit(solution)/shard_map/ppermute | solution.py:28
  21.8 39.4 %collective-permute-start.5 = (f32[1536,128]{1,0:T(8,128)S(1)}, f32[1536,128]{1,0:T(8,128)S(1)}, u32[]{:S(2)}, u32[]{:S(2)}) collective-permute-start(f32[1536,128]{1,0:T(8,128)S(1)} %get-tuple-element.56.after_ref), channel_id=1, source_target_pairs={{28,0},{0,4},{4,8},{8,12},{12,16},{16,20},{20,24},{24,28},{29,1},{... | collective-permute-start | bytes 2359304 | tf_op jit(solution)/shard_map/ppermute | solution.py:34
  23.4 37.8 %collective-permute-start.6 = (f32[1536,128]{1,0:T(8,128)S(1)}, f32[1536,128]{1,0:T(8,128)S(1)}, u32[]{:S(2)}, u32[]{:S(2)}) collective-permute-start(f32[1536,128]{1,0:T(8,128)S(1)} %get-tuple-element.67), channel_id=1, source_target_pairs={{4,0},{8,4},{12,8},{16,12},{20,16},{24,20},{28,24},{0,28},{5,1},{9... | collective-permute-start | bytes 2359304 | tf_op jit(solution)/shard_map/ppermute | solution.py:34
  26.6 35.8 %collective-permute-start.7 = (f32[1536,128]{1,0:T(8,128)S(1)}, f32[1536,128]{1,0:T(8,128)S(1)}, u32[]{:S(2)}, u32[]{:S(2)}) collective-permute-start(f32[1536,128]{1,0:T(8,128)S(1)} %get-tuple-element.68), channel_id=1, source_target_pairs={{24,0},{28,4},{0,8},{4,12},{8,16},{12,20},{16,24},{20,28},{25,1},{... | collective-permute-start | bytes 2359304 | tf_op jit(solution)/shard_map/ppermute | solution.py:34
  54.8 6.4 %collective-permute-start.4 = (f32[2,128]{1,0:T(2,128)S(1)}, f32[2,128]{1,0:T(2,128)S(1)}, u32[]{:S(2)}, u32[]{:S(2)}) collective-permute-start(f32[2,128]{1,0:T(2,128)S(1)} %get-tuple-element.66), channel_id=1, source_target_pairs={{0,4},{1,29},{2,10},{3,27},{4,8},{5,1},{6,14},{7,31},{8,12},{9,5},... | collective-permute-start | bytes 3080 | tf_op jit(solution)/shard_map/ppermute | solution.py:28
  62.4 19.0 %collective-permute-start.8 = (f32[1536,128]{1,0:T(8,128)S(1)}, f32[1536,128]{1,0:T(8,128)S(1)}, u32[]{:S(2)}, u32[]{:S(2)}) collective-permute-start(f32[1536,128]{1,0:T(8,128)S(1)} %send_scaled.1), channel_id=1, source_target_pairs={{8,0},{12,4},{16,8},{20,12},{24,16},{28,20},{0,24},{4,28},{9,1},{1... | collective-permute-start | bytes 2359304 | tf_op jit(solution)/shard_map/ppermute | solution.py:34

commit v8 on v7

--- a/solution.py
+++ b/solution.py
@@ -104,26 +104,32 @@
     return jnp.where(rows == index, 1.0, 0.0)
 
 
+def in_parts(x):
+    high = x.astype(jnp.bfloat16)
+    rest = x - high.astype(F32)
+    middle = rest.astype(jnp.bfloat16)
+    low = (rest - middle.astype(F32)).astype(jnp.bfloat16)
+    return jnp.concatenate([high, middle, low], axis=0)
+
+
+def selected(values, choice, dims):
+    count = values.shape[0]
+    product = lax.dot_general(
+        in_parts(values), choice.astype(jnp.bfloat16), (dims, ((), ())),
+        preferred_element_type=F32,
+    )
+    return product[:count, :] + product[count : 2 * count, :] + product[2 * count :, :]
+
+
 def look_up(table, index):
-    picked = lax.dot_general(
-        table.T,
-        one_hot(index // LANES, table.shape[0]),
-        (((1,), (0,)), ((), ())),
-        preferred_element_type=F32,
-        precision=EXACT,
-    )
+    picked = selected(table.T, one_hot(index // LANES, table.shape[0]), ((1,), (0,)))
     return jnp.sum(picked * one_hot(index % LANES, LANES), axis=0, keepdims=True)
 
 
 def scatter(index, values, height):
     high = jnp.where(index >= 0, index // LANES, -1)
-    return lax.dot_general(
-        one_hot(high, height) * values,
-        one_hot(jnp.where(index >= 0, index % LANES, -1), LANES),
-        (((1,), (1,)), ((), ())),
-        preferred_element_type=F32,
-        precision=EXACT,
-    )
+    low = jnp.where(index >= 0, index % LANES, -1)
+    return selected(one_hot(high, height) * values, one_hot(low, LANES), ((1,), (1,)))
 
 
 def home_cells(node_out, region_no, cells):
@@ -200,20 +206,9 @@
 
 def turn_rows_kernel(sizes, chunk, x_hbm, after_ref, *rest):
     cells, nodes, branches, cap, sub = sizes
-    lists, rows_ref, made, held, (recv, x, sems, list_sems) = (
-        rest[:4], rest[4], rest[5:11], rest[11:14], rest[14:]
-    )
-    held = (*held, recv)
-    list_copies = [
-        pltpu.make_async_copy(source, target, list_sems.at[k])
-        for k, (source, target) in enumerate(zip(lists, held))
-    ]
-    for copy in list_copies:
-        copy.start()
+    lists, rows_ref, made, (x, sems) = rest[:4], rest[4], rest[5:11], rest[11:]
     copies = copies_in(x_hbm, x, sems, chunk)
-    for copy in list_copies:
-        copy.wait()
-    make_lists(sizes, *held, *made)
+    make_lists(sizes, *lists, *made)
     for number, copy in enumerate(copies):
         copy.wait()
 
@@ -225,14 +220,17 @@
         lax.fori_loop(0, chunk // 16, body, 0)
 
 
-def gathered_flow(node, in_cell, scaled, sizes):
-    cells, nodes, branches, cap, sub = sizes
-    return tree_sum(
-        [row_of(scaled, in_cell[i * nodes + node], sub)[...] for i in range(branches)]
-    )
-
-
-def scale_kernel(sizes, fraction, rows, scaled):
+def gathered_flow(node, in_cell, fraction, rows, sizes):
+    cells, nodes, branches, cap, sub = sizes
+    parts = []
+    for i in range(branches):
+        cell = in_cell[i * nodes + node]
+        part = row_of(rows, cell, sub)[...]
+        parts.append(part if fraction is None else part * fraction[cell])
+    return tree_sum(parts)
+
+
+def scale_kernel(sizes, fraction, rows, after_ref, scaled):
     cells, nodes, branches, cap, sub = sizes
 
     def body(step, carry):
@@ -248,9 +246,8 @@
     row_of(scaled, cells, sub)[...] = jnp.zeros((sub, LANES), F32)
 
 
-def send_kernel(sizes, sides, in_cell, send_node, send_outlet, scaled, turns, *rest):
-    cells, nodes, branches, cap, sub = sizes
-    sends = rest
+def send_kernel(sizes, sides, fraction, in_cell, send_node, send_outlet, rows, turns, *sends):
+    cells, nodes, branches, cap, sub = sizes
     batch = 8
     for side, send in zip(sides, sends):
 
@@ -260,7 +257,7 @@
             for i in range(batch):
                 slot = side * padded(cap) + first + i
                 node = send_node[slot]
-                value = gathered_flow(node, in_cell, scaled, sizes)
+                value = gathered_flow(node, in_cell, fraction, rows, sizes)
                 choice = row_of(turns, node, sub)[...]
                 values.append(jnp.where(choice == send_outlet[slot], value, 0.0))
             for i in range(batch):
@@ -296,7 +293,7 @@
     def gather(step, carry):
         first = step * 8
         values = [
-            gathered_flow(first + i, in_cell, scaled, sizes) for i in range(8)
+            gathered_flow(first + i, in_cell, None, scaled, sizes) for i in range(8)
         ]
         for i in range(8):
             row_of(flow, first + i, sub)[...] = values[i]
@@ -325,12 +322,12 @@
 
 
 def theta_kernel(
-    sizes, regions, commodities, supply, shared, node_in, node_out, send_list, fraction,
-    after_ref, keep, home_theta, theta_out, slot_theta,
+    sizes, regions, commodities, supply, shared, node_out, send_list, after_ref,
+    theta_out, slot_theta,
 ):
     cells, nodes, branches, cap, sub = sizes
+    per_outlet = nodes // LANES
     height = cells // LANES
-    per_outlet = nodes // LANES
     block = branches * per_outlet + height
     region_no = lax.axis_index("region")
     members = shared.shape[0] // block
@@ -357,7 +354,17 @@
         ratio = room / jnp.maximum(demand[j * per_outlet : (j + 1) * per_outlet, :], room)
         tall = jnp.minimum(tall, jnp.where(stacked(outs) >= 0, ratio, 1.0))
     theta_out[...] = tall
-    theta = strung(tall)
+    slots = send_list[pl.ds(lax.axis_index("dest") % 4, 1), :]
+    put_row(slot_theta, 0, look_up(tall, jnp.where(slots >= 0, slots % nodes, 0)), 0.0)
+
+
+def keep_kernel(
+    sizes, theta_ref, node_in, node_out, fraction, sent_ref, arrived_ref, keep, home_theta
+):
+    cells, nodes, branches, cap, sub = sizes
+    height = cells // LANES
+    region_no = lax.axis_index("region")
+    theta = strung(theta_ref[...])
     cell_theta = jnp.zeros((height, LANES), F32)
     into = jnp.zeros((height, LANES), F32)
     for j in range(branches):
@@ -366,8 +373,6 @@
         into = into + scatter(home, theta, height)
     keep[...] = 1.0 - cell_theta * fraction[...]
     home_theta[...] = into
-    slots = send_list[pl.ds(lax.axis_index("dest") % 4, 1), :]
-    put_row(slot_theta, 0, look_up(tall, jnp.where(slots >= 0, slots % nodes, 0)), 0.0)
 
 
 def home_kernel(sizes, source, outlet, turns, flow, after_ref, home):
@@ -475,10 +480,6 @@
     row_bytes = width * 4
     occupancy = pltpu.with_memory_space_constraint(occupancy, pltpu.HBM)
     turn = pltpu.with_memory_space_constraint(turn, pltpu.HBM)
-    node_in, node_out, send_list, recv_list = (
-        pltpu.with_memory_space_constraint(x, pltpu.HBM)
-        for x in (node_in, node_out, send_list, recv_list)
-    )
 
     local_sum, rows = pl.pallas_call(
         functools.partial(cell_sum_kernel, chunk, sub),
@@ -502,28 +503,24 @@
 
     turns, *lists = pl.pallas_call(
         functools.partial(turn_rows_kernel, sizes, chunk),
-        in_specs=[ANYWHERE] * 6,
-        out_specs=[VMEM_WHOLE] * 10,
+        in_specs=[ANYWHERE] * 2 + [VMEM_WHOLE] * 4,
+        out_specs=[VMEM_WHOLE] * 7,
         out_shape=[
             pltpu.VMEM((nodes * sub, LANES), I32),
             jax.ShapeDtypeStruct((branches * nodes // LANES, LANES), I32),
         ]
         + [jax.ShapeDtypeStruct(list_shape, I32)] * 3
-        + [jax.ShapeDtypeStruct(per_cell, I32)] * 2
-        + [pltpu.VMEM(x.shape, I32) for x in (node_in, node_out, send_list)],
+        + [jax.ShapeDtypeStruct(per_cell, I32)] * 2,
         scratch_shapes=[
-            pltpu.VMEM(recv_list.shape, I32),
             pltpu.VMEM((nodes, width), I32),
             pltpu.SemaphoreType.DMA((nodes // chunk,)),
-            pltpu.SemaphoreType.DMA((4,)),
         ],
         compiler_params=params(8),
         cost_estimate=cost(0, nodes * row_bytes),
         name="turn_rows",
     )(turn, local_sum, node_in, node_out, send_list, recv_list)
-    node_in, node_out, send_list = lists[6:]
     in_cell, send_node, send_outlet, land, source_node, source_outlet = (
-        x.reshape(-1) for x in lists[:6]
+        x.reshape(-1) for x in lists
     )
 
     turns, *sums = lax.optimization_barrier((turns, *sums))
@@ -535,29 +532,38 @@
     send_shape = pltpu.VMEM((cap * sub, LANES), F32)
 
     supply_there = to_neighbours(supply)
+    weights = jnp.concatenate([fraction.reshape(-1), jnp.zeros((LANES,), F32)])
+    (ahead,) = pl.pallas_call(
+        functools.partial(send_kernel, sizes, (2,)),
+        in_specs=[SMEM_WHOLE] * 4 + [VMEM_WHOLE] * 2,
+        out_specs=[VMEM_WHOLE],
+        out_shape=[send_shape],
+        compiler_params=params(4),
+        cost_estimate=cost(1, 1),
+        name="send_ahead",
+    )(weights, in_cell, send_node, send_outlet, rows, turns)
+    ahead, supply_there = lax.optimization_barrier((ahead, supply_there))
     scaled = pl.pallas_call(
         functools.partial(scale_kernel, sizes),
-        in_specs=[SMEM_WHOLE, VMEM_WHOLE],
+        in_specs=[SMEM_WHOLE, VMEM_WHOLE, ANYWHERE],
         out_specs=VMEM_WHOLE,
         out_shape=rows_shape,
         compiler_params=params(4),
         cost_estimate=cost(1, 1),
         name="scale_rows",
-    )(fraction.reshape(-1), rows)
-    early = pl.pallas_call(
-        functools.partial(send_kernel, sizes, (0, 1, 2)),
+    )(fraction.reshape(-1), rows, ahead)
+    near = pl.pallas_call(
+        functools.partial(send_kernel, sizes, (0, 1), None),
         in_specs=[SMEM_WHOLE] * 3 + [VMEM_WHOLE] * 2,
-        out_specs=[VMEM_WHOLE] * 3,
-        out_shape=[send_shape] * 3,
+        out_specs=[VMEM_WHOLE] * 2,
+        out_shape=[send_shape] * 2,
         compiler_params=params(4),
         cost_estimate=cost(1, 1),
-        name="send_rows",
+        name="send_near",
     )(in_cell, send_node, send_outlet, scaled, turns)
-    supply_there, *early = lax.optimization_barrier((supply_there, *early))
     arrived = [
-        shifted(send, "region", SHIFTS[side]) for side, send in enumerate(early)
+        shifted(send, "region", SHIFTS[side]) for side, send in enumerate([*near, ahead])
     ]
-
 
     flow, demand = pl.pallas_call(
         functools.partial(node_flow_kernel, sizes),
@@ -571,7 +577,7 @@
         compiler_params=params(8),
         cost_estimate=cost(1, 1),
         name="node_flow",
-    )(in_cell, scaled, turns, early[0])
+    )(in_cell, scaled, turns, near[0])
 
     joined = jnp.concatenate([demand, supply_there])
     shared = lax.all_gather(joined, "dest", axis=0, tiled=True)
@@ -584,19 +590,18 @@
         cost_estimate=cost(1, 1),
         name="home_rows",
     )(source_node, source_outlet, turns, flow, joined)
-    keep, home_theta, theta, slot_theta = pl.pallas_call(
+    theta, slot_theta = pl.pallas_call(
         functools.partial(theta_kernel, sizes, regions, commodities),
-        in_specs=[VMEM_WHOLE] * 6 + [ANYWHERE],
-        out_specs=[VMEM_WHOLE] * 4,
-        out_shape=[jax.ShapeDtypeStruct(per_cell, F32)] * 2
-        + [
+        in_specs=[VMEM_WHOLE] * 4 + [ANYWHERE],
+        out_specs=[VMEM_WHOLE] * 2,
+        out_shape=[
             jax.ShapeDtypeStruct((nodes // LANES, LANES), F32),
             jax.ShapeDtypeStruct((padded(cap) // LANES, LANES), F32),
         ],
         compiler_params=params(8),
         cost_estimate=cost(1, 1),
         name="theta",
-    )(supply, shared, node_in, node_out, send_list, fraction, home)
+    )(supply, shared, node_out, send_list, home)
     theta_there = to_neighbours(slot_theta)
 
     (behind,) = pl.pallas_call(
@@ -608,7 +613,16 @@
         cost_estimate=cost(1, 1),
         name="send_scaled",
     )(theta.reshape(-1), send_node, send_outlet, flow, turns)
-    behind, theta_there, *arrived = lax.optimization_barrier((behind, theta_there, *arrived))
+    keep, home_theta = pl.pallas_call(
+        functools.partial(keep_kernel, sizes),
+        in_specs=[VMEM_WHOLE] * 4 + [ANYWHERE] * 2,
+        out_specs=[VMEM_WHOLE] * 2,
+        out_shape=[jax.ShapeDtypeStruct(per_cell, F32)] * 2,
+        compiler_params=params(8),
+        cost_estimate=cost(100000000, 1),
+        name="keep",
+    )(theta, node_in, node_out, fraction, behind, arrived[2])
+    keep, theta_there, *arrived = lax.optimization_barrier((keep, theta_there, *arrived))
     last = shifted(behind, "region", SHIFTS[3])
     scale = lax.all_gather(theta_there, "dest", axis=0, tiled=True)[: list_shape[0]]
 
@@ -618,7 +632,7 @@
         out_specs=VMEM_WHOLE,
         out_shape=rows_shape,
         compiler_params=params(4),
-        cost_estimate=cost(1, 1),
+        cost_estimate=pl.CostEstimate(flops=100000000000, bytes_accessed=1, transcendentals=0),
         name="base_rows",
     )(keep.reshape(-1), home_theta.reshape(-1), rows, home)
 
@@ -629,7 +643,7 @@
         out_shape=rows_shape,
         input_output_aliases={5: 0},
         compiler_params=params(4),
-        cost_estimate=cost(1, 1),
+        cost_estimate=pl.CostEstimate(flops=100000000000, bytes_accessed=1, transcendentals=0),
         name="land_first",
     )(scale.reshape(-1), land, *arrived, base)
 

time: 86.1 us -> 78.6 us (0.913)
  waiting for transfers between devices: 11.2 us -> 7.2 us
  Pallas kernels: 50.4 us -> 47.3 us
  blocking collectives: 12.7 us -> 11.1 us
  starting transfers between devices: 11.5 us -> 12.6 us
    ppermute x4, waiting for transfers between devices: 6.05 us -> 0.97 us  [shifted(): return lax.ppermute(block, axis, route)]
    pallas_call x1, Pallas kernels: 5.76 us -> 1.4 us  [on_device(): pl.pallas_call(functools.partial(theta_kernel, sizes, regions, commoditie...]
    pallas_call x1, Pallas kernels: 4.76 us -> 2.5 us  [on_device(): pl.pallas_call(functools.partial(turn_rows_kernel, sizes, chunk), in_spec...]
    pallas_call x1 -> x3, Pallas kernels: 4.82 us -> 6.82 us  [the longest x1 3.52 us: on_device(): pl.pallas_call(functools.partial(send_kernel, sizes, (0, 1), None), in_sp...]
    pallas_call x1, Pallas kernels: 1.25 us -> 2.13 us  [on_device(): pl.pallas_call(functools.partial(scaled_send_kernel, sizes, 3), in_specs=...]
    ppermute x4, starting transfers between devices: 6.47 us -> 7.35 us  [shifted(): return lax.ppermute(block, axis, route)]
    all_gather x1, blocking collectives: 6.85 us -> 5.99 us  [on_device(): shared = lax.all_gather(joined, 'dest', axis=0, tiled=True)]
  transfers between devices with their start and end apart: 9 -> 9, of which waited for: 3 -> 4; matrix products, arithmetic and copies ran while one was open for 0% -> 0% of each run, Pallas kernels for 48% -> 48%
where the time goes in v8:
time: 78.6 us; the launch traced here: 78.5 us
  Pallas kernels  47.3 us (60%)
  starting transfers between devices  12.6 us (16%)
  blocking collectives  11.1 us (14%)
  waiting for transfers between devices  7.2 us (9%)
    pallas_call x1, Pallas kernels, on_device(): pl.pallas_call(functools.partial(node_flow_kernel, sizes), in_specs=[SMEM...  10.1 us
    ppermute x4, starting transfers between devices, shifted(): return lax.ppermute(block, axis, route)  7.35 us
    all_gather x1, blocking collectives, on_device(): shared = lax.all_gather(joined, 'dest', axis=0, tiled=True)  5.99 us
    ppermute x2, waiting for transfers between devices, to_neighbours(): return lax.ppermute(block, ('region', 'dest'), route)  5.79 us
    pallas_call x1, Pallas kernels, on_device(): pl.pallas_call(functools.partial(home_kernel, sizes), in_specs=[SMEM_WHOL...  5.38 us
    all_gather x1, blocking collectives, on_device(): lax.all_gather(theta_there, 'dest', axis=0, tiled=True)[:list_shape[0]]  5.15 us
    pallas_call x1, Pallas kernels, on_device(): pl.pallas_call(functools.partial(finish_kernel, sizes, (3,), chunk), in_s...  5.06 us
    pallas_call x1, Pallas kernels, on_device(): pl.pallas_call(functools.partial(cell_sum_kernel, chunk, sub), in_specs=[...  4.71 us
  transfers between devices with their start and end apart: 9, of which 4 were waited for; matrix products, arithmetic and copies ran while one was open for 0% of the time, Pallas kernels for 48%

profile of v8, /device:TPU:0, one launch (start us, length us, event | category | flops | bytes accessed | tf_op | source)
XLA Modules:
  0.0 78.5 jit_solution(11322310430640036899)
XLA Ops:
  0.0 4.7 %cell_sum.1 = (f32[16,128]{1,0:T(8,128)S(1)}, f32[16392,128]{1,0:T(8,128)S(1)}) custom-call(f32[2048,1024]{1,0:T(8,128)} %x_hbm.2), custom_call_target="tpu_custom_call" | custom-call | flops 2097152 | bytes 8388608 | tf_op jit(solution)/shard_map/cell_sum/pallas_call | solution.py:484
  4.7 2.4 %collective-permute-start.2 = (f32[16,128]{1,0:T(8,128)S(1)}, f32[16,128]{1,0:T(8,128)S(1)}, u32[]{:S(2)}, u32[]{:S(2)}) collective-permute-start(f32[16,128]{1,0:T(8,128)S(1)} %get-tuple-element.38.after_ref), channel_id=1, source_target_pairs={{0,3},{1,2},{2,1},{3,0},{4,7},{5,6},{6,5},{7,4},{8,11},{9,10},{10,... | collective-permute-start | bytes 24584 | tf_op jit(solution)/shard_map/ppermute | solution.py:40
  7.2 0.6 collective-permute-start.1
  7.8 0.0 collective-permute-start
  7.9 2.5 %turn_rows.1 = (s32[8192,128]{1,0:T(8,128)S(1)}, s32[32,128]{1,0:T(8,128)S(1)}, s32[8,128]{1,0:T(8,128)S(1)}, s32[8,128]{1,0:T(8,128)S(1)}, s32[8,128]{1,0:T(8,1...) custom-call(s32[1024,1024]{1,0:T(8,128)} %x_hbm.3, f32[16,128]{1,0:T(8,128)S(1)} %get-tuple-element.38.after_ref, ...), custom_call_target="tpu_custom_call" | custom-call | bytes 4194304 | tf_op jit(solution)/shard_map/turn_rows/pallas_call | solution.py:504
  10.4 0.0 collective-permute-done.2
  10.4 0.4 collective-permute-done.1
  10.8 0.0 collective-permute-done
  10.9 1.6 %collective-permute-start.3 = (f32[16,128]{1,0:T(8,128)S(1)}, f32[16,128]{1,0:T(8,128)S(1)}, u32[]{:S(2)}, u32[]{:S(2)}) collective-permute-start(f32[16,128]{1,0:T(8,128)S(1)} %fusion.1.supply), channel_id=1, source_target_pairs={{0,4},{1,29},{2,10},{3,27},{4,8},{5,1},{6,14},{7,31},{8,12},{9,5},... | collective-permute-start | bytes 24584 | tf_op jit(solution)/shard_map/ppermute | solution.py:28
  12.5 2.6 %send_ahead.1.after_ref = f32[1536,128]{1,0:T(8,128)S(1)} custom-call(f32[2176]{0:T(1024)S(1)} %concatenate.6.fraction, s32[4096]{0:T(1024)S(1)} %bitcast.23, s32[1024]{0:T(1024)S(1)} %bitcast.28, s32[1024]{0:T(1024)S(1)} %bitcast.31, f32[16392,128]{1,0:T(8,128)S(1)} %get-tuple-element.43.rows, s32[8192,128]{1,0:T(8,128)S(1)} %get-tuple-element.46.turns), custom_call_target="tpu_custom_call" | custom-call | flops 1 | bytes 1 | tf_op jit(solution)/shard_map/send_ahead/pallas_call | solution.py:536
  15.1 2.2 %collective-permute-done.3 = f32[16,128]{1,0:T(8,128)S(1)} collective-permute-done((f32[16,128]{1,0:T(8,128)S(1)}, f32[16,128]{1,0:T(8,128)S(1)}, u32[]{:S(2)}, u32[]{:S(2)}) %collective-permute-start.3) | collective-permute-done | bytes 8224 | tf_op jit(solution)/shard_map/ppermute | solution.py:28
  17.3 0.0 collective-permute-start.5
  17.3 2.5 %scale_rows.1.rows.scaled = f32[16392,128]{1,0:T(8,128)S(1)} custom-call(f32[2048]{0:T(1024)S(1)} %bitcast.27, f32[16392,128]{1,0:T(8,128)S(1)} %get-tuple-element.43.rows, f32[1536,128]{1,0:T(8,128)S(1)} %send_ahead.1.after_ref), custom_call_target="tpu_custom_call" | custom-call | flops 1 | bytes 1 | tf_op jit(solution)/shard_map/scale_rows/pallas_call | solution.py:546
  19.8 3.5 %send_near.1 = (f32[1536,128]{1,0:T(8,128)S(1)}, f32[1536,128]{1,0:T(8,128)S(1)}) custom-call(s32[4096]{0:T(1024)S(1)} %bitcast.24, s32[1024]{0:T(1024)S(1)} %bitcast.29, s32[1024]{0:T(1024)S(1)} %bitcast.32, f32[16392,128]{1,0:T(8,128)S(1)} %scale_rows.1.rows.scaled, s32[8192,128]{1,0:T(8,128)S(1)} %get-tuple-element.46.turns), custom_call_target="tpu_custom_call" | custom-call | flops 1 | bytes 1 | tf_op jit(solution)/shard_map/send_near/pallas_call | solution.py:555
  23.3 2.7 %collective-permute-start.8 = (f32[1536,128]{1,0:T(8,128)S(1)}, f32[1536,128]{1,0:T(8,128)S(1)}, u32[]{:S(2)}, u32[]{:S(2)}) collective-permute-start(f32[1536,128]{1,0:T(8,128)S(1)} %get-tuple-element.57), channel_id=1, source_target_pairs={{4,0},{8,4},{12,8},{16,12},{20,16},{24,20},{28,24},{0,28},{5,1},{9... | collective-permute-start | bytes 2359304 | tf_op jit(solution)/shard_map/ppermute | solution.py:34
  26.0 0.0 collective-permute-start.7
  26.0 10.1 %node_flow.1 = (f32[8192,128]{1,0:T(8,128)S(1)}, f32[32,128]{1,0:T(8,128)S(1)}) custom-call(s32[4096]{0:T(1024)S(1)} %bitcast.25, f32[16392,128]{1,0:T(8,128)S(1)} %scale_rows.1.rows.scaled, s32[8192,128]{1,0:T(8,128)S(1)} %get-tuple-element.46.turns, f32[1536,128]{1,0:T(8,128)S(1)} %get-tuple-element.48.after_ref), custom_call_target="tpu_custom_call" | custom-call | flops 1 | bytes 1 | tf_op jit(solution)/shard_map/node_flow/pallas_call | solution.py:568
  36.2 6.0 %all_gather.6.shared = f32[192,128]{1,0:T(8,128)S(1)} all-gather(f32[48,128]{1,0:T(8,128)S(1)} %constant_dynamic-update-slice_fusion.after_ref), channel_id=1, replica_groups=mesh['region'=8,'dest'=4] {'dest'}, dimensions={0}, use_global_device_ids=true | all-gather | bytes 122880 | tf_op jit(solution)/shard_map/all_gather | solution.py:583
  42.2 5.4 %home_rows.1.after_ref.home = f32[16392,128]{1,0:T(8,128)S(1)} custom-call(s32[2048]{0:T(1024)S(1)} %bitcast.35, s32[2048]{0:T(1024)S(1)} %bitcast.36, s32[8192,128]{1,0:T(8,128)S(1)} %get-tuple-element.46.turns, f32[8192,128]{1,0:T(8,128)S(1)} %get-tuple-element.53.flow, f32[48,128]{1,0:T(8,128)S(1)} %constant_dynamic-update-slice_fusion.after_ref), custom_call_target="tpu_custom_call" | custom-call | flops 1 | bytes 1 | tf_op jit(solution)/shard_map/home_rows/pallas_call | solution.py:584
  47.6 1.4 %theta.1 = (f32[8,128]{1,0:T(8,128)S(1)}, f32[2,128]{1,0:T(2,128)S(1)}) custom-call(f32[16,128]{1,0:T(8,128)S(1)} %fusion.1.supply, f32[192,128]{1,0:T(8,128)S(1)} %all_gather.6.shared, s32[4,1024]{1,0:T(4,128)S(1)} %copy-done, s32[4,192]{1,0:T(4,128)S(1)} %copy-done.2, f32[16392,128]{1,0:T(8,128)S(1)} %home_rows.1.after_ref.home), custom_call_target="tpu_custom_call" | custom-call | flops 1 | bytes 1 | tf_op jit(solution)/shard_map/theta/pallas_call | solution.py:593
  49.0 2.1 %send_scaled.1.sent_ref = f32[1536,128]{1,0:T(8,128)} custom-call(f32[1024]{0:T(1024)S(1)} %bitcast.34, s32[1024]{0:T(1024)S(1)} %bitcast.30, s32[1024]{0:T(1024)S(1)} %bitcast.33, f32[8192,128]{1,0:T(8,128)S(1)} %get-tuple-element.53.flow, s32[8192,128]{1,0:T(8,128)S(1)} %get-tuple-element.46.turns), custom_call_target="tpu_custom_call" | custom-call | flops 1 | bytes 1 | tf_op jit(solution)/shard_map/send_scaled/pallas_call | solution.py:607
  51.1 0.6 collective-permute-start.6
  51.7 4.6 %collective-permute-start.4 = (f32[1536,128]{1,0:T(8,128)}, f32[1536,128]{1,0:T(8,128)}, u32[]{:S(2)}, u32[]{:S(2)}) collective-permute-start(f32[1536,128]{1,0:T(8,128)} %send_scaled.1.sent_ref), channel_id=1, source_target_pairs={{8,0},{12,4},{16,8},{20,12},{24,16},{28,20},{0,24},{4,28},{9,1},{1... | collective-permute-start | bytes 2359304 | tf_op jit(solution)/shard_map/ppermute | solution.py:34
  56.3 0.0 collective-permute-done.5.arrived_ref.rest_2_
  56.3 0.7 keep.1
  57.0 3.6 %collective-permute-done.6 = f32[2,128]{1,0:T(2,128)S(1)} collective-permute-done((f32[2,128]{1,0:T(2,128)S(1)}, f32[2,128]{1,0:T(2,128)S(1)}, u32[]{:S(2)}, u32[]{:S(2)}) %collective-permute-start.6) | collective-permute-done | bytes 1056 | tf_op jit(solution)/shard_map/ppermute | solution.py:28
  60.6 0.0 collective-permute-done.7.rest_0_
  60.6 5.1 %all-gather = f32[4,2,128]{2,1,0:T(2,128)S(1)} all-gather(f32[1,2,128]{2,1,0:T(2,128)S(1)} %bitcast.42), channel_id=1, replica_groups=mesh['region'=8,'dest'=4] {'dest'}, dimensions={0}, use_global_device_ids=true | all-gather | bytes 5120 | tf_op jit(solution)/shard_map/all_gather | solution.py:627
  65.8 4.7 %base_rows.1.rest_3_ = f32[16392,128]{1,0:T(8,128)S(1)} custom-call(f32[2048]{0:T(1024)S(1)} %bitcast.40, f32[2048]{0:T(1024)S(1)} %bitcast.41, f32[16392,128]{1,0:T(8,128)S(1)} %get-tuple-element.43.rows, f32[16392,128]{1,0:T(8,128)S(1)} %home_rows.1.after_ref.home), custom_call_target="tpu_custom_call" | custom-call | flops 99999997952 | bytes 1 | tf_op jit(solution)/shard_map/base_rows/pallas_call | solution.py:629
  70.5 2.0 %land_first.1.rest_1_ = f32[16392,128]{1,0:T(8,128)S(1)} custom-call(f32[1024]{0:T(1024)S(1)} %bitcast.39, s32[1024]{0:T(1024)S(1)} %bitcast.37, f32[1536,128]{1,0:T(8,128)S(1)} %collective-permute-done.7.rest_0_, f32[1536,128]{1,0:T(8,128)S(1)} %collective-permute-done.8.rest_1_, ...), custom_call_target="tpu_custom_call", output_to_operand_aliasing={{}: (5, {})} | custom-call | flops 99999997952 | bytes 1 | tf_op jit(solution)/shard_map/land_first/pallas_call | solution.py:639
  72.4 1.0 %collective-permute-done.4.rest_0_ = f32[1536,128]{1,0:T(8,128)} collective-permute-done((f32[1536,128]{1,0:T(8,128)}, f32[1536,128]{1,0:T(8,128)}, u32[]{:S(2)}, u32[]{:S(2)}) %collective-permute-start.4) | collective-permute-done | bytes 786464 | tf_op jit(solution)/shard_map/ppermute | solution.py:34
  73.4 5.1 %finish.1 = (f32[2048,1024]{1,0:T(8,128)}, f32[16392,128]{1,0:T(8,128)S(1)}) custom-call(s32[1024]{0:T(1024)S(1)} %bitcast.38, f32[1536,128]{1,0:T(8,128)} %collective-permute-done.4.rest_0_, f32[16392,128]{1,0:T(8,128)S(1)} %land_first.1.rest_1_), custom_call_target="tpu_custom_call", output_to_operand_aliasing={{1}: (2, {})} | custom-call | flops 2097152 | bytes 8388608 | tf_op jit(solution)/shard_map/finish/pallas_call | solution.py:650
  (20 shorter events, 0.1 us)
Async XLA Ops:
  0.0 7.9 %copy-start = (s32[4,1024]{1,0:T(4,128)S(1)}, s32[4,1024]{1,0:T(4,128)}, u32[]{:S(2)}) copy-start(s32[4,1024]{1,0:T(4,128)} %node_out.3) | copy-start | bytes 49156
  0.0 7.9 %copy-start.2 = (s32[4,192]{1,0:T(4,128)S(1)}, s32[4,192]{1,0:T(4,128)}, u32[]{:S(2)}) copy-start(s32[4,192]{1,0:T(4,128)} %send_list.1) | copy-start | bytes 9220
  0.0 7.9 %copy-start.1 = (s32[4,1024]{1,0:T(4,128)S(1)}, s32[4,1024]{1,0:T(4,128)}, u32[]{:S(2)}) copy-start(s32[4,1024]{1,0:T(4,128)} %node_in.1) | copy-start | bytes 49156
  0.0 7.9 %copy-start.3 = (s32[4,192]{1,0:T(4,128)S(1)}, s32[4,192]{1,0:T(4,128)}, u32[]{:S(2)}) copy-start(s32[4,192]{1,0:T(4,128)} %rest_3_.1) | copy-start | bytes 9220
  0.0 10.8 %copy-start.4 = (f32[2048]{0:T(1024)S(1)}, f32[2048]{0:T(1024)}, u32[]{:S(2)}) copy-start(f32[2048]{0:T(1024)} %param.10) | copy-start | bytes 24580
  0.0 10.9 %copy-start.6 = (f32[2048]{0:T(1024)S(1)}, f32[2048]{0:T(1024)}, u32[]{:S(2)}) copy-start(f32[2048]{0:T(1024)} %param.12) | copy-start | bytes 24580
  0.0 10.9 %copy-start.5 = (f32[2048]{0:T(1024)S(1)}, f32[2048]{0:T(1024)}, u32[]{:S(2)}) copy-start(f32[2048]{0:T(1024)} %param.11) | copy-start | bytes 24580
  4.7 5.6 %collective-permute-start.2 = (f32[16,128]{1,0:T(8,128)S(1)}, f32[16,128]{1,0:T(8,128)S(1)}, u32[]{:S(2)}, u32[]{:S(2)}) collective-permute-start(f32[16,128]{1,0:T(8,128)S(1)} %get-tuple-element.38.after_ref), channel_id=1, source_target_pairs={{0,3},{1,2},{2,1},{3,0},{4,7},{5,6},{6,5},{7,4},{8,11},{9,10},{10,... | collective-permute-start | bytes 24584 | tf_op jit(solution)/shard_map/ppermute | solution.py:40
  7.2 3.7 %collective-permute-start.1 = (f32[16,128]{1,0:T(8,128)S(1)}, f32[16,128]{1,0:T(8,128)S(1)}, u32[]{:S(2)}, u32[]{:S(2)}) collective-permute-start(f32[16,128]{1,0:T(8,128)S(1)} %get-tuple-element.38.after_ref), channel_id=1, source_target_pairs={{0,2},{1,3},{2,0},{3,1},{4,6},{5,7},{6,4},{7,5},{8,10},{9,11},{10,... | collective-permute-start | bytes 24584 | tf_op jit(solution)/shard_map/ppermute | solution.py:40
  7.8 3.0 %collective-permute-start = (f32[16,128]{1,0:T(8,128)S(1)}, f32[16,128]{1,0:T(8,128)S(1)}, u32[]{:S(2)}, u32[]{:S(2)}) collective-permute-start(f32[16,128]{1,0:T(8,128)S(1)} %get-tuple-element.38.after_ref), channel_id=1, source_target_pairs={{0,1},{1,0},{2,3},{3,2},{4,5},{5,4},{6,7},{7,6},{8,9},{9,8},{10,11... | collective-permute-start | bytes 24584 | tf_op jit(solution)/shard_map/ppermute | solution.py:40
  10.9 6.4 %collective-permute-start.3 = (f32[16,128]{1,0:T(8,128)S(1)}, f32[16,128]{1,0:T(8,128)S(1)}, u32[]{:S(2)}, u32[]{:S(2)}) collective-permute-start(f32[16,128]{1,0:T(8,128)S(1)} %fusion.1.supply), channel_id=1, source_target_pairs={{0,4},{1,29},{2,10},{3,27},{4,8},{5,1},{6,14},{7,31},{8,12},{9,5},... | collective-permute-start | bytes 24584 | tf_op jit(solution)/shard_map/ppermute | solution.py:28
  17.3 39.0 %collective-permute-start.5 = (f32[1536,128]{1,0:T(8,128)S(1)}, f32[1536,128]{1,0:T(8,128)S(1)}, u32[]{:S(2)}, u32[]{:S(2)}) collective-permute-start(f32[1536,128]{1,0:T(8,128)S(1)} %send_ahead.1.after_ref), channel_id=1, source_target_pairs={{24,0},{28,4},{0,8},{4,12},{8,16},{12,20},{16,24},{20,28},{25,1},{... | collective-permute-start | bytes 2359304 | tf_op jit(solution)/shard_map/ppermute | solution.py:34
  23.3 37.3 %collective-permute-start.8 = (f32[1536,128]{1,0:T(8,128)S(1)}, f32[1536,128]{1,0:T(8,128)S(1)}, u32[]{:S(2)}, u32[]{:S(2)}) collective-permute-start(f32[1536,128]{1,0:T(8,128)S(1)} %get-tuple-element.57), channel_id=1, source_target_pairs={{4,0},{8,4},{12,8},{16,12},{20,16},{24,20},{28,24},{0,28},{5,1},{9... | collective-permute-start | bytes 2359304 | tf_op jit(solution)/shard_map/ppermute | solution.py:34
  26.0 34.6 %collective-permute-start.7 = (f32[1536,128]{1,0:T(8,128)S(1)}, f32[1536,128]{1,0:T(8,128)S(1)}, u32[]{:S(2)}, u32[]{:S(2)}) collective-permute-start(f32[1536,128]{1,0:T(8,128)S(1)} %get-tuple-element.48.after_ref), channel_id=1, source_target_pairs={{28,0},{0,4},{4,8},{8,12},{12,16},{16,20},{20,24},{24,28},{29,1},{... | collective-permute-start | bytes 2359304 | tf_op jit(solution)/shard_map/ppermute | solution.py:34
  51.1 9.5 %collective-permute-start.6 = (f32[2,128]{1,0:T(2,128)S(1)}, f32[2,128]{1,0:T(2,128)S(1)}, u32[]{:S(2)}, u32[]{:S(2)}) collective-permute-start(f32[2,128]{1,0:T(2,128)S(1)} %get-tuple-element.56), channel_id=1, source_target_pairs={{0,4},{1,29},{2,10},{3,27},{4,8},{5,1},{6,14},{7,31},{8,12},{9,5},... | collective-permute-start | bytes 3080 | tf_op jit(solution)/shard_map/ppermute | solution.py:28
  51.7 21.7 %collective-permute-start.4 = (f32[1536,128]{1,0:T(8,128)}, f32[1536,128]{1,0:T(8,128)}, u32[]{:S(2)}, u32[]{:S(2)}) collective-permute-start(f32[1536,128]{1,0:T(8,128)} %send_scaled.1.sent_ref), channel_id=1, source_target_pairs={{8,0},{12,4},{16,8},{20,12},{24,16},{28,20},{0,24},{4,28},{9,1},{1... | collective-permute-start | bytes 2359304 | tf_op jit(solution)/shard_map/ppermute | solution.py:34

commit v9 on v8

--- a/solution.py
+++ b/solution.py
@@ -230,7 +230,7 @@
     return tree_sum(parts)
 
 
-def scale_kernel(sizes, fraction, rows, after_ref, scaled):
+def scale_kernel(sizes, fraction, rows, sent_ref, supply_ref, scaled):
     cells, nodes, branches, cap, sub = sizes
 
     def body(step, carry):
@@ -322,8 +322,7 @@
 
 
 def theta_kernel(
-    sizes, regions, commodities, supply, shared, node_out, send_list, after_ref,
-    theta_out, slot_theta,
+    sizes, regions, commodities, supply, shared, node_out, send_list, theta_out, slot_theta
 ):
     cells, nodes, branches, cap, sub = sizes
     per_outlet = nodes // LANES
@@ -542,16 +541,15 @@
         cost_estimate=cost(1, 1),
         name="send_ahead",
     )(weights, in_cell, send_node, send_outlet, rows, turns)
-    ahead, supply_there = lax.optimization_barrier((ahead, supply_there))
     scaled = pl.pallas_call(
         functools.partial(scale_kernel, sizes),
-        in_specs=[SMEM_WHOLE, VMEM_WHOLE, ANYWHERE],
+        in_specs=[SMEM_WHOLE, VMEM_WHOLE, ANYWHERE, ANYWHERE],
         out_specs=VMEM_WHOLE,
         out_shape=rows_shape,
         compiler_params=params(4),
         cost_estimate=cost(1, 1),
         name="scale_rows",
-    )(fraction.reshape(-1), rows, ahead)
+    )(fraction.reshape(-1), rows, ahead, supply_there)
     near = pl.pallas_call(
         functools.partial(send_kernel, sizes, (0, 1), None),
         in_specs=[SMEM_WHOLE] * 3 + [VMEM_WHOLE] * 2,
@@ -581,18 +579,9 @@
 
     joined = jnp.concatenate([demand, supply_there])
     shared = lax.all_gather(joined, "dest", axis=0, tiled=True)
-    home = pl.pallas_call(
-        functools.partial(home_kernel, sizes),
-        in_specs=[SMEM_WHOLE] * 2 + [VMEM_WHOLE] * 2 + [ANYWHERE],
-        out_specs=VMEM_WHOLE,
-        out_shape=rows_shape,
-        compiler_params=params(4),
-        cost_estimate=cost(1, 1),
-        name="home_rows",
-    )(source_node, source_outlet, turns, flow, joined)
     theta, slot_theta = pl.pallas_call(
         functools.partial(theta_kernel, sizes, regions, commodities),
-        in_specs=[VMEM_WHOLE] * 4 + [ANYWHERE],
+        in_specs=[VMEM_WHOLE] * 4,
         out_specs=[VMEM_WHOLE] * 2,
         out_shape=[
             jax.ShapeDtypeStruct((nodes // LANES, LANES), F32),
@@ -601,7 +590,7 @@
         compiler_params=params(8),
         cost_estimate=cost(1, 1),
         name="theta",
-    )(supply, shared, node_out, send_list, home)
+    )(supply, shared, node_out, send_list)
     theta_there = to_neighbours(slot_theta)
 
     (behind,) = pl.pallas_call(
@@ -613,28 +602,37 @@
         cost_estimate=cost(1, 1),
         name="send_scaled",
     )(theta.reshape(-1), send_node, send_outlet, flow, turns)
+    home = pl.pallas_call(
+        functools.partial(home_kernel, sizes),
+        in_specs=[SMEM_WHOLE] * 2 + [VMEM_WHOLE] * 2 + [ANYWHERE],
+        out_specs=VMEM_WHOLE,
+        out_shape=rows_shape,
+        compiler_params=params(4),
+        cost_estimate=cost(1, 1),
+        name="home_rows",
+    )(source_node, source_outlet, turns, flow, behind)
     keep, home_theta = pl.pallas_call(
         functools.partial(keep_kernel, sizes),
         in_specs=[VMEM_WHOLE] * 4 + [ANYWHERE] * 2,
         out_specs=[VMEM_WHOLE] * 2,
         out_shape=[jax.ShapeDtypeStruct(per_cell, F32)] * 2,
         compiler_params=params(8),
-        cost_estimate=cost(100000000, 1),
+        cost_estimate=cost(10000000, 1),
         name="keep",
     )(theta, node_in, node_out, fraction, behind, arrived[2])
-    keep, theta_there, *arrived = lax.optimization_barrier((keep, theta_there, *arrived))
-    last = shifted(behind, "region", SHIFTS[3])
-    scale = lax.all_gather(theta_there, "dest", axis=0, tiled=True)[: list_shape[0]]
-
     base = pl.pallas_call(
         functools.partial(base_kernel, sizes),
         in_specs=[SMEM_WHOLE] * 2 + [VMEM_WHOLE] * 2,
         out_specs=VMEM_WHOLE,
         out_shape=rows_shape,
         compiler_params=params(4),
-        cost_estimate=pl.CostEstimate(flops=100000000000, bytes_accessed=1, transcendentals=0),
+        cost_estimate=cost(10000000, 1),
         name="base_rows",
     )(keep.reshape(-1), home_theta.reshape(-1), rows, home)
+
+    base, theta_there, *arrived = lax.optimization_barrier((base, theta_there, *arrived))
+    last = shifted(behind, "region", SHIFTS[3])
+    scale = lax.all_gather(theta_there, "dest", axis=0, tiled=True)[: list_shape[0]]
 
     base = pl.pallas_call(
         functools.partial(land_kernel, sizes, (0, 1, 2)),
@@ -643,7 +641,7 @@
         out_shape=rows_shape,
         input_output_aliases={5: 0},
         compiler_params=params(4),
-        cost_estimate=pl.CostEstimate(flops=100000000000, bytes_accessed=1, transcendentals=0),
+        cost_estimate=cost(100000000000, 1),
         name="land_first",
     )(scale.reshape(-1), land, *arrived, base)
 

time: 78.6 us -> 78.9 us (level)
  the two profiles are of different devices: /device:TPU:0 before, /device:TPU:25 now
where the time goes in v9:
time: 78.9 us; the launch traced here: 78.7 us
  Pallas kernels  45.9 us (58%)
  blocking collectives  19.1 us (24%)
  starting transfers between devices  11 us (14%)
  waiting for transfers between devices  2.43 us (3%)
    all_gather x1, blocking collectives, on_device(): lax.all_gather(theta_there, 'dest', axis=0, tiled=True)[:list_shape[0]]  14.7 us
    pallas_call x1, Pallas kernels, on_device(): pl.pallas_call(functools.partial(node_flow_kernel, sizes), in_specs=[SMEM...  10.1 us
    ppermute x4, starting transfers between devices, shifted(): return lax.ppermute(block, axis, route)  6.02 us
    pallas_call x1, Pallas kernels, on_device(): pl.pallas_call(functools.partial(home_kernel, sizes), in_specs=[SMEM_WHOL...  5.38 us
    pallas_call x1, Pallas kernels, on_device(): pl.pallas_call(functools.partial(base_kernel, sizes), in_specs=[SMEM_WHOL...  4.72 us
    pallas_call x1, Pallas kernels, on_device(): pl.pallas_call(functools.partial(cell_sum_kernel, chunk, sub), in_specs=[...  4.69 us
    pallas_call x1, Pallas kernels, on_device(): pl.pallas_call(functools.partial(finish_kernel, sizes, (3,), chunk), in_s...  4.52 us
    all_gather x1, blocking collectives, on_device(): shared = lax.all_gather(joined, 'dest', axis=0, tiled=True)  4.48 us
  transfers between devices with their start and end apart: 9, of which 1 were waited for; matrix products, arithmetic and copies ran while one was open for 0% of the time, Pallas kernels for 47%

profile of v9, /device:TPU:25, one launch (start us, length us, event | category | flops | bytes accessed | tf_op | source)
XLA Modules:
  0.0 78.7 jit_solution(932367317961460092)
XLA Ops:
  0.0 4.7 %cell_sum.1 = (f32[16,128]{1,0:T(8,128)S(1)}, f32[16392,128]{1,0:T(8,128)S(1)}) custom-call(f32[2048,1024]{1,0:T(8,128)} %x_hbm.2), custom_call_target="tpu_custom_call" | custom-call | flops 2097152 | bytes 8388608 | tf_op jit(solution)/shard_map/cell_sum/pallas_call | solution.py:483
  4.7 1.8 %collective-permute-start.2 = (f32[16,128]{1,0:T(8,128)S(1)}, f32[16,128]{1,0:T(8,128)S(1)}, u32[]{:S(2)}, u32[]{:S(2)}) collective-permute-start(f32[16,128]{1,0:T(8,128)S(1)} %get-tuple-element.36.after_ref), channel_id=1, source_target_pairs={{0,3},{1,2},{2,1},{3,0},{4,7},{5,6},{6,5},{7,4},{8,11},{9,10},{10,... | collective-permute-start | bytes 24584 | tf_op jit(solution)/shard_map/ppermute | solution.py:40
  6.6 0.3 collective-permute-start.1
  6.8 0.2 collective-permute-start
  7.1 2.5 %turn_rows.1 = (s32[8192,128]{1,0:T(8,128)S(1)}, s32[32,128]{1,0:T(8,128)S(1)}, s32[8,128]{1,0:T(8,128)S(1)}, s32[8,128]{1,0:T(8,128)S(1)}, s32[8,128]{1,0:T(8,1...) custom-call(s32[1024,1024]{1,0:T(8,128)} %x_hbm.3, f32[16,128]{1,0:T(8,128)S(1)} %get-tuple-element.36.after_ref, ...), custom_call_target="tpu_custom_call" | custom-call | bytes 4194304 | tf_op jit(solution)/shard_map/turn_rows/pallas_call | solution.py:503
  9.6 0.0 collective-permute-done.2
  9.6 0.0 collective-permute-done.1
  9.6 0.0 collective-permute-done
  9.7 1.2 %collective-permute-start.3 = (f32[16,128]{1,0:T(8,128)S(1)}, f32[16,128]{1,0:T(8,128)S(1)}, u32[]{:S(2)}, u32[]{:S(2)}) collective-permute-start(f32[16,128]{1,0:T(8,128)S(1)} %fusion.1.supply), channel_id=1, source_target_pairs={{0,4},{1,29},{2,10},{3,27},{4,8},{5,1},{6,14},{7,31},{8,12},{9,5},... | collective-permute-start | bytes 24584 | tf_op jit(solution)/shard_map/ppermute | solution.py:28
  10.9 2.6 %send_ahead.1.sent_ref = f32[1536,128]{1,0:T(8,128)S(1)} custom-call(f32[2176]{0:T(1024)S(1)} %concatenate.6.fraction, s32[4096]{0:T(1024)S(1)} %bitcast.23, s32[1024]{0:T(1024)S(1)} %bitcast.28, s32[1024]{0:T(1024)S(1)} %bitcast.31, f32[16392,128]{1,0:T(8,128)S(1)} %get-tuple-element.41.rows, s32[8192,128]{1,0:T(8,128)S(1)} %get-tuple-element.44.turns), custom_call_target="tpu_custom_call" | custom-call | flops 1 | bytes 1 | tf_op jit(solution)/shard_map/send_ahead/pallas_call | solution.py:535
  13.5 3.1 %collective-permute-start.5 = (f32[1536,128]{1,0:T(8,128)S(1)}, f32[1536,128]{1,0:T(8,128)S(1)}, u32[]{:S(2)}, u32[]{:S(2)}) collective-permute-start(f32[1536,128]{1,0:T(8,128)S(1)} %send_ahead.1.sent_ref), channel_id=1, source_target_pairs={{24,0},{28,4},{0,8},{4,12},{8,16},{12,20},{16,24},{20,28},{25,1},{... | collective-permute-start | bytes 2359304 | tf_op jit(solution)/shard_map/ppermute | solution.py:34
  16.6 0.0 collective-permute-done.3.supply_ref
  16.6 2.5 %scale_rows.1.rows.scaled = f32[16392,128]{1,0:T(8,128)S(1)} custom-call(f32[2048]{0:T(1024)S(1)} %bitcast.27, f32[16392,128]{1,0:T(8,128)S(1)} %get-tuple-element.41.rows, f32[1536,128]{1,0:T(8,128)S(1)} %send_ahead.1.sent_ref, f32[16,128]{1,0:T(8,128)S(1)} %collective-permute-done.3.supply_ref), custom_call_target="tpu_custom_call" | custom-call | flops 1 | bytes 1 | tf_op jit(solution)/shard_map/scale_rows/pallas_call | solution.py:544
  19.1 3.5 %send_near.1 = (f32[1536,128]{1,0:T(8,128)S(1)}, f32[1536,128]{1,0:T(8,128)S(1)}) custom-call(s32[4096]{0:T(1024)S(1)} %bitcast.24, s32[1024]{0:T(1024)S(1)} %bitcast.29, s32[1024]{0:T(1024)S(1)} %bitcast.32, f32[16392,128]{1,0:T(8,128)S(1)} %scale_rows.1.rows.scaled, s32[8192,128]{1,0:T(8,128)S(1)} %get-tuple-element.44.turns), custom_call_target="tpu_custom_call" | custom-call | flops 1 | bytes 1 | tf_op jit(solution)/shard_map/send_near/pallas_call | solution.py:553
  22.7 0.1 collective-permute-start.8
  22.7 1.5 %collective-permute-start.7 = (f32[1536,128]{1,0:T(8,128)S(1)}, f32[1536,128]{1,0:T(8,128)S(1)}, u32[]{:S(2)}, u32[]{:S(2)}) collective-permute-start(f32[1536,128]{1,0:T(8,128)S(1)} %get-tuple-element.45.after_ref), channel_id=1, source_target_pairs={{28,0},{0,4},{4,8},{8,12},{12,16},{16,20},{20,24},{24,28},{29,1},{... | collective-permute-start | bytes 2359304 | tf_op jit(solution)/shard_map/ppermute | solution.py:34
  24.2 10.1 %node_flow.1 = (f32[8192,128]{1,0:T(8,128)S(1)}, f32[32,128]{1,0:T(8,128)S(1)}) custom-call(s32[4096]{0:T(1024)S(1)} %bitcast.25, f32[16392,128]{1,0:T(8,128)S(1)} %scale_rows.1.rows.scaled, s32[8192,128]{1,0:T(8,128)S(1)} %get-tuple-element.44.turns, f32[1536,128]{1,0:T(8,128)S(1)} %get-tuple-element.45.after_ref), custom_call_target="tpu_custom_call" | custom-call | flops 1 | bytes 1 | tf_op jit(solution)/shard_map/node_flow/pallas_call | solution.py:566
  34.4 4.5 %all_gather.6.shared = f32[192,128]{1,0:T(8,128)S(1)} all-gather(f32[48,128]{1,0:T(8,128)S(1)} %pad_maximum_fusion), channel_id=1, replica_groups=mesh['region'=8,'dest'=4] {'dest'}, dimensions={0}, use_global_device_ids=true | all-gather | bytes 122880 | tf_op jit(solution)/shard_map/all_gather | solution.py:581
  38.8 1.4 %theta.1 = (f32[8,128]{1,0:T(8,128)S(1)}, f32[2,128]{1,0:T(2,128)S(1)}) custom-call(f32[16,128]{1,0:T(8,128)S(1)} %fusion.1.supply, f32[192,128]{1,0:T(8,128)S(1)} %all_gather.6.shared, s32[4,1024]{1,0:T(4,128)S(1)} %copy-done, s32[4,192]{1,0:T(4,128)S(1)} %copy-done.2), custom_call_target="tpu_custom_call" | custom-call | flops 1 | bytes 1 | tf_op jit(solution)/shard_map/theta/pallas_call | solution.py:582
  40.2 1.5 %collective-permute-start.6 = (f32[2,128]{1,0:T(2,128)S(1)}, f32[2,128]{1,0:T(2,128)S(1)}, u32[]{:S(2)}, u32[]{:S(2)}) collective-permute-start(f32[2,128]{1,0:T(2,128)S(1)} %get-tuple-element.53), channel_id=1, source_target_pairs={{0,4},{1,29},{2,10},{3,27},{4,8},{5,1},{6,14},{7,31},{8,12},{9,5},... | collective-permute-start | bytes 3080 | tf_op jit(solution)/shard_map/ppermute | solution.py:28
  41.7 1.2 %send_scaled.1.sent_ref.after_ref = f32[1536,128]{1,0:T(8,128)S(1)} custom-call(f32[1024]{0:T(1024)S(1)} %bitcast.34, s32[1024]{0:T(1024)S(1)} %bitcast.30, s32[1024]{0:T(1024)S(1)} %bitcast.33, f32[8192,128]{1,0:T(8,128)S(1)} %get-tuple-element.48.flow, s32[8192,128]{1,0:T(8,128)S(1)} %get-tuple-element.44.turns), custom_call_target="tpu_custom_call" | custom-call | flops 1 | bytes 1 | tf_op jit(solution)/shard_map/send_scaled/pallas_call | solution.py:596
  43.0 1.4 %collective-permute-start.4 = (f32[1536,128]{1,0:T(8,128)S(1)}, f32[1536,128]{1,0:T(8,128)S(1)}, u32[]{:S(2)}, u32[]{:S(2)}) collective-permute-start(f32[1536,128]{1,0:T(8,128)S(1)} %send_scaled.1.sent_ref.after_ref), channel_id=1, source_target_pairs={{8,0},{12,4},{16,8},{20,12},{24,16},{28,20},{0,24},{4,28},{9,1},{1... | collective-permute-start | bytes 2359304 | tf_op jit(solution)/shard_map/ppermute | solution.py:34
  44.4 5.4 %home_rows.1.home = f32[16392,128]{1,0:T(8,128)S(1)} custom-call(s32[2048]{0:T(1024)S(1)} %bitcast.35, s32[2048]{0:T(1024)S(1)} %bitcast.36, s32[8192,128]{1,0:T(8,128)S(1)} %get-tuple-element.44.turns, f32[8192,128]{1,0:T(8,128)S(1)} %get-tuple-element.48.flow, f32[1536,128]{1,0:T(8,128)S(1)} %send_scaled.1.sent_ref.after_ref), custom_call_target="tpu_custom_call" | custom-call | flops 1 | bytes 1 | tf_op jit(solution)/shard_map/home_rows/pallas_call | solution.py:605
  49.8 0.7 keep.1
  50.4 4.7 %base_rows.1.rest_3_ = f32[16392,128]{1,0:T(8,128)S(1)} custom-call(f32[2048]{0:T(1024)S(1)} %bitcast.37, f32[2048]{0:T(1024)S(1)} %bitcast.38, f32[16392,128]{1,0:T(8,128)S(1)} %get-tuple-element.41.rows, f32[16392,128]{1,0:T(8,128)S(1)} %home_rows.1.home), custom_call_target="tpu_custom_call" | custom-call | flops 10000000 | bytes 1 | tf_op jit(solution)/shard_map/base_rows/pallas_call | solution.py:623
  55.2 2.4 %collective-permute-done.6 = f32[2,128]{1,0:T(2,128)S(1)} collective-permute-done((f32[2,128]{1,0:T(2,128)S(1)}, f32[2,128]{1,0:T(2,128)S(1)}, u32[]{:S(2)}, u32[]{:S(2)}) %collective-permute-start.6) | collective-permute-done | bytes 1056 | tf_op jit(solution)/shard_map/ppermute | solution.py:28
  57.6 0.0 collective-permute-done.8.rest_1_
  57.6 0.0 collective-permute-done.7.rest_0_
  57.6 14.7 %all-gather = f32[4,2,128]{2,1,0:T(2,128)S(1)} all-gather(f32[1,2,128]{2,1,0:T(2,128)S(1)} %bitcast.42), channel_id=1, replica_groups=mesh['region'=8,'dest'=4] {'dest'}, dimensions={0}, use_global_device_ids=true | all-gather | bytes 5120 | tf_op jit(solution)/shard_map/all_gather | solution.py:635
  72.2 1.9 %land_first.1.rest_1_ = f32[16392,128]{1,0:T(8,128)S(1)} custom-call(f32[1024]{0:T(1024)S(1)} %bitcast.41, s32[1024]{0:T(1024)S(1)} %bitcast.39, f32[1536,128]{1,0:T(8,128)S(1)} %collective-permute-done.7.rest_0_, f32[1536,128]{1,0:T(8,128)S(1)} %collective-permute-done.8.rest_1_, ...), custom_call_target="tpu_custom_call", output_to_operand_aliasing={{}: (5, {})} | custom-call | flops 99999997952 | bytes 1 | tf_op jit(solution)/shard_map/land_first/pallas_call | solution.py:637
  74.2 0.0 collective-permute-done.4.rest_0_
  74.2 4.5 %finish.1 = (f32[2048,1024]{1,0:T(8,128)}, f32[16392,128]{1,0:T(8,128)S(1)}) custom-call(s32[1024]{0:T(1024)S(1)} %bitcast.40, f32[1536,128]{1,0:T(8,128)S(1)} %collective-permute-done.4.rest_0_, f32[16392,128]{1,0:T(8,128)S(1)} %land_first.1.rest_1_), custom_call_target="tpu_custom_call", output_to_operand_aliasing={{1}: (2, {})} | custom-call | flops 2097152 | bytes 8388608 | tf_op jit(solution)/shard_map/finish/pallas_call | solution.py:648
  (19 shorter events, 0.1 us)
Async XLA Ops:
  0.0 7.1 %copy-start = (s32[4,1024]{1,0:T(4,128)S(1)}, s32[4,1024]{1,0:T(4,128)}, u32[]{:S(2)}) copy-start(s32[4,1024]{1,0:T(4,128)} %node_out.3) | copy-start | bytes 49156
  0.0 7.1 %copy-start.2 = (s32[4,192]{1,0:T(4,128)S(1)}, s32[4,192]{1,0:T(4,128)}, u32[]{:S(2)}) copy-start(s32[4,192]{1,0:T(4,128)} %send_list.1) | copy-start | bytes 9220
  0.0 7.1 %copy-start.1 = (s32[4,1024]{1,0:T(4,128)S(1)}, s32[4,1024]{1,0:T(4,128)}, u32[]{:S(2)}) copy-start(s32[4,1024]{1,0:T(4,128)} %node_in.1) | copy-start | bytes 49156
  0.0 7.1 %copy-start.3 = (s32[4,192]{1,0:T(4,128)S(1)}, s32[4,192]{1,0:T(4,128)}, u32[]{:S(2)}) copy-start(s32[4,192]{1,0:T(4,128)} %rest_3_.1) | copy-start | bytes 9220
  0.0 9.6 %copy-start.4 = (f32[2048]{0:T(1024)S(1)}, f32[2048]{0:T(1024)}, u32[]{:S(2)}) copy-start(f32[2048]{0:T(1024)} %param.10) | copy-start | bytes 24580
  0.0 9.6 %copy-start.6 = (f32[2048]{0:T(1024)S(1)}, f32[2048]{0:T(1024)}, u32[]{:S(2)}) copy-start(f32[2048]{0:T(1024)} %param.12) | copy-start | bytes 24580
  0.0 9.6 %copy-start.5 = (f32[2048]{0:T(1024)S(1)}, f32[2048]{0:T(1024)}, u32[]{:S(2)}) copy-start(f32[2048]{0:T(1024)} %param.11) | copy-start | bytes 24580
  4.7 4.8 %collective-permute-start.2 = (f32[16,128]{1,0:T(8,128)S(1)}, f32[16,128]{1,0:T(8,128)S(1)}, u32[]{:S(2)}, u32[]{:S(2)}) collective-permute-start(f32[16,128]{1,0:T(8,128)S(1)} %get-tuple-element.36.after_ref), channel_id=1, source_target_pairs={{0,3},{1,2},{2,1},{3,0},{4,7},{5,6},{6,5},{7,4},{8,11},{9,10},{10,... | collective-permute-start | bytes 24584 | tf_op jit(solution)/shard_map/ppermute | solution.py:40
  6.6 3.0 %collective-permute-start.1 = (f32[16,128]{1,0:T(8,128)S(1)}, f32[16,128]{1,0:T(8,128)S(1)}, u32[]{:S(2)}, u32[]{:S(2)}) collective-permute-start(f32[16,128]{1,0:T(8,128)S(1)} %get-tuple-element.36.after_ref), channel_id=1, source_target_pairs={{0,2},{1,3},{2,0},{3,1},{4,6},{5,7},{6,4},{7,5},{8,10},{9,11},{10,... | collective-permute-start | bytes 24584 | tf_op jit(solution)/shard_map/ppermute | solution.py:40
  6.8 2.8 %collective-permute-start = (f32[16,128]{1,0:T(8,128)S(1)}, f32[16,128]{1,0:T(8,128)S(1)}, u32[]{:S(2)}, u32[]{:S(2)}) collective-permute-start(f32[16,128]{1,0:T(8,128)S(1)} %get-tuple-element.36.after_ref), channel_id=1, source_target_pairs={{0,1},{1,0},{2,3},{3,2},{4,5},{5,4},{6,7},{7,6},{8,9},{9,8},{10,11... | collective-permute-start | bytes 24584 | tf_op jit(solution)/shard_map/ppermute | solution.py:40
  9.7 7.0 %collective-permute-start.3 = (f32[16,128]{1,0:T(8,128)S(1)}, f32[16,128]{1,0:T(8,128)S(1)}, u32[]{:S(2)}, u32[]{:S(2)}) collective-permute-start(f32[16,128]{1,0:T(8,128)S(1)} %fusion.1.supply), channel_id=1, source_target_pairs={{0,4},{1,29},{2,10},{3,27},{4,8},{5,1},{6,14},{7,31},{8,12},{9,5},... | collective-permute-start | bytes 24584 | tf_op jit(solution)/shard_map/ppermute | solution.py:28
  13.5 36.3 %collective-permute-start.5 = (f32[1536,128]{1,0:T(8,128)S(1)}, f32[1536,128]{1,0:T(8,128)S(1)}, u32[]{:S(2)}, u32[]{:S(2)}) collective-permute-start(f32[1536,128]{1,0:T(8,128)S(1)} %send_ahead.1.sent_ref), channel_id=1, source_target_pairs={{24,0},{28,4},{0,8},{4,12},{8,16},{12,20},{16,24},{20,28},{25,1},{... | collective-permute-start | bytes 2359304 | tf_op jit(solution)/shard_map/ppermute | solution.py:34
  22.7 34.9 %collective-permute-start.8 = (f32[1536,128]{1,0:T(8,128)S(1)}, f32[1536,128]{1,0:T(8,128)S(1)}, u32[]{:S(2)}, u32[]{:S(2)}) collective-permute-start(f32[1536,128]{1,0:T(8,128)S(1)} %get-tuple-element.54), channel_id=1, source_target_pairs={{4,0},{8,4},{12,8},{16,12},{20,16},{24,20},{28,24},{0,28},{5,1},{9... | collective-permute-start | bytes 2359304 | tf_op jit(solution)/shard_map/ppermute | solution.py:34
  22.7 34.8 %collective-permute-start.7 = (f32[1536,128]{1,0:T(8,128)S(1)}, f32[1536,128]{1,0:T(8,128)S(1)}, u32[]{:S(2)}, u32[]{:S(2)}) collective-permute-start(f32[1536,128]{1,0:T(8,128)S(1)} %get-tuple-element.45.after_ref), channel_id=1, source_target_pairs={{28,0},{0,4},{4,8},{8,12},{12,16},{16,20},{20,24},{24,28},{29,1},{... | collective-permute-start | bytes 2359304 | tf_op jit(solution)/shard_map/ppermute | solution.py:34
  40.2 17.3 %collective-permute-start.6 = (f32[2,128]{1,0:T(2,128)S(1)}, f32[2,128]{1,0:T(2,128)S(1)}, u32[]{:S(2)}, u32[]{:S(2)}) collective-permute-start(f32[2,128]{1,0:T(2,128)S(1)} %get-tuple-element.53), channel_id=1, source_target_pairs={{0,4},{1,29},{2,10},{3,27},{4,8},{5,1},{6,14},{7,31},{8,12},{9,5},... | collective-permute-start | bytes 3080 | tf_op jit(solution)/shard_map/ppermute | solution.py:28
  43.0 31.2 %collective-permute-start.4 = (f32[1536,128]{1,0:T(8,128)S(1)}, f32[1536,128]{1,0:T(8,128)S(1)}, u32[]{:S(2)}, u32[]{:S(2)}) collective-permute-start(f32[1536,128]{1,0:T(8,128)S(1)} %send_scaled.1.sent_ref.after_ref), channel_id=1, source_target_pairs={{8,0},{12,4},{16,8},{20,12},{24,16},{28,20},{0,24},{4,28},{9,1},{1... | collective-permute-start | bytes 2359304 | tf_op jit(solution)/shard_map/ppermute | solution.py:34

commit v10 on v9

--- a/solution.py
+++ b/solution.py
@@ -201,7 +201,10 @@
             return carry
 
         lax.fori_loop(0, chunk // 16, body, 0)
-    sum_ref[...] = lane_sums(partial[...])
+        done = number + 1
+        if done % 4 == 0:
+            part = lane_sums(partial[(done - 4) * chunk : done * chunk, :])
+            sum_ref[(done - 4) * chunk // LANES : done * chunk // LANES, :] = part
 
 
 def turn_rows_kernel(sizes, chunk, x_hbm, after_ref, *rest):
@@ -353,8 +356,11 @@
         ratio = room / jnp.maximum(demand[j * per_outlet : (j + 1) * per_outlet, :], room)
         tall = jnp.minimum(tall, jnp.where(stacked(outs) >= 0, ratio, 1.0))
     theta_out[...] = tall
-    slots = send_list[pl.ds(lax.axis_index("dest") % 4, 1), :]
-    put_row(slot_theta, 0, look_up(tall, jnp.where(slots >= 0, slots % nodes, 0)), 0.0)
+    per_side = padded(cap) // LANES
+    for side in range(3):
+        slots = send_list[side : side + 1, :]
+        there = look_up(tall, jnp.where(slots >= 0, slots % nodes, 0))
+        put_row(slot_theta, side * per_side, there, 0.0)
 
 
 def keep_kernel(
@@ -374,7 +380,7 @@
     home_theta[...] = into
 
 
-def home_kernel(sizes, source, outlet, turns, flow, after_ref, home):
+def home_kernel(sizes, source, outlet, turns, flow, sent_ref, theta_ref, home):
     cells, nodes, branches, cap, sub = sizes
     batch = 8
 
@@ -585,13 +591,17 @@
         out_specs=[VMEM_WHOLE] * 2,
         out_shape=[
             jax.ShapeDtypeStruct((nodes // LANES, LANES), F32),
-            jax.ShapeDtypeStruct((padded(cap) // LANES, LANES), F32),
+            jax.ShapeDtypeStruct((3 * padded(cap) // LANES, LANES), F32),
         ],
         compiler_params=params(8),
         cost_estimate=cost(1, 1),
         name="theta",
     )(supply, shared, node_out, send_list)
-    theta_there = to_neighbours(slot_theta)
+    per_side = padded(cap) // LANES
+    theta_there = [
+        shifted(slot_theta[side * per_side : (side + 1) * per_side], "region", SHIFTS[side])
+        for side in range(3)
+    ]
 
     (behind,) = pl.pallas_call(
         functools.partial(scaled_send_kernel, sizes, 3),
@@ -604,13 +614,13 @@
     )(theta.reshape(-1), send_node, send_outlet, flow, turns)
     home = pl.pallas_call(
         functools.partial(home_kernel, sizes),
-        in_specs=[SMEM_WHOLE] * 2 + [VMEM_WHOLE] * 2 + [ANYWHERE],
+        in_specs=[SMEM_WHOLE] * 2 + [VMEM_WHOLE] * 2 + [ANYWHERE] * 2,
         out_specs=VMEM_WHOLE,
         out_shape=rows_shape,
         compiler_params=params(4),
         cost_estimate=cost(1, 1),
         name="home_rows",
-    )(source_node, source_outlet, turns, flow, behind)
+    )(source_node, source_outlet, turns, flow, behind, theta_there[2])
     keep, home_theta = pl.pallas_call(
         functools.partial(keep_kernel, sizes),
         in_specs=[VMEM_WHOLE] * 4 + [ANYWHERE] * 2,
@@ -632,7 +642,7 @@
 
     base, theta_there, *arrived = lax.optimization_barrier((base, theta_there, *arrived))
     last = shifted(behind, "region", SHIFTS[3])
-    scale = lax.all_gather(theta_there, "dest", axis=0, tiled=True)[: list_shape[0]]
+    scale = jnp.concatenate(theta_there)
 
     base = pl.pallas_call(
         functools.partial(land_kernel, sizes, (0, 1, 2)),

time: 78.9 us -> 79.5 us (level)
  the two profiles are of different devices: /device:TPU:25 before, /device:TPU:0 now
where the time goes in v10:
time: 79.5 us; the launch traced here: 79.4 us
  Pallas kernels  47 us (59%)
  starting transfers between devices  16.6 us (21%)
  waiting for transfers between devices  9.5 us (12%)
  blocking collectives  5.97 us (8%)
    ppermute x7, starting transfers between devices, shifted(): return lax.ppermute(block, axis, route)  11.9 us
    pallas_call x1, Pallas kernels, on_device(): pl.pallas_call(functools.partial(node_flow_kernel, sizes), in_specs=[SMEM...  10.1 us
    ppermute x7, waiting for transfers between devices, shifted(): return lax.ppermute(block, axis, route)  8.5 us
    all_gather x1, blocking collectives, on_device(): shared = lax.all_gather(joined, 'dest', axis=0, tiled=True)  5.97 us
    pallas_call x1, Pallas kernels, on_device(): pl.pallas_call(functools.partial(cell_sum_kernel, chunk, sub), in_specs=[...  5.72 us
    pallas_call x1, Pallas kernels, on_device(): pl.pallas_call(functools.partial(home_kernel, sizes), in_specs=[SMEM_WHOL...  5.38 us
    pallas_call x1, Pallas kernels, on_device(): pl.pallas_call(functools.partial(base_kernel, sizes), in_specs=[SMEM_WHOL...  4.72 us
    pallas_call x1, Pallas kernels, on_device(): pl.pallas_call(functools.partial(finish_kernel, sizes, (3,), chunk), in_s...  4.52 us
  transfers between devices with their start and end apart: 11, of which 4 were waited for; matrix products, arithmetic and copies ran while one was open for 0% of the time, Pallas kernels for 46%

profile of v10, /device:TPU:0, one launch (start us, length us, event | category | flops | bytes accessed | tf_op | source)
XLA Modules:
  0.0 79.4 jit_solution(14661584265107238125)
XLA Ops:
  0.0 5.7 %cell_sum.1 = (f32[16,128]{1,0:T(8,128)S(1)}, f32[16392,128]{1,0:T(8,128)S(1)}) custom-call(f32[2048,1024]{1,0:T(8,128)} %x_hbm.2), custom_call_target="tpu_custom_call" | custom-call | flops 2097152 | bytes 8388608 | tf_op jit(solution)/shard_map/cell_sum/pallas_call | solution.py:489
  5.8 2.4 %collective-permute-start.2 = (f32[16,128]{1,0:T(8,128)S(1)}, f32[16,128]{1,0:T(8,128)S(1)}, u32[]{:S(2)}, u32[]{:S(2)}) collective-permute-start(f32[16,128]{1,0:T(8,128)S(1)} %get-tuple-element.38.after_ref), channel_id=1, source_target_pairs={{0,3},{1,2},{2,1},{3,0},{4,7},{5,6},{6,5},{7,4},{8,11},{9,10},{10,... | collective-permute-start | bytes 24584 | tf_op jit(solution)/shard_map/ppermute | solution.py:40
  8.2 0.6 collective-permute-start.1
  8.8 0.0 collective-permute-start
  8.9 2.5 %turn_rows.1 = (s32[8192,128]{1,0:T(8,128)S(1)}, s32[32,128]{1,0:T(8,128)S(1)}, s32[8,128]{1,0:T(8,128)S(1)}, s32[8,128]{1,0:T(8,128)S(1)}, s32[8,128]{1,0:T(8,1...) custom-call(s32[1024,1024]{1,0:T(8,128)} %x_hbm.3, f32[16,128]{1,0:T(8,128)S(1)} %get-tuple-element.38.after_ref, ...), custom_call_target="tpu_custom_call" | custom-call | bytes 4194304 | tf_op jit(solution)/shard_map/turn_rows/pallas_call | solution.py:509
  11.4 0.0 collective-permute-done.2
  11.4 0.4 collective-permute-done.1
  11.9 0.0 collective-permute-done
  11.9 1.6 %collective-permute-start.3 = (f32[16,128]{1,0:T(8,128)S(1)}, f32[16,128]{1,0:T(8,128)S(1)}, u32[]{:S(2)}, u32[]{:S(2)}) collective-permute-start(f32[16,128]{1,0:T(8,128)S(1)} %fusion.1.supply), channel_id=1, source_target_pairs={{0,4},{1,29},{2,10},{3,27},{4,8},{5,1},{6,14},{7,31},{8,12},{9,5},... | collective-permute-start | bytes 24584 | tf_op jit(solution)/shard_map/ppermute | solution.py:28
  13.5 2.6 %send_ahead.1.sent_ref = f32[1536,128]{1,0:T(8,128)S(1)} custom-call(f32[2176]{0:T(1024)S(1)} %concatenate.9.fraction, s32[4096]{0:T(1024)S(1)} %bitcast.23, s32[1024]{0:T(1024)S(1)} %bitcast.28, s32[1024]{0:T(1024)S(1)} %bitcast.31, f32[16392,128]{1,0:T(8,128)S(1)} %get-tuple-element.43.rows, s32[8192,128]{1,0:T(8,128)S(1)} %get-tuple-element.46.turns), custom_call_target="tpu_custom_call" | custom-call | flops 1 | bytes 1 | tf_op jit(solution)/shard_map/send_ahead/pallas_call | solution.py:541
  16.1 1.6 %collective-permute-start.5 = (f32[1536,128]{1,0:T(8,128)S(1)}, f32[1536,128]{1,0:T(8,128)S(1)}, u32[]{:S(2)}, u32[]{:S(2)}) collective-permute-start(f32[1536,128]{1,0:T(8,128)S(1)} %send_ahead.1.sent_ref), channel_id=1, source_target_pairs={{24,0},{28,4},{0,8},{4,12},{8,16},{12,20},{16,24},{20,28},{25,1},{... | collective-permute-start | bytes 2359304 | tf_op jit(solution)/shard_map/ppermute | solution.py:34
  17.8 0.6 collective-permute-done.3.supply_ref
  18.3 2.5 %scale_rows.1.rows.scaled = f32[16392,128]{1,0:T(8,128)S(1)} custom-call(f32[2048]{0:T(1024)S(1)} %bitcast.27, f32[16392,128]{1,0:T(8,128)S(1)} %get-tuple-element.43.rows, f32[1536,128]{1,0:T(8,128)S(1)} %send_ahead.1.sent_ref, f32[16,128]{1,0:T(8,128)S(1)} %collective-permute-done.3.supply_ref), custom_call_target="tpu_custom_call" | custom-call | flops 1 | bytes 1 | tf_op jit(solution)/shard_map/scale_rows/pallas_call | solution.py:550
  20.8 3.5 %send_near.1 = (f32[1536,128]{1,0:T(8,128)S(1)}, f32[1536,128]{1,0:T(8,128)S(1)}) custom-call(s32[4096]{0:T(1024)S(1)} %bitcast.24, s32[1024]{0:T(1024)S(1)} %bitcast.29, s32[1024]{0:T(1024)S(1)} %bitcast.32, f32[16392,128]{1,0:T(8,128)S(1)} %scale_rows.1.rows.scaled, s32[8192,128]{1,0:T(8,128)S(1)} %get-tuple-element.46.turns), custom_call_target="tpu_custom_call" | custom-call | flops 1 | bytes 1 | tf_op jit(solution)/shard_map/send_near/pallas_call | solution.py:559
  24.3 2.7 %collective-permute-start.10 = (f32[1536,128]{1,0:T(8,128)S(1)}, f32[1536,128]{1,0:T(8,128)S(1)}, u32[]{:S(2)}, u32[]{:S(2)}) collective-permute-start(f32[1536,128]{1,0:T(8,128)S(1)} %get-tuple-element.56), channel_id=1, source_target_pairs={{4,0},{8,4},{12,8},{16,12},{20,16},{24,20},{28,24},{0,28},{5,1},{9... | collective-permute-start | bytes 2359304 | tf_op jit(solution)/shard_map/ppermute | solution.py:34
  27.0 10.1 %node_flow.1 = (f32[8192,128]{1,0:T(8,128)S(1)}, f32[32,128]{1,0:T(8,128)S(1)}) custom-call(s32[4096]{0:T(1024)S(1)} %bitcast.25, f32[16392,128]{1,0:T(8,128)S(1)} %scale_rows.1.rows.scaled, s32[8192,128]{1,0:T(8,128)S(1)} %get-tuple-element.46.turns, f32[1536,128]{1,0:T(8,128)S(1)} %get-tuple-element.47.after_ref), custom_call_target="tpu_custom_call" | custom-call | flops 1 | bytes 1 | tf_op jit(solution)/shard_map/node_flow/pallas_call | solution.py:572
  37.2 6.0 %all_gather.3.shared = f32[192,128]{1,0:T(8,128)S(1)} all-gather(f32[48,128]{1,0:T(8,128)S(1)} %pad_maximum_fusion), channel_id=1, replica_groups=mesh['region'=8,'dest'=4] {'dest'}, dimensions={0}, use_global_device_ids=true | all-gather | bytes 122880 | tf_op jit(solution)/shard_map/all_gather | solution.py:587
  43.2 1.5 %theta.1 = (f32[8,128]{1,0:T(8,128)S(1)}, f32[6,128]{1,0:T(8,128)S(1)}) custom-call(f32[16,128]{1,0:T(8,128)S(1)} %fusion.1.supply, f32[192,128]{1,0:T(8,128)S(1)} %all_gather.3.shared, s32[4,1024]{1,0:T(4,128)S(1)} %copy-done, s32[4,192]{1,0:T(4,128)S(1)} %copy-done.2), custom_call_target="tpu_custom_call" | custom-call | flops 1 | bytes 1 | tf_op jit(solution)/shard_map/theta/pallas_call | solution.py:588
  44.7 0.1 collective-permute-start.6
  44.8 4.5 %collective-permute-start.8 = (f32[2,128]{1,0:T(2,128)S(1)}, f32[2,128]{1,0:T(2,128)S(1)}, u32[]{:S(2)}, u32[]{:S(2)}) collective-permute-start(f32[2,128]{1,0:T(2,128)S(1)} %get-tuple-element.67), channel_id=1, source_target_pairs={{4,0},{8,4},{12,8},{16,12},{20,16},{24,20},{28,24},{0,28},{5,1},{9... | collective-permute-start | bytes 3080 | tf_op jit(solution)/shard_map/ppermute | solution.py:34
  49.3 1.2 %send_scaled.1.sent_ref = f32[1536,128]{1,0:T(8,128)S(1)} custom-call(f32[1024]{0:T(1024)S(1)} %bitcast.34, s32[1024]{0:T(1024)S(1)} %bitcast.30, s32[1024]{0:T(1024)S(1)} %bitcast.33, f32[8192,128]{1,0:T(8,128)S(1)} %get-tuple-element.50.flow, s32[8192,128]{1,0:T(8,128)S(1)} %get-tuple-element.46.turns), custom_call_target="tpu_custom_call" | custom-call | flops 1 | bytes 1 | tf_op jit(solution)/shard_map/send_scaled/pallas_call | solution.py:606
  50.5 2.9 %collective-permute-done.6.theta_ref = f32[2,128]{1,0:T(2,128)S(1)} collective-permute-done((f32[2,128]{1,0:T(2,128)S(1)}, f32[2,128]{1,0:T(2,128)S(1)}, u32[]{:S(2)}, u32[]{:S(2)}) %collective-permute-start.6) | collective-permute-done | bytes 1056 | tf_op jit(solution)/shard_map/ppermute | solution.py:34
  53.4 0.0 collective-permute-start.4
  53.4 5.4 %home_rows.1.home = f32[16392,128]{1,0:T(8,128)S(1)} custom-call(s32[2048]{0:T(1024)S(1)} %bitcast.35, s32[2048]{0:T(1024)S(1)} %bitcast.36, s32[8192,128]{1,0:T(8,128)S(1)} %get-tuple-element.46.turns, f32[8192,128]{1,0:T(8,128)S(1)} %get-tuple-element.50.flow, f32[1536,128]{1,0:T(8,128)S(1)} %send_scaled.1.sent_ref, ...), custom_call_target="tpu_custom_call" | custom-call | flops 1 | bytes 1 | tf_op jit(solution)/shard_map/home_rows/pallas_call | solution.py:615
  58.8 0.0 collective-permute-done.5.arrived_ref.rest_2_
  58.8 3.0 %collective-permute-start.7 = (f32[2,128]{1,0:T(2,128)S(1)}, f32[2,128]{1,0:T(2,128)S(1)}, u32[]{:S(2)}, u32[]{:S(2)}) collective-permute-start(f32[2,128]{1,0:T(2,128)S(1)} %get-tuple-element.68), channel_id=1, source_target_pairs={{28,0},{0,4},{4,8},{8,12},{12,16},{16,20},{20,24},{24,28},{29,1},{... | collective-permute-start | bytes 3080 | tf_op jit(solution)/shard_map/ppermute | solution.py:34
  61.9 0.7 keep.1
  62.5 4.7 %base_rows.1.rest_3_ = f32[16392,128]{1,0:T(8,128)S(1)} custom-call(f32[2048]{0:T(1024)S(1)} %bitcast.37, f32[2048]{0:T(1024)S(1)} %bitcast.38, f32[16392,128]{1,0:T(8,128)S(1)} %get-tuple-element.43.rows, f32[16392,128]{1,0:T(8,128)S(1)} %home_rows.1.home), custom_call_target="tpu_custom_call" | custom-call | flops 10000000 | bytes 1 | tf_op jit(solution)/shard_map/base_rows/pallas_call | solution.py:633
  67.3 0.0 collective-permute-done.8
  67.3 5.6 %collective-permute-done.7 = f32[2,128]{1,0:T(2,128)S(1)} collective-permute-done((f32[2,128]{1,0:T(2,128)S(1)}, f32[2,128]{1,0:T(2,128)S(1)}, u32[]{:S(2)}, u32[]{:S(2)}) %collective-permute-start.7) | collective-permute-done | bytes 1056 | tf_op jit(solution)/shard_map/ppermute | solution.py:34
  72.9 1.9 %land_first.1.rest_1_ = f32[16392,128]{1,0:T(8,128)S(1)} custom-call(f32[768]{0:T(1024)S(1)} %maximum_bitcast_fusion.scale, s32[1024]{0:T(1024)S(1)} %bitcast.39, f32[1536,128]{1,0:T(8,128)S(1)} %collective-permute-done.9.rest_0_, f32[1536,128]{1,0:T(8,128)S(1)} %collective-permute-done.10.rest_1_, ...), custom_call_target="tpu_custom_call", output_to_operand_aliasing={{}: (5, {})} | custom-call | flops 99999997952 | bytes 1 | tf_op jit(solution)/shard_map/land_first/pallas_call | solution.py:647
  74.8 4.5 %finish.1 = (f32[2048,1024]{1,0:T(8,128)}, f32[16392,128]{1,0:T(8,128)S(1)}) custom-call(s32[1024]{0:T(1024)S(1)} %bitcast.40, f32[1536,128]{1,0:T(8,128)S(1)} %collective-permute-done.4.rest_0_, f32[16392,128]{1,0:T(8,128)S(1)} %land_first.1.rest_1_), custom_call_target="tpu_custom_call", output_to_operand_aliasing={{1}: (2, {})} | custom-call | flops 2097152 | bytes 8388608 | tf_op jit(solution)/shard_map/finish/pallas_call | solution.py:658
  (24 shorter events, 0.1 us)
Async XLA Ops:
  0.0 8.9 %copy-start = (s32[4,1024]{1,0:T(4,128)S(1)}, s32[4,1024]{1,0:T(4,128)}, u32[]{:S(2)}) copy-start(s32[4,1024]{1,0:T(4,128)} %node_out.3) | copy-start | bytes 49156
  0.0 8.9 %copy-start.2 = (s32[4,192]{1,0:T(4,128)S(1)}, s32[4,192]{1,0:T(4,128)}, u32[]{:S(2)}) copy-start(s32[4,192]{1,0:T(4,128)} %send_list.1) | copy-start | bytes 9220
  0.0 8.9 %copy-start.1 = (s32[4,1024]{1,0:T(4,128)S(1)}, s32[4,1024]{1,0:T(4,128)}, u32[]{:S(2)}) copy-start(s32[4,1024]{1,0:T(4,128)} %node_in.1) | copy-start | bytes 49156
  0.0 8.9 %copy-start.3 = (s32[4,192]{1,0:T(4,128)S(1)}, s32[4,192]{1,0:T(4,128)}, u32[]{:S(2)}) copy-start(s32[4,192]{1,0:T(4,128)} %rest_3_.1) | copy-start | bytes 9220
  0.0 11.9 %copy-start.4 = (f32[2048]{0:T(1024)S(1)}, f32[2048]{0:T(1024)}, u32[]{:S(2)}) copy-start(f32[2048]{0:T(1024)} %param.10) | copy-start | bytes 24580
  0.0 11.9 %copy-start.6 = (f32[2048]{0:T(1024)S(1)}, f32[2048]{0:T(1024)}, u32[]{:S(2)}) copy-start(f32[2048]{0:T(1024)} %param.12) | copy-start | bytes 24580
  0.0 11.9 %copy-start.5 = (f32[2048]{0:T(1024)S(1)}, f32[2048]{0:T(1024)}, u32[]{:S(2)}) copy-start(f32[2048]{0:T(1024)} %param.11) | copy-start | bytes 24580
  5.8 5.6 %collective-permute-start.2 = (f32[16,128]{1,0:T(8,128)S(1)}, f32[16,128]{1,0:T(8,128)S(1)}, u32[]{:S(2)}, u32[]{:S(2)}) collective-permute-start(f32[16,128]{1,0:T(8,128)S(1)} %get-tuple-element.38.after_ref), channel_id=1, source_target_pairs={{0,3},{1,2},{2,1},{3,0},{4,7},{5,6},{6,5},{7,4},{8,11},{9,10},{10,... | collective-permute-start | bytes 24584 | tf_op jit(solution)/shard_map/ppermute | solution.py:40
  8.2 3.7 %collective-permute-start.1 = (f32[16,128]{1,0:T(8,128)S(1)}, f32[16,128]{1,0:T(8,128)S(1)}, u32[]{:S(2)}, u32[]{:S(2)}) collective-permute-start(f32[16,128]{1,0:T(8,128)S(1)} %get-tuple-element.38.after_ref), channel_id=1, source_target_pairs={{0,2},{1,3},{2,0},{3,1},{4,6},{5,7},{6,4},{7,5},{8,10},{9,11},{10,... | collective-permute-start | bytes 24584 | tf_op jit(solution)/shard_map/ppermute | solution.py:40
  8.8 3.0 %collective-permute-start = (f32[16,128]{1,0:T(8,128)S(1)}, f32[16,128]{1,0:T(8,128)S(1)}, u32[]{:S(2)}, u32[]{:S(2)}) collective-permute-start(f32[16,128]{1,0:T(8,128)S(1)} %get-tuple-element.38.after_ref), channel_id=1, source_target_pairs={{0,1},{1,0},{2,3},{3,2},{4,5},{5,4},{6,7},{7,6},{8,9},{9,8},{10,11... | collective-permute-start | bytes 24584 | tf_op jit(solution)/shard_map/ppermute | solution.py:40
  11.9 6.4 %collective-permute-start.3 = (f32[16,128]{1,0:T(8,128)S(1)}, f32[16,128]{1,0:T(8,128)S(1)}, u32[]{:S(2)}, u32[]{:S(2)}) collective-permute-start(f32[16,128]{1,0:T(8,128)S(1)} %fusion.1.supply), channel_id=1, source_target_pairs={{0,4},{1,29},{2,10},{3,27},{4,8},{5,1},{6,14},{7,31},{8,12},{9,5},... | collective-permute-start | bytes 24584 | tf_op jit(solution)/shard_map/ppermute | solution.py:28
  16.1 42.7 %collective-permute-start.5 = (f32[1536,128]{1,0:T(8,128)S(1)}, f32[1536,128]{1,0:T(8,128)S(1)}, u32[]{:S(2)}, u32[]{:S(2)}) collective-permute-start(f32[1536,128]{1,0:T(8,128)S(1)} %send_ahead.1.sent_ref), channel_id=1, source_target_pairs={{24,0},{28,4},{0,8},{4,12},{8,16},{12,20},{16,24},{20,28},{25,1},{... | collective-permute-start | bytes 2359304 | tf_op jit(solution)/shard_map/ppermute | solution.py:34
  24.3 48.5 %collective-permute-start.10 = (f32[1536,128]{1,0:T(8,128)S(1)}, f32[1536,128]{1,0:T(8,128)S(1)}, u32[]{:S(2)}, u32[]{:S(2)}) collective-permute-start(f32[1536,128]{1,0:T(8,128)S(1)} %get-tuple-element.56), channel_id=1, source_target_pairs={{4,0},{8,4},{12,8},{16,12},{20,16},{24,20},{28,24},{0,28},{5,1},{9... | collective-permute-start | bytes 2359304 | tf_op jit(solution)/shard_map/ppermute | solution.py:34
  27.0 45.8 %collective-permute-start.9 = (f32[1536,128]{1,0:T(8,128)S(1)}, f32[1536,128]{1,0:T(8,128)S(1)}, u32[]{:S(2)}, u32[]{:S(2)}) collective-permute-start(f32[1536,128]{1,0:T(8,128)S(1)} %get-tuple-element.47.after_ref), channel_id=1, source_target_pairs={{28,0},{0,4},{4,8},{8,12},{12,16},{16,20},{20,24},{24,28},{29,1},{... | collective-permute-start | bytes 2359304 | tf_op jit(solution)/shard_map/ppermute | solution.py:34
  44.7 8.7 %collective-permute-start.6 = (f32[2,128]{1,0:T(2,128)S(1)}, f32[2,128]{1,0:T(2,128)S(1)}, u32[]{:S(2)}, u32[]{:S(2)}) collective-permute-start(f32[2,128]{1,0:T(2,128)S(1)} %get-tuple-element.69), channel_id=1, source_target_pairs={{24,0},{28,4},{0,8},{4,12},{8,16},{12,20},{16,24},{20,28},{25,1},{... | collective-permute-start | bytes 3080 | tf_op jit(solution)/shard_map/ppermute | solution.py:34
  44.8 22.5 %collective-permute-start.8 = (f32[2,128]{1,0:T(2,128)S(1)}, f32[2,128]{1,0:T(2,128)S(1)}, u32[]{:S(2)}, u32[]{:S(2)}) collective-permute-start(f32[2,128]{1,0:T(2,128)S(1)} %get-tuple-element.67), channel_id=1, source_target_pairs={{4,0},{8,4},{12,8},{16,12},{20,16},{24,20},{28,24},{0,28},{5,1},{9... | collective-permute-start | bytes 3080 | tf_op jit(solution)/shard_map/ppermute | solution.py:34
  53.4 21.4 %collective-permute-start.4 = (f32[1536,128]{1,0:T(8,128)S(1)}, f32[1536,128]{1,0:T(8,128)S(1)}, u32[]{:S(2)}, u32[]{:S(2)}) collective-permute-start(f32[1536,128]{1,0:T(8,128)S(1)} %send_scaled.1.sent_ref), channel_id=1, source_target_pairs={{8,0},{12,4},{16,8},{20,12},{24,16},{28,20},{0,24},{4,28},{9,1},{1... | collective-permute-start | bytes 2359304 | tf_op jit(solution)/shard_map/ppermute | solution.py:34
  58.8 14.0 %collective-permute-start.7 = (f32[2,128]{1,0:T(2,128)S(1)}, f32[2,128]{1,0:T(2,128)S(1)}, u32[]{:S(2)}, u32[]{:S(2)}) collective-permute-start(f32[2,128]{1,0:T(2,128)S(1)} %get-tuple-element.68), channel_id=1, source_target_pairs={{28,0},{0,4},{4,8},{8,12},{12,16},{16,20},{20,24},{24,28},{29,1},{... | collective-permute-start | bytes 3080 | tf_op jit(solution)/shard_map/ppermute | solution.py:34

commit v11 on v9

--- a/solution.py
+++ b/solution.py
@@ -246,16 +246,16 @@
     row_of(scaled, cells, sub)[...] = jnp.zeros((sub, LANES), F32)
 
 
-def send_kernel(sizes, sides, fraction, in_cell, send_node, send_outlet, rows, turns, *sends):
+def send_kernel(sizes, parts, fraction, in_cell, send_node, send_outlet, rows, turns, *sends):
     cells, nodes, branches, cap, sub = sizes
     batch = 8
-    for side, send in zip(sides, sends):
-
-        def body(step, carry, side=side, send=send):
+    for (side, start, count), send in zip(parts, sends):
+
+        def body(step, carry, side=side, start=start, send=send):
             first = step * batch
             values = []
             for i in range(batch):
-                slot = side * padded(cap) + first + i
+                slot = side * padded(cap) + start + first + i
                 node = send_node[slot]
                 value = gathered_flow(node, in_cell, fraction, rows, sizes)
                 choice = row_of(turns, node, sub)[...]
@@ -264,18 +264,21 @@
                 row_of(send, first + i, sub)[...] = values[i]
             return carry
 
-        lax.fori_loop(0, cap // batch, body, 0)
-
-
-def scaled_send_kernel(sizes, side, theta, send_node, send_outlet, flow, turns, send):
-    cells, nodes, branches, cap, sub = sizes
+        lax.fori_loop(0, count // batch, body, 0)
+
+
+def scaled_send_kernel(
+    sizes, part, theta, send_node, send_outlet, flow, turns, after_ref, send
+):
+    cells, nodes, branches, cap, sub = sizes
+    side, start, count = part
     batch = 8
 
     def body(step, carry):
         first = step * batch
         values = []
         for i in range(batch):
-            slot = side * padded(cap) + first + i
+            slot = side * padded(cap) + start + first + i
             node = send_node[slot]
             value = row_of(flow, node, sub)[...] * theta[node]
             choice = row_of(turns, node, sub)[...]
@@ -284,7 +287,7 @@
             row_of(send, first + i, sub)[...] = values[i]
         return carry
 
-    lax.fori_loop(0, cap // batch, body, 0)
+    lax.fori_loop(0, count // batch, body, 0)
 
 
 def node_flow_kernel(sizes, in_cell, scaled, turns, after_ref, flow, demand, partial):
@@ -411,16 +414,16 @@
     lax.fori_loop(0, cells // batch, body, 0)
 
 
-def land_rows(sizes, sides, scale, land, received, base):
+def land_rows(sizes, parts, scale, land, received, base):
     cells, nodes, branches, cap, sub = sizes
     batch = 8
-    for side, rows in zip(sides, received):
-
-        def body(step, carry, side=side, rows=rows):
+    for (side, start, count), rows in zip(parts, received):
+
+        def body(step, carry, side=side, start=start, rows=rows):
             first = step * batch
             stores = []
             for i in range(batch):
-                slot = side * padded(cap) + first + i
+                slot = side * padded(cap) + start + first + i
                 at = row_of(base, land[slot], sub)
                 value = row_of(rows, first + i, sub)[...]
                 if scale is not None:
@@ -430,18 +433,18 @@
                 at[...] = value
             return carry
 
-        lax.fori_loop(0, cap // batch, body, 0)
-
-
-def land_kernel(sizes, sides, scale, land, *rest):
-    received, (base_in, base) = rest[: len(sides)], rest[len(sides) :]
-    land_rows(sizes, sides, scale, land, received, base)
-
-
-def finish_kernel(sizes, sides, chunk, land, *rest):
-    cells, nodes, branches, cap, sub = sizes
-    received, (base_in, out, base, staged, sems) = rest[: len(sides)], rest[len(sides) :]
-    land_rows(sizes, sides, None, land, received, base)
+        lax.fori_loop(0, count // batch, body, 0)
+
+
+def land_kernel(sizes, parts, scale, land, *rest):
+    received, (base_in, base) = rest[: len(parts)], rest[len(parts) :]
+    land_rows(sizes, parts, scale, land, received, base)
+
+
+def finish_kernel(sizes, parts, chunk, land, *rest):
+    cells, nodes, branches, cap, sub = sizes
+    received, (base_in, out, base, staged, sems) = rest[: len(parts)], rest[len(parts) :]
+    land_rows(sizes, parts, None, land, received, base)
     copies = []
     for number in range(cells // chunk):
 
@@ -528,15 +531,22 @@
     fraction = jnp.minimum(vehicles, cap_of) / vehicles
     supply = jnp.minimum(cap_of, wave.reshape(per_cell) * (jam.reshape(per_cell) - vehicles))
     rows_shape = pltpu.VMEM(((cells + 1) * sub, LANES), F32)
-    send_shape = pltpu.VMEM((cap * sub, LANES), F32)
+    early = cap * 2 // 3 // 8 * 8
+    whole = [(side, 0, cap) for side in range(4)]
+    parts = (*whole[:3], (3, 0, early))
+    last_part = (3, early, cap - early)
+
+    def send_shape(part):
+        return pltpu.VMEM((part[2] * sub, LANES), F32)
+
 
     supply_there = to_neighbours(supply)
     weights = jnp.concatenate([fraction.reshape(-1), jnp.zeros((LANES,), F32)])
     (ahead,) = pl.pallas_call(
-        functools.partial(send_kernel, sizes, (2,)),
+        functools.partial(send_kernel, sizes, parts[2:3]),
         in_specs=[SMEM_WHOLE] * 4 + [VMEM_WHOLE] * 2,
         out_specs=[VMEM_WHOLE],
-        out_shape=[send_shape],
+        out_shape=[send_shape(parts[2])],
         compiler_params=params(4),
         cost_estimate=cost(1, 1),
         name="send_ahead",
@@ -551,16 +561,16 @@
         name="scale_rows",
     )(fraction.reshape(-1), rows, ahead, supply_there)
     near = pl.pallas_call(
-        functools.partial(send_kernel, sizes, (0, 1), None),
+        functools.partial(send_kernel, sizes, (parts[0], parts[1], parts[3]), None),
         in_specs=[SMEM_WHOLE] * 3 + [VMEM_WHOLE] * 2,
-        out_specs=[VMEM_WHOLE] * 2,
-        out_shape=[send_shape] * 2,
+        out_specs=[VMEM_WHOLE] * 3,
+        out_shape=[send_shape(part) for part in (parts[0], parts[1], parts[3])],
         compiler_params=params(4),
         cost_estimate=cost(1, 1),
         name="send_near",
     )(in_cell, send_node, send_outlet, scaled, turns)
     arrived = [
-        shifted(send, "region", SHIFTS[side]) for side, send in enumerate([*near, ahead])
+        shifted(send, "region", SHIFTS[side]) for side, send in enumerate([near[0], near[1], ahead, near[2]])
     ]
 
     flow, demand = pl.pallas_call(
@@ -593,15 +603,6 @@
     )(supply, shared, node_out, send_list)
     theta_there = to_neighbours(slot_theta)
 
-    (behind,) = pl.pallas_call(
-        functools.partial(scaled_send_kernel, sizes, 3),
-        in_specs=[SMEM_WHOLE] * 3 + [VMEM_WHOLE] * 2,
-        out_specs=[VMEM_WHOLE],
-        out_shape=[send_shape],
-        compiler_params=params(4),
-        cost_estimate=cost(1, 1),
-        name="send_scaled",
-    )(theta.reshape(-1), send_node, send_outlet, flow, turns)
     home = pl.pallas_call(
         functools.partial(home_kernel, sizes),
         in_specs=[SMEM_WHOLE] * 2 + [VMEM_WHOLE] * 2 + [ANYWHERE],
@@ -610,7 +611,16 @@
         compiler_params=params(4),
         cost_estimate=cost(1, 1),
         name="home_rows",
-    )(source_node, source_outlet, turns, flow, behind)
+    )(source_node, source_outlet, turns, flow, slot_theta)
+    (behind,) = pl.pallas_call(
+        functools.partial(scaled_send_kernel, sizes, last_part),
+        in_specs=[SMEM_WHOLE] * 3 + [VMEM_WHOLE] * 2 + [ANYWHERE],
+        out_specs=[VMEM_WHOLE],
+        out_shape=[send_shape(last_part)],
+        compiler_params=params(4),
+        cost_estimate=cost(1, 1),
+        name="send_scaled",
+    )(theta.reshape(-1), send_node, send_outlet, flow, turns, home)
     keep, home_theta = pl.pallas_call(
         functools.partial(keep_kernel, sizes),
         in_specs=[VMEM_WHOLE] * 4 + [ANYWHERE] * 2,
@@ -635,18 +645,18 @@
     scale = lax.all_gather(theta_there, "dest", axis=0, tiled=True)[: list_shape[0]]
 
     base = pl.pallas_call(
-        functools.partial(land_kernel, sizes, (0, 1, 2)),
-        in_specs=[SMEM_WHOLE] * 2 + [VMEM_WHOLE] * 4,
+        functools.partial(land_kernel, sizes, parts),
+        in_specs=[SMEM_WHOLE] * 2 + [VMEM_WHOLE] * 5,
         out_specs=VMEM_WHOLE,
         out_shape=rows_shape,
-        input_output_aliases={5: 0},
+        input_output_aliases={6: 0},
         compiler_params=params(4),
         cost_estimate=cost(100000000000, 1),
         name="land_first",
     )(scale.reshape(-1), land, *arrived, base)
 
     out, _ = pl.pallas_call(
-        functools.partial(finish_kernel, sizes, (3,), chunk),
+        functools.partial(finish_kernel, sizes, (last_part,), chunk),
         in_specs=[SMEM_WHOLE] + [VMEM_WHOLE] * 2,
         out_specs=[ANYWHERE, VMEM_WHOLE],
         out_shape=[jax.ShapeDtypeStruct((cells, width), F32), rows_shape],

time: 78.9 us -> 78.9 us (level)
  the two profiles are of different devices: /device:TPU:25 before, /device:TPU:0 now
where the time goes in v11:
time: 78.9 us; the launch traced here: 78.2 us
  Pallas kernels  46.5 us (59%)
  starting transfers between devices  14.2 us (18%)
  blocking collectives  11 us (14%)
  waiting for transfers between devices  6.38 us (8%)
    pallas_call x1, Pallas kernels, on_device(): pl.pallas_call(functools.partial(node_flow_kernel, sizes), in_specs=[SMEM...  10.1 us
    ppermute x2, waiting for transfers between devices, to_neighbours(): return lax.ppermute(block, ('region', 'dest'), route)  5.93 us
    all_gather x1, blocking collectives, on_device(): shared = lax.all_gather(joined, 'dest', axis=0, tiled=True)  5.9 us
    ppermute x5, starting transfers between devices, shifted(): return lax.ppermute(block, axis, route)  5.84 us
    pallas_call x1, Pallas kernels, on_device(): pl.pallas_call(functools.partial(home_kernel, sizes), in_specs=[SMEM_WHOL...  5.38 us
    ppermute x2, starting transfers between devices, to_neighbours(): return lax.ppermute(block, ('region', 'dest'), route)  5.24 us
    all_gather x1, blocking collectives, on_device(): lax.all_gather(theta_there, 'dest', axis=0, tiled=True)[:list_shape[0]]  5.07 us
    pallas_call x1, Pallas kernels, on_device(): pl.pallas_call(functools.partial(base_kernel, sizes), in_specs=[SMEM_WHOL...  4.72 us
  transfers between devices with their start and end apart: 10, of which 3 were waited for; matrix products, arithmetic and copies ran while one was open for 0% of the time, Pallas kernels for 48%

profile of v11, /device:TPU:0, one launch (start us, length us, event | category | flops | bytes accessed | tf_op | source)
XLA Modules:
  0.0 78.2 jit_solution(12446679734930951424)
XLA Ops:
  0.0 4.7 %cell_sum.1 = (f32[16,128]{1,0:T(8,128)S(1)}, f32[16392,128]{1,0:T(8,128)S(1)}) custom-call(f32[2048,1024]{1,0:T(8,128)} %x_hbm.2), custom_call_target="tpu_custom_call" | custom-call | flops 2097152 | bytes 8388608 | tf_op jit(solution)/shard_map/cell_sum/pallas_call | solution.py:486
  4.7 2.4 %collective-permute-start.2 = (f32[16,128]{1,0:T(8,128)S(1)}, f32[16,128]{1,0:T(8,128)S(1)}, u32[]{:S(2)}, u32[]{:S(2)}) collective-permute-start(f32[16,128]{1,0:T(8,128)S(1)} %get-tuple-element.38.after_ref), channel_id=1, source_target_pairs={{0,3},{1,2},{2,1},{3,0},{4,7},{5,6},{6,5},{7,4},{8,11},{9,10},{10,... | collective-permute-start | bytes 24584 | tf_op jit(solution)/shard_map/ppermute | solution.py:40
  7.2 0.6 collective-permute-start.1
  7.8 0.0 collective-permute-start
  7.9 2.5 %turn_rows.1 = (s32[8192,128]{1,0:T(8,128)S(1)}, s32[32,128]{1,0:T(8,128)S(1)}, s32[8,128]{1,0:T(8,128)S(1)}, s32[8,128]{1,0:T(8,128)S(1)}, s32[8,128]{1,0:T(8,1...) custom-call(s32[1024,1024]{1,0:T(8,128)} %x_hbm.3, f32[16,128]{1,0:T(8,128)S(1)} %get-tuple-element.38.after_ref, ...), custom_call_target="tpu_custom_call" | custom-call | bytes 4194304 | tf_op jit(solution)/shard_map/turn_rows/pallas_call | solution.py:506
  10.4 0.4 collective-permute-done.1
  10.8 0.0 collective-permute-done
  10.9 1.6 %collective-permute-start.3 = (f32[16,128]{1,0:T(8,128)S(1)}, f32[16,128]{1,0:T(8,128)S(1)}, u32[]{:S(2)}, u32[]{:S(2)}) collective-permute-start(f32[16,128]{1,0:T(8,128)S(1)} %fusion.1.supply), channel_id=1, source_target_pairs={{0,4},{1,29},{2,10},{3,27},{4,8},{5,1},{6,14},{7,31},{8,12},{9,5},... | collective-permute-start | bytes 24584 | tf_op jit(solution)/shard_map/ppermute | solution.py:28
  12.5 2.6 %send_ahead.1.sent_ref = f32[1536,128]{1,0:T(8,128)S(1)} custom-call(f32[2176]{0:T(1024)S(1)} %concatenate.6.fraction, s32[4096]{0:T(1024)S(1)} %bitcast.23, s32[1024]{0:T(1024)S(1)} %bitcast.28, s32[1024]{0:T(1024)S(1)} %bitcast.31, f32[16392,128]{1,0:T(8,128)S(1)} %get-tuple-element.43.rows, s32[8192,128]{1,0:T(8,128)S(1)} %get-tuple-element.46.turns), custom_call_target="tpu_custom_call" | custom-call | flops 1 | bytes 1 | tf_op jit(solution)/shard_map/send_ahead/pallas_call | solution.py:545
  15.1 1.6 %collective-permute-start.5 = (f32[1536,128]{1,0:T(8,128)S(1)}, f32[1536,128]{1,0:T(8,128)S(1)}, u32[]{:S(2)}, u32[]{:S(2)}) collective-permute-start(f32[1536,128]{1,0:T(8,128)S(1)} %send_ahead.1.sent_ref), channel_id=1, source_target_pairs={{24,0},{28,4},{0,8},{4,12},{8,16},{12,20},{16,24},{20,28},{25,1},{... | collective-permute-start | bytes 2359304 | tf_op jit(solution)/shard_map/ppermute | solution.py:34
  16.7 0.6 collective-permute-done.3.supply_ref
  17.3 2.5 %scale_rows.1.rows.scaled = f32[16392,128]{1,0:T(8,128)S(1)} custom-call(f32[2048]{0:T(1024)S(1)} %bitcast.27, f32[16392,128]{1,0:T(8,128)S(1)} %get-tuple-element.43.rows, f32[1536,128]{1,0:T(8,128)S(1)} %send_ahead.1.sent_ref, f32[16,128]{1,0:T(8,128)S(1)} %collective-permute-done.3.supply_ref), custom_call_target="tpu_custom_call" | custom-call | flops 1 | bytes 1 | tf_op jit(solution)/shard_map/scale_rows/pallas_call | solution.py:554
  19.8 4.4 %send_near.1 = (f32[1536,128]{1,0:T(8,128)S(1)}, f32[1536,128]{1,0:T(8,128)S(1)}, f32[1024,128]{1,0:T(8,128)S(1)}) custom-call(s32[4096]{0:T(1024)S(1)} %bitcast.24, s32[1024]{0:T(1024)S(1)} %bitcast.29, s32[1024]{0:T(1024)S(1)} %bitcast.32, f32[16392,128]{1,0:T(8,128)S(1)} %scale_rows.1.rows.scaled, s32[8192,128]{1,0:T(8,128)S(1)} %get-tuple-element.46.turns), custom_call_target="tpu_custom_call" | custom-call | flops 1 | bytes 1 | tf_op jit(solution)/shard_map/send_near/pallas_call | solution.py:563
  24.2 2.7 %collective-permute-start.8 = (f32[1536,128]{1,0:T(8,128)S(1)}, f32[1536,128]{1,0:T(8,128)S(1)}, u32[]{:S(2)}, u32[]{:S(2)}) collective-permute-start(f32[1536,128]{1,0:T(8,128)S(1)} %get-tuple-element.56), channel_id=1, source_target_pairs={{4,0},{8,4},{12,8},{16,12},{20,16},{24,20},{28,24},{0,28},{5,1},{9... | collective-permute-start | bytes 2359304 | tf_op jit(solution)/shard_map/ppermute | solution.py:34
  26.9 1.2 %collective-permute-start.9 = (f32[1024,128]{1,0:T(8,128)S(1)}, f32[1024,128]{1,0:T(8,128)S(1)}, u32[]{:S(2)}, u32[]{:S(2)}) collective-permute-start(f32[1024,128]{1,0:T(8,128)S(1)} %get-tuple-element.57), channel_id=1, source_target_pairs={{8,0},{12,4},{16,8},{20,12},{24,16},{28,20},{0,24},{4,28},{9,1},{1... | collective-permute-start | bytes 1572872 | tf_op jit(solution)/shard_map/ppermute | solution.py:34
  28.1 10.1 %node_flow.1 = (f32[8192,128]{1,0:T(8,128)S(1)}, f32[32,128]{1,0:T(8,128)S(1)}) custom-call(s32[4096]{0:T(1024)S(1)} %bitcast.25, f32[16392,128]{1,0:T(8,128)S(1)} %scale_rows.1.rows.scaled, s32[8192,128]{1,0:T(8,128)S(1)} %get-tuple-element.46.turns, f32[1536,128]{1,0:T(8,128)S(1)} %get-tuple-element.47.after_ref), custom_call_target="tpu_custom_call" | custom-call | flops 1 | bytes 1 | tf_op jit(solution)/shard_map/node_flow/pallas_call | solution.py:576
  38.2 5.9 %all_gather.6.shared = f32[192,128]{1,0:T(8,128)S(1)} all-gather(f32[48,128]{1,0:T(8,128)S(1)} %pad_maximum_fusion), channel_id=1, replica_groups=mesh['region'=8,'dest'=4] {'dest'}, dimensions={0}, use_global_device_ids=true | all-gather | bytes 122880 | tf_op jit(solution)/shard_map/all_gather | solution.py:591
  44.1 1.4 %theta.1 = (f32[8,128]{1,0:T(8,128)S(1)}, f32[2,128]{1,0:T(2,128)S(1)}) custom-call(f32[16,128]{1,0:T(8,128)S(1)} %fusion.1.supply, f32[192,128]{1,0:T(8,128)S(1)} %all_gather.6.shared, s32[4,1024]{1,0:T(4,128)S(1)} %copy-done, s32[4,192]{1,0:T(4,128)S(1)} %copy-done.2), custom_call_target="tpu_custom_call" | custom-call | flops 1 | bytes 1 | tf_op jit(solution)/shard_map/theta/pallas_call | solution.py:592
  45.5 3.7 %collective-permute-start.6 = (f32[2,128]{1,0:T(2,128)S(1)}, f32[2,128]{1,0:T(2,128)S(1)}, u32[]{:S(2)}, u32[]{:S(2)}) collective-permute-start(f32[2,128]{1,0:T(2,128)S(1)} %get-tuple-element.53.after_ref), channel_id=1, source_target_pairs={{0,4},{1,29},{2,10},{3,27},{4,8},{5,1},{6,14},{7,31},{8,12},{9,5},... | collective-permute-start | bytes 3080 | tf_op jit(solution)/shard_map/ppermute | solution.py:28
  49.2 5.4 %home_rows.1.after_ref.home = f32[16392,128]{1,0:T(8,128)S(1)} custom-call(s32[2048]{0:T(1024)S(1)} %bitcast.35, s32[2048]{0:T(1024)S(1)} %bitcast.36, s32[8192,128]{1,0:T(8,128)S(1)} %get-tuple-element.46.turns, f32[8192,128]{1,0:T(8,128)S(1)} %get-tuple-element.50.flow, f32[2,128]{1,0:T(2,128)S(1)} %get-tuple-element.53.after_ref), custom_call_target="tpu_custom_call" | custom-call | flops 1 | bytes 1 | tf_op jit(solution)/shard_map/home_rows/pallas_call | solution.py:606
  54.6 0.9 %send_scaled.1.sent_ref = f32[512,128]{1,0:T(8,128)S(1)} custom-call(f32[1024]{0:T(1024)S(1)} %bitcast.34, s32[1024]{0:T(1024)S(1)} %bitcast.30, s32[1024]{0:T(1024)S(1)} %bitcast.33, f32[8192,128]{1,0:T(8,128)S(1)} %get-tuple-element.50.flow, s32[8192,128]{1,0:T(8,128)S(1)} %get-tuple-element.46.turns, f32[16392,128]{1,0:T(8,128)S(1)} %home_rows.1.after_ref.home), custom_call_target="tpu_custom_call" | custom-call | flops 1 | bytes 1 | tf_op jit(solution)/shard_map/send_scaled/pallas_call | solution.py:615
  55.5 0.0 collective-permute-done.5.arrived_ref.rest_2_
  55.5 0.3 collective-permute-start.4
  55.9 0.7 keep.1
  56.5 4.7 %base_rows.1.rest_4_ = f32[16392,128]{1,0:T(8,128)S(1)} custom-call(f32[2048]{0:T(1024)S(1)} %bitcast.37, f32[2048]{0:T(1024)S(1)} %bitcast.38, f32[16392,128]{1,0:T(8,128)S(1)} %get-tuple-element.43.rows, f32[16392,128]{1,0:T(8,128)S(1)} %home_rows.1.after_ref.home), custom_call_target="tpu_custom_call" | custom-call | flops 10000000 | bytes 1 | tf_op jit(solution)/shard_map/base_rows/pallas_call | solution.py:633
  61.3 5.4 %collective-permute-done.6 = f32[2,128]{1,0:T(2,128)S(1)} collective-permute-done((f32[2,128]{1,0:T(2,128)S(1)}, f32[2,128]{1,0:T(2,128)S(1)}, u32[]{:S(2)}, u32[]{:S(2)}) %collective-permute-start.6) | collective-permute-done | bytes 1056 | tf_op jit(solution)/shard_map/ppermute | solution.py:28
  66.6 0.0 collective-permute-done.8.rest_1_
  66.6 0.0 collective-permute-done.7.rest_0_
  66.6 5.1 %all-gather = f32[4,2,128]{2,1,0:T(2,128)S(1)} all-gather(f32[1,2,128]{2,1,0:T(2,128)S(1)} %bitcast.42), channel_id=1, replica_groups=mesh['region'=8,'dest'=4] {'dest'}, dimensions={0}, use_global_device_ids=true | all-gather | bytes 5120 | tf_op jit(solution)/shard_map/all_gather | solution.py:645
  71.7 2.3 %land_first.1.rest_1_ = f32[16392,128]{1,0:T(8,128)S(1)} custom-call(f32[1024]{0:T(1024)S(1)} %bitcast.41, s32[1024]{0:T(1024)S(1)} %bitcast.39, f32[1536,128]{1,0:T(8,128)S(1)} %collective-permute-done.7.rest_0_, f32[1536,128]{1,0:T(8,128)S(1)} %collective-permute-done.8.rest_1_, ...), custom_call_target="tpu_custom_call", output_to_operand_aliasing={{}: (6, {})} | custom-call | flops 99999997952 | bytes 1 | tf_op jit(solution)/shard_map/land_first/pallas_call | solution.py:647
  74.0 0.0 collective-permute-done.4.rest_0_
  74.0 4.3 %finish.1 = (f32[2048,1024]{1,0:T(8,128)}, f32[16392,128]{1,0:T(8,128)S(1)}) custom-call(s32[1024]{0:T(1024)S(1)} %bitcast.40, f32[512,128]{1,0:T(8,128)S(1)} %collective-permute-done.4.rest_0_, f32[16392,128]{1,0:T(8,128)S(1)} %land_first.1.rest_1_), custom_call_target="tpu_custom_call", output_to_operand_aliasing={{1}: (2, {})} | custom-call | flops 2097152 | bytes 8388608 | tf_op jit(solution)/shard_map/finish/pallas_call | solution.py:658
  (21 shorter events, 0.1 us)
Async XLA Ops:
  0.0 7.9 %copy-start = (s32[4,1024]{1,0:T(4,128)S(1)}, s32[4,1024]{1,0:T(4,128)}, u32[]{:S(2)}) copy-start(s32[4,1024]{1,0:T(4,128)} %node_out.3) | copy-start | bytes 49156
  0.0 7.9 %copy-start.2 = (s32[4,192]{1,0:T(4,128)S(1)}, s32[4,192]{1,0:T(4,128)}, u32[]{:S(2)}) copy-start(s32[4,192]{1,0:T(4,128)} %send_list.1) | copy-start | bytes 9220
  0.0 7.9 %copy-start.1 = (s32[4,1024]{1,0:T(4,128)S(1)}, s32[4,1024]{1,0:T(4,128)}, u32[]{:S(2)}) copy-start(s32[4,1024]{1,0:T(4,128)} %node_in.1) | copy-start | bytes 49156
  0.0 7.9 %copy-start.3 = (s32[4,192]{1,0:T(4,128)S(1)}, s32[4,192]{1,0:T(4,128)}, u32[]{:S(2)}) copy-start(s32[4,192]{1,0:T(4,128)} %rest_3_.1) | copy-start | bytes 9220
  0.0 10.8 %copy-start.4 = (f32[2048]{0:T(1024)S(1)}, f32[2048]{0:T(1024)}, u32[]{:S(2)}) copy-start(f32[2048]{0:T(1024)} %param.10) | copy-start | bytes 24580
  0.0 10.9 %copy-start.6 = (f32[2048]{0:T(1024)S(1)}, f32[2048]{0:T(1024)}, u32[]{:S(2)}) copy-start(f32[2048]{0:T(1024)} %param.12) | copy-start | bytes 24580
  0.0 10.9 %copy-start.5 = (f32[2048]{0:T(1024)S(1)}, f32[2048]{0:T(1024)}, u32[]{:S(2)}) copy-start(f32[2048]{0:T(1024)} %param.11) | copy-start | bytes 24580
  4.7 5.6 %collective-permute-start.2 = (f32[16,128]{1,0:T(8,128)S(1)}, f32[16,128]{1,0:T(8,128)S(1)}, u32[]{:S(2)}, u32[]{:S(2)}) collective-permute-start(f32[16,128]{1,0:T(8,128)S(1)} %get-tuple-element.38.after_ref), channel_id=1, source_target_pairs={{0,3},{1,2},{2,1},{3,0},{4,7},{5,6},{6,5},{7,4},{8,11},{9,10},{10,... | collective-permute-start | bytes 24584 | tf_op jit(solution)/shard_map/ppermute | solution.py:40
  7.2 3.7 %collective-permute-start.1 = (f32[16,128]{1,0:T(8,128)S(1)}, f32[16,128]{1,0:T(8,128)S(1)}, u32[]{:S(2)}, u32[]{:S(2)}) collective-permute-start(f32[16,128]{1,0:T(8,128)S(1)} %get-tuple-element.38.after_ref), channel_id=1, source_target_pairs={{0,2},{1,3},{2,0},{3,1},{4,6},{5,7},{6,4},{7,5},{8,10},{9,11},{10,... | collective-permute-start | bytes 24584 | tf_op jit(solution)/shard_map/ppermute | solution.py:40
  7.8 3.0 %collective-permute-start = (f32[16,128]{1,0:T(8,128)S(1)}, f32[16,128]{1,0:T(8,128)S(1)}, u32[]{:S(2)}, u32[]{:S(2)}) collective-permute-start(f32[16,128]{1,0:T(8,128)S(1)} %get-tuple-element.38.after_ref), channel_id=1, source_target_pairs={{0,1},{1,0},{2,3},{3,2},{4,5},{5,4},{6,7},{7,6},{8,9},{9,8},{10,11... | collective-permute-start | bytes 24584 | tf_op jit(solution)/shard_map/ppermute | solution.py:40
  10.9 6.4 %collective-permute-start.3 = (f32[16,128]{1,0:T(8,128)S(1)}, f32[16,128]{1,0:T(8,128)S(1)}, u32[]{:S(2)}, u32[]{:S(2)}) collective-permute-start(f32[16,128]{1,0:T(8,128)S(1)} %fusion.1.supply), channel_id=1, source_target_pairs={{0,4},{1,29},{2,10},{3,27},{4,8},{5,1},{6,14},{7,31},{8,12},{9,5},... | collective-permute-start | bytes 24584 | tf_op jit(solution)/shard_map/ppermute | solution.py:28
  15.1 40.4 %collective-permute-start.5 = (f32[1536,128]{1,0:T(8,128)S(1)}, f32[1536,128]{1,0:T(8,128)S(1)}, u32[]{:S(2)}, u32[]{:S(2)}) collective-permute-start(f32[1536,128]{1,0:T(8,128)S(1)} %send_ahead.1.sent_ref), channel_id=1, source_target_pairs={{24,0},{28,4},{0,8},{4,12},{8,16},{12,20},{16,24},{20,28},{25,1},{... | collective-permute-start | bytes 2359304 | tf_op jit(solution)/shard_map/ppermute | solution.py:34
  24.2 42.4 %collective-permute-start.8 = (f32[1536,128]{1,0:T(8,128)S(1)}, f32[1536,128]{1,0:T(8,128)S(1)}, u32[]{:S(2)}, u32[]{:S(2)}) collective-permute-start(f32[1536,128]{1,0:T(8,128)S(1)} %get-tuple-element.56), channel_id=1, source_target_pairs={{4,0},{8,4},{12,8},{16,12},{20,16},{24,20},{28,24},{0,28},{5,1},{9... | collective-permute-start | bytes 2359304 | tf_op jit(solution)/shard_map/ppermute | solution.py:34
  26.9 39.7 %collective-permute-start.7 = (f32[1536,128]{1,0:T(8,128)S(1)}, f32[1536,128]{1,0:T(8,128)S(1)}, u32[]{:S(2)}, u32[]{:S(2)}) collective-permute-start(f32[1536,128]{1,0:T(8,128)S(1)} %get-tuple-element.47.after_ref), channel_id=1, source_target_pairs={{28,0},{0,4},{4,8},{8,12},{12,16},{16,20},{20,24},{24,28},{29,1},{... | collective-permute-start | bytes 2359304 | tf_op jit(solution)/shard_map/ppermute | solution.py:34
  26.9 39.7 %collective-permute-start.9 = (f32[1024,128]{1,0:T(8,128)S(1)}, f32[1024,128]{1,0:T(8,128)S(1)}, u32[]{:S(2)}, u32[]{:S(2)}) collective-permute-start(f32[1024,128]{1,0:T(8,128)S(1)} %get-tuple-element.57), channel_id=1, source_target_pairs={{8,0},{12,4},{16,8},{20,12},{24,16},{28,20},{0,24},{4,28},{9,1},{1... | collective-permute-start | bytes 1572872 | tf_op jit(solution)/shard_map/ppermute | solution.py:34
  45.5 21.1 %collective-permute-start.6 = (f32[2,128]{1,0:T(2,128)S(1)}, f32[2,128]{1,0:T(2,128)S(1)}, u32[]{:S(2)}, u32[]{:S(2)}) collective-permute-start(f32[2,128]{1,0:T(2,128)S(1)} %get-tuple-element.53.after_ref), channel_id=1, source_target_pairs={{0,4},{1,29},{2,10},{3,27},{4,8},{5,1},{6,14},{7,31},{8,12},{9,5},... | collective-permute-start | bytes 3080 | tf_op jit(solution)/shard_map/ppermute | solution.py:28
  55.5 18.5 %collective-permute-start.4 = (f32[512,128]{1,0:T(8,128)S(1)}, f32[512,128]{1,0:T(8,128)S(1)}, u32[]{:S(2)}, u32[]{:S(2)}) collective-permute-start(f32[512,128]{1,0:T(8,128)S(1)} %send_scaled.1.sent_ref), channel_id=1, source_target_pairs={{8,0},{12,4},{16,8},{20,12},{24,16},{28,20},{0,24},{4,28},{9,1},{1... | collective-permute-start | bytes 786440 | tf_op jit(solution)/shard_map/ppermute | solution.py:34

commit v12 on v11

--- a/solution.py
+++ b/solution.py
@@ -22,6 +22,16 @@
     regions, members = lax.axis_size("region"), lax.axis_size("dest")
     route = [
         (r * members + d, (r + SHIFTS[d % 4]) % regions * members + d)
+        for r in range(regions)
+        for d in range(members)
+    ]
+    return lax.ppermute(block, ("region", "dest"), route)
+
+
+def to_two(block, first):
+    regions, members = lax.axis_size("region"), lax.axis_size("dest")
+    route = [
+        (r * members + d, (r + SHIFTS[first + d % 2]) % regions * members + d)
         for r in range(regions)
         for d in range(members)
     ]
@@ -265,29 +275,6 @@
             return carry
 
         lax.fori_loop(0, count // batch, body, 0)
-
-
-def scaled_send_kernel(
-    sizes, part, theta, send_node, send_outlet, flow, turns, after_ref, send
-):
-    cells, nodes, branches, cap, sub = sizes
-    side, start, count = part
-    batch = 8
-
-    def body(step, carry):
-        first = step * batch
-        values = []
-        for i in range(batch):
-            slot = side * padded(cap) + start + first + i
-            node = send_node[slot]
-            value = row_of(flow, node, sub)[...] * theta[node]
-            choice = row_of(turns, node, sub)[...]
-            values.append(jnp.where(choice == send_outlet[slot], value, 0.0))
-        for i in range(batch):
-            row_of(send, first + i, sub)[...] = values[i]
-        return carry
-
-    lax.fori_loop(0, count // batch, body, 0)
 
 
 def node_flow_kernel(sizes, in_cell, scaled, turns, after_ref, flow, demand, partial):
@@ -356,13 +343,14 @@
         ratio = room / jnp.maximum(demand[j * per_outlet : (j + 1) * per_outlet, :], room)
         tall = jnp.minimum(tall, jnp.where(stacked(outs) >= 0, ratio, 1.0))
     theta_out[...] = tall
-    slots = send_list[pl.ds(lax.axis_index("dest") % 4, 1), :]
-    put_row(slot_theta, 0, look_up(tall, jnp.where(slots >= 0, slots % nodes, 0)), 0.0)
-
-
-def keep_kernel(
-    sizes, theta_ref, node_in, node_out, fraction, sent_ref, arrived_ref, keep, home_theta
-):
+    per_side = padded(cap) // LANES
+    for k in range(2):
+        slots = send_list[pl.ds(2 * k + lax.axis_index("dest") % 2, 1), :]
+        there = look_up(tall, jnp.where(slots >= 0, slots % nodes, 0))
+        put_row(slot_theta, k * per_side, there, 0.0)
+
+
+def keep_kernel(sizes, theta_ref, node_in, node_out, fraction, after_ref, keep, home_theta):
     cells, nodes, branches, cap, sub = sizes
     height = cells // LANES
     region_no = lax.axis_index("region")
@@ -414,37 +402,31 @@
     lax.fori_loop(0, cells // batch, body, 0)
 
 
-def land_rows(sizes, parts, scale, land, received, base):
+def land_rows(sizes, scale, land, received, base):
     cells, nodes, branches, cap, sub = sizes
     batch = 8
-    for (side, start, count), rows in zip(parts, received):
-
-        def body(step, carry, side=side, start=start, rows=rows):
+    core = lax.axis_index("dest") % 2
+    for side, rows in enumerate(received):
+        offset = jnp.where(core == side % 2, 0, 2 * padded(cap)) + side // 2 * padded(cap)
+
+        def body(step, carry, side=side, rows=rows, offset=offset):
             first = step * batch
             stores = []
             for i in range(batch):
-                slot = side * padded(cap) + start + first + i
-                at = row_of(base, land[slot], sub)
-                value = row_of(rows, first + i, sub)[...]
-                if scale is not None:
-                    value = value * scale[slot]
+                at = row_of(base, land[side * padded(cap) + first + i], sub)
+                value = row_of(rows, first + i, sub)[...] * scale[offset + first + i]
                 stores.append((at, at[...] + value))
             for at, value in stores:
                 at[...] = value
             return carry
 
-        lax.fori_loop(0, count // batch, body, 0)
-
-
-def land_kernel(sizes, parts, scale, land, *rest):
-    received, (base_in, base) = rest[: len(parts)], rest[len(parts) :]
-    land_rows(sizes, parts, scale, land, received, base)
-
-
-def finish_kernel(sizes, parts, chunk, land, *rest):
-    cells, nodes, branches, cap, sub = sizes
-    received, (base_in, out, base, staged, sems) = rest[: len(parts)], rest[len(parts) :]
-    land_rows(sizes, parts, None, land, received, base)
+        lax.fori_loop(0, cap // batch, body, 0)
+
+
+def finish_kernel(sizes, chunk, scale, land, *rest):
+    cells, nodes, branches, cap, sub = sizes
+    received, (base_in, out, base, staged, sems) = rest[:4], rest[4:]
+    land_rows(sizes, scale, land, received, base)
     copies = []
     for number in range(cells // chunk):
 
@@ -531,10 +513,7 @@
     fraction = jnp.minimum(vehicles, cap_of) / vehicles
     supply = jnp.minimum(cap_of, wave.reshape(per_cell) * (jam.reshape(per_cell) - vehicles))
     rows_shape = pltpu.VMEM(((cells + 1) * sub, LANES), F32)
-    early = cap * 2 // 3 // 8 * 8
-    whole = [(side, 0, cap) for side in range(4)]
-    parts = (*whole[:3], (3, 0, early))
-    last_part = (3, early, cap - early)
+    parts = tuple((side, 0, cap) for side in range(4))
 
     def send_shape(part):
         return pltpu.VMEM((part[2] * sub, LANES), F32)
@@ -551,6 +530,7 @@
         cost_estimate=cost(1, 1),
         name="send_ahead",
     )(weights, in_cell, send_node, send_outlet, rows, turns)
+    ahead, supply_there = lax.optimization_barrier((ahead, supply_there))
     scaled = pl.pallas_call(
         functools.partial(scale_kernel, sizes),
         in_specs=[SMEM_WHOLE, VMEM_WHOLE, ANYWHERE, ANYWHERE],
@@ -595,13 +575,15 @@
         out_specs=[VMEM_WHOLE] * 2,
         out_shape=[
             jax.ShapeDtypeStruct((nodes // LANES, LANES), F32),
-            jax.ShapeDtypeStruct((padded(cap) // LANES, LANES), F32),
+            jax.ShapeDtypeStruct((2 * padded(cap) // LANES, LANES), F32),
         ],
         compiler_params=params(8),
         cost_estimate=cost(1, 1),
         name="theta",
     )(supply, shared, node_out, send_list)
-    theta_there = to_neighbours(slot_theta)
+    slot_theta, arrived[2] = lax.optimization_barrier((slot_theta, arrived[2]))
+    per_side = padded(cap) // LANES
+    theta_there = [to_two(slot_theta[:per_side], 0), to_two(slot_theta[per_side:], 2)]
 
     home = pl.pallas_call(
         functools.partial(home_kernel, sizes),
@@ -612,24 +594,15 @@
         cost_estimate=cost(1, 1),
         name="home_rows",
     )(source_node, source_outlet, turns, flow, slot_theta)
-    (behind,) = pl.pallas_call(
-        functools.partial(scaled_send_kernel, sizes, last_part),
-        in_specs=[SMEM_WHOLE] * 3 + [VMEM_WHOLE] * 2 + [ANYWHERE],
-        out_specs=[VMEM_WHOLE],
-        out_shape=[send_shape(last_part)],
-        compiler_params=params(4),
-        cost_estimate=cost(1, 1),
-        name="send_scaled",
-    )(theta.reshape(-1), send_node, send_outlet, flow, turns, home)
     keep, home_theta = pl.pallas_call(
         functools.partial(keep_kernel, sizes),
-        in_specs=[VMEM_WHOLE] * 4 + [ANYWHERE] * 2,
+        in_specs=[VMEM_WHOLE] * 4 + [ANYWHERE],
         out_specs=[VMEM_WHOLE] * 2,
         out_shape=[jax.ShapeDtypeStruct(per_cell, F32)] * 2,
         compiler_params=params(8),
         cost_estimate=cost(10000000, 1),
         name="keep",
-    )(theta, node_in, node_out, fraction, behind, arrived[2])
+    )(theta, node_in, node_out, fraction, home)
     base = pl.pallas_call(
         functools.partial(base_kernel, sizes),
         in_specs=[SMEM_WHOLE] * 2 + [VMEM_WHOLE] * 2,
@@ -640,35 +613,27 @@
         name="base_rows",
     )(keep.reshape(-1), home_theta.reshape(-1), rows, home)
 
-    base, theta_there, *arrived = lax.optimization_barrier((base, theta_there, *arrived))
-    last = shifted(behind, "region", SHIFTS[3])
-    scale = lax.all_gather(theta_there, "dest", axis=0, tiled=True)[: list_shape[0]]
-
-    base = pl.pallas_call(
-        functools.partial(land_kernel, sizes, parts),
+    base, *rest = lax.optimization_barrier((base, *theta_there, *arrived))
+    theta_there, arrived = rest[:2], rest[2:]
+    got = jnp.concatenate(theta_there)
+    members = lax.axis_size("dest")
+    other = lax.ppermute(got, "dest", [(i, i ^ 1) for i in range(members)])
+    scale = jnp.concatenate([got, other])
+
+    out, _ = pl.pallas_call(
+        functools.partial(finish_kernel, sizes, chunk),
         in_specs=[SMEM_WHOLE] * 2 + [VMEM_WHOLE] * 5,
-        out_specs=VMEM_WHOLE,
-        out_shape=rows_shape,
-        input_output_aliases={6: 0},
-        compiler_params=params(4),
-        cost_estimate=cost(100000000000, 1),
-        name="land_first",
-    )(scale.reshape(-1), land, *arrived, base)
-
-    out, _ = pl.pallas_call(
-        functools.partial(finish_kernel, sizes, (last_part,), chunk),
-        in_specs=[SMEM_WHOLE] + [VMEM_WHOLE] * 2,
         out_specs=[ANYWHERE, VMEM_WHOLE],
         out_shape=[jax.ShapeDtypeStruct((cells, width), F32), rows_shape],
         scratch_shapes=[
             pltpu.VMEM((cells, width), F32),
             pltpu.SemaphoreType.DMA((cells // chunk,)),
         ],
-        input_output_aliases={2: 1},
+        input_output_aliases={6: 1},
         compiler_params=params(12),
         cost_estimate=cost(cells * width, cells * row_bytes),
         name="finish",
-    )(land, last, base)
+    )(scale.reshape(-1), land, *arrived, base)
     return out
 
 

time: 78.9 us -> 80.6 us (1.022)
  blocking collectives: 11 us -> 5.34 us
  waiting for transfers between devices: 6.38 us -> 11.8 us
  starting transfers between devices: 14.2 us -> 17.4 us
    ppermute x5 -> x4, waiting for transfers between devices: 0.01 us -> 7.95 us  [shifted(): return lax.ppermute(block, axis, route)]
    ppermute x0 -> x3, starting transfers between devices: none -> 6.82 us  [the longest x2 6.75 us: to_two(): return lax.ppermute(block, ('region', 'dest'), route)]
    all_gather x1 -> x0, blocking collectives: 5.07 us -> none  [on_device(): lax.all_gather(theta_there, 'dest', axis=0, tiled=True)[:list_shape[0]]]
    ppermute x2 -> x1, waiting for transfers between devices: 5.93 us -> 2.19 us  [to_neighbours(): return lax.ppermute(block, ('region', 'dest'), route)]
    ppermute x2 -> x1, starting transfers between devices: 5.24 us -> 1.57 us  [to_neighbours(): return lax.ppermute(block, ('region', 'dest'), route)]
    pallas_call x3 -> x1, Pallas kernels: 7.42 us -> 6.14 us  [on_device(): pl.pallas_call(functools.partial(finish_kernel, sizes, chunk), in_specs=[...]
    ppermute x0 -> x3, waiting for transfers between devices: none -> 1.19 us  [the longest x1 1.14 us: on_device(): other = lax.ppermute(got, 'dest', [(i, i ^ 1) for i in range(members)])]
    ppermute x5 -> x4, starting transfers between devices: 5.84 us -> 5.9 us  [shifted(): return lax.ppermute(block, axis, route)]
  transfers between devices with their start and end apart: 10 -> 11, of which waited for: 3 -> 4; matrix products, arithmetic and copies ran while one was open for 0% -> 0% of each run, Pallas kernels for 48% -> 43%
where the time goes in v12:
time: 80.6 us; the launch traced here: 80.4 us
  Pallas kernels  45.7 us (57%)
  starting transfers between devices  17.4 us (22%)
  waiting for transfers between devices  11.8 us (15%)
  blocking collectives  5.34 us (7%)
    pallas_call x1, Pallas kernels, on_device(): pl.pallas_call(functools.partial(node_flow_kernel, sizes), in_specs=[SMEM...  10.1 us
    ppermute x4, waiting for transfers between devices, shifted(): return lax.ppermute(block, axis, route)  7.95 us
    ppermute x2, starting transfers between devices, to_two(): return lax.ppermute(block, ('region', 'dest'), route)  6.75 us
    pallas_call x1, Pallas kernels, on_device(): pl.pallas_call(functools.partial(finish_kernel, sizes, chunk), in_specs=[...  6.14 us
    ppermute x4, starting transfers between devices, shifted(): return lax.ppermute(block, axis, route)  5.9 us
    pallas_call x1, Pallas kernels, on_device(): pl.pallas_call(functools.partial(home_kernel, sizes), in_specs=[SMEM_WHOL...  5.38 us
    all_gather x1, blocking collectives, on_device(): shared = lax.all_gather(joined, 'dest', axis=0, tiled=True)  5.34 us
    pallas_call x1, Pallas kernels, on_device(): pl.pallas_call(functools.partial(send_kernel, sizes, (parts[0], parts[1],...  4.82 us
  transfers between devices with their start and end apart: 11, of which 4 were waited for; matrix products, arithmetic and copies ran while one was open for 0% of the time, Pallas kernels for 43%

profile of v12, /device:TPU:0, one launch (start us, length us, event | category | flops | bytes accessed | tf_op | source)
XLA Modules:
  0.0 80.4 jit_solution(8791183497380992094)
XLA Ops:
  0.0 4.7 %cell_sum.1 = (f32[16,128]{1,0:T(8,128)S(1)}, f32[16392,128]{1,0:T(8,128)S(1)}) custom-call(f32[2048,1024]{1,0:T(8,128)} %x_hbm.2), custom_call_target="tpu_custom_call" | custom-call | flops 2097152 | bytes 8388608 | tf_op jit(solution)/shard_map/cell_sum/pallas_call | solution.py:468
  4.7 2.4 %collective-permute-start.2 = (f32[16,128]{1,0:T(8,128)S(1)}, f32[16,128]{1,0:T(8,128)S(1)}, u32[]{:S(2)}, u32[]{:S(2)}) collective-permute-start(f32[16,128]{1,0:T(8,128)S(1)} %get-tuple-element.42.after_ref), channel_id=1, source_target_pairs={{0,3},{1,2},{2,1},{3,0},{4,7},{5,6},{6,5},{7,4},{8,11},{9,10},{10,... | collective-permute-start | bytes 24584 | tf_op jit(solution)/shard_map/ppermute | solution.py:50
  7.2 0.6 collective-permute-start.1
  7.8 0.0 collective-permute-start
  7.9 2.5 %turn_rows.1 = (s32[8192,128]{1,0:T(8,128)S(1)}, s32[32,128]{1,0:T(8,128)S(1)}, s32[8,128]{1,0:T(8,128)S(1)}, s32[8,128]{1,0:T(8,128)S(1)}, s32[8,128]{1,0:T(8,1...) custom-call(s32[1024,1024]{1,0:T(8,128)} %x_hbm.3, f32[16,128]{1,0:T(8,128)S(1)} %get-tuple-element.42.after_ref, ...), custom_call_target="tpu_custom_call" | custom-call | bytes 4194304 | tf_op jit(solution)/shard_map/turn_rows/pallas_call | solution.py:488
  10.4 0.0 collective-permute-done.2
  10.4 0.4 collective-permute-done.1
  10.8 0.0 collective-permute-done
  10.9 1.6 %collective-permute-start.3 = (f32[16,128]{1,0:T(8,128)S(1)}, f32[16,128]{1,0:T(8,128)S(1)}, u32[]{:S(2)}, u32[]{:S(2)}) collective-permute-start(f32[16,128]{1,0:T(8,128)S(1)} %fusion.1.supply), channel_id=1, source_target_pairs={{0,4},{1,29},{2,10},{3,27},{4,8},{5,1},{6,14},{7,31},{8,12},{9,5},... | collective-permute-start | bytes 24584 | tf_op jit(solution)/shard_map/ppermute | solution.py:28
  12.5 2.6 %send_ahead.1.sent_ref = f32[1536,128]{1,0:T(8,128)S(1)} custom-call(f32[2176]{0:T(1024)S(1)} %concatenate.13.fraction, s32[4096]{0:T(1024)S(1)} %bitcast.22, s32[1024]{0:T(1024)S(1)} %bitcast.27, s32[1024]{0:T(1024)S(1)} %bitcast.29, f32[16392,128]{1,0:T(8,128)S(1)} %get-tuple-element.47.rows, s32[8192,128]{1,0:T(8,128)S(1)} %get-tuple-element.50.turns), custom_call_target="tpu_custom_call" | custom-call | flops 1 | bytes 1 | tf_op jit(solution)/shard_map/send_ahead/pallas_call | solution.py:524
  15.1 2.2 %collective-permute-done.3.supply_ref = f32[16,128]{1,0:T(8,128)S(1)} collective-permute-done((f32[16,128]{1,0:T(8,128)S(1)}, f32[16,128]{1,0:T(8,128)S(1)}, u32[]{:S(2)}, u32[]{:S(2)}) %collective-permute-start.3) | collective-permute-done | bytes 8224 | tf_op jit(solution)/shard_map/ppermute | solution.py:28
  17.3 0.0 collective-permute-start.4
  17.3 2.5 %scale_rows.1.rows.scaled = f32[16392,128]{1,0:T(8,128)S(1)} custom-call(f32[2048]{0:T(1024)S(1)} %bitcast.26, f32[16392,128]{1,0:T(8,128)S(1)} %get-tuple-element.47.rows, f32[1536,128]{1,0:T(8,128)S(1)} %send_ahead.1.sent_ref, f32[16,128]{1,0:T(8,128)S(1)} %collective-permute-done.3.supply_ref), custom_call_target="tpu_custom_call" | custom-call | flops 1 | bytes 1 | tf_op jit(solution)/shard_map/scale_rows/pallas_call | solution.py:534
  19.8 4.8 %send_near.1 = (f32[1536,128]{1,0:T(8,128)S(1)}, f32[1536,128]{1,0:T(8,128)S(1)}, f32[1536,128]{1,0:T(8,128)S(1)}) custom-call(s32[4096]{0:T(1024)S(1)} %bitcast.23, s32[1024]{0:T(1024)S(1)} %bitcast.28, s32[1024]{0:T(1024)S(1)} %bitcast.30, f32[16392,128]{1,0:T(8,128)S(1)} %scale_rows.1.rows.scaled, s32[8192,128]{1,0:T(8,128)S(1)} %get-tuple-element.50.turns), custom_call_target="tpu_custom_call" | custom-call | flops 1 | bytes 1 | tf_op jit(solution)/shard_map/send_near/pallas_call | solution.py:543
  24.6 2.7 %collective-permute-start.8 = (f32[1536,128]{1,0:T(8,128)S(1)}, f32[1536,128]{1,0:T(8,128)S(1)}, u32[]{:S(2)}, u32[]{:S(2)}) collective-permute-start(f32[1536,128]{1,0:T(8,128)S(1)} %get-tuple-element.63), channel_id=1, source_target_pairs={{4,0},{8,4},{12,8},{16,12},{20,16},{24,20},{28,24},{0,28},{5,1},{9... | collective-permute-start | bytes 2359304 | tf_op jit(solution)/shard_map/ppermute | solution.py:44
  27.3 1.2 %collective-permute-start.9 = (f32[1536,128]{1,0:T(8,128)S(1)}, f32[1536,128]{1,0:T(8,128)S(1)}, u32[]{:S(2)}, u32[]{:S(2)}) collective-permute-start(f32[1536,128]{1,0:T(8,128)S(1)} %get-tuple-element.65), channel_id=1, source_target_pairs={{8,0},{12,4},{16,8},{20,12},{24,16},{28,20},{0,24},{4,28},{9,1},{1... | collective-permute-start | bytes 2359304 | tf_op jit(solution)/shard_map/ppermute | solution.py:44
  28.6 2.0 %collective-permute-start.7 = (f32[1536,128]{1,0:T(8,128)S(1)}, f32[1536,128]{1,0:T(8,128)S(1)}, u32[]{:S(2)}, u32[]{:S(2)}) collective-permute-start(f32[1536,128]{1,0:T(8,128)S(1)} %get-tuple-element.53.after_ref), channel_id=1, source_target_pairs={{28,0},{0,4},{4,8},{8,12},{12,16},{16,20},{20,24},{24,28},{29,1},{... | collective-permute-start | bytes 2359304 | tf_op jit(solution)/shard_map/ppermute | solution.py:44
  30.5 10.1 %node_flow.1 = (f32[8192,128]{1,0:T(8,128)S(1)}, f32[32,128]{1,0:T(8,128)S(1)}) custom-call(s32[4096]{0:T(1024)S(1)} %bitcast.24, f32[16392,128]{1,0:T(8,128)S(1)} %scale_rows.1.rows.scaled, s32[8192,128]{1,0:T(8,128)S(1)} %get-tuple-element.50.turns, f32[1536,128]{1,0:T(8,128)S(1)} %get-tuple-element.53.after_ref), custom_call_target="tpu_custom_call" | custom-call | flops 1 | bytes 1 | tf_op jit(solution)/shard_map/node_flow/pallas_call | solution.py:556
  40.7 5.3 %all_gather.3.shared = f32[192,128]{1,0:T(8,128)S(1)} all-gather(f32[48,128]{1,0:T(8,128)S(1)} %pad_maximum_fusion), channel_id=1, replica_groups=mesh['region'=8,'dest'=4] {'dest'}, dimensions={0}, use_global_device_ids=true | all-gather | bytes 122880 | tf_op jit(solution)/shard_map/all_gather | solution.py:571
  46.0 1.5 %theta.1 = (f32[8,128]{1,0:T(8,128)S(1)}, f32[4,128]{1,0:T(4,128)S(1)}) custom-call(f32[16,128]{1,0:T(8,128)S(1)} %fusion.1.supply, f32[192,128]{1,0:T(8,128)S(1)} %all_gather.3.shared, s32[4,1024]{1,0:T(4,128)S(1)} %copy-done, s32[4,192]{1,0:T(4,128)S(1)} %copy-done.2), custom_call_target="tpu_custom_call" | custom-call | flops 1 | bytes 1 | tf_op jit(solution)/shard_map/theta/pallas_call | solution.py:572
  47.5 0.1 collective-permute-start.6
  47.6 6.7 %collective-permute-start.5 = (f32[2,128]{1,0:T(2,128)S(1)}, f32[2,128]{1,0:T(2,128)S(1)}, u32[]{:S(2)}, u32[]{:S(2)}) collective-permute-start(f32[2,128]{1,0:T(2,128)S(1)} %get-tuple-element.78), channel_id=1, source_target_pairs={{0,4},{1,29},{2,6},{3,31},{4,8},{5,1},{6,10},{7,3},{8,12},{9,5},{1... | collective-permute-start | bytes 3080 | tf_op jit(solution)/shard_map/ppermute | solution.py:38
  54.3 5.4 %home_rows.1.after_ref.home = f32[16392,128]{1,0:T(8,128)S(1)} custom-call(s32[2048]{0:T(1024)S(1)} %bitcast.31, s32[2048]{0:T(1024)S(1)} %bitcast.32, s32[8192,128]{1,0:T(8,128)S(1)} %get-tuple-element.50.turns, f32[8192,128]{1,0:T(8,128)S(1)} %get-tuple-element.58.flow, f32[4,128]{1,0:T(4,128)S(1)} %get-tuple-element.60.after_ref), custom_call_target="tpu_custom_call" | custom-call | flops 1 | bytes 1 | tf_op jit(solution)/shard_map/home_rows/pallas_call | solution.py:588
  59.6 0.7 keep.1
  60.3 4.7 %base_rows.1.rest_4_ = f32[16392,128]{1,0:T(8,128)S(1)} custom-call(f32[2048]{0:T(1024)S(1)} %bitcast.33, f32[2048]{0:T(1024)S(1)} %bitcast.34, f32[16392,128]{1,0:T(8,128)S(1)} %get-tuple-element.47.rows, f32[16392,128]{1,0:T(8,128)S(1)} %home_rows.1.after_ref.home), custom_call_target="tpu_custom_call" | custom-call | flops 10000000 | bytes 1 | tf_op jit(solution)/shard_map/base_rows/pallas_call | solution.py:606
  65.1 7.9 %collective-permute-done.9.rest_3_ = f32[1536,128]{1,0:T(8,128)S(1)} collective-permute-done((f32[1536,128]{1,0:T(8,128)S(1)}, f32[1536,128]{1,0:T(8,128)S(1)}, u32[]{:S(2)}, u32[]{:S(2)}) %collective-permute-start.9) | collective-permute-done | bytes 786464 | tf_op jit(solution)/shard_map/ppermute | solution.py:44
  73.0 0.0 collective-permute-done.7.rest_0_
  73.0 0.0 collective-permute-done.6
  73.1 0.0 collective-permute-done.5
  73.1 0.1 collective-permute-start.10
  73.2 1.1 %collective-permute-done.10 = f32[4,128]{1,0:T(4,128)S(1)} collective-permute-done((f32[4,128]{1,0:T(4,128)S(1)}, f32[4,128]{1,0:T(4,128)S(1)}, u32[]{:S(2)}, u32[]{:S(2)}) %collective-permute-start.10) | collective-permute-done | bytes 2080 | tf_op jit(solution)/shard_map/ppermute | solution.py:620
  74.3 6.1 %finish.1 = (f32[2048,1024]{1,0:T(8,128)}, f32[16392,128]{1,0:T(8,128)S(1)}) custom-call(f32[1024]{0:T(1024)S(1)} %maximum_bitcast_fusion.scale, s32[1024]{0:T(1024)S(1)} %bitcast.35, f32[1536,128]{1,0:T(8,128)S(1)} %collective-permute-done.7.rest_0_, f32[1536,128]{1,0:T(8,128)S(1)} %collective-permute-done.8.rest_1_, ...), custom_call_target="tpu_custom_call", output_to_operand_aliasing={{1}: (6, {})} | custom-call | flops 2097152 | bytes 8388608 | tf_op jit(solution)/shard_map/finish/pallas_call | solution.py:623
  (23 shorter events, 0.1 us)
Async XLA Ops:
  0.0 7.9 %copy-start = (s32[4,1024]{1,0:T(4,128)S(1)}, s32[4,1024]{1,0:T(4,128)}, u32[]{:S(2)}) copy-start(s32[4,1024]{1,0:T(4,128)} %node_out.3) | copy-start | bytes 49156
  0.0 7.9 %copy-start.2 = (s32[4,192]{1,0:T(4,128)S(1)}, s32[4,192]{1,0:T(4,128)}, u32[]{:S(2)}) copy-start(s32[4,192]{1,0:T(4,128)} %send_list.1) | copy-start | bytes 9220
  0.0 7.9 %copy-start.1 = (s32[4,1024]{1,0:T(4,128)S(1)}, s32[4,1024]{1,0:T(4,128)}, u32[]{:S(2)}) copy-start(s32[4,1024]{1,0:T(4,128)} %node_in.1) | copy-start | bytes 49156
  0.0 7.9 %copy-start.3 = (s32[4,192]{1,0:T(4,128)S(1)}, s32[4,192]{1,0:T(4,128)}, u32[]{:S(2)}) copy-start(s32[4,192]{1,0:T(4,128)} %rest_3_.1) | copy-start | bytes 9220
  0.0 10.8 %copy-start.4 = (f32[2048]{0:T(1024)S(1)}, f32[2048]{0:T(1024)}, u32[]{:S(2)}) copy-start(f32[2048]{0:T(1024)} %param.10) | copy-start | bytes 24580
  0.0 10.9 %copy-start.6 = (f32[2048]{0:T(1024)S(1)}, f32[2048]{0:T(1024)}, u32[]{:S(2)}) copy-start(f32[2048]{0:T(1024)} %param.12) | copy-start | bytes 24580
  0.0 10.9 %copy-start.5 = (f32[2048]{0:T(1024)S(1)}, f32[2048]{0:T(1024)}, u32[]{:S(2)}) copy-start(f32[2048]{0:T(1024)} %param.11) | copy-start | bytes 24580
  4.7 5.6 %collective-permute-start.2 = (f32[16,128]{1,0:T(8,128)S(1)}, f32[16,128]{1,0:T(8,128)S(1)}, u32[]{:S(2)}, u32[]{:S(2)}) collective-permute-start(f32[16,128]{1,0:T(8,128)S(1)} %get-tuple-element.42.after_ref), channel_id=1, source_target_pairs={{0,3},{1,2},{2,1},{3,0},{4,7},{5,6},{6,5},{7,4},{8,11},{9,10},{10,... | collective-permute-start | bytes 24584 | tf_op jit(solution)/shard_map/ppermute | solution.py:50
  7.2 3.7 %collective-permute-start.1 = (f32[16,128]{1,0:T(8,128)S(1)}, f32[16,128]{1,0:T(8,128)S(1)}, u32[]{:S(2)}, u32[]{:S(2)}) collective-permute-start(f32[16,128]{1,0:T(8,128)S(1)} %get-tuple-element.42.after_ref), channel_id=1, source_target_pairs={{0,2},{1,3},{2,0},{3,1},{4,6},{5,7},{6,4},{7,5},{8,10},{9,11},{10,... | collective-permute-start | bytes 24584 | tf_op jit(solution)/shard_map/ppermute | solution.py:50
  7.8 3.0 %collective-permute-start = (f32[16,128]{1,0:T(8,128)S(1)}, f32[16,128]{1,0:T(8,128)S(1)}, u32[]{:S(2)}, u32[]{:S(2)}) collective-permute-start(f32[16,128]{1,0:T(8,128)S(1)} %get-tuple-element.42.after_ref), channel_id=1, source_target_pairs={{0,1},{1,0},{2,3},{3,2},{4,5},{5,4},{6,7},{7,6},{8,9},{9,8},{10,11... | collective-permute-start | bytes 24584 | tf_op jit(solution)/shard_map/ppermute | solution.py:50
  10.9 6.4 %collective-permute-start.3 = (f32[16,128]{1,0:T(8,128)S(1)}, f32[16,128]{1,0:T(8,128)S(1)}, u32[]{:S(2)}, u32[]{:S(2)}) collective-permute-start(f32[16,128]{1,0:T(8,128)S(1)} %fusion.1.supply), channel_id=1, source_target_pairs={{0,4},{1,29},{2,10},{3,27},{4,8},{5,1},{6,14},{7,31},{8,12},{9,5},... | collective-permute-start | bytes 24584 | tf_op jit(solution)/shard_map/ppermute | solution.py:28
  17.3 30.2 %collective-permute-start.4 = (f32[1536,128]{1,0:T(8,128)S(1)}, f32[1536,128]{1,0:T(8,128)S(1)}, u32[]{:S(2)}, u32[]{:S(2)}) collective-permute-start(f32[1536,128]{1,0:T(8,128)S(1)} %send_ahead.1.sent_ref), channel_id=1, source_target_pairs={{24,0},{28,4},{0,8},{4,12},{8,16},{12,20},{16,24},{20,28},{25,1},{... | collective-permute-start | bytes 2359304 | tf_op jit(solution)/shard_map/ppermute | solution.py:44
  24.6 40.4 %collective-permute-start.8 = (f32[1536,128]{1,0:T(8,128)S(1)}, f32[1536,128]{1,0:T(8,128)S(1)}, u32[]{:S(2)}, u32[]{:S(2)}) collective-permute-start(f32[1536,128]{1,0:T(8,128)S(1)} %get-tuple-element.63), channel_id=1, source_target_pairs={{4,0},{8,4},{12,8},{16,12},{20,16},{24,20},{28,24},{0,28},{5,1},{9... | collective-permute-start | bytes 2359304 | tf_op jit(solution)/shard_map/ppermute | solution.py:44
  27.3 45.7 %collective-permute-start.9 = (f32[1536,128]{1,0:T(8,128)S(1)}, f32[1536,128]{1,0:T(8,128)S(1)}, u32[]{:S(2)}, u32[]{:S(2)}) collective-permute-start(f32[1536,128]{1,0:T(8,128)S(1)} %get-tuple-element.65), channel_id=1, source_target_pairs={{8,0},{12,4},{16,8},{20,12},{24,16},{28,20},{0,24},{4,28},{9,1},{1... | collective-permute-start | bytes 2359304 | tf_op jit(solution)/shard_map/ppermute | solution.py:44
  28.6 44.4 %collective-permute-start.7 = (f32[1536,128]{1,0:T(8,128)S(1)}, f32[1536,128]{1,0:T(8,128)S(1)}, u32[]{:S(2)}, u32[]{:S(2)}) collective-permute-start(f32[1536,128]{1,0:T(8,128)S(1)} %get-tuple-element.53.after_ref), channel_id=1, source_target_pairs={{28,0},{0,4},{4,8},{8,12},{12,16},{16,20},{20,24},{24,28},{29,1},{... | collective-permute-start | bytes 2359304 | tf_op jit(solution)/shard_map/ppermute | solution.py:44
  47.5 25.6 %collective-permute-start.6 = (f32[2,128]{1,0:T(2,128)S(1)}, f32[2,128]{1,0:T(2,128)S(1)}, u32[]{:S(2)}, u32[]{:S(2)}) collective-permute-start(f32[2,128]{1,0:T(2,128)S(1)} %get-tuple-element.77), channel_id=1, source_target_pairs={{0,8},{1,25},{2,10},{3,27},{4,12},{5,29},{6,14},{7,31},{8,16},{9,1... | collective-permute-start | bytes 3080 | tf_op jit(solution)/shard_map/ppermute | solution.py:38
  47.6 25.5 %collective-permute-start.5 = (f32[2,128]{1,0:T(2,128)S(1)}, f32[2,128]{1,0:T(2,128)S(1)}, u32[]{:S(2)}, u32[]{:S(2)}) collective-permute-start(f32[2,128]{1,0:T(2,128)S(1)} %get-tuple-element.78), channel_id=1, source_target_pairs={{0,4},{1,29},{2,6},{3,31},{4,8},{5,1},{6,10},{7,3},{8,12},{9,5},{1... | collective-permute-start | bytes 3080 | tf_op jit(solution)/shard_map/ppermute | solution.py:38
  73.1 1.2 %collective-permute-start.10 = (f32[4,128]{1,0:T(4,128)S(1)}, f32[4,128]{1,0:T(4,128)S(1)}, u32[]{:S(2)}, u32[]{:S(2)}) collective-permute-start(f32[4,128]{1,0:T(4,128)S(1)} %pad_maximum_fusion.1), channel_id=1, source_target_pairs={{0,1},{1,0},{2,3},{3,2},{4,5},{5,4},{6,7},{7,6},{8,9},{9,8},{10,11... | collective-permute-start | bytes 6152 | tf_op jit(solution)/shard_map/ppermute | solution.py:620

commit v13 on v9

--- a/solution.py
+++ b/solution.py
@@ -8,7 +8,6 @@
 from jax.sharding import PartitionSpec as P
 
 SHIFTS = (1, -1, 2, -2)
-EXACT = lax.Precision.HIGHEST
 LANES = 128
 MIB = 1 << 20
 F32 = jnp.float32
@@ -28,6 +27,16 @@
     return lax.ppermute(block, ("region", "dest"), route)
 
 
+def to_two(block, first):
+    regions, members = lax.axis_size("region"), lax.axis_size("dest")
+    route = [
+        (r * members + d, (r + SHIFTS[first + d % 2]) % regions * members + d)
+        for r in range(regions)
+        for d in range(members)
+    ]
+    return lax.ppermute(block, ("region", "dest"), route)
+
+
 def shifted(block, axis, distance):
     devices = range(lax.axis_size(axis))
     route = [((i - distance) % len(devices), i) for i in devices]
@@ -57,9 +66,11 @@
 
 
 def lane_sums(partial):
-    sums = jnp.dot(
-        partial, jnp.ones((LANES, LANES), F32), preferred_element_type=F32, precision=EXACT
+    count = partial.shape[0]
+    parts = jnp.dot(
+        in_parts(partial), jnp.ones((LANES, LANES), jnp.bfloat16), preferred_element_type=F32
     )
+    sums = parts[:count, :] + parts[count : 2 * count, :] + parts[2 * count :, :]
     row = lax.broadcasted_iota(I32, (LANES, LANES), 0)
     lane = lax.broadcasted_iota(I32, (LANES, LANES), 1)
     pieces = [
@@ -248,7 +259,7 @@
 
 def send_kernel(sizes, sides, fraction, in_cell, send_node, send_outlet, rows, turns, *sends):
     cells, nodes, branches, cap, sub = sizes
-    batch = 8
+    batch = 16
     for side, send in zip(sides, sends):
 
         def body(step, carry, side=side, send=send):
@@ -269,7 +280,7 @@
 
 def scaled_send_kernel(sizes, side, theta, send_node, send_outlet, flow, turns, send):
     cells, nodes, branches, cap, sub = sizes
-    batch = 8
+    batch = 16
 
     def body(step, carry):
         first = step * batch
@@ -291,11 +302,11 @@
     cells, nodes, branches, cap, sub = sizes
 
     def gather(step, carry):
-        first = step * 8
+        first = step * 16
         values = [
-            gathered_flow(first + i, in_cell, None, scaled, sizes) for i in range(8)
+            gathered_flow(first + i, in_cell, None, scaled, sizes) for i in range(16)
         ]
-        for i in range(8):
+        for i in range(16):
             row_of(flow, first + i, sub)[...] = values[i]
         return carry
 
@@ -314,7 +325,7 @@
                 partial[j, pl.ds(pl.multiple_of(first, 8), 8), :] = totals[j]
         return carry
 
-    lax.fori_loop(0, nodes // 8, gather, 0)
+    lax.fori_loop(0, nodes // 16, gather, 0)
     lax.fori_loop(0, nodes // 16, measure, 0)
     per_outlet = nodes // LANES
     for j in range(branches):
@@ -353,8 +364,11 @@
         ratio = room / jnp.maximum(demand[j * per_outlet : (j + 1) * per_outlet, :], room)
         tall = jnp.minimum(tall, jnp.where(stacked(outs) >= 0, ratio, 1.0))
     theta_out[...] = tall
-    slots = send_list[pl.ds(lax.axis_index("dest") % 4, 1), :]
-    put_row(slot_theta, 0, look_up(tall, jnp.where(slots >= 0, slots % nodes, 0)), 0.0)
+    per_side = padded(cap) // LANES
+    for k in range(2):
+        slots = send_list[pl.ds(2 * k + lax.axis_index("dest") % 2, 1), :]
+        there = look_up(tall, jnp.where(slots >= 0, slots % nodes, 0))
+        put_row(slot_theta, k * per_side, there, 0.0)
 
 
 def keep_kernel(
@@ -376,7 +390,7 @@
 
 def home_kernel(sizes, source, outlet, turns, flow, after_ref, home):
     cells, nodes, branches, cap, sub = sizes
-    batch = 8
+    batch = 16
 
     def body(step, carry):
         first = step * batch
@@ -395,7 +409,7 @@
 
 def base_kernel(sizes, keep, home_theta, rows, home, base):
     cells, nodes, branches, cap, sub = sizes
-    batch = 8
+    batch = 16
 
     def body(step, carry):
         first = step * batch
@@ -413,18 +427,19 @@
 
 def land_rows(sizes, sides, scale, land, received, base):
     cells, nodes, branches, cap, sub = sizes
-    batch = 8
+    batch = 16
+    core = lax.axis_index("dest") % 2
     for side, rows in zip(sides, received):
-
-        def body(step, carry, side=side, rows=rows):
+        offset = jnp.where(core == side % 2, 0, 2 * padded(cap)) + side // 2 * padded(cap)
+
+        def body(step, carry, side=side, rows=rows, offset=offset):
             first = step * batch
             stores = []
             for i in range(batch):
-                slot = side * padded(cap) + first + i
-                at = row_of(base, land[slot], sub)
+                at = row_of(base, land[side * padded(cap) + first + i], sub)
                 value = row_of(rows, first + i, sub)[...]
                 if scale is not None:
-                    value = value * scale[slot]
+                    value = value * scale[offset + first + i]
                 stores.append((at, at[...] + value))
             for at, value in stores:
                 at[...] = value
@@ -541,6 +556,7 @@
         cost_estimate=cost(1, 1),
         name="send_ahead",
     )(weights, in_cell, send_node, send_outlet, rows, turns)
+    ahead, supply_there = lax.optimization_barrier((ahead, supply_there))
     scaled = pl.pallas_call(
         functools.partial(scale_kernel, sizes),
         in_specs=[SMEM_WHOLE, VMEM_WHOLE, ANYWHERE, ANYWHERE],
@@ -585,13 +601,15 @@
         out_specs=[VMEM_WHOLE] * 2,
         out_shape=[
             jax.ShapeDtypeStruct((nodes // LANES, LANES), F32),
-            jax.ShapeDtypeStruct((padded(cap) // LANES, LANES), F32),
+            jax.ShapeDtypeStruct((2 * padded(cap) // LANES, LANES), F32),
         ],
         compiler_params=params(8),
         cost_estimate=cost(1, 1),
         name="theta",
     )(supply, shared, node_out, send_list)
-    theta_there = to_neighbours(slot_theta)
+    theta, slot_theta, arrived[2] = lax.optimization_barrier((theta, slot_theta, arrived[2]))
+    per_side = padded(cap) // LANES
+    theta_there = [to_two(slot_theta[:per_side], 0), to_two(slot_theta[per_side:], 2)]
 
     (behind,) = pl.pallas_call(
         functools.partial(scaled_send_kernel, sizes, 3),
@@ -608,7 +626,7 @@
         out_specs=VMEM_WHOLE,
         out_shape=rows_shape,
         compiler_params=params(4),
-        cost_estimate=cost(1, 1),
+        cost_estimate=cost(4000000000, 1),
         name="home_rows",
     )(source_node, source_outlet, turns, flow, behind)
     keep, home_theta = pl.pallas_call(
@@ -630,9 +648,13 @@
         name="base_rows",
     )(keep.reshape(-1), home_theta.reshape(-1), rows, home)
 
-    base, theta_there, *arrived = lax.optimization_barrier((base, theta_there, *arrived))
+    base, *rest = lax.optimization_barrier((base, *theta_there, *arrived))
+    theta_there, arrived = rest[:2], rest[2:]
     last = shifted(behind, "region", SHIFTS[3])
-    scale = lax.all_gather(theta_there, "dest", axis=0, tiled=True)[: list_shape[0]]
+    got = jnp.concatenate(theta_there)
+    members = lax.axis_size("dest")
+    other = lax.ppermute(got, "dest", [(i, i ^ 1) for i in range(members)])
+    scale = jnp.concatenate([got, other])
 
     base = pl.pallas_call(
         functools.partial(land_kernel, sizes, (0, 1, 2)),
@@ -641,7 +663,7 @@
         out_shape=rows_shape,
         input_output_aliases={5: 0},
         compiler_params=params(4),
-        cost_estimate=cost(100000000000, 1),
+        cost_estimate=cost(4000000000, 1),
         name="land_first",
     )(scale.reshape(-1), land, *arrived, base)
 

time: 78.9 us -> 77.1 us (0.977)
  the two profiles are of different devices: /device:TPU:25 before, /device:TPU:0 now
where the time goes in v13:
time: 77.1 us; the launch traced here: 76.9 us
  Pallas kernels  42.4 us (55%)
  waiting for transfers between devices  15.2 us (20%)
  starting transfers between devices  12.9 us (17%)
  blocking collectives  6.1 us (8%)
    ppermute x4, waiting for transfers between devices, shifted(): return lax.ppermute(block, axis, route)  11.4 us
    pallas_call x1, Pallas kernels, on_device(): pl.pallas_call(functools.partial(node_flow_kernel, sizes), in_specs=[SMEM...  8.97 us
    all_gather x1, blocking collectives, on_device(): shared = lax.all_gather(joined, 'dest', axis=0, tiled=True)  6.1 us
    ppermute x4, starting transfers between devices, shifted(): return lax.ppermute(block, axis, route)  5.88 us
    pallas_call x1, Pallas kernels, on_device(): pl.pallas_call(functools.partial(home_kernel, sizes), in_specs=[SMEM_WHOL...  4.63 us
    pallas_call x1, Pallas kernels, on_device(): pl.pallas_call(functools.partial(finish_kernel, sizes, (3,), chunk), in_s...  4.48 us
    pallas_call x1, Pallas kernels, on_device(): pl.pallas_call(functools.partial(cell_sum_kernel, chunk, sub), in_specs=[...  4.31 us
    pallas_call x1, Pallas kernels, on_device(): pl.pallas_call(functools.partial(base_kernel, sizes), in_specs=[SMEM_WHOL...  3.85 us
  transfers between devices with their start and end apart: 11, of which 6 were waited for; matrix products, arithmetic and copies ran while one was open for 0% of the time, Pallas kernels for 44%

profile of v13, /device:TPU:0, one launch (start us, length us, event | category | flops | bytes accessed | tf_op | source)
XLA Modules:
  0.0 76.9 jit_solution(17418127216476145281)
XLA Ops:
  0.0 4.3 %cell_sum.1 = (f32[16,128]{1,0:T(8,128)S(1)}, f32[16392,128]{1,0:T(8,128)S(1)}) custom-call(f32[2048,1024]{1,0:T(8,128)} %x_hbm.2), custom_call_target="tpu_custom_call" | custom-call | flops 2097152 | bytes 8388608 | tf_op jit(solution)/shard_map/cell_sum/pallas_call | solution.py:498
  4.3 2.4 %collective-permute-start.2 = (f32[16,128]{1,0:T(8,128)S(1)}, f32[16,128]{1,0:T(8,128)S(1)}, u32[]{:S(2)}, u32[]{:S(2)}) collective-permute-start(f32[16,128]{1,0:T(8,128)S(1)} %get-tuple-element.42.after_ref), channel_id=1, source_target_pairs={{0,3},{1,2},{2,1},{3,0},{4,7},{5,6},{6,5},{7,4},{8,11},{9,10},{10,... | collective-permute-start | bytes 24584 | tf_op jit(solution)/shard_map/ppermute | solution.py:49
  6.8 0.6 collective-permute-start.1
  7.4 0.0 collective-permute-start
  7.5 2.5 %turn_rows.1 = (s32[8192,128]{1,0:T(8,128)S(1)}, s32[32,128]{1,0:T(8,128)S(1)}, s32[8,128]{1,0:T(8,128)S(1)}, s32[8,128]{1,0:T(8,128)S(1)}, s32[8,128]{1,0:T(8,1...) custom-call(s32[1024,1024]{1,0:T(8,128)} %x_hbm.3, f32[16,128]{1,0:T(8,128)S(1)} %get-tuple-element.42.after_ref, ...), custom_call_target="tpu_custom_call" | custom-call | bytes 4194304 | tf_op jit(solution)/shard_map/turn_rows/pallas_call | solution.py:518
  10.0 0.0 collective-permute-done.2
  10.0 0.4 collective-permute-done.1
  10.4 0.0 collective-permute-done
  10.5 1.6 %collective-permute-start.3 = (f32[16,128]{1,0:T(8,128)S(1)}, f32[16,128]{1,0:T(8,128)S(1)}, u32[]{:S(2)}, u32[]{:S(2)}) collective-permute-start(f32[16,128]{1,0:T(8,128)S(1)} %fusion.1.supply), channel_id=1, source_target_pairs={{0,4},{1,29},{2,10},{3,27},{4,8},{5,1},{6,14},{7,31},{8,12},{9,5},... | collective-permute-start | bytes 24584 | tf_op jit(solution)/shard_map/ppermute | solution.py:27
  12.1 2.5 %send_ahead.1.sent_ref = f32[1536,128]{1,0:T(8,128)S(1)} custom-call(f32[2176]{0:T(1024)S(1)} %concatenate.13.fraction, s32[4096]{0:T(1024)S(1)} %bitcast.23, s32[1024]{0:T(1024)S(1)} %bitcast.28, s32[1024]{0:T(1024)S(1)} %bitcast.31, f32[16392,128]{1,0:T(8,128)S(1)} %get-tuple-element.47.rows, s32[8192,128]{1,0:T(8,128)S(1)} %get-tuple-element.50.turns), custom_call_target="tpu_custom_call" | custom-call | flops 1 | bytes 1 | tf_op jit(solution)/shard_map/send_ahead/pallas_call | solution.py:550
  14.5 2.4 %collective-permute-done.3.supply_ref = f32[16,128]{1,0:T(8,128)S(1)} collective-permute-done((f32[16,128]{1,0:T(8,128)S(1)}, f32[16,128]{1,0:T(8,128)S(1)}, u32[]{:S(2)}, u32[]{:S(2)}) %collective-permute-start.3) | collective-permute-done | bytes 8224 | tf_op jit(solution)/shard_map/ppermute | solution.py:27
  16.9 2.5 %scale_rows.1.rows.scaled = f32[16392,128]{1,0:T(8,128)S(1)} custom-call(f32[2048]{0:T(1024)S(1)} %bitcast.27, f32[16392,128]{1,0:T(8,128)S(1)} %get-tuple-element.47.rows, f32[1536,128]{1,0:T(8,128)S(1)} %send_ahead.1.sent_ref, f32[16,128]{1,0:T(8,128)S(1)} %collective-permute-done.3.supply_ref), custom_call_target="tpu_custom_call" | custom-call | flops 1 | bytes 1 | tf_op jit(solution)/shard_map/scale_rows/pallas_call | solution.py:560
  19.4 3.3 %send_near.1 = (f32[1536,128]{1,0:T(8,128)S(1)}, f32[1536,128]{1,0:T(8,128)S(1)}) custom-call(s32[4096]{0:T(1024)S(1)} %bitcast.24, s32[1024]{0:T(1024)S(1)} %bitcast.29, s32[1024]{0:T(1024)S(1)} %bitcast.32, f32[16392,128]{1,0:T(8,128)S(1)} %scale_rows.1.rows.scaled, s32[8192,128]{1,0:T(8,128)S(1)} %get-tuple-element.50.turns), custom_call_target="tpu_custom_call" | custom-call | flops 1 | bytes 1 | tf_op jit(solution)/shard_map/send_near/pallas_call | solution.py:569
  22.7 2.5 %collective-permute-start.9 = (f32[1536,128]{1,0:T(8,128)S(1)}, f32[1536,128]{1,0:T(8,128)S(1)}, u32[]{:S(2)}, u32[]{:S(2)}) collective-permute-start(f32[1536,128]{1,0:T(8,128)S(1)} %get-tuple-element.65), channel_id=1, source_target_pairs={{4,0},{8,4},{12,8},{16,12},{20,16},{24,20},{28,24},{0,28},{5,1},{9... | collective-permute-start | bytes 2359304 | tf_op jit(solution)/shard_map/ppermute | solution.py:43
  25.2 9.0 %node_flow.1 = (f32[8192,128]{1,0:T(8,128)S(1)}, f32[32,128]{1,0:T(8,128)S(1)}) custom-call(s32[4096]{0:T(1024)S(1)} %bitcast.25, f32[16392,128]{1,0:T(8,128)S(1)} %scale_rows.1.rows.scaled, s32[8192,128]{1,0:T(8,128)S(1)} %get-tuple-element.50.turns, f32[1536,128]{1,0:T(8,128)S(1)} %get-tuple-element.53.after_ref), custom_call_target="tpu_custom_call" | custom-call | flops 1 | bytes 1 | tf_op jit(solution)/shard_map/node_flow/pallas_call | solution.py:582
  34.2 6.1 %all_gather.3.shared = f32[192,128]{1,0:T(8,128)S(1)} all-gather(f32[48,128]{1,0:T(8,128)S(1)} %pad_maximum_fusion), channel_id=1, replica_groups=mesh['region'=8,'dest'=4] {'dest'}, dimensions={0}, use_global_device_ids=true | all-gather | bytes 122880 | tf_op jit(solution)/shard_map/all_gather | solution.py:597
  40.3 1.5 %theta.1 = (f32[8,128]{1,0:T(8,128)S(1)}, f32[4,128]{1,0:T(4,128)S(1)}) custom-call(f32[16,128]{1,0:T(8,128)S(1)} %fusion.1.supply, f32[192,128]{1,0:T(8,128)S(1)} %all_gather.3.shared, s32[4,1024]{1,0:T(4,128)S(1)} %copy-done, s32[4,192]{1,0:T(4,128)S(1)} %copy-done.2), custom_call_target="tpu_custom_call" | custom-call | flops 1 | bytes 1 | tf_op jit(solution)/shard_map/theta/pallas_call | solution.py:598
  41.8 0.2 collective-permute-start.7
  42.0 1.9 %collective-permute-start.6 = (f32[2,128]{1,0:T(2,128)S(1)}, f32[2,128]{1,0:T(2,128)S(1)}, u32[]{:S(2)}, u32[]{:S(2)}) collective-permute-start(f32[2,128]{1,0:T(2,128)S(1)} %get-tuple-element.76), channel_id=1, source_target_pairs={{0,4},{1,29},{2,6},{3,31},{4,8},{5,1},{6,10},{7,3},{8,12},{9,5},{1... | collective-permute-start | bytes 3080 | tf_op jit(solution)/shard_map/ppermute | solution.py:37
  43.9 1.2 %send_scaled.1.sent_ref.after_ref = f32[1536,128]{1,0:T(8,128)S(1)} custom-call(f32[1024]{0:T(1024)S(1)} %bitcast.34, s32[1024]{0:T(1024)S(1)} %bitcast.30, s32[1024]{0:T(1024)S(1)} %bitcast.33, f32[8192,128]{1,0:T(8,128)S(1)} %get-tuple-element.58.flow, s32[8192,128]{1,0:T(8,128)S(1)} %get-tuple-element.50.turns), custom_call_target="tpu_custom_call" | custom-call | flops 1 | bytes 1 | tf_op jit(solution)/shard_map/send_scaled/pallas_call | solution.py:614
  45.1 3.3 %collective-permute-start.5 = (f32[1536,128]{1,0:T(8,128)S(1)}, f32[1536,128]{1,0:T(8,128)S(1)}, u32[]{:S(2)}, u32[]{:S(2)}) collective-permute-start(f32[1536,128]{1,0:T(8,128)S(1)} %send_scaled.1.sent_ref.after_ref), channel_id=1, source_target_pairs={{8,0},{12,4},{16,8},{20,12},{24,16},{28,20},{0,24},{4,28},{9,1},{1... | collective-permute-start | bytes 2359304 | tf_op jit(solution)/shard_map/ppermute | solution.py:43
  48.4 4.6 %home_rows.1.home = f32[16392,128]{1,0:T(8,128)S(1)} custom-call(s32[2048]{0:T(1024)S(1)} %bitcast.37, s32[2048]{0:T(1024)S(1)} %bitcast.38, s32[8192,128]{1,0:T(8,128)S(1)} %get-tuple-element.50.turns, f32[8192,128]{1,0:T(8,128)S(1)} %get-tuple-element.58.flow, f32[1536,128]{1,0:T(8,128)S(1)} %send_scaled.1.sent_ref.after_ref), custom_call_target="tpu_custom_call" | custom-call | flops 4000000000 | bytes 1 | tf_op jit(solution)/shard_map/home_rows/pallas_call | solution.py:623
  53.1 0.7 keep.1
  53.7 3.8 %base_rows.1.rest_3_ = f32[16392,128]{1,0:T(8,128)S(1)} custom-call(f32[2048]{0:T(1024)S(1)} %bitcast.39, f32[2048]{0:T(1024)S(1)} %bitcast.40, f32[16392,128]{1,0:T(8,128)S(1)} %get-tuple-element.47.rows, f32[16392,128]{1,0:T(8,128)S(1)} %home_rows.1.home), custom_call_target="tpu_custom_call" | custom-call | flops 10000000 | bytes 1 | tf_op jit(solution)/shard_map/base_rows/pallas_call | solution.py:641
  57.6 2.0 %collective-permute-done.9.rest_1_ = f32[1536,128]{1,0:T(8,128)S(1)} collective-permute-done((f32[1536,128]{1,0:T(8,128)S(1)}, f32[1536,128]{1,0:T(8,128)S(1)}, u32[]{:S(2)}, u32[]{:S(2)}) %collective-permute-start.9) | collective-permute-done | bytes 786464 | tf_op jit(solution)/shard_map/ppermute | solution.py:43
  59.6 0.3 collective-permute-done.8.rest_0_
  59.9 0.0 collective-permute-done.6
  59.9 0.2 collective-permute-start.10
  60.1 1.0 %collective-permute-done.10 = f32[4,128]{1,0:T(4,128)S(1)} collective-permute-done((f32[4,128]{1,0:T(4,128)S(1)}, f32[4,128]{1,0:T(4,128)S(1)}, u32[]{:S(2)}, u32[]{:S(2)}) %collective-permute-start.10) | collective-permute-done | bytes 2080 | tf_op jit(solution)/shard_map/ppermute | solution.py:656
  61.1 2.2 %land_first.1.rest_1_ = f32[16392,128]{1,0:T(8,128)S(1)} custom-call(f32[1024]{0:T(1024)S(1)} %maximum_bitcast_fusion.scale, s32[1024]{0:T(1024)S(1)} %bitcast.35, f32[1536,128]{1,0:T(8,128)S(1)} %collective-permute-done.8.rest_0_, f32[1536,128]{1,0:T(8,128)S(1)} %collective-permute-done.9.rest_1_, ...), custom_call_target="tpu_custom_call", output_to_operand_aliasing={{}: (5, {})} | custom-call | flops 4000000000 | bytes 1 | tf_op jit(solution)/shard_map/land_first/pallas_call | solution.py:659
  63.3 9.1 %collective-permute-done.5.rest_0_ = f32[1536,128]{1,0:T(8,128)S(1)} collective-permute-done((f32[1536,128]{1,0:T(8,128)S(1)}, f32[1536,128]{1,0:T(8,128)S(1)}, u32[]{:S(2)}, u32[]{:S(2)}) %collective-permute-start.5) | collective-permute-done | bytes 786464 | tf_op jit(solution)/shard_map/ppermute | solution.py:43
  72.5 4.5 %finish.1 = (f32[2048,1024]{1,0:T(8,128)}, f32[16392,128]{1,0:T(8,128)S(1)}) custom-call(s32[1024]{0:T(1024)S(1)} %bitcast.36, f32[1536,128]{1,0:T(8,128)S(1)} %collective-permute-done.5.rest_0_, f32[16392,128]{1,0:T(8,128)S(1)} %land_first.1.rest_1_), custom_call_target="tpu_custom_call", output_to_operand_aliasing={{1}: (2, {})} | custom-call | flops 2097152 | bytes 8388608 | tf_op jit(solution)/shard_map/finish/pallas_call | solution.py:670
  (25 shorter events, 0.1 us)
Async XLA Ops:
  0.0 7.5 %copy-start = (s32[4,1024]{1,0:T(4,128)S(1)}, s32[4,1024]{1,0:T(4,128)}, u32[]{:S(2)}) copy-start(s32[4,1024]{1,0:T(4,128)} %node_out.3) | copy-start | bytes 49156
  0.0 7.5 %copy-start.2 = (s32[4,192]{1,0:T(4,128)S(1)}, s32[4,192]{1,0:T(4,128)}, u32[]{:S(2)}) copy-start(s32[4,192]{1,0:T(4,128)} %send_list.1) | copy-start | bytes 9220
  0.0 7.5 %copy-start.1 = (s32[4,1024]{1,0:T(4,128)S(1)}, s32[4,1024]{1,0:T(4,128)}, u32[]{:S(2)}) copy-start(s32[4,1024]{1,0:T(4,128)} %node_in.1) | copy-start | bytes 49156
  0.0 7.5 %copy-start.3 = (s32[4,192]{1,0:T(4,128)S(1)}, s32[4,192]{1,0:T(4,128)}, u32[]{:S(2)}) copy-start(s32[4,192]{1,0:T(4,128)} %rest_3_.1) | copy-start | bytes 9220
  0.0 10.4 %copy-start.4 = (f32[2048]{0:T(1024)S(1)}, f32[2048]{0:T(1024)}, u32[]{:S(2)}) copy-start(f32[2048]{0:T(1024)} %param.10) | copy-start | bytes 24580
  0.0 10.5 %copy-start.6 = (f32[2048]{0:T(1024)S(1)}, f32[2048]{0:T(1024)}, u32[]{:S(2)}) copy-start(f32[2048]{0:T(1024)} %param.12) | copy-start | bytes 24580
  0.0 10.5 %copy-start.5 = (f32[2048]{0:T(1024)S(1)}, f32[2048]{0:T(1024)}, u32[]{:S(2)}) copy-start(f32[2048]{0:T(1024)} %param.11) | copy-start | bytes 24580
  4.3 5.7 %collective-permute-start.2 = (f32[16,128]{1,0:T(8,128)S(1)}, f32[16,128]{1,0:T(8,128)S(1)}, u32[]{:S(2)}, u32[]{:S(2)}) collective-permute-start(f32[16,128]{1,0:T(8,128)S(1)} %get-tuple-element.42.after_ref), channel_id=1, source_target_pairs={{0,3},{1,2},{2,1},{3,0},{4,7},{5,6},{6,5},{7,4},{8,11},{9,10},{10,... | collective-permute-start | bytes 24584 | tf_op jit(solution)/shard_map/ppermute | solution.py:49
  6.8 3.7 %collective-permute-start.1 = (f32[16,128]{1,0:T(8,128)S(1)}, f32[16,128]{1,0:T(8,128)S(1)}, u32[]{:S(2)}, u32[]{:S(2)}) collective-permute-start(f32[16,128]{1,0:T(8,128)S(1)} %get-tuple-element.42.after_ref), channel_id=1, source_target_pairs={{0,2},{1,3},{2,0},{3,1},{4,6},{5,7},{6,4},{7,5},{8,10},{9,11},{10,... | collective-permute-start | bytes 24584 | tf_op jit(solution)/shard_map/ppermute | solution.py:49
  7.4 3.0 %collective-permute-start = (f32[16,128]{1,0:T(8,128)S(1)}, f32[16,128]{1,0:T(8,128)S(1)}, u32[]{:S(2)}, u32[]{:S(2)}) collective-permute-start(f32[16,128]{1,0:T(8,128)S(1)} %get-tuple-element.42.after_ref), channel_id=1, source_target_pairs={{0,1},{1,0},{2,3},{3,2},{4,5},{5,4},{6,7},{7,6},{8,9},{9,8},{10,11... | collective-permute-start | bytes 24584 | tf_op jit(solution)/shard_map/ppermute | solution.py:49
  10.5 6.4 %collective-permute-start.3 = (f32[16,128]{1,0:T(8,128)S(1)}, f32[16,128]{1,0:T(8,128)S(1)}, u32[]{:S(2)}, u32[]{:S(2)}) collective-permute-start(f32[16,128]{1,0:T(8,128)S(1)} %fusion.1.supply), channel_id=1, source_target_pairs={{0,4},{1,29},{2,10},{3,27},{4,8},{5,1},{6,14},{7,31},{8,12},{9,5},... | collective-permute-start | bytes 24584 | tf_op jit(solution)/shard_map/ppermute | solution.py:27
  16.9 24.9 %collective-permute-start.4 = (f32[1536,128]{1,0:T(8,128)S(1)}, f32[1536,128]{1,0:T(8,128)S(1)}, u32[]{:S(2)}, u32[]{:S(2)}) collective-permute-start(f32[1536,128]{1,0:T(8,128)S(1)} %send_ahead.1.sent_ref), channel_id=1, source_target_pairs={{24,0},{28,4},{0,8},{4,12},{8,16},{12,20},{16,24},{20,28},{25,1},{... | collective-permute-start | bytes 2359304 | tf_op jit(solution)/shard_map/ppermute | solution.py:43
  22.7 36.9 %collective-permute-start.9 = (f32[1536,128]{1,0:T(8,128)S(1)}, f32[1536,128]{1,0:T(8,128)S(1)}, u32[]{:S(2)}, u32[]{:S(2)}) collective-permute-start(f32[1536,128]{1,0:T(8,128)S(1)} %get-tuple-element.65), channel_id=1, source_target_pairs={{4,0},{8,4},{12,8},{16,12},{20,16},{24,20},{28,24},{0,28},{5,1},{9... | collective-permute-start | bytes 2359304 | tf_op jit(solution)/shard_map/ppermute | solution.py:43
  25.2 34.7 %collective-permute-start.8 = (f32[1536,128]{1,0:T(8,128)S(1)}, f32[1536,128]{1,0:T(8,128)S(1)}, u32[]{:S(2)}, u32[]{:S(2)}) collective-permute-start(f32[1536,128]{1,0:T(8,128)S(1)} %get-tuple-element.53.after_ref), channel_id=1, source_target_pairs={{28,0},{0,4},{4,8},{8,12},{12,16},{16,20},{20,24},{24,28},{29,1},{... | collective-permute-start | bytes 2359304 | tf_op jit(solution)/shard_map/ppermute | solution.py:43
  41.8 18.1 %collective-permute-start.7 = (f32[2,128]{1,0:T(2,128)S(1)}, f32[2,128]{1,0:T(2,128)S(1)}, u32[]{:S(2)}, u32[]{:S(2)}) collective-permute-start(f32[2,128]{1,0:T(2,128)S(1)} %get-tuple-element.75), channel_id=1, source_target_pairs={{0,8},{1,25},{2,10},{3,27},{4,12},{5,29},{6,14},{7,31},{8,16},{9,1... | collective-permute-start | bytes 3080 | tf_op jit(solution)/shard_map/ppermute | solution.py:37
  42.0 17.9 %collective-permute-start.6 = (f32[2,128]{1,0:T(2,128)S(1)}, f32[2,128]{1,0:T(2,128)S(1)}, u32[]{:S(2)}, u32[]{:S(2)}) collective-permute-start(f32[2,128]{1,0:T(2,128)S(1)} %get-tuple-element.76), channel_id=1, source_target_pairs={{0,4},{1,29},{2,6},{3,31},{4,8},{5,1},{6,10},{7,3},{8,12},{9,5},{1... | collective-permute-start | bytes 3080 | tf_op jit(solution)/shard_map/ppermute | solution.py:37
  45.1 27.4 %collective-permute-start.5 = (f32[1536,128]{1,0:T(8,128)S(1)}, f32[1536,128]{1,0:T(8,128)S(1)}, u32[]{:S(2)}, u32[]{:S(2)}) collective-permute-start(f32[1536,128]{1,0:T(8,128)S(1)} %send_scaled.1.sent_ref.after_ref), channel_id=1, source_target_pairs={{8,0},{12,4},{16,8},{20,12},{24,16},{28,20},{0,24},{4,28},{9,1},{1... | collective-permute-start | bytes 2359304 | tf_op jit(solution)/shard_map/ppermute | solution.py:43
  59.9 1.2 %collective-permute-start.10 = (f32[4,128]{1,0:T(4,128)S(1)}, f32[4,128]{1,0:T(4,128)S(1)}, u32[]{:S(2)}, u32[]{:S(2)}) collective-permute-start(f32[4,128]{1,0:T(4,128)S(1)} %pad_maximum_fusion.1), channel_id=1, source_target_pairs={{0,1},{1,0},{2,3},{3,2},{4,5},{5,4},{6,7},{7,6},{8,9},{9,8},{10,11... | collective-permute-start | bytes 6152 | tf_op jit(solution)/shard_map/ppermute | solution.py:656

commit v14 on v13

--- a/solution.py
+++ b/solution.py
@@ -556,14 +556,13 @@
         cost_estimate=cost(1, 1),
         name="send_ahead",
     )(weights, in_cell, send_node, send_outlet, rows, turns)
-    ahead, supply_there = lax.optimization_barrier((ahead, supply_there))
     scaled = pl.pallas_call(
         functools.partial(scale_kernel, sizes),
         in_specs=[SMEM_WHOLE, VMEM_WHOLE, ANYWHERE, ANYWHERE],
         out_specs=VMEM_WHOLE,
         out_shape=rows_shape,
         compiler_params=params(4),
-        cost_estimate=cost(1, 1),
+        cost_estimate=cost(10000000000, 1),
         name="scale_rows",
     )(fraction.reshape(-1), rows, ahead, supply_there)
     near = pl.pallas_call(

time: 77.1 us -> 75.2 us (0.975)
  waiting for transfers between devices: 15.2 us -> 12.2 us
  starting transfers between devices: 12.9 us -> 14.2 us
    ppermute x4, waiting for transfers between devices: 11.4 us -> 7.26 us  [shifted(): return lax.ppermute(block, axis, route)]
    ppermute x2, waiting for transfers between devices: 0.02 us -> 2.71 us  [to_two(): return lax.ppermute(block, ('region', 'dest'), route)]
    ppermute x1, waiting for transfers between devices: 2.36 us -> 0.73 us  [to_neighbours(): return lax.ppermute(block, ('region', 'dest'), route)]
    ppermute x4, starting transfers between devices: 5.88 us -> 7.1 us  [shifted(): return lax.ppermute(block, axis, route)]
  transfers between devices with their start and end apart: 11 -> 11, of which waited for: 6 -> 5; matrix products, arithmetic and copies ran while one was open for 0% -> 0% of each run, Pallas kernels for 44% -> 45%
where the time goes in v14:
time: 75.2 us; the launch traced here: 75.1 us
  Pallas kernels  42.4 us (56%)
  starting transfers between devices  14.2 us (19%)
  waiting for transfers between devices  12.2 us (16%)
  blocking collectives  5.97 us (8%)
    pallas_call x1, Pallas kernels, on_device(): pl.pallas_call(functools.partial(node_flow_kernel, sizes), in_specs=[SMEM...  8.97 us
    ppermute x4, waiting for transfers between devices, shifted(): return lax.ppermute(block, axis, route)  7.26 us
    ppermute x4, starting transfers between devices, shifted(): return lax.ppermute(block, axis, route)  7.1 us
    all_gather x1, blocking collectives, on_device(): shared = lax.all_gather(joined, 'dest', axis=0, tiled=True)  5.97 us
    pallas_call x1, Pallas kernels, on_device(): pl.pallas_call(functools.partial(home_kernel, sizes), in_specs=[SMEM_WHOL...  4.63 us
    pallas_call x1, Pallas kernels, on_device(): pl.pallas_call(functools.partial(finish_kernel, sizes, (3,), chunk), in_s...  4.48 us
    pallas_call x1, Pallas kernels, on_device(): pl.pallas_call(functools.partial(cell_sum_kernel, chunk, sub), in_specs=[...  4.31 us
    pallas_call x1, Pallas kernels, on_device(): pl.pallas_call(functools.partial(base_kernel, sizes), in_specs=[SMEM_WHOL...  3.85 us
  transfers between devices with their start and end apart: 11, of which 5 were waited for; matrix products, arithmetic and copies ran while one was open for 0% of the time, Pallas kernels for 45%

profile of v14, /device:TPU:0, one launch (start us, length us, event | category | flops | bytes accessed | tf_op | source)
XLA Modules:
  0.0 75.1 jit_solution(9607359875118036945)
XLA Ops:
  0.0 4.3 %cell_sum.1 = (f32[16,128]{1,0:T(8,128)S(1)}, f32[16392,128]{1,0:T(8,128)S(1)}) custom-call(f32[2048,1024]{1,0:T(8,128)} %x_hbm.2), custom_call_target="tpu_custom_call" | custom-call | flops 2097152 | bytes 8388608 | tf_op jit(solution)/shard_map/cell_sum/pallas_call | solution.py:498
  4.3 2.4 %collective-permute-start.2 = (f32[16,128]{1,0:T(8,128)S(1)}, f32[16,128]{1,0:T(8,128)S(1)}, u32[]{:S(2)}, u32[]{:S(2)}) collective-permute-start(f32[16,128]{1,0:T(8,128)S(1)} %get-tuple-element.40.after_ref), channel_id=1, source_target_pairs={{0,3},{1,2},{2,1},{3,0},{4,7},{5,6},{6,5},{7,4},{8,11},{9,10},{10,... | collective-permute-start | bytes 24584 | tf_op jit(solution)/shard_map/ppermute | solution.py:49
  6.8 0.6 collective-permute-start.1
  7.4 0.0 collective-permute-start
  7.5 2.5 %turn_rows.1 = (s32[8192,128]{1,0:T(8,128)S(1)}, s32[32,128]{1,0:T(8,128)S(1)}, s32[8,128]{1,0:T(8,128)S(1)}, s32[8,128]{1,0:T(8,128)S(1)}, s32[8,128]{1,0:T(8,1...) custom-call(s32[1024,1024]{1,0:T(8,128)} %x_hbm.3, f32[16,128]{1,0:T(8,128)S(1)} %get-tuple-element.40.after_ref, ...), custom_call_target="tpu_custom_call" | custom-call | bytes 4194304 | tf_op jit(solution)/shard_map/turn_rows/pallas_call | solution.py:518
  10.0 0.4 collective-permute-done.1
  10.4 0.0 collective-permute-done
  10.5 1.6 %collective-permute-start.3 = (f32[16,128]{1,0:T(8,128)S(1)}, f32[16,128]{1,0:T(8,128)S(1)}, u32[]{:S(2)}, u32[]{:S(2)}) collective-permute-start(f32[16,128]{1,0:T(8,128)S(1)} %fusion.1.supply), channel_id=1, source_target_pairs={{0,4},{1,29},{2,10},{3,27},{4,8},{5,1},{6,14},{7,31},{8,12},{9,5},... | collective-permute-start | bytes 24584 | tf_op jit(solution)/shard_map/ppermute | solution.py:27
  12.1 2.5 %send_ahead.1.sent_ref = f32[1536,128]{1,0:T(8,128)S(1)} custom-call(f32[2176]{0:T(1024)S(1)} %concatenate.13.fraction, s32[4096]{0:T(1024)S(1)} %bitcast.23, s32[1024]{0:T(1024)S(1)} %bitcast.28, s32[1024]{0:T(1024)S(1)} %bitcast.31, f32[16392,128]{1,0:T(8,128)S(1)} %get-tuple-element.45.rows, s32[8192,128]{1,0:T(8,128)S(1)} %get-tuple-element.48.turns), custom_call_target="tpu_custom_call" | custom-call | flops 1 | bytes 1 | tf_op jit(solution)/shard_map/send_ahead/pallas_call | solution.py:550
  14.5 1.6 %collective-permute-start.4 = (f32[1536,128]{1,0:T(8,128)S(1)}, f32[1536,128]{1,0:T(8,128)S(1)}, u32[]{:S(2)}, u32[]{:S(2)}) collective-permute-start(f32[1536,128]{1,0:T(8,128)S(1)} %send_ahead.1.sent_ref), channel_id=1, source_target_pairs={{24,0},{28,4},{0,8},{4,12},{8,16},{12,20},{16,24},{20,28},{25,1},{... | collective-permute-start | bytes 2359304 | tf_op jit(solution)/shard_map/ppermute | solution.py:43
  16.2 0.7 collective-permute-done.3.supply_ref
  16.9 2.5 %scale_rows.1.rows.scaled = f32[16392,128]{1,0:T(8,128)S(1)} custom-call(f32[2048]{0:T(1024)S(1)} %bitcast.27, f32[16392,128]{1,0:T(8,128)S(1)} %get-tuple-element.45.rows, f32[1536,128]{1,0:T(8,128)S(1)} %send_ahead.1.sent_ref, f32[16,128]{1,0:T(8,128)S(1)} %collective-permute-done.3.supply_ref), custom_call_target="tpu_custom_call" | custom-call | flops 10000000000 | bytes 1 | tf_op jit(solution)/shard_map/scale_rows/pallas_call | solution.py:559
  19.4 3.3 %send_near.1 = (f32[1536,128]{1,0:T(8,128)S(1)}, f32[1536,128]{1,0:T(8,128)S(1)}) custom-call(s32[4096]{0:T(1024)S(1)} %bitcast.24, s32[1024]{0:T(1024)S(1)} %bitcast.29, s32[1024]{0:T(1024)S(1)} %bitcast.32, f32[16392,128]{1,0:T(8,128)S(1)} %scale_rows.1.rows.scaled, s32[8192,128]{1,0:T(8,128)S(1)} %get-tuple-element.48.turns), custom_call_target="tpu_custom_call" | custom-call | flops 1 | bytes 1 | tf_op jit(solution)/shard_map/send_near/pallas_call | solution.py:568
  22.7 2.5 %collective-permute-start.9 = (f32[1536,128]{1,0:T(8,128)S(1)}, f32[1536,128]{1,0:T(8,128)S(1)}, u32[]{:S(2)}, u32[]{:S(2)}) collective-permute-start(f32[1536,128]{1,0:T(8,128)S(1)} %get-tuple-element.61), channel_id=1, source_target_pairs={{4,0},{8,4},{12,8},{16,12},{20,16},{24,20},{28,24},{0,28},{5,1},{9... | collective-permute-start | bytes 2359304 | tf_op jit(solution)/shard_map/ppermute | solution.py:43
  25.2 9.0 %node_flow.1 = (f32[8192,128]{1,0:T(8,128)S(1)}, f32[32,128]{1,0:T(8,128)S(1)}) custom-call(s32[4096]{0:T(1024)S(1)} %bitcast.25, f32[16392,128]{1,0:T(8,128)S(1)} %scale_rows.1.rows.scaled, s32[8192,128]{1,0:T(8,128)S(1)} %get-tuple-element.48.turns, f32[1536,128]{1,0:T(8,128)S(1)} %get-tuple-element.49.after_ref), custom_call_target="tpu_custom_call" | custom-call | flops 1 | bytes 1 | tf_op jit(solution)/shard_map/node_flow/pallas_call | solution.py:581
  34.2 6.0 %all_gather.3.shared = f32[192,128]{1,0:T(8,128)S(1)} all-gather(f32[48,128]{1,0:T(8,128)S(1)} %pad_maximum_fusion), channel_id=1, replica_groups=mesh['region'=8,'dest'=4] {'dest'}, dimensions={0}, use_global_device_ids=true | all-gather | bytes 122880 | tf_op jit(solution)/shard_map/all_gather | solution.py:596
  40.2 1.5 %theta.1 = (f32[8,128]{1,0:T(8,128)S(1)}, f32[4,128]{1,0:T(4,128)S(1)}) custom-call(f32[16,128]{1,0:T(8,128)S(1)} %fusion.1.supply, f32[192,128]{1,0:T(8,128)S(1)} %all_gather.3.shared, s32[4,1024]{1,0:T(4,128)S(1)} %copy-done, s32[4,192]{1,0:T(4,128)S(1)} %copy-done.2), custom_call_target="tpu_custom_call" | custom-call | flops 1 | bytes 1 | tf_op jit(solution)/shard_map/theta/pallas_call | solution.py:597
  41.6 0.0 collective-permute-done.4.arrived_ref.rest_2_
  41.6 0.1 collective-permute-start.7
  41.7 2.2 %collective-permute-start.6 = (f32[2,128]{1,0:T(2,128)S(1)}, f32[2,128]{1,0:T(2,128)S(1)}, u32[]{:S(2)}, u32[]{:S(2)}) collective-permute-start(f32[2,128]{1,0:T(2,128)S(1)} %get-tuple-element.72), channel_id=1, source_target_pairs={{0,4},{1,29},{2,6},{3,31},{4,8},{5,1},{6,10},{7,3},{8,12},{9,5},{1... | collective-permute-start | bytes 3080 | tf_op jit(solution)/shard_map/ppermute | solution.py:37
  43.9 1.2 %send_scaled.1.sent_ref.after_ref = f32[1536,128]{1,0:T(8,128)S(1)} custom-call(f32[1024]{0:T(1024)S(1)} %bitcast.34, s32[1024]{0:T(1024)S(1)} %bitcast.30, s32[1024]{0:T(1024)S(1)} %bitcast.33, f32[8192,128]{1,0:T(8,128)S(1)} %get-tuple-element.54.flow, s32[8192,128]{1,0:T(8,128)S(1)} %get-tuple-element.48.turns), custom_call_target="tpu_custom_call" | custom-call | flops 1 | bytes 1 | tf_op jit(solution)/shard_map/send_scaled/pallas_call | solution.py:613
  45.1 2.9 %collective-permute-start.5 = (f32[1536,128]{1,0:T(8,128)S(1)}, f32[1536,128]{1,0:T(8,128)S(1)}, u32[]{:S(2)}, u32[]{:S(2)}) collective-permute-start(f32[1536,128]{1,0:T(8,128)S(1)} %send_scaled.1.sent_ref.after_ref), channel_id=1, source_target_pairs={{8,0},{12,4},{16,8},{20,12},{24,16},{28,20},{0,24},{4,28},{9,1},{1... | collective-permute-start | bytes 2359304 | tf_op jit(solution)/shard_map/ppermute | solution.py:43
  48.0 4.6 %home_rows.1.home = f32[16392,128]{1,0:T(8,128)S(1)} custom-call(s32[2048]{0:T(1024)S(1)} %bitcast.37, s32[2048]{0:T(1024)S(1)} %bitcast.38, s32[8192,128]{1,0:T(8,128)S(1)} %get-tuple-element.48.turns, f32[8192,128]{1,0:T(8,128)S(1)} %get-tuple-element.54.flow, f32[1536,128]{1,0:T(8,128)S(1)} %send_scaled.1.sent_ref.after_ref), custom_call_target="tpu_custom_call" | custom-call | flops 4000000000 | bytes 1 | tf_op jit(solution)/shard_map/home_rows/pallas_call | solution.py:622
  52.6 0.7 keep.1
  53.3 3.8 %base_rows.1.rest_3_ = f32[16392,128]{1,0:T(8,128)S(1)} custom-call(f32[2048]{0:T(1024)S(1)} %bitcast.39, f32[2048]{0:T(1024)S(1)} %bitcast.40, f32[16392,128]{1,0:T(8,128)S(1)} %get-tuple-element.45.rows, f32[16392,128]{1,0:T(8,128)S(1)} %home_rows.1.home), custom_call_target="tpu_custom_call" | custom-call | flops 10000000 | bytes 1 | tf_op jit(solution)/shard_map/base_rows/pallas_call | solution.py:640
  57.2 0.0 collective-permute-done.7
  57.2 2.7 %collective-permute-done.6 = f32[2,128]{1,0:T(2,128)S(1)} collective-permute-done((f32[2,128]{1,0:T(2,128)S(1)}, f32[2,128]{1,0:T(2,128)S(1)}, u32[]{:S(2)}, u32[]{:S(2)}) %collective-permute-start.6) | collective-permute-done | bytes 1056 | tf_op jit(solution)/shard_map/ppermute | solution.py:37
  59.9 0.1 collective-permute-start.10
  60.0 1.1 %collective-permute-done.10 = f32[4,128]{1,0:T(4,128)S(1)} collective-permute-done((f32[4,128]{1,0:T(4,128)S(1)}, f32[4,128]{1,0:T(4,128)S(1)}, u32[]{:S(2)}, u32[]{:S(2)}) %collective-permute-start.10) | collective-permute-done | bytes 2080 | tf_op jit(solution)/shard_map/ppermute | solution.py:655
  61.1 2.2 %land_first.1.rest_1_ = f32[16392,128]{1,0:T(8,128)S(1)} custom-call(f32[1024]{0:T(1024)S(1)} %maximum_bitcast_fusion.scale, s32[1024]{0:T(1024)S(1)} %bitcast.35, f32[1536,128]{1,0:T(8,128)S(1)} %collective-permute-done.8.rest_0_, f32[1536,128]{1,0:T(8,128)S(1)} %collective-permute-done.9.rest_1_, ...), custom_call_target="tpu_custom_call", output_to_operand_aliasing={{}: (5, {})} | custom-call | flops 4000000000 | bytes 1 | tf_op jit(solution)/shard_map/land_first/pallas_call | solution.py:658
  63.3 7.3 %collective-permute-done.5.rest_0_ = f32[1536,128]{1,0:T(8,128)S(1)} collective-permute-done((f32[1536,128]{1,0:T(8,128)S(1)}, f32[1536,128]{1,0:T(8,128)S(1)}, u32[]{:S(2)}, u32[]{:S(2)}) %collective-permute-start.5) | collective-permute-done | bytes 786464 | tf_op jit(solution)/shard_map/ppermute | solution.py:43
  70.6 4.5 %finish.1 = (f32[2048,1024]{1,0:T(8,128)}, f32[16392,128]{1,0:T(8,128)S(1)}) custom-call(s32[1024]{0:T(1024)S(1)} %bitcast.36, f32[1536,128]{1,0:T(8,128)S(1)} %collective-permute-done.5.rest_0_, f32[16392,128]{1,0:T(8,128)S(1)} %land_first.1.rest_1_), custom_call_target="tpu_custom_call", output_to_operand_aliasing={{1}: (2, {})} | custom-call | flops 2097152 | bytes 8388608 | tf_op jit(solution)/shard_map/finish/pallas_call | solution.py:669
  (25 shorter events, 0.1 us)
Async XLA Ops:
  0.0 7.5 %copy-start = (s32[4,1024]{1,0:T(4,128)S(1)}, s32[4,1024]{1,0:T(4,128)}, u32[]{:S(2)}) copy-start(s32[4,1024]{1,0:T(4,128)} %node_out.3) | copy-start | bytes 49156
  0.0 7.5 %copy-start.2 = (s32[4,192]{1,0:T(4,128)S(1)}, s32[4,192]{1,0:T(4,128)}, u32[]{:S(2)}) copy-start(s32[4,192]{1,0:T(4,128)} %send_list.1) | copy-start | bytes 9220
  0.0 7.5 %copy-start.1 = (s32[4,1024]{1,0:T(4,128)S(1)}, s32[4,1024]{1,0:T(4,128)}, u32[]{:S(2)}) copy-start(s32[4,1024]{1,0:T(4,128)} %node_in.1) | copy-start | bytes 49156
  0.0 7.5 %copy-start.3 = (s32[4,192]{1,0:T(4,128)S(1)}, s32[4,192]{1,0:T(4,128)}, u32[]{:S(2)}) copy-start(s32[4,192]{1,0:T(4,128)} %rest_3_.1) | copy-start | bytes 9220
  0.0 10.4 %copy-start.4 = (f32[2048]{0:T(1024)S(1)}, f32[2048]{0:T(1024)}, u32[]{:S(2)}) copy-start(f32[2048]{0:T(1024)} %param.10) | copy-start | bytes 24580
  0.0 10.5 %copy-start.6 = (f32[2048]{0:T(1024)S(1)}, f32[2048]{0:T(1024)}, u32[]{:S(2)}) copy-start(f32[2048]{0:T(1024)} %param.12) | copy-start | bytes 24580
  0.0 10.5 %copy-start.5 = (f32[2048]{0:T(1024)S(1)}, f32[2048]{0:T(1024)}, u32[]{:S(2)}) copy-start(f32[2048]{0:T(1024)} %param.11) | copy-start | bytes 24580
  4.3 5.7 %collective-permute-start.2 = (f32[16,128]{1,0:T(8,128)S(1)}, f32[16,128]{1,0:T(8,128)S(1)}, u32[]{:S(2)}, u32[]{:S(2)}) collective-permute-start(f32[16,128]{1,0:T(8,128)S(1)} %get-tuple-element.40.after_ref), channel_id=1, source_target_pairs={{0,3},{1,2},{2,1},{3,0},{4,7},{5,6},{6,5},{7,4},{8,11},{9,10},{10,... | collective-permute-start | bytes 24584 | tf_op jit(solution)/shard_map/ppermute | solution.py:49
  6.8 3.7 %collective-permute-start.1 = (f32[16,128]{1,0:T(8,128)S(1)}, f32[16,128]{1,0:T(8,128)S(1)}, u32[]{:S(2)}, u32[]{:S(2)}) collective-permute-start(f32[16,128]{1,0:T(8,128)S(1)} %get-tuple-element.40.after_ref), channel_id=1, source_target_pairs={{0,2},{1,3},{2,0},{3,1},{4,6},{5,7},{6,4},{7,5},{8,10},{9,11},{10,... | collective-permute-start | bytes 24584 | tf_op jit(solution)/shard_map/ppermute | solution.py:49
  7.4 3.0 %collective-permute-start = (f32[16,128]{1,0:T(8,128)S(1)}, f32[16,128]{1,0:T(8,128)S(1)}, u32[]{:S(2)}, u32[]{:S(2)}) collective-permute-start(f32[16,128]{1,0:T(8,128)S(1)} %get-tuple-element.40.after_ref), channel_id=1, source_target_pairs={{0,1},{1,0},{2,3},{3,2},{4,5},{5,4},{6,7},{7,6},{8,9},{9,8},{10,11... | collective-permute-start | bytes 24584 | tf_op jit(solution)/shard_map/ppermute | solution.py:49
  10.5 6.4 %collective-permute-start.3 = (f32[16,128]{1,0:T(8,128)S(1)}, f32[16,128]{1,0:T(8,128)S(1)}, u32[]{:S(2)}, u32[]{:S(2)}) collective-permute-start(f32[16,128]{1,0:T(8,128)S(1)} %fusion.1.supply), channel_id=1, source_target_pairs={{0,4},{1,29},{2,10},{3,27},{4,8},{5,1},{6,14},{7,31},{8,12},{9,5},... | collective-permute-start | bytes 24584 | tf_op jit(solution)/shard_map/ppermute | solution.py:27
  14.5 27.1 %collective-permute-start.4 = (f32[1536,128]{1,0:T(8,128)S(1)}, f32[1536,128]{1,0:T(8,128)S(1)}, u32[]{:S(2)}, u32[]{:S(2)}) collective-permute-start(f32[1536,128]{1,0:T(8,128)S(1)} %send_ahead.1.sent_ref), channel_id=1, source_target_pairs={{24,0},{28,4},{0,8},{4,12},{8,16},{12,20},{16,24},{20,28},{25,1},{... | collective-permute-start | bytes 2359304 | tf_op jit(solution)/shard_map/ppermute | solution.py:43
  22.7 37.2 %collective-permute-start.9 = (f32[1536,128]{1,0:T(8,128)S(1)}, f32[1536,128]{1,0:T(8,128)S(1)}, u32[]{:S(2)}, u32[]{:S(2)}) collective-permute-start(f32[1536,128]{1,0:T(8,128)S(1)} %get-tuple-element.61), channel_id=1, source_target_pairs={{4,0},{8,4},{12,8},{16,12},{20,16},{24,20},{28,24},{0,28},{5,1},{9... | collective-permute-start | bytes 2359304 | tf_op jit(solution)/shard_map/ppermute | solution.py:43
  25.2 34.7 %collective-permute-start.8 = (f32[1536,128]{1,0:T(8,128)S(1)}, f32[1536,128]{1,0:T(8,128)S(1)}, u32[]{:S(2)}, u32[]{:S(2)}) collective-permute-start(f32[1536,128]{1,0:T(8,128)S(1)} %get-tuple-element.49.after_ref), channel_id=1, source_target_pairs={{28,0},{0,4},{4,8},{8,12},{12,16},{16,20},{20,24},{24,28},{29,1},{... | collective-permute-start | bytes 2359304 | tf_op jit(solution)/shard_map/ppermute | solution.py:43
  41.6 15.5 %collective-permute-start.7 = (f32[2,128]{1,0:T(2,128)S(1)}, f32[2,128]{1,0:T(2,128)S(1)}, u32[]{:S(2)}, u32[]{:S(2)}) collective-permute-start(f32[2,128]{1,0:T(2,128)S(1)} %get-tuple-element.71), channel_id=1, source_target_pairs={{0,8},{1,25},{2,10},{3,27},{4,12},{5,29},{6,14},{7,31},{8,16},{9,1... | collective-permute-start | bytes 3080 | tf_op jit(solution)/shard_map/ppermute | solution.py:37
  41.7 18.2 %collective-permute-start.6 = (f32[2,128]{1,0:T(2,128)S(1)}, f32[2,128]{1,0:T(2,128)S(1)}, u32[]{:S(2)}, u32[]{:S(2)}) collective-permute-start(f32[2,128]{1,0:T(2,128)S(1)} %get-tuple-element.72), channel_id=1, source_target_pairs={{0,4},{1,29},{2,6},{3,31},{4,8},{5,1},{6,10},{7,3},{8,12},{9,5},{1... | collective-permute-start | bytes 3080 | tf_op jit(solution)/shard_map/ppermute | solution.py:37
  45.1 25.5 %collective-permute-start.5 = (f32[1536,128]{1,0:T(8,128)S(1)}, f32[1536,128]{1,0:T(8,128)S(1)}, u32[]{:S(2)}, u32[]{:S(2)}) collective-permute-start(f32[1536,128]{1,0:T(8,128)S(1)} %send_scaled.1.sent_ref.after_ref), channel_id=1, source_target_pairs={{8,0},{12,4},{16,8},{20,12},{24,16},{28,20},{0,24},{4,28},{9,1},{1... | collective-permute-start | bytes 2359304 | tf_op jit(solution)/shard_map/ppermute | solution.py:43
  59.9 1.2 %collective-permute-start.10 = (f32[4,128]{1,0:T(4,128)S(1)}, f32[4,128]{1,0:T(4,128)S(1)}, u32[]{:S(2)}, u32[]{:S(2)}) collective-permute-start(f32[4,128]{1,0:T(4,128)S(1)} %pad_maximum_fusion.1), channel_id=1, source_target_pairs={{0,1},{1,0},{2,3},{3,2},{4,5},{5,4},{6,7},{7,6},{8,9},{9,8},{10,11... | collective-permute-start | bytes 6152 | tf_op jit(solution)/shard_map/ppermute | solution.py:655

commit v15 on v14

--- a/solution.py
+++ b/solution.py
@@ -257,16 +257,16 @@
     row_of(scaled, cells, sub)[...] = jnp.zeros((sub, LANES), F32)
 
 
-def send_kernel(sizes, sides, fraction, in_cell, send_node, send_outlet, rows, turns, *sends):
+def send_kernel(sizes, parts, fraction, in_cell, send_node, send_outlet, rows, turns, *sends):
     cells, nodes, branches, cap, sub = sizes
     batch = 16
-    for side, send in zip(sides, sends):
-
-        def body(step, carry, side=side, send=send):
+    for (side, start, count), send in zip(parts, sends):
+
+        def body(step, carry, side=side, start=start, send=send):
             first = step * batch
             values = []
             for i in range(batch):
-                slot = side * padded(cap) + first + i
+                slot = side * padded(cap) + start + first + i
                 node = send_node[slot]
                 value = gathered_flow(node, in_cell, fraction, rows, sizes)
                 choice = row_of(turns, node, sub)[...]
@@ -275,18 +275,19 @@
                 row_of(send, first + i, sub)[...] = values[i]
             return carry
 
-        lax.fori_loop(0, cap // batch, body, 0)
-
-
-def scaled_send_kernel(sizes, side, theta, send_node, send_outlet, flow, turns, send):
-    cells, nodes, branches, cap, sub = sizes
+        lax.fori_loop(0, count // batch, body, 0)
+
+
+def scaled_send_kernel(sizes, part, theta, send_node, send_outlet, flow, turns, send):
+    cells, nodes, branches, cap, sub = sizes
+    side, start, count = part
     batch = 16
 
     def body(step, carry):
         first = step * batch
         values = []
         for i in range(batch):
-            slot = side * padded(cap) + first + i
+            slot = side * padded(cap) + start + first + i
             node = send_node[slot]
             value = row_of(flow, node, sub)[...] * theta[node]
             choice = row_of(turns, node, sub)[...]
@@ -295,7 +296,7 @@
             row_of(send, first + i, sub)[...] = values[i]
         return carry
 
-    lax.fori_loop(0, cap // batch, body, 0)
+    lax.fori_loop(0, count // batch, body, 0)
 
 
 def node_flow_kernel(sizes, in_cell, scaled, turns, after_ref, flow, demand, partial):
@@ -425,18 +426,19 @@
     lax.fori_loop(0, cells // batch, body, 0)
 
 
-def land_rows(sizes, sides, scale, land, received, base):
+def land_rows(sizes, parts, scale, land, received, base):
     cells, nodes, branches, cap, sub = sizes
     batch = 16
     core = lax.axis_index("dest") % 2
-    for side, rows in zip(sides, received):
+    for (side, start, count), rows in zip(parts, received):
         offset = jnp.where(core == side % 2, 0, 2 * padded(cap)) + side // 2 * padded(cap)
-
-        def body(step, carry, side=side, rows=rows, offset=offset):
+        offset = offset + start
+
+        def body(step, carry, side=side, start=start, rows=rows, offset=offset):
             first = step * batch
             stores = []
             for i in range(batch):
-                at = row_of(base, land[side * padded(cap) + first + i], sub)
+                at = row_of(base, land[side * padded(cap) + start + first + i], sub)
                 value = row_of(rows, first + i, sub)[...]
                 if scale is not None:
                     value = value * scale[offset + first + i]
@@ -445,18 +447,18 @@
                 at[...] = value
             return carry
 
-        lax.fori_loop(0, cap // batch, body, 0)
-
-
-def land_kernel(sizes, sides, scale, land, *rest):
-    received, (base_in, base) = rest[: len(sides)], rest[len(sides) :]
-    land_rows(sizes, sides, scale, land, received, base)
-
-
-def finish_kernel(sizes, sides, chunk, land, *rest):
-    cells, nodes, branches, cap, sub = sizes
-    received, (base_in, out, base, staged, sems) = rest[: len(sides)], rest[len(sides) :]
-    land_rows(sizes, sides, None, land, received, base)
+        lax.fori_loop(0, count // batch, body, 0)
+
+
+def land_kernel(sizes, parts, scale, land, *rest):
+    received, (base_in, base) = rest[: len(parts)], rest[len(parts) :]
+    land_rows(sizes, parts, scale, land, received, base)
+
+
+def finish_kernel(sizes, parts, chunk, land, *rest):
+    cells, nodes, branches, cap, sub = sizes
+    received, (base_in, out, base, staged, sems) = rest[: len(parts)], rest[len(parts) :]
+    land_rows(sizes, parts, None, land, received, base)
     copies = []
     for number in range(cells // chunk):
 
@@ -543,15 +545,21 @@
     fraction = jnp.minimum(vehicles, cap_of) / vehicles
     supply = jnp.minimum(cap_of, wave.reshape(per_cell) * (jam.reshape(per_cell) - vehicles))
     rows_shape = pltpu.VMEM(((cells + 1) * sub, LANES), F32)
-    send_shape = pltpu.VMEM((cap * sub, LANES), F32)
+    early = cap // 2 // 16 * 16
+    parts = (*((side, 0, cap) for side in range(3)), (3, 0, early))
+    last_part = (3, early, cap - early)
+
+    def send_shape(part):
+        return pltpu.VMEM((part[2] * sub, LANES), F32)
+
 
     supply_there = to_neighbours(supply)
     weights = jnp.concatenate([fraction.reshape(-1), jnp.zeros((LANES,), F32)])
     (ahead,) = pl.pallas_call(
-        functools.partial(send_kernel, sizes, (2,)),
+        functools.partial(send_kernel, sizes, parts[2:3]),
         in_specs=[SMEM_WHOLE] * 4 + [VMEM_WHOLE] * 2,
         out_specs=[VMEM_WHOLE],
-        out_shape=[send_shape],
+        out_shape=[send_shape(parts[2])],
         compiler_params=params(4),
         cost_estimate=cost(1, 1),
         name="send_ahead",
@@ -566,16 +574,16 @@
         name="scale_rows",
     )(fraction.reshape(-1), rows, ahead, supply_there)
     near = pl.pallas_call(
-        functools.partial(send_kernel, sizes, (0, 1), None),
+        functools.partial(send_kernel, sizes, (*parts[:2], parts[3]), None),
         in_specs=[SMEM_WHOLE] * 3 + [VMEM_WHOLE] * 2,
-        out_specs=[VMEM_WHOLE] * 2,
-        out_shape=[send_shape] * 2,
+        out_specs=[VMEM_WHOLE] * 3,
+        out_shape=[send_shape(part) for part in (*parts[:2], parts[3])],
         compiler_params=params(4),
         cost_estimate=cost(1, 1),
         name="send_near",
     )(in_cell, send_node, send_outlet, scaled, turns)
     arrived = [
-        shifted(send, "region", SHIFTS[side]) for side, send in enumerate([*near, ahead])
+        shifted(send, "region", SHIFTS[side]) for side, send in enumerate([*near[:2], ahead, near[2]])
     ]
 
     flow, demand = pl.pallas_call(
@@ -611,21 +619,23 @@
     theta_there = [to_two(slot_theta[:per_side], 0), to_two(slot_theta[per_side:], 2)]
 
     (behind,) = pl.pallas_call(
-        functools.partial(scaled_send_kernel, sizes, 3),
+        functools.partial(scaled_send_kernel, sizes, last_part),
         in_specs=[SMEM_WHOLE] * 3 + [VMEM_WHOLE] * 2,
         out_specs=[VMEM_WHOLE],
-        out_shape=[send_shape],
+        out_shape=[send_shape(last_part)],
         compiler_params=params(4),
         cost_estimate=cost(1, 1),
         name="send_scaled",
     )(theta.reshape(-1), send_node, send_outlet, flow, turns)
+    behind, arrived[3] = lax.optimization_barrier((behind, arrived[3]))
+    last = shifted(behind, "region", SHIFTS[3])
     home = pl.pallas_call(
         functools.partial(home_kernel, sizes),
         in_specs=[SMEM_WHOLE] * 2 + [VMEM_WHOLE] * 2 + [ANYWHERE],
         out_specs=VMEM_WHOLE,
         out_shape=rows_shape,
         compiler_params=params(4),
-        cost_estimate=cost(4000000000, 1),
+        cost_estimate=cost(2000000000, 1),
         name="home_rows",
     )(source_node, source_outlet, turns, flow, behind)
     keep, home_theta = pl.pallas_call(
@@ -649,25 +659,24 @@
 
     base, *rest = lax.optimization_barrier((base, *theta_there, *arrived))
     theta_there, arrived = rest[:2], rest[2:]
-    last = shifted(behind, "region", SHIFTS[3])
     got = jnp.concatenate(theta_there)
     members = lax.axis_size("dest")
     other = lax.ppermute(got, "dest", [(i, i ^ 1) for i in range(members)])
     scale = jnp.concatenate([got, other])
 
     base = pl.pallas_call(
-        functools.partial(land_kernel, sizes, (0, 1, 2)),
-        in_specs=[SMEM_WHOLE] * 2 + [VMEM_WHOLE] * 4,
+        functools.partial(land_kernel, sizes, parts),
+        in_specs=[SMEM_WHOLE] * 2 + [VMEM_WHOLE] * 5,
         out_specs=VMEM_WHOLE,
         out_shape=rows_shape,
-        input_output_aliases={5: 0},
+        input_output_aliases={6: 0},
         compiler_params=params(4),
-        cost_estimate=cost(4000000000, 1),
+        cost_estimate=cost(2000000000, 1),
         name="land_first",
     )(scale.reshape(-1), land, *arrived, base)
 
     out, _ = pl.pallas_call(
-        functools.partial(finish_kernel, sizes, (3,), chunk),
+        functools.partial(finish_kernel, sizes, (last_part,), chunk),
         in_specs=[SMEM_WHOLE] + [VMEM_WHOLE] * 2,
         out_specs=[ANYWHERE, VMEM_WHOLE],
         out_shape=[jax.ShapeDtypeStruct((cells, width), F32), rows_shape],

time: 75.2 us -> 80.6 us (1.072)
  waiting for transfers between devices: 12.2 us -> 16.4 us
  starting transfers between devices: 14.2 us -> 15.1 us
    ppermute x4 -> x5, waiting for transfers between devices: 7.26 us -> 14.1 us  [shifted(): return lax.ppermute(block, axis, route)]
    ppermute x2, waiting for transfers between devices: 2.71 us -> 0.01 us  [to_two(): return lax.ppermute(block, ('region', 'dest'), route)]
    ppermute x2, starting transfers between devices: 2.22 us -> 3.73 us  [to_two(): return lax.ppermute(block, ('region', 'dest'), route)]
    ppermute x4 -> x5, starting transfers between devices: 7.1 us -> 6.57 us  [shifted(): return lax.ppermute(block, axis, route)]
  transfers between devices with their start and end apart: 11 -> 12, of which waited for: 5 -> 4; matrix products, arithmetic and copies ran while one was open for 0% -> 0% of each run, Pallas kernels for 45% -> 43%
where the time goes in v15:
time: 80.6 us; the launch traced here: 80.5 us
  Pallas kernels  42.9 us (53%)
  waiting for transfers between devices  16.4 us (20%)
  starting transfers between devices  15.1 us (19%)
  blocking collectives  5.72 us (7%)
    ppermute x5, waiting for transfers between devices, shifted(): return lax.ppermute(block, axis, route)  14.1 us
    pallas_call x1, Pallas kernels, on_device(): pl.pallas_call(functools.partial(node_flow_kernel, sizes), in_specs=[SMEM...  8.98 us
    ppermute x5, starting transfers between devices, shifted(): return lax.ppermute(block, axis, route)  6.57 us
    all_gather x1, blocking collectives, on_device(): shared = lax.all_gather(joined, 'dest', axis=0, tiled=True)  5.72 us
    pallas_call x1, Pallas kernels, on_device(): pl.pallas_call(functools.partial(home_kernel, sizes), in_specs=[SMEM_WHOL...  4.66 us
    pallas_call x1, Pallas kernels, on_device(): pl.pallas_call(functools.partial(finish_kernel, sizes, (last_part,), chun...  4.31 us
    pallas_call x1, Pallas kernels, on_device(): pl.pallas_call(functools.partial(cell_sum_kernel, chunk, sub), in_specs=[...  4.31 us
    pallas_call x1, Pallas kernels, on_device(): pl.pallas_call(functools.partial(send_kernel, sizes, (*parts[:2], parts[3...  3.86 us
  transfers between devices with their start and end apart: 12, of which 4 were waited for; matrix products, arithmetic and copies ran while one was open for 0% of the time, Pallas kernels for 43%

profile of v15, /device:TPU:0, one launch (start us, length us, event | category | flops | bytes accessed | tf_op | source)
XLA Modules:
  0.0 80.5 jit_solution(8810385877071894903)
XLA Ops:
  0.0 4.3 %cell_sum.1 = (f32[16,128]{1,0:T(8,128)S(1)}, f32[16392,128]{1,0:T(8,128)S(1)}) custom-call(f32[2048,1024]{1,0:T(8,128)} %x_hbm.2), custom_call_target="tpu_custom_call" | custom-call | flops 2097152 | bytes 8388608 | tf_op jit(solution)/shard_map/cell_sum/pallas_call | solution.py:500
  4.3 2.4 %collective-permute-start.2 = (f32[16,128]{1,0:T(8,128)S(1)}, f32[16,128]{1,0:T(8,128)S(1)}, u32[]{:S(2)}, u32[]{:S(2)}) collective-permute-start(f32[16,128]{1,0:T(8,128)S(1)} %get-tuple-element.44.after_ref), channel_id=1, source_target_pairs={{0,3},{1,2},{2,1},{3,0},{4,7},{5,6},{6,5},{7,4},{8,11},{9,10},{10,... | collective-permute-start | bytes 24584 | tf_op jit(solution)/shard_map/ppermute | solution.py:49
  6.8 0.6 collective-permute-start.1
  7.4 0.0 collective-permute-start
  7.5 2.5 %turn_rows.1 = (s32[8192,128]{1,0:T(8,128)S(1)}, s32[32,128]{1,0:T(8,128)S(1)}, s32[8,128]{1,0:T(8,128)S(1)}, s32[8,128]{1,0:T(8,128)S(1)}, s32[8,128]{1,0:T(8,1...) custom-call(s32[1024,1024]{1,0:T(8,128)} %x_hbm.3, f32[16,128]{1,0:T(8,128)S(1)} %get-tuple-element.44.after_ref, ...), custom_call_target="tpu_custom_call" | custom-call | bytes 4194304 | tf_op jit(solution)/shard_map/turn_rows/pallas_call | solution.py:520
  10.0 0.0 collective-permute-done.2
  10.0 0.4 collective-permute-done.1
  10.4 0.0 collective-permute-done
  10.5 1.6 %collective-permute-start.3 = (f32[16,128]{1,0:T(8,128)S(1)}, f32[16,128]{1,0:T(8,128)S(1)}, u32[]{:S(2)}, u32[]{:S(2)}) collective-permute-start(f32[16,128]{1,0:T(8,128)S(1)} %fusion.1.supply), channel_id=1, source_target_pairs={{0,4},{1,29},{2,10},{3,27},{4,8},{5,1},{6,14},{7,31},{8,12},{9,5},... | collective-permute-start | bytes 24584 | tf_op jit(solution)/shard_map/ppermute | solution.py:27
  12.1 2.5 %send_ahead.1.sent_ref = f32[1536,128]{1,0:T(8,128)S(1)} custom-call(f32[2176]{0:T(1024)S(1)} %concatenate.13.fraction, s32[4096]{0:T(1024)S(1)} %bitcast.23, s32[1024]{0:T(1024)S(1)} %bitcast.28, s32[1024]{0:T(1024)S(1)} %bitcast.31, f32[16392,128]{1,0:T(8,128)S(1)} %get-tuple-element.49.rows, s32[8192,128]{1,0:T(8,128)S(1)} %get-tuple-element.52.turns), custom_call_target="tpu_custom_call" | custom-call | flops 1 | bytes 1 | tf_op jit(solution)/shard_map/send_ahead/pallas_call | solution.py:558
  14.5 1.6 %collective-permute-start.4 = (f32[1536,128]{1,0:T(8,128)S(1)}, f32[1536,128]{1,0:T(8,128)S(1)}, u32[]{:S(2)}, u32[]{:S(2)}) collective-permute-start(f32[1536,128]{1,0:T(8,128)S(1)} %send_ahead.1.sent_ref), channel_id=1, source_target_pairs={{24,0},{28,4},{0,8},{4,12},{8,16},{12,20},{16,24},{20,28},{25,1},{... | collective-permute-start | bytes 2359304 | tf_op jit(solution)/shard_map/ppermute | solution.py:43
  16.2 0.7 collective-permute-done.3.supply_ref
  16.9 2.5 %scale_rows.1.rows.scaled = f32[16392,128]{1,0:T(8,128)S(1)} custom-call(f32[2048]{0:T(1024)S(1)} %bitcast.27, f32[16392,128]{1,0:T(8,128)S(1)} %get-tuple-element.49.rows, f32[1536,128]{1,0:T(8,128)S(1)} %send_ahead.1.sent_ref, f32[16,128]{1,0:T(8,128)S(1)} %collective-permute-done.3.supply_ref), custom_call_target="tpu_custom_call" | custom-call | flops 10000000000 | bytes 1 | tf_op jit(solution)/shard_map/scale_rows/pallas_call | solution.py:567
  19.4 3.9 %send_near.1 = (f32[1536,128]{1,0:T(8,128)S(1)}, f32[1536,128]{1,0:T(8,128)S(1)}, f32[768,128]{1,0:T(8,128)S(1)}) custom-call(s32[4096]{0:T(1024)S(1)} %bitcast.24, s32[1024]{0:T(1024)S(1)} %bitcast.29, s32[1024]{0:T(1024)S(1)} %bitcast.32, f32[16392,128]{1,0:T(8,128)S(1)} %scale_rows.1.rows.scaled, s32[8192,128]{1,0:T(8,128)S(1)} %get-tuple-element.52.turns), custom_call_target="tpu_custom_call" | custom-call | flops 1 | bytes 1 | tf_op jit(solution)/shard_map/send_near/pallas_call | solution.py:576
  23.3 2.5 %collective-permute-start.10 = (f32[1536,128]{1,0:T(8,128)S(1)}, f32[1536,128]{1,0:T(8,128)S(1)}, u32[]{:S(2)}, u32[]{:S(2)}) collective-permute-start(f32[1536,128]{1,0:T(8,128)S(1)} %get-tuple-element.67), channel_id=1, source_target_pairs={{4,0},{8,4},{12,8},{16,12},{20,16},{24,20},{28,24},{0,28},{5,1},{9... | collective-permute-start | bytes 2359304 | tf_op jit(solution)/shard_map/ppermute | solution.py:43
  25.8 0.0 collective-permute-start.9
  25.8 1.4 %collective-permute-start.5 = (f32[768,128]{1,0:T(8,128)S(1)}, f32[768,128]{1,0:T(8,128)S(1)}, u32[]{:S(2)}, u32[]{:S(2)}) collective-permute-start(f32[768,128]{1,0:T(8,128)S(1)} %get-tuple-element.59), channel_id=1, source_target_pairs={{8,0},{12,4},{16,8},{20,12},{24,16},{28,20},{0,24},{4,28},{9,1},{1... | collective-permute-start | bytes 1179656 | tf_op jit(solution)/shard_map/ppermute | solution.py:43
  27.1 9.0 %node_flow.1 = (f32[8192,128]{1,0:T(8,128)S(1)}, f32[32,128]{1,0:T(8,128)S(1)}) custom-call(s32[4096]{0:T(1024)S(1)} %bitcast.25, f32[16392,128]{1,0:T(8,128)S(1)} %scale_rows.1.rows.scaled, s32[8192,128]{1,0:T(8,128)S(1)} %get-tuple-element.52.turns, f32[1536,128]{1,0:T(8,128)S(1)} %get-tuple-element.53.after_ref), custom_call_target="tpu_custom_call" | custom-call | flops 1 | bytes 1 | tf_op jit(solution)/shard_map/node_flow/pallas_call | solution.py:589
  36.1 5.7 %all_gather.3.shared = f32[192,128]{1,0:T(8,128)S(1)} all-gather(f32[48,128]{1,0:T(8,128)S(1)} %pad_maximum_fusion), channel_id=1, replica_groups=mesh['region'=8,'dest'=4] {'dest'}, dimensions={0}, use_global_device_ids=true | all-gather | bytes 122880 | tf_op jit(solution)/shard_map/all_gather | solution.py:604
  41.9 1.5 %theta.1 = (f32[8,128]{1,0:T(8,128)S(1)}, f32[4,128]{1,0:T(4,128)S(1)}) custom-call(f32[16,128]{1,0:T(8,128)S(1)} %fusion.1.supply, f32[192,128]{1,0:T(8,128)S(1)} %all_gather.3.shared, s32[4,1024]{1,0:T(4,128)S(1)} %copy-done, s32[4,192]{1,0:T(4,128)S(1)} %copy-done.2), custom_call_target="tpu_custom_call" | custom-call | flops 1 | bytes 1 | tf_op jit(solution)/shard_map/theta/pallas_call | solution.py:605
  43.4 0.7 collective-permute-start.8
  44.0 3.0 %collective-permute-start.7 = (f32[2,128]{1,0:T(2,128)S(1)}, f32[2,128]{1,0:T(2,128)S(1)}, u32[]{:S(2)}, u32[]{:S(2)}) collective-permute-start(f32[2,128]{1,0:T(2,128)S(1)} %get-tuple-element.80), channel_id=1, source_target_pairs={{0,4},{1,29},{2,6},{3,31},{4,8},{5,1},{6,10},{7,3},{8,12},{9,5},{1... | collective-permute-start | bytes 3080 | tf_op jit(solution)/shard_map/ppermute | solution.py:37
  47.1 1.0 %send_scaled.1.sent_ref.after_ref = f32[768,128]{1,0:T(8,128)S(1)} custom-call(f32[1024]{0:T(1024)S(1)} %bitcast.34, s32[1024]{0:T(1024)S(1)} %bitcast.30, s32[1024]{0:T(1024)S(1)} %bitcast.33, f32[8192,128]{1,0:T(8,128)S(1)} %get-tuple-element.58.flow, s32[8192,128]{1,0:T(8,128)S(1)} %get-tuple-element.52.turns), custom_call_target="tpu_custom_call" | custom-call | flops 1 | bytes 1 | tf_op jit(solution)/shard_map/send_scaled/pallas_call | solution.py:621
  48.0 14.1 %collective-permute-done.5.rest_3_ = f32[768,128]{1,0:T(8,128)S(1)} collective-permute-done((f32[768,128]{1,0:T(8,128)S(1)}, f32[768,128]{1,0:T(8,128)S(1)}, u32[]{:S(2)}, u32[]{:S(2)}) %collective-permute-start.5) | collective-permute-done | bytes 393248 | tf_op jit(solution)/shard_map/ppermute | solution.py:43
  62.2 1.1 %collective-permute-start.6 = (f32[768,128]{1,0:T(8,128)S(1)}, f32[768,128]{1,0:T(8,128)S(1)}, u32[]{:S(2)}, u32[]{:S(2)}) collective-permute-start(f32[768,128]{1,0:T(8,128)S(1)} %send_scaled.1.sent_ref.after_ref), channel_id=1, source_target_pairs={{8,0},{12,4},{16,8},{20,12},{24,16},{28,20},{0,24},{4,28},{9,1},{1... | collective-permute-start | bytes 1179656 | tf_op jit(solution)/shard_map/ppermute | solution.py:43
  63.2 0.7 keep.1
  63.9 4.7 %home_rows.1.home = f32[16392,128]{1,0:T(8,128)S(1)} custom-call(s32[2048]{0:T(1024)S(1)} %bitcast.37, s32[2048]{0:T(1024)S(1)} %bitcast.38, s32[8192,128]{1,0:T(8,128)S(1)} %get-tuple-element.52.turns, f32[8192,128]{1,0:T(8,128)S(1)} %get-tuple-element.58.flow, f32[768,128]{1,0:T(8,128)S(1)} %send_scaled.1.sent_ref.after_ref), custom_call_target="tpu_custom_call" | custom-call | flops 2000000000 | bytes 1 | tf_op jit(solution)/shard_map/home_rows/pallas_call | solution.py:632
  68.6 3.8 %base_rows.1.rest_4_ = f32[16392,128]{1,0:T(8,128)S(1)} custom-call(f32[2048]{0:T(1024)S(1)} %bitcast.39, f32[2048]{0:T(1024)S(1)} %bitcast.40, f32[16392,128]{1,0:T(8,128)S(1)} %get-tuple-element.49.rows, f32[16392,128]{1,0:T(8,128)S(1)} %home_rows.1.home), custom_call_target="tpu_custom_call" | custom-call | flops 10000000 | bytes 1 | tf_op jit(solution)/shard_map/base_rows/pallas_call | solution.py:650
  72.5 0.1 collective-permute-start.11
  72.6 1.1 %collective-permute-done.11 = f32[4,128]{1,0:T(4,128)S(1)} collective-permute-done((f32[4,128]{1,0:T(4,128)S(1)}, f32[4,128]{1,0:T(4,128)S(1)}, u32[]{:S(2)}, u32[]{:S(2)}) %collective-permute-start.11) | collective-permute-done | bytes 2080 | tf_op jit(solution)/shard_map/ppermute | solution.py:664
  73.7 2.4 %land_first.1.rest_1_ = f32[16392,128]{1,0:T(8,128)S(1)} custom-call(f32[1024]{0:T(1024)S(1)} %maximum_bitcast_fusion.scale, s32[1024]{0:T(1024)S(1)} %bitcast.35, f32[1536,128]{1,0:T(8,128)S(1)} %collective-permute-done.9.rest_0_, f32[1536,128]{1,0:T(8,128)S(1)} %collective-permute-done.10.rest_1_, ...), custom_call_target="tpu_custom_call", output_to_operand_aliasing={{}: (6, {})} | custom-call | flops 2000000000 | bytes 1 | tf_op jit(solution)/shard_map/land_first/pallas_call | solution.py:667
  76.2 4.3 %finish.1 = (f32[2048,1024]{1,0:T(8,128)}, f32[16392,128]{1,0:T(8,128)S(1)}) custom-call(s32[1024]{0:T(1024)S(1)} %bitcast.36, f32[768,128]{1,0:T(8,128)S(1)} %collective-permute-done.6.rest_0_, f32[16392,128]{1,0:T(8,128)S(1)} %land_first.1.rest_1_), custom_call_target="tpu_custom_call", output_to_operand_aliasing={{1}: (2, {})} | custom-call | flops 2097152 | bytes 8388608 | tf_op jit(solution)/shard_map/finish/pallas_call | solution.py:678
  (27 shorter events, 0.1 us)
Async XLA Ops:
  0.0 7.5 %copy-start = (s32[4,1024]{1,0:T(4,128)S(1)}, s32[4,1024]{1,0:T(4,128)}, u32[]{:S(2)}) copy-start(s32[4,1024]{1,0:T(4,128)} %node_out.3) | copy-start | bytes 49156
  0.0 7.5 %copy-start.2 = (s32[4,192]{1,0:T(4,128)S(1)}, s32[4,192]{1,0:T(4,128)}, u32[]{:S(2)}) copy-start(s32[4,192]{1,0:T(4,128)} %send_list.1) | copy-start | bytes 9220
  0.0 7.5 %copy-start.1 = (s32[4,1024]{1,0:T(4,128)S(1)}, s32[4,1024]{1,0:T(4,128)}, u32[]{:S(2)}) copy-start(s32[4,1024]{1,0:T(4,128)} %node_in.1) | copy-start | bytes 49156
  0.0 7.5 %copy-start.3 = (s32[4,192]{1,0:T(4,128)S(1)}, s32[4,192]{1,0:T(4,128)}, u32[]{:S(2)}) copy-start(s32[4,192]{1,0:T(4,128)} %rest_3_.1) | copy-start | bytes 9220
  0.0 10.4 %copy-start.4 = (f32[2048]{0:T(1024)S(1)}, f32[2048]{0:T(1024)}, u32[]{:S(2)}) copy-start(f32[2048]{0:T(1024)} %param.10) | copy-start | bytes 24580
  0.0 10.5 %copy-start.6 = (f32[2048]{0:T(1024)S(1)}, f32[2048]{0:T(1024)}, u32[]{:S(2)}) copy-start(f32[2048]{0:T(1024)} %param.12) | copy-start | bytes 24580
  0.0 10.5 %copy-start.5 = (f32[2048]{0:T(1024)S(1)}, f32[2048]{0:T(1024)}, u32[]{:S(2)}) copy-start(f32[2048]{0:T(1024)} %param.11) | copy-start | bytes 24580
  4.3 5.7 %collective-permute-start.2 = (f32[16,128]{1,0:T(8,128)S(1)}, f32[16,128]{1,0:T(8,128)S(1)}, u32[]{:S(2)}, u32[]{:S(2)}) collective-permute-start(f32[16,128]{1,0:T(8,128)S(1)} %get-tuple-element.44.after_ref), channel_id=1, source_target_pairs={{0,3},{1,2},{2,1},{3,0},{4,7},{5,6},{6,5},{7,4},{8,11},{9,10},{10,... | collective-permute-start | bytes 24584 | tf_op jit(solution)/shard_map/ppermute | solution.py:49
  6.8 3.7 %collective-permute-start.1 = (f32[16,128]{1,0:T(8,128)S(1)}, f32[16,128]{1,0:T(8,128)S(1)}, u32[]{:S(2)}, u32[]{:S(2)}) collective-permute-start(f32[16,128]{1,0:T(8,128)S(1)} %get-tuple-element.44.after_ref), channel_id=1, source_target_pairs={{0,2},{1,3},{2,0},{3,1},{4,6},{5,7},{6,4},{7,5},{8,10},{9,11},{10,... | collective-permute-start | bytes 24584 | tf_op jit(solution)/shard_map/ppermute | solution.py:49
  7.4 3.0 %collective-permute-start = (f32[16,128]{1,0:T(8,128)S(1)}, f32[16,128]{1,0:T(8,128)S(1)}, u32[]{:S(2)}, u32[]{:S(2)}) collective-permute-start(f32[16,128]{1,0:T(8,128)S(1)} %get-tuple-element.44.after_ref), channel_id=1, source_target_pairs={{0,1},{1,0},{2,3},{3,2},{4,5},{5,4},{6,7},{7,6},{8,9},{9,8},{10,11... | collective-permute-start | bytes 24584 | tf_op jit(solution)/shard_map/ppermute | solution.py:49
  10.5 6.4 %collective-permute-start.3 = (f32[16,128]{1,0:T(8,128)S(1)}, f32[16,128]{1,0:T(8,128)S(1)}, u32[]{:S(2)}, u32[]{:S(2)}) collective-permute-start(f32[16,128]{1,0:T(8,128)S(1)} %fusion.1.supply), channel_id=1, source_target_pairs={{0,4},{1,29},{2,10},{3,27},{4,8},{5,1},{6,14},{7,31},{8,12},{9,5},... | collective-permute-start | bytes 24584 | tf_op jit(solution)/shard_map/ppermute | solution.py:27
  14.5 28.8 %collective-permute-start.4 = (f32[1536,128]{1,0:T(8,128)S(1)}, f32[1536,128]{1,0:T(8,128)S(1)}, u32[]{:S(2)}, u32[]{:S(2)}) collective-permute-start(f32[1536,128]{1,0:T(8,128)S(1)} %send_ahead.1.sent_ref), channel_id=1, source_target_pairs={{24,0},{28,4},{0,8},{4,12},{8,16},{12,20},{16,24},{20,28},{25,1},{... | collective-permute-start | bytes 2359304 | tf_op jit(solution)/shard_map/ppermute | solution.py:43
  23.3 49.2 %collective-permute-start.10 = (f32[1536,128]{1,0:T(8,128)S(1)}, f32[1536,128]{1,0:T(8,128)S(1)}, u32[]{:S(2)}, u32[]{:S(2)}) collective-permute-start(f32[1536,128]{1,0:T(8,128)S(1)} %get-tuple-element.67), channel_id=1, source_target_pairs={{4,0},{8,4},{12,8},{16,12},{20,16},{24,20},{28,24},{0,28},{5,1},{9... | collective-permute-start | bytes 2359304 | tf_op jit(solution)/shard_map/ppermute | solution.py:43
  25.8 46.6 %collective-permute-start.9 = (f32[1536,128]{1,0:T(8,128)S(1)}, f32[1536,128]{1,0:T(8,128)S(1)}, u32[]{:S(2)}, u32[]{:S(2)}) collective-permute-start(f32[1536,128]{1,0:T(8,128)S(1)} %get-tuple-element.53.after_ref), channel_id=1, source_target_pairs={{28,0},{0,4},{4,8},{8,12},{12,16},{16,20},{20,24},{24,28},{29,1},{... | collective-permute-start | bytes 2359304 | tf_op jit(solution)/shard_map/ppermute | solution.py:43
  25.8 36.4 %collective-permute-start.5 = (f32[768,128]{1,0:T(8,128)S(1)}, f32[768,128]{1,0:T(8,128)S(1)}, u32[]{:S(2)}, u32[]{:S(2)}) collective-permute-start(f32[768,128]{1,0:T(8,128)S(1)} %get-tuple-element.59), channel_id=1, source_target_pairs={{8,0},{12,4},{16,8},{20,12},{24,16},{28,20},{0,24},{4,28},{9,1},{1... | collective-permute-start | bytes 1179656 | tf_op jit(solution)/shard_map/ppermute | solution.py:43
  43.4 29.0 %collective-permute-start.8 = (f32[2,128]{1,0:T(2,128)S(1)}, f32[2,128]{1,0:T(2,128)S(1)}, u32[]{:S(2)}, u32[]{:S(2)}) collective-permute-start(f32[2,128]{1,0:T(2,128)S(1)} %get-tuple-element.79), channel_id=1, source_target_pairs={{0,8},{1,25},{2,10},{3,27},{4,12},{5,29},{6,14},{7,31},{8,16},{9,1... | collective-permute-start | bytes 3080 | tf_op jit(solution)/shard_map/ppermute | solution.py:37
  44.0 28.4 %collective-permute-start.7 = (f32[2,128]{1,0:T(2,128)S(1)}, f32[2,128]{1,0:T(2,128)S(1)}, u32[]{:S(2)}, u32[]{:S(2)}) collective-permute-start(f32[2,128]{1,0:T(2,128)S(1)} %get-tuple-element.80), channel_id=1, source_target_pairs={{0,4},{1,29},{2,6},{3,31},{4,8},{5,1},{6,10},{7,3},{8,12},{9,5},{1... | collective-permute-start | bytes 3080 | tf_op jit(solution)/shard_map/ppermute | solution.py:37
  62.2 14.0 %collective-permute-start.6 = (f32[768,128]{1,0:T(8,128)S(1)}, f32[768,128]{1,0:T(8,128)S(1)}, u32[]{:S(2)}, u32[]{:S(2)}) collective-permute-start(f32[768,128]{1,0:T(8,128)S(1)} %send_scaled.1.sent_ref.after_ref), channel_id=1, source_target_pairs={{8,0},{12,4},{16,8},{20,12},{24,16},{28,20},{0,24},{4,28},{9,1},{1... | collective-permute-start | bytes 1179656 | tf_op jit(solution)/shard_map/ppermute | solution.py:43
  72.5 1.2 %collective-permute-start.11 = (f32[4,128]{1,0:T(4,128)S(1)}, f32[4,128]{1,0:T(4,128)S(1)}, u32[]{:S(2)}, u32[]{:S(2)}) collective-permute-start(f32[4,128]{1,0:T(4,128)S(1)} %pad_maximum_fusion.1), channel_id=1, source_target_pairs={{0,1},{1,0},{2,3},{3,2},{4,5},{5,4},{6,7},{7,6},{8,9},{9,8},{10,11... | collective-permute-start | bytes 6152 | tf_op jit(solution)/shard_map/ppermute | solution.py:664

commit v16 on v14

--- a/solution.py
+++ b/solution.py
@@ -8,6 +8,7 @@
 from jax.sharding import PartitionSpec as P
 
 SHIFTS = (1, -1, 2, -2)
+AHEAD = 2
 LANES = 128
 MIB = 1 << 20
 F32 = jnp.float32
@@ -171,7 +172,7 @@
 
 def make_lists(
     sizes, node_in, node_out, send_list, recv_list,
-    in_cell, send_node, send_outlet, land, source_node, source_outlet,
+    in_cell, send_node, send_outlet, land, ahead, source_node, source_outlet,
 ):
     cells, nodes, branches, cap, sub = sizes
     height = cells // LANES
@@ -192,9 +193,18 @@
     for side in range(4):
         slots = send_list[side : side + 1, :]
         lands = recv_list[side : side + 1, :]
-        put_row(send_node, side * per_side, jnp.where(slots >= 0, slots % nodes, 0), 0)
-        put_row(send_outlet, side * per_side, jnp.where(slots >= 0, slots // nodes, -1), -1)
+        node = jnp.where(slots >= 0, slots % nodes, 0)
+        outlet = jnp.where(slots >= 0, slots // nodes, -1)
+        put_row(send_node, side * per_side, node, 0)
+        put_row(send_outlet, side * per_side, outlet, -1)
         put_row(land, side * per_side, jnp.where(lands >= 0, lands, cells), cells)
+        if side == AHEAD:
+            for j in range(branches):
+                ins = node_in[j : j + 1, :]
+                table = stacked(jnp.where(ins >= 0, ins, cells)).astype(F32)
+                put_row(ahead, j * per_side, (look_up(table, node) + 0.5).astype(I32), cells)
+            put_row(ahead, branches * per_side, node, 0)
+            put_row(ahead, (branches + 1) * per_side, outlet, -1)
 
 
 def cell_sum_kernel(chunk, sub, x_hbm, sum_ref, rows_ref, x, partial, sems):
@@ -217,7 +227,7 @@
 
 def turn_rows_kernel(sizes, chunk, x_hbm, after_ref, *rest):
     cells, nodes, branches, cap, sub = sizes
-    lists, rows_ref, made, (x, sems) = rest[:4], rest[4], rest[5:11], rest[11:]
+    lists, rows_ref, made, (x, sems) = rest[:4], rest[4], rest[5:12], rest[12:]
     copies = copies_in(x_hbm, x, sems, chunk)
     make_lists(sizes, *lists, *made)
     for number, copy in enumerate(copies):
@@ -231,14 +241,35 @@
         lax.fori_loop(0, chunk // 16, body, 0)
 
 
-def gathered_flow(node, in_cell, fraction, rows, sizes):
-    cells, nodes, branches, cap, sub = sizes
-    parts = []
-    for i in range(branches):
-        cell = in_cell[i * nodes + node]
-        part = row_of(rows, cell, sub)[...]
-        parts.append(part if fraction is None else part * fraction[cell])
-    return tree_sum(parts)
+def gathered_flow(node, in_cell, scaled, sizes):
+    cells, nodes, branches, cap, sub = sizes
+    return tree_sum(
+        [row_of(scaled, in_cell[i * nodes + node], sub)[...] for i in range(branches)]
+    )
+
+
+def send_ahead_kernel(sizes, fraction, slots, rows, turns, send):
+    cells, nodes, branches, cap, sub = sizes
+    batch = 16
+
+    def body(step, carry):
+        first = step * batch
+        values = []
+        for i in range(batch):
+            slot = first + i
+            parts = []
+            for j in range(branches):
+                cell = slots[j * padded(cap) + slot]
+                parts.append(row_of(rows, cell, sub)[...] * fraction[cell])
+            node = slots[branches * padded(cap) + slot]
+            choice = row_of(turns, node, sub)[...]
+            outlet = slots[(branches + 1) * padded(cap) + slot]
+            values.append(jnp.where(choice == outlet, tree_sum(parts), 0.0))
+        for i in range(batch):
+            row_of(send, first + i, sub)[...] = values[i]
+        return carry
+
+    lax.fori_loop(0, cap // batch, body, 0)
 
 
 def scale_kernel(sizes, fraction, rows, sent_ref, supply_ref, scaled):
@@ -257,7 +288,7 @@
     row_of(scaled, cells, sub)[...] = jnp.zeros((sub, LANES), F32)
 
 
-def send_kernel(sizes, sides, fraction, in_cell, send_node, send_outlet, rows, turns, *sends):
+def send_kernel(sizes, sides, in_cell, send_node, send_outlet, scaled, turns, *sends):
     cells, nodes, branches, cap, sub = sizes
     batch = 16
     for side, send in zip(sides, sends):
@@ -268,7 +299,7 @@
             for i in range(batch):
                 slot = side * padded(cap) + first + i
                 node = send_node[slot]
-                value = gathered_flow(node, in_cell, fraction, rows, sizes)
+                value = gathered_flow(node, in_cell, scaled, sizes)
                 choice = row_of(turns, node, sub)[...]
                 values.append(jnp.where(choice == send_outlet[slot], value, 0.0))
             for i in range(batch):
@@ -304,7 +335,7 @@
     def gather(step, carry):
         first = step * 16
         values = [
-            gathered_flow(first + i, in_cell, None, scaled, sizes) for i in range(16)
+            gathered_flow(first + i, in_cell, scaled, sizes) for i in range(16)
         ]
         for i in range(16):
             row_of(flow, first + i, sub)[...] = values[i]
@@ -490,6 +521,7 @@
     height = cells // LANES
     per_cell = (height, LANES)
     list_shape = (4 * padded(cap) // LANES, LANES)
+    ahead_rows = -(-(branches + 2) * padded(cap) // LANES // 8) * 8
     chunk = 128
     row_bytes = width * 4
     occupancy = pltpu.with_memory_space_constraint(occupancy, pltpu.HBM)
@@ -518,12 +550,13 @@
     turns, *lists = pl.pallas_call(
         functools.partial(turn_rows_kernel, sizes, chunk),
         in_specs=[ANYWHERE] * 2 + [VMEM_WHOLE] * 4,
-        out_specs=[VMEM_WHOLE] * 7,
+        out_specs=[VMEM_WHOLE] * 8,
         out_shape=[
             pltpu.VMEM((nodes * sub, LANES), I32),
             jax.ShapeDtypeStruct((branches * nodes // LANES, LANES), I32),
         ]
         + [jax.ShapeDtypeStruct(list_shape, I32)] * 3
+        + [jax.ShapeDtypeStruct((ahead_rows, LANES), I32)]
         + [jax.ShapeDtypeStruct(per_cell, I32)] * 2,
         scratch_shapes=[
             pltpu.VMEM((nodes, width), I32),
@@ -533,7 +566,7 @@
         cost_estimate=cost(0, nodes * row_bytes),
         name="turn_rows",
     )(turn, local_sum, node_in, node_out, send_list, recv_list)
-    in_cell, send_node, send_outlet, land, source_node, source_outlet = (
+    in_cell, send_node, send_outlet, land, ahead_list, source_node, source_outlet = (
         x.reshape(-1) for x in lists
     )
 
@@ -548,14 +581,14 @@
     supply_there = to_neighbours(supply)
     weights = jnp.concatenate([fraction.reshape(-1), jnp.zeros((LANES,), F32)])
     (ahead,) = pl.pallas_call(
-        functools.partial(send_kernel, sizes, (2,)),
-        in_specs=[SMEM_WHOLE] * 4 + [VMEM_WHOLE] * 2,
+        functools.partial(send_ahead_kernel, sizes),
+        in_specs=[SMEM_WHOLE] * 2 + [VMEM_WHOLE] * 2,
         out_specs=[VMEM_WHOLE],
         out_shape=[send_shape],
         compiler_params=params(4),
         cost_estimate=cost(1, 1),
         name="send_ahead",
-    )(weights, in_cell, send_node, send_outlet, rows, turns)
+    )(weights, ahead_list, rows, turns)
     scaled = pl.pallas_call(
         functools.partial(scale_kernel, sizes),
         in_specs=[SMEM_WHOLE, VMEM_WHOLE, ANYWHERE, ANYWHERE],
@@ -566,7 +599,7 @@
         name="scale_rows",
     )(fraction.reshape(-1), rows, ahead, supply_there)
     near = pl.pallas_call(
-        functools.partial(send_kernel, sizes, (0, 1), None),
+        functools.partial(send_kernel, sizes, (0, 1)),
         in_specs=[SMEM_WHOLE] * 3 + [VMEM_WHOLE] * 2,
         out_specs=[VMEM_WHOLE] * 2,
         out_shape=[send_shape] * 2,

time: 75.2 us -> 75 us (level)
  transfers between devices with their start and end apart: 11 -> 11, of which waited for: 5 -> 6; matrix products, arithmetic and copies ran while one was open for 0% -> 0% of each run, Pallas kernels for 45% -> 45%
where the time goes in v16:
time: 75 us; the launch traced here: 74.8 us
  Pallas kernels  42.3 us (56%)
  starting transfers between devices  14.1 us (19%)
  waiting for transfers between devices  12.1 us (16%)
  blocking collectives  6.09 us (8%)
    pallas_call x1, Pallas kernels, on_device(): pl.pallas_call(functools.partial(node_flow_kernel, sizes), in_specs=[SMEM...  8.97 us
    ppermute x4, waiting for transfers between devices, shifted(): return lax.ppermute(block, axis, route)  7.54 us
    ppermute x4, starting transfers between devices, shifted(): return lax.ppermute(block, axis, route)  6.96 us
    all_gather x1, blocking collectives, on_device(): shared = lax.all_gather(joined, 'dest', axis=0, tiled=True)  6.09 us
    pallas_call x1, Pallas kernels, on_device(): pl.pallas_call(functools.partial(home_kernel, sizes), in_specs=[SMEM_WHOL...  4.63 us
    pallas_call x1, Pallas kernels, on_device(): pl.pallas_call(functools.partial(finish_kernel, sizes, (3,), chunk), in_s...  4.48 us
    pallas_call x1, Pallas kernels, on_device(): pl.pallas_call(functools.partial(cell_sum_kernel, chunk, sub), in_specs=[...  4.31 us
    pallas_call x1, Pallas kernels, on_device(): pl.pallas_call(functools.partial(base_kernel, sizes), in_specs=[SMEM_WHOL...  3.85 us
  transfers between devices with their start and end apart: 11, of which 6 were waited for; matrix products, arithmetic and copies ran while one was open for 0% of the time, Pallas kernels for 45%

profile of v16, /device:TPU:0, one launch (start us, length us, event | category | flops | bytes accessed | tf_op | source)
XLA Modules:
  0.0 74.8 jit_solution(9246817053910704784)
XLA Ops:
  0.0 4.3 %cell_sum.1 = (f32[16,128]{1,0:T(8,128)S(1)}, f32[16392,128]{1,0:T(8,128)S(1)}) custom-call(f32[2048,1024]{1,0:T(8,128)} %x_hbm.2), custom_call_target="tpu_custom_call" | custom-call | flops 2097152 | bytes 8388608 | tf_op jit(solution)/shard_map/cell_sum/pallas_call | solution.py:530
  4.3 2.4 %collective-permute-start.2 = (f32[16,128]{1,0:T(8,128)S(1)}, f32[16,128]{1,0:T(8,128)S(1)}, u32[]{:S(2)}, u32[]{:S(2)}) collective-permute-start(f32[16,128]{1,0:T(8,128)S(1)} %get-tuple-element.41.after_ref), channel_id=1, source_target_pairs={{0,3},{1,2},{2,1},{3,0},{4,7},{5,6},{6,5},{7,4},{8,11},{9,10},{10,... | collective-permute-start | bytes 24584 | tf_op jit(solution)/shard_map/ppermute | solution.py:50
  6.8 0.6 collective-permute-start.1
  7.4 0.0 collective-permute-start
  7.5 2.6 %turn_rows.1 = (s32[8192,128]{1,0:T(8,128)S(1)}, s32[32,128]{1,0:T(8,128)S(1)}, s32[8,128]{1,0:T(8,128)S(1)}, s32[8,128]{1,0:T(8,128)S(1)}, s32[8,128]{1,0:T(8,1...) custom-call(s32[1024,1024]{1,0:T(8,128)} %x_hbm.3, ...), custom_call_target="tpu_custom_call" | custom-call | bytes 4194304 | tf_op jit(solution)/shard_map/turn_rows/pallas_call | solution.py:550
  10.1 0.0 collective-permute-done.2
  10.1 0.3 collective-permute-done.1
  10.5 1.6 %collective-permute-start.3 = (f32[16,128]{1,0:T(8,128)S(1)}, f32[16,128]{1,0:T(8,128)S(1)}, u32[]{:S(2)}, u32[]{:S(2)}) collective-permute-start(f32[16,128]{1,0:T(8,128)S(1)} %fusion.1.supply), channel_id=1, source_target_pairs={{0,4},{1,29},{2,10},{3,27},{4,8},{5,1},{6,14},{7,31},{8,12},{9,5},... | collective-permute-start | bytes 24584 | tf_op jit(solution)/shard_map/ppermute | solution.py:28
  12.1 2.2 %send_ahead.1.sent_ref = f32[1536,128]{1,0:T(8,128)S(1)} custom-call(f32[2176]{0:T(1024)S(1)} %concatenate.13.fraction, s32[2048]{0:T(1024)S(1)} %bitcast.39, f32[16392,128]{1,0:T(8,128)S(1)} %get-tuple-element.46.rows, s32[8192,128]{1,0:T(8,128)S(1)} %get-tuple-element.48.turns), custom_call_target="tpu_custom_call" | custom-call | flops 1 | bytes 1 | tf_op jit(solution)/shard_map/send_ahead/pallas_call | solution.py:583
  14.3 1.6 %collective-permute-start.4 = (f32[1536,128]{1,0:T(8,128)S(1)}, f32[1536,128]{1,0:T(8,128)S(1)}, u32[]{:S(2)}, u32[]{:S(2)}) collective-permute-start(f32[1536,128]{1,0:T(8,128)S(1)} %send_ahead.1.sent_ref), channel_id=1, source_target_pairs={{24,0},{28,4},{0,8},{4,12},{8,16},{12,20},{16,24},{20,28},{25,1},{... | collective-permute-start | bytes 2359304 | tf_op jit(solution)/shard_map/ppermute | solution.py:44
  15.9 1.0 %collective-permute-done.3.supply_ref = f32[16,128]{1,0:T(8,128)S(1)} collective-permute-done((f32[16,128]{1,0:T(8,128)S(1)}, f32[16,128]{1,0:T(8,128)S(1)}, u32[]{:S(2)}, u32[]{:S(2)}) %collective-permute-start.3) | collective-permute-done | bytes 8224 | tf_op jit(solution)/shard_map/ppermute | solution.py:28
  16.9 2.5 %scale_rows.1.scaled = f32[16392,128]{1,0:T(8,128)S(1)} custom-call(f32[2048]{0:T(1024)S(1)} %bitcast.25, f32[16392,128]{1,0:T(8,128)S(1)} %get-tuple-element.46.rows, f32[1536,128]{1,0:T(8,128)S(1)} %send_ahead.1.sent_ref, f32[16,128]{1,0:T(8,128)S(1)} %collective-permute-done.3.supply_ref), custom_call_target="tpu_custom_call" | custom-call | flops 10000000000 | bytes 1 | tf_op jit(solution)/shard_map/scale_rows/pallas_call | solution.py:592
  19.4 3.3 %send_near.1 = (f32[1536,128]{1,0:T(8,128)S(1)}, f32[1536,128]{1,0:T(8,128)S(1)}) custom-call(s32[4096]{0:T(1024)S(1)} %bitcast.26, s32[1024]{0:T(1024)S(1)} %bitcast.28, s32[1024]{0:T(1024)S(1)} %bitcast.30, f32[16392,128]{1,0:T(8,128)S(1)} %scale_rows.1.scaled, s32[8192,128]{1,0:T(8,128)S(1)} %get-tuple-element.48.turns), custom_call_target="tpu_custom_call" | custom-call | flops 1 | bytes 1 | tf_op jit(solution)/shard_map/send_near/pallas_call | solution.py:601
  22.7 2.3 %collective-permute-start.9 = (f32[1536,128]{1,0:T(8,128)S(1)}, f32[1536,128]{1,0:T(8,128)S(1)}, u32[]{:S(2)}, u32[]{:S(2)}) collective-permute-start(f32[1536,128]{1,0:T(8,128)S(1)} %get-tuple-element.63), channel_id=1, source_target_pairs={{4,0},{8,4},{12,8},{16,12},{20,16},{24,20},{28,24},{0,28},{5,1},{9... | collective-permute-start | bytes 2359304 | tf_op jit(solution)/shard_map/ppermute | solution.py:44
  24.9 9.0 %node_flow.1 = (f32[8192,128]{1,0:T(8,128)S(1)}, f32[32,128]{1,0:T(8,128)S(1)}) custom-call(s32[4096]{0:T(1024)S(1)} %bitcast.27, f32[16392,128]{1,0:T(8,128)S(1)} %scale_rows.1.scaled, s32[8192,128]{1,0:T(8,128)S(1)} %get-tuple-element.48.turns, f32[1536,128]{1,0:T(8,128)S(1)} %get-tuple-element.51.after_ref), custom_call_target="tpu_custom_call" | custom-call | flops 1 | bytes 1 | tf_op jit(solution)/shard_map/node_flow/pallas_call | solution.py:614
  33.9 6.1 %all_gather.3.shared = f32[192,128]{1,0:T(8,128)S(1)} all-gather(f32[48,128]{1,0:T(8,128)S(1)} %pad_maximum_fusion), channel_id=1, replica_groups=mesh['region'=8,'dest'=4] {'dest'}, dimensions={0}, use_global_device_ids=true | all-gather | bytes 122880 | tf_op jit(solution)/shard_map/all_gather | solution.py:629
  40.0 1.4 %theta.1 = (f32[8,128]{1,0:T(8,128)S(1)}, f32[4,128]{1,0:T(4,128)S(1)}) custom-call(f32[16,128]{1,0:T(8,128)S(1)} %fusion.1.supply, f32[192,128]{1,0:T(8,128)S(1)} %all_gather.3.shared, s32[4,1024]{1,0:T(4,128)S(1)} %copy-done, s32[4,192]{1,0:T(4,128)S(1)} %copy-done.2), custom_call_target="tpu_custom_call" | custom-call | flops 1 | bytes 1 | tf_op jit(solution)/shard_map/theta/pallas_call | solution.py:630
  41.5 0.0 collective-permute-done.4.arrived_ref.rest_2_
  41.5 0.1 collective-permute-start.7
  41.6 2.1 %collective-permute-start.6 = (f32[2,128]{1,0:T(2,128)S(1)}, f32[2,128]{1,0:T(2,128)S(1)}, u32[]{:S(2)}, u32[]{:S(2)}) collective-permute-start(f32[2,128]{1,0:T(2,128)S(1)} %get-tuple-element.74), channel_id=1, source_target_pairs={{0,4},{1,29},{2,6},{3,31},{4,8},{5,1},{6,10},{7,3},{8,12},{9,5},{1... | collective-permute-start | bytes 3080 | tf_op jit(solution)/shard_map/ppermute | solution.py:38
  43.6 1.2 %send_scaled.1.sent_ref.after_ref = f32[1536,128]{1,0:T(8,128)S(1)} custom-call(f32[1024]{0:T(1024)S(1)} %bitcast.32, s32[1024]{0:T(1024)S(1)} %bitcast.29, s32[1024]{0:T(1024)S(1)} %bitcast.31, f32[8192,128]{1,0:T(8,128)S(1)} %get-tuple-element.56.flow, s32[8192,128]{1,0:T(8,128)S(1)} %get-tuple-element.48.turns), custom_call_target="tpu_custom_call" | custom-call | flops 1 | bytes 1 | tf_op jit(solution)/shard_map/send_scaled/pallas_call | solution.py:646
  44.8 3.1 %collective-permute-start.5 = (f32[1536,128]{1,0:T(8,128)S(1)}, f32[1536,128]{1,0:T(8,128)S(1)}, u32[]{:S(2)}, u32[]{:S(2)}) collective-permute-start(f32[1536,128]{1,0:T(8,128)S(1)} %send_scaled.1.sent_ref.after_ref), channel_id=1, source_target_pairs={{8,0},{12,4},{16,8},{20,12},{24,16},{28,20},{0,24},{4,28},{9,1},{1... | collective-permute-start | bytes 2359304 | tf_op jit(solution)/shard_map/ppermute | solution.py:44
  47.9 4.6 %home_rows.1.home = f32[16392,128]{1,0:T(8,128)S(1)} custom-call(s32[2048]{0:T(1024)S(1)} %bitcast.35, s32[2048]{0:T(1024)S(1)} %bitcast.36, s32[8192,128]{1,0:T(8,128)S(1)} %get-tuple-element.48.turns, f32[8192,128]{1,0:T(8,128)S(1)} %get-tuple-element.56.flow, f32[1536,128]{1,0:T(8,128)S(1)} %send_scaled.1.sent_ref.after_ref), custom_call_target="tpu_custom_call" | custom-call | flops 4000000000 | bytes 1 | tf_op jit(solution)/shard_map/home_rows/pallas_call | solution.py:655
  52.5 0.7 keep.1
  53.2 3.8 %base_rows.1.rest_3_ = f32[16392,128]{1,0:T(8,128)S(1)} custom-call(f32[2048]{0:T(1024)S(1)} %bitcast.37, f32[2048]{0:T(1024)S(1)} %bitcast.38, f32[16392,128]{1,0:T(8,128)S(1)} %get-tuple-element.46.rows, f32[16392,128]{1,0:T(8,128)S(1)} %home_rows.1.home), custom_call_target="tpu_custom_call" | custom-call | flops 10000000 | bytes 1 | tf_op jit(solution)/shard_map/base_rows/pallas_call | solution.py:673
  57.1 2.3 %collective-permute-done.6 = f32[2,128]{1,0:T(2,128)S(1)} collective-permute-done((f32[2,128]{1,0:T(2,128)S(1)}, f32[2,128]{1,0:T(2,128)S(1)}, u32[]{:S(2)}, u32[]{:S(2)}) %collective-permute-start.6) | collective-permute-done | bytes 1056 | tf_op jit(solution)/shard_map/ppermute | solution.py:38
  59.4 0.1 collective-permute-done.9.rest_1_
  59.5 0.3 collective-permute-start.10
  59.8 0.9 %collective-permute-done.10 = f32[4,128]{1,0:T(4,128)S(1)} collective-permute-done((f32[4,128]{1,0:T(4,128)S(1)}, f32[4,128]{1,0:T(4,128)S(1)}, u32[]{:S(2)}, u32[]{:S(2)}) %collective-permute-start.10) | collective-permute-done | bytes 2080 | tf_op jit(solution)/shard_map/ppermute | solution.py:688
  60.7 2.2 %land_first.1.rest_1_ = f32[16392,128]{1,0:T(8,128)S(1)} custom-call(f32[1024]{0:T(1024)S(1)} %maximum_bitcast_fusion.scale, s32[1024]{0:T(1024)S(1)} %bitcast.33, f32[1536,128]{1,0:T(8,128)S(1)} %collective-permute-done.8.rest_0_, f32[1536,128]{1,0:T(8,128)S(1)} %collective-permute-done.9.rest_1_, ...), custom_call_target="tpu_custom_call", output_to_operand_aliasing={{}: (5, {})} | custom-call | flops 4000000000 | bytes 1 | tf_op jit(solution)/shard_map/land_first/pallas_call | solution.py:691
  62.9 7.4 %collective-permute-done.5.rest_0_ = f32[1536,128]{1,0:T(8,128)S(1)} collective-permute-done((f32[1536,128]{1,0:T(8,128)S(1)}, f32[1536,128]{1,0:T(8,128)S(1)}, u32[]{:S(2)}, u32[]{:S(2)}) %collective-permute-start.5) | collective-permute-done | bytes 786464 | tf_op jit(solution)/shard_map/ppermute | solution.py:44
  70.3 4.5 %finish.1 = (f32[2048,1024]{1,0:T(8,128)}, f32[16392,128]{1,0:T(8,128)S(1)}) custom-call(s32[1024]{0:T(1024)S(1)} %bitcast.34, f32[1536,128]{1,0:T(8,128)S(1)} %collective-permute-done.5.rest_0_, f32[16392,128]{1,0:T(8,128)S(1)} %land_first.1.rest_1_), custom_call_target="tpu_custom_call", output_to_operand_aliasing={{1}: (2, {})} | custom-call | flops 2097152 | bytes 8388608 | tf_op jit(solution)/shard_map/finish/pallas_call | solution.py:702
  (25 shorter events, 0.1 us)
Async XLA Ops:
  0.0 7.5 %copy-start = (s32[4,1024]{1,0:T(4,128)S(1)}, s32[4,1024]{1,0:T(4,128)}, u32[]{:S(2)}) copy-start(s32[4,1024]{1,0:T(4,128)} %node_out.3) | copy-start | bytes 49156
  0.0 7.5 %copy-start.2 = (s32[4,192]{1,0:T(4,128)S(1)}, s32[4,192]{1,0:T(4,128)}, u32[]{:S(2)}) copy-start(s32[4,192]{1,0:T(4,128)} %send_list.1) | copy-start | bytes 9220
  0.0 7.5 %copy-start.1 = (s32[4,1024]{1,0:T(4,128)S(1)}, s32[4,1024]{1,0:T(4,128)}, u32[]{:S(2)}) copy-start(s32[4,1024]{1,0:T(4,128)} %node_in.1) | copy-start | bytes 49156
  0.0 7.5 %copy-start.3 = (s32[4,192]{1,0:T(4,128)S(1)}, s32[4,192]{1,0:T(4,128)}, u32[]{:S(2)}) copy-start(s32[4,192]{1,0:T(4,128)} %rest_3_.1) | copy-start | bytes 9220
  0.0 10.4 %copy-start.4 = (f32[2048]{0:T(1024)S(1)}, f32[2048]{0:T(1024)}, u32[]{:S(2)}) copy-start(f32[2048]{0:T(1024)} %param.10) | copy-start | bytes 24580
  0.0 10.5 %copy-start.6 = (f32[2048]{0:T(1024)S(1)}, f32[2048]{0:T(1024)}, u32[]{:S(2)}) copy-start(f32[2048]{0:T(1024)} %param.12) | copy-start | bytes 24580
  0.0 10.5 %copy-start.5 = (f32[2048]{0:T(1024)S(1)}, f32[2048]{0:T(1024)}, u32[]{:S(2)}) copy-start(f32[2048]{0:T(1024)} %param.11) | copy-start | bytes 24580
  4.3 5.8 %collective-permute-start.2 = (f32[16,128]{1,0:T(8,128)S(1)}, f32[16,128]{1,0:T(8,128)S(1)}, u32[]{:S(2)}, u32[]{:S(2)}) collective-permute-start(f32[16,128]{1,0:T(8,128)S(1)} %get-tuple-element.41.after_ref), channel_id=1, source_target_pairs={{0,3},{1,2},{2,1},{3,0},{4,7},{5,6},{6,5},{7,4},{8,11},{9,10},{10,... | collective-permute-start | bytes 24584 | tf_op jit(solution)/shard_map/ppermute | solution.py:50
  6.8 3.7 %collective-permute-start.1 = (f32[16,128]{1,0:T(8,128)S(1)}, f32[16,128]{1,0:T(8,128)S(1)}, u32[]{:S(2)}, u32[]{:S(2)}) collective-permute-start(f32[16,128]{1,0:T(8,128)S(1)} %get-tuple-element.41.after_ref), channel_id=1, source_target_pairs={{0,2},{1,3},{2,0},{3,1},{4,6},{5,7},{6,4},{7,5},{8,10},{9,11},{10,... | collective-permute-start | bytes 24584 | tf_op jit(solution)/shard_map/ppermute | solution.py:50
  7.4 3.0 %collective-permute-start = (f32[16,128]{1,0:T(8,128)S(1)}, f32[16,128]{1,0:T(8,128)S(1)}, u32[]{:S(2)}, u32[]{:S(2)}) collective-permute-start(f32[16,128]{1,0:T(8,128)S(1)} %get-tuple-element.41.after_ref), channel_id=1, source_target_pairs={{0,1},{1,0},{2,3},{3,2},{4,5},{5,4},{6,7},{7,6},{8,9},{9,8},{10,11... | collective-permute-start | bytes 24584 | tf_op jit(solution)/shard_map/ppermute | solution.py:50
  10.5 6.4 %collective-permute-start.3 = (f32[16,128]{1,0:T(8,128)S(1)}, f32[16,128]{1,0:T(8,128)S(1)}, u32[]{:S(2)}, u32[]{:S(2)}) collective-permute-start(f32[16,128]{1,0:T(8,128)S(1)} %fusion.1.supply), channel_id=1, source_target_pairs={{0,4},{1,29},{2,10},{3,27},{4,8},{5,1},{6,14},{7,31},{8,12},{9,5},... | collective-permute-start | bytes 24584 | tf_op jit(solution)/shard_map/ppermute | solution.py:28
  14.3 27.2 %collective-permute-start.4 = (f32[1536,128]{1,0:T(8,128)S(1)}, f32[1536,128]{1,0:T(8,128)S(1)}, u32[]{:S(2)}, u32[]{:S(2)}) collective-permute-start(f32[1536,128]{1,0:T(8,128)S(1)} %send_ahead.1.sent_ref), channel_id=1, source_target_pairs={{24,0},{28,4},{0,8},{4,12},{8,16},{12,20},{16,24},{20,28},{25,1},{... | collective-permute-start | bytes 2359304 | tf_op jit(solution)/shard_map/ppermute | solution.py:44
  22.7 36.8 %collective-permute-start.9 = (f32[1536,128]{1,0:T(8,128)S(1)}, f32[1536,128]{1,0:T(8,128)S(1)}, u32[]{:S(2)}, u32[]{:S(2)}) collective-permute-start(f32[1536,128]{1,0:T(8,128)S(1)} %get-tuple-element.63), channel_id=1, source_target_pairs={{4,0},{8,4},{12,8},{16,12},{20,16},{24,20},{28,24},{0,28},{5,1},{9... | collective-permute-start | bytes 2359304 | tf_op jit(solution)/shard_map/ppermute | solution.py:44
  24.9 34.5 %collective-permute-start.8 = (f32[1536,128]{1,0:T(8,128)S(1)}, f32[1536,128]{1,0:T(8,128)S(1)}, u32[]{:S(2)}, u32[]{:S(2)}) collective-permute-start(f32[1536,128]{1,0:T(8,128)S(1)} %get-tuple-element.51.after_ref), channel_id=1, source_target_pairs={{28,0},{0,4},{4,8},{8,12},{12,16},{16,20},{20,24},{24,28},{29,1},{... | collective-permute-start | bytes 2359304 | tf_op jit(solution)/shard_map/ppermute | solution.py:44
  41.5 15.5 %collective-permute-start.7 = (f32[2,128]{1,0:T(2,128)S(1)}, f32[2,128]{1,0:T(2,128)S(1)}, u32[]{:S(2)}, u32[]{:S(2)}) collective-permute-start(f32[2,128]{1,0:T(2,128)S(1)} %get-tuple-element.73), channel_id=1, source_target_pairs={{0,8},{1,25},{2,10},{3,27},{4,12},{5,29},{6,14},{7,31},{8,16},{9,1... | collective-permute-start | bytes 3080 | tf_op jit(solution)/shard_map/ppermute | solution.py:38
  41.6 17.8 %collective-permute-start.6 = (f32[2,128]{1,0:T(2,128)S(1)}, f32[2,128]{1,0:T(2,128)S(1)}, u32[]{:S(2)}, u32[]{:S(2)}) collective-permute-start(f32[2,128]{1,0:T(2,128)S(1)} %get-tuple-element.74), channel_id=1, source_target_pairs={{0,4},{1,29},{2,6},{3,31},{4,8},{5,1},{6,10},{7,3},{8,12},{9,5},{1... | collective-permute-start | bytes 3080 | tf_op jit(solution)/shard_map/ppermute | solution.py:38
  44.8 25.5 %collective-permute-start.5 = (f32[1536,128]{1,0:T(8,128)S(1)}, f32[1536,128]{1,0:T(8,128)S(1)}, u32[]{:S(2)}, u32[]{:S(2)}) collective-permute-start(f32[1536,128]{1,0:T(8,128)S(1)} %send_scaled.1.sent_ref.after_ref), channel_id=1, source_target_pairs={{8,0},{12,4},{16,8},{20,12},{24,16},{28,20},{0,24},{4,28},{9,1},{1... | collective-permute-start | bytes 2359304 | tf_op jit(solution)/shard_map/ppermute | solution.py:44
  59.5 1.2 %collective-permute-start.10 = (f32[4,128]{1,0:T(4,128)S(1)}, f32[4,128]{1,0:T(4,128)S(1)}, u32[]{:S(2)}, u32[]{:S(2)}) collective-permute-start(f32[4,128]{1,0:T(4,128)S(1)} %pad_maximum_fusion.1), channel_id=1, source_target_pairs={{0,1},{1,0},{2,3},{3,2},{4,5},{5,4},{6,7},{7,6},{8,9},{9,8},{10,11... | collective-permute-start | bytes 6152 | tf_op jit(solution)/shard_map/ppermute | solution.py:688

commit v17 on v16

--- a/solution.py
+++ b/solution.py
@@ -9,6 +9,7 @@
 
 SHIFTS = (1, -1, 2, -2)
 AHEAD = 2
+BATCH = 32
 LANES = 128
 MIB = 1 << 20
 F32 = jnp.float32
@@ -250,7 +251,7 @@
 
 def send_ahead_kernel(sizes, fraction, slots, rows, turns, send):
     cells, nodes, branches, cap, sub = sizes
-    batch = 16
+    batch = BATCH
 
     def body(step, carry):
         first = step * batch
@@ -272,25 +273,29 @@
     lax.fori_loop(0, cap // batch, body, 0)
 
 
-def scale_kernel(sizes, fraction, rows, sent_ref, supply_ref, scaled):
+def scale_rows(sizes, fraction, rows, scaled):
     cells, nodes, branches, cap, sub = sizes
 
     def body(step, carry):
-        first = step * 16
+        first = step * BATCH
         values = [
-            row_of(rows, first + i, sub)[...] * fraction[first + i] for i in range(16)
+            row_of(rows, first + i, sub)[...] * fraction[first + i] for i in range(BATCH)
         ]
-        for i in range(16):
+        for i in range(BATCH):
             row_of(scaled, first + i, sub)[...] = values[i]
         return carry
 
-    lax.fori_loop(0, cells // 16, body, 0)
+    lax.fori_loop(0, cells // BATCH, body, 0)
     row_of(scaled, cells, sub)[...] = jnp.zeros((sub, LANES), F32)
 
 
-def send_kernel(sizes, sides, in_cell, send_node, send_outlet, scaled, turns, *sends):
-    cells, nodes, branches, cap, sub = sizes
-    batch = 16
+def scale_send_kernel(
+    sizes, sides, fraction, in_cell, send_node, send_outlet, rows, turns, sent_ref, supply_ref,
+    scaled, *sends,
+):
+    cells, nodes, branches, cap, sub = sizes
+    scale_rows(sizes, fraction, rows, scaled)
+    batch = BATCH
     for side, send in zip(sides, sends):
 
         def body(step, carry, side=side, send=send):
@@ -311,7 +316,7 @@
 
 def scaled_send_kernel(sizes, side, theta, send_node, send_outlet, flow, turns, send):
     cells, nodes, branches, cap, sub = sizes
-    batch = 16
+    batch = BATCH
 
     def body(step, carry):
         first = step * batch
@@ -333,11 +338,11 @@
     cells, nodes, branches, cap, sub = sizes
 
     def gather(step, carry):
-        first = step * 16
+        first = step * BATCH
         values = [
-            gathered_flow(first + i, in_cell, scaled, sizes) for i in range(16)
+            gathered_flow(first + i, in_cell, scaled, sizes) for i in range(BATCH)
         ]
-        for i in range(16):
+        for i in range(BATCH):
             row_of(flow, first + i, sub)[...] = values[i]
         return carry
 
@@ -356,7 +361,7 @@
                 partial[j, pl.ds(pl.multiple_of(first, 8), 8), :] = totals[j]
         return carry
 
-    lax.fori_loop(0, nodes // 16, gather, 0)
+    lax.fori_loop(0, nodes // BATCH, gather, 0)
     lax.fori_loop(0, nodes // 16, measure, 0)
     per_outlet = nodes // LANES
     for j in range(branches):
@@ -421,7 +426,7 @@
 
 def home_kernel(sizes, source, outlet, turns, flow, after_ref, home):
     cells, nodes, branches, cap, sub = sizes
-    batch = 16
+    batch = BATCH
 
     def body(step, carry):
         first = step * batch
@@ -440,7 +445,7 @@
 
 def base_kernel(sizes, keep, home_theta, rows, home, base):
     cells, nodes, branches, cap, sub = sizes
-    batch = 16
+    batch = BATCH
 
     def body(step, carry):
         first = step * batch
@@ -458,7 +463,7 @@
 
 def land_rows(sizes, sides, scale, land, received, base):
     cells, nodes, branches, cap, sub = sizes
-    batch = 16
+    batch = BATCH
     core = lax.axis_index("dest") % 2
     for side, rows in zip(sides, received):
         offset = jnp.where(core == side % 2, 0, 2 * padded(cap)) + side // 2 * padded(cap)
@@ -589,24 +594,15 @@
         cost_estimate=cost(1, 1),
         name="send_ahead",
     )(weights, ahead_list, rows, turns)
-    scaled = pl.pallas_call(
-        functools.partial(scale_kernel, sizes),
-        in_specs=[SMEM_WHOLE, VMEM_WHOLE, ANYWHERE, ANYWHERE],
-        out_specs=VMEM_WHOLE,
-        out_shape=rows_shape,
+    scaled, *near = pl.pallas_call(
+        functools.partial(scale_send_kernel, sizes, (0, 1)),
+        in_specs=[SMEM_WHOLE] * 4 + [VMEM_WHOLE] * 2 + [ANYWHERE] * 2,
+        out_specs=[VMEM_WHOLE] * 3,
+        out_shape=[rows_shape] + [send_shape] * 2,
         compiler_params=params(4),
         cost_estimate=cost(10000000000, 1),
-        name="scale_rows",
-    )(fraction.reshape(-1), rows, ahead, supply_there)
-    near = pl.pallas_call(
-        functools.partial(send_kernel, sizes, (0, 1)),
-        in_specs=[SMEM_WHOLE] * 3 + [VMEM_WHOLE] * 2,
-        out_specs=[VMEM_WHOLE] * 2,
-        out_shape=[send_shape] * 2,
-        compiler_params=params(4),
-        cost_estimate=cost(1, 1),
-        name="send_near",
-    )(in_cell, send_node, send_outlet, scaled, turns)
+        name="scale_send",
+    )(fraction.reshape(-1), in_cell, send_node, send_outlet, rows, turns, ahead, supply_there)
     arrived = [
         shifted(send, "region", SHIFTS[side]) for side, send in enumerate([*near, ahead])
     ]

time: 75 us -> 75 us (level)
  waiting for transfers between devices: 12.1 us -> 13.8 us
  Pallas kernels: 42.3 us -> 40.6 us
    pallas_call x2 -> x1, Pallas kernels: 5.75 us -> 4.75 us  [on_device(): pl.pallas_call(functools.partial(scale_send_kernel, sizes, (0, 1)), in_sp...]
    ppermute x4, waiting for transfers between devices: 7.54 us -> 8.45 us  [shifted(): return lax.ppermute(block, axis, route)]
    ppermute x2, waiting for transfers between devices: 2.31 us -> 3.11 us  [to_two(): return lax.ppermute(block, ('region', 'dest'), route)]
  transfers between devices with their start and end apart: 11 -> 11, of which waited for: 6 -> 6; matrix products, arithmetic and copies ran while one was open for 0% -> 0% of each run, Pallas kernels for 45% -> 42%
where the time goes in v17:
time: 75 us; the launch traced here: 74.9 us
  Pallas kernels  40.6 us (54%)
  starting transfers between devices  14.1 us (19%)
  waiting for transfers between devices  13.8 us (18%)
  blocking collectives  6.09 us (8%)
    pallas_call x1, Pallas kernels, on_device(): pl.pallas_call(functools.partial(node_flow_kernel, sizes), in_specs=[SMEM...  8.77 us
    ppermute x4, waiting for transfers between devices, shifted(): return lax.ppermute(block, axis, route)  8.45 us
    ppermute x4, starting transfers between devices, shifted(): return lax.ppermute(block, axis, route)  6.93 us
    all_gather x1, blocking collectives, on_device(): shared = lax.all_gather(joined, 'dest', axis=0, tiled=True)  6.09 us
    pallas_call x1, Pallas kernels, on_device(): pl.pallas_call(functools.partial(scale_send_kernel, sizes, (0, 1)), in_sp...  4.75 us
    pallas_call x1, Pallas kernels, on_device(): pl.pallas_call(functools.partial(finish_kernel, sizes, (3,), chunk), in_s...  4.57 us
    pallas_call x1, Pallas kernels, on_device(): pl.pallas_call(functools.partial(home_kernel, sizes), in_specs=[SMEM_WHOL...  4.37 us
    pallas_call x1, Pallas kernels, on_device(): pl.pallas_call(functools.partial(cell_sum_kernel, chunk, sub), in_specs=[...  4.31 us
  transfers between devices with their start and end apart: 11, of which 6 were waited for; matrix products, arithmetic and copies ran while one was open for 0% of the time, Pallas kernels for 42%

profile of v17, /device:TPU:0, one launch (start us, length us, event | category | flops | bytes accessed | tf_op | source)
XLA Modules:
  0.0 74.9 jit_solution(9944566198143998799)
XLA Ops:
  0.0 4.3 %cell_sum.1 = (f32[16,128]{1,0:T(8,128)S(1)}, f32[16392,128]{1,0:T(8,128)S(1)}) custom-call(f32[2048,1024]{1,0:T(8,128)} %x_hbm.2), custom_call_target="tpu_custom_call" | custom-call | flops 2097152 | bytes 8388608 | tf_op jit(solution)/shard_map/cell_sum/pallas_call | solution.py:535
  4.3 2.4 %collective-permute-start.2 = (f32[16,128]{1,0:T(8,128)S(1)}, f32[16,128]{1,0:T(8,128)S(1)}, u32[]{:S(2)}, u32[]{:S(2)}) collective-permute-start(f32[16,128]{1,0:T(8,128)S(1)} %get-tuple-element.42.after_ref), channel_id=1, source_target_pairs={{0,3},{1,2},{2,1},{3,0},{4,7},{5,6},{6,5},{7,4},{8,11},{9,10},{10,... | collective-permute-start | bytes 24584 | tf_op jit(solution)/shard_map/ppermute | solution.py:51
  6.8 0.6 collective-permute-start.1
  7.4 0.0 collective-permute-start
  7.5 2.6 %turn_rows.1 = (s32[8192,128]{1,0:T(8,128)S(1)}, s32[32,128]{1,0:T(8,128)S(1)}, s32[8,128]{1,0:T(8,128)S(1)}, s32[8,128]{1,0:T(8,128)S(1)}, s32[8,128]{1,0:T(8,1...) custom-call(s32[1024,1024]{1,0:T(8,128)} %x_hbm.3, ...), custom_call_target="tpu_custom_call" | custom-call | bytes 4194304 | tf_op jit(solution)/shard_map/turn_rows/pallas_call | solution.py:555
  10.1 0.0 collective-permute-done.2
  10.1 0.3 collective-permute-done.1
  10.5 1.6 %collective-permute-start.3 = (f32[16,128]{1,0:T(8,128)S(1)}, f32[16,128]{1,0:T(8,128)S(1)}, u32[]{:S(2)}, u32[]{:S(2)}) collective-permute-start(f32[16,128]{1,0:T(8,128)S(1)} %fusion.1.supply), channel_id=1, source_target_pairs={{0,4},{1,29},{2,10},{3,27},{4,8},{5,1},{6,14},{7,31},{8,12},{9,5},... | collective-permute-start | bytes 24584 | tf_op jit(solution)/shard_map/ppermute | solution.py:29
  12.1 2.2 %send_ahead.1.sent_ref = f32[1536,128]{1,0:T(8,128)S(1)} custom-call(f32[2176]{0:T(1024)S(1)} %concatenate.13.fraction, s32[2048]{0:T(1024)S(1)} %bitcast.35, f32[16392,128]{1,0:T(8,128)S(1)} %get-tuple-element.49.rows, s32[8192,128]{1,0:T(8,128)S(1)} %get-tuple-element.50.turns), custom_call_target="tpu_custom_call" | custom-call | flops 1 | bytes 1 | tf_op jit(solution)/shard_map/send_ahead/pallas_call | solution.py:588
  14.2 1.6 %collective-permute-start.4 = (f32[1536,128]{1,0:T(8,128)S(1)}, f32[1536,128]{1,0:T(8,128)S(1)}, u32[]{:S(2)}, u32[]{:S(2)}) collective-permute-start(f32[1536,128]{1,0:T(8,128)S(1)} %send_ahead.1.sent_ref), channel_id=1, source_target_pairs={{24,0},{28,4},{0,8},{4,12},{8,16},{12,20},{16,24},{20,28},{25,1},{... | collective-permute-start | bytes 2359304 | tf_op jit(solution)/shard_map/ppermute | solution.py:45
  15.9 1.0 %collective-permute-done.3.supply_ref = f32[16,128]{1,0:T(8,128)S(1)} collective-permute-done((f32[16,128]{1,0:T(8,128)S(1)}, f32[16,128]{1,0:T(8,128)S(1)}, u32[]{:S(2)}, u32[]{:S(2)}) %collective-permute-start.3) | collective-permute-done | bytes 8224 | tf_op jit(solution)/shard_map/ppermute | solution.py:29
  16.9 4.7 %scale_send.1 = (f32[16392,128]{1,0:T(8,128)S(1)}, f32[1536,128]{1,0:T(8,128)S(1)}, f32[1536,128]{1,0:T(8,128)S(1)}) custom-call(f32[2048]{0:T(1024)S(1)} %bitcast.25, s32[4096]{0:T(1024)S(1)} %bitcast.27, s32[1024]{0:T(1024)S(1)} %bitcast.36, s32[1024]{0:T(1024)S(1)} %bitcast.38, f32[16392,128]{1,0:T(8,128)S(1)} %get-tuple-element.49.rows, ...), custom_call_target="tpu_custom_call" | custom-call | flops 10000000000 | bytes 1 | tf_op jit(solution)/shard_map/scale_send/pallas_call | solution.py:597
  21.7 2.2 %collective-permute-start.9 = (f32[1536,128]{1,0:T(8,128)S(1)}, f32[1536,128]{1,0:T(8,128)S(1)}, u32[]{:S(2)}, u32[]{:S(2)}) collective-permute-start(f32[1536,128]{1,0:T(8,128)S(1)} %get-tuple-element.65), channel_id=1, source_target_pairs={{4,0},{8,4},{12,8},{16,12},{20,16},{24,20},{28,24},{0,28},{5,1},{9... | collective-permute-start | bytes 2359304 | tf_op jit(solution)/shard_map/ppermute | solution.py:45
  23.9 0.0 collective-permute-start.8
  23.9 8.8 %node_flow.1 = (f32[8192,128]{1,0:T(8,128)S(1)}, f32[32,128]{1,0:T(8,128)S(1)}) custom-call(s32[4096]{0:T(1024)S(1)} %bitcast.28, f32[16392,128]{1,0:T(8,128)S(1)} %get-tuple-element.52.scaled, s32[8192,128]{1,0:T(8,128)S(1)} %get-tuple-element.50.turns, f32[1536,128]{1,0:T(8,128)S(1)} %get-tuple-element.53.after_ref), custom_call_target="tpu_custom_call" | custom-call | flops 1 | bytes 1 | tf_op jit(solution)/shard_map/node_flow/pallas_call | solution.py:610
  32.7 6.1 %all_gather.3.shared = f32[192,128]{1,0:T(8,128)S(1)} all-gather(f32[48,128]{1,0:T(8,128)S(1)} %pad_maximum_fusion), channel_id=1, replica_groups=mesh['region'=8,'dest'=4] {'dest'}, dimensions={0}, use_global_device_ids=true | all-gather | bytes 122880 | tf_op jit(solution)/shard_map/all_gather | solution.py:625
  38.8 1.4 %theta.1 = (f32[8,128]{1,0:T(8,128)S(1)}, f32[4,128]{1,0:T(4,128)S(1)}) custom-call(f32[16,128]{1,0:T(8,128)S(1)} %fusion.1.supply, f32[192,128]{1,0:T(8,128)S(1)} %all_gather.3.shared, s32[4,1024]{1,0:T(4,128)S(1)} %copy-done, s32[4,192]{1,0:T(4,128)S(1)} %copy-done.2), custom_call_target="tpu_custom_call" | custom-call | flops 1 | bytes 1 | tf_op jit(solution)/shard_map/theta/pallas_call | solution.py:626
  40.2 0.0 collective-permute-done.4.arrived_ref.rest_2_
  40.2 0.1 collective-permute-start.7
  40.3 2.1 %collective-permute-start.6 = (f32[2,128]{1,0:T(2,128)S(1)}, f32[2,128]{1,0:T(2,128)S(1)}, u32[]{:S(2)}, u32[]{:S(2)}) collective-permute-start(f32[2,128]{1,0:T(2,128)S(1)} %get-tuple-element.76), channel_id=1, source_target_pairs={{0,4},{1,29},{2,6},{3,31},{4,8},{5,1},{6,10},{7,3},{8,12},{9,5},{1... | collective-permute-start | bytes 3080 | tf_op jit(solution)/shard_map/ppermute | solution.py:39
  42.4 1.1 %send_scaled.1.sent_ref.after_ref = f32[1536,128]{1,0:T(8,128)S(1)} custom-call(f32[1024]{0:T(1024)S(1)} %bitcast.26, s32[1024]{0:T(1024)S(1)} %bitcast.37, s32[1024]{0:T(1024)S(1)} %bitcast.39, f32[8192,128]{1,0:T(8,128)S(1)} %get-tuple-element.58.flow, s32[8192,128]{1,0:T(8,128)S(1)} %get-tuple-element.50.turns), custom_call_target="tpu_custom_call" | custom-call | flops 1 | bytes 1 | tf_op jit(solution)/shard_map/send_scaled/pallas_call | solution.py:642
  43.5 3.1 %collective-permute-start.5 = (f32[1536,128]{1,0:T(8,128)S(1)}, f32[1536,128]{1,0:T(8,128)S(1)}, u32[]{:S(2)}, u32[]{:S(2)}) collective-permute-start(f32[1536,128]{1,0:T(8,128)S(1)} %send_scaled.1.sent_ref.after_ref), channel_id=1, source_target_pairs={{8,0},{12,4},{16,8},{20,12},{24,16},{28,20},{0,24},{4,28},{9,1},{1... | collective-permute-start | bytes 2359304 | tf_op jit(solution)/shard_map/ppermute | solution.py:45
  46.6 4.4 %home_rows.1.home = f32[16392,128]{1,0:T(8,128)S(1)} custom-call(s32[2048]{0:T(1024)S(1)} %bitcast.31, s32[2048]{0:T(1024)S(1)} %bitcast.32, s32[8192,128]{1,0:T(8,128)S(1)} %get-tuple-element.50.turns, f32[8192,128]{1,0:T(8,128)S(1)} %get-tuple-element.58.flow, f32[1536,128]{1,0:T(8,128)S(1)} %send_scaled.1.sent_ref.after_ref), custom_call_target="tpu_custom_call" | custom-call | flops 4000000000 | bytes 1 | tf_op jit(solution)/shard_map/home_rows/pallas_call | solution.py:651
  51.0 0.7 keep.1
  51.6 3.5 %base_rows.1.rest_3_ = f32[16392,128]{1,0:T(8,128)S(1)} custom-call(f32[2048]{0:T(1024)S(1)} %bitcast.33, f32[2048]{0:T(1024)S(1)} %bitcast.34, f32[16392,128]{1,0:T(8,128)S(1)} %get-tuple-element.49.rows, f32[16392,128]{1,0:T(8,128)S(1)} %home_rows.1.home), custom_call_target="tpu_custom_call" | custom-call | flops 10000000 | bytes 1 | tf_op jit(solution)/shard_map/base_rows/pallas_call | solution.py:669
  55.2 3.1 %collective-permute-done.6 = f32[2,128]{1,0:T(2,128)S(1)} collective-permute-done((f32[2,128]{1,0:T(2,128)S(1)}, f32[2,128]{1,0:T(2,128)S(1)}, u32[]{:S(2)}, u32[]{:S(2)}) %collective-permute-start.6) | collective-permute-done | bytes 1056 | tf_op jit(solution)/shard_map/ppermute | solution.py:39
  58.3 0.1 collective-permute-done.9.rest_1_
  58.4 0.3 collective-permute-start.10
  58.7 0.9 %collective-permute-done.10 = f32[4,128]{1,0:T(4,128)S(1)} collective-permute-done((f32[4,128]{1,0:T(4,128)S(1)}, f32[4,128]{1,0:T(4,128)S(1)}, u32[]{:S(2)}, u32[]{:S(2)}) %collective-permute-start.10) | collective-permute-done | bytes 2080 | tf_op jit(solution)/shard_map/ppermute | solution.py:684
  59.6 2.3 %land_first.1.rest_1_ = f32[16392,128]{1,0:T(8,128)S(1)} custom-call(f32[1024]{0:T(1024)S(1)} %maximum_bitcast_fusion.scale, s32[1024]{0:T(1024)S(1)} %bitcast.29, f32[1536,128]{1,0:T(8,128)S(1)} %collective-permute-done.8.rest_0_, f32[1536,128]{1,0:T(8,128)S(1)} %collective-permute-done.9.rest_1_, ...), custom_call_target="tpu_custom_call", output_to_operand_aliasing={{}: (5, {})} | custom-call | flops 4000000000 | bytes 1 | tf_op jit(solution)/shard_map/land_first/pallas_call | solution.py:687
  62.0 8.3 %collective-permute-done.5.rest_0_ = f32[1536,128]{1,0:T(8,128)S(1)} collective-permute-done((f32[1536,128]{1,0:T(8,128)S(1)}, f32[1536,128]{1,0:T(8,128)S(1)}, u32[]{:S(2)}, u32[]{:S(2)}) %collective-permute-start.5) | collective-permute-done | bytes 786464 | tf_op jit(solution)/shard_map/ppermute | solution.py:45
  70.3 4.6 %finish.1 = (f32[2048,1024]{1,0:T(8,128)}, f32[16392,128]{1,0:T(8,128)S(1)}) custom-call(s32[1024]{0:T(1024)S(1)} %bitcast.30, f32[1536,128]{1,0:T(8,128)S(1)} %collective-permute-done.5.rest_0_, f32[16392,128]{1,0:T(8,128)S(1)} %land_first.1.rest_1_), custom_call_target="tpu_custom_call", output_to_operand_aliasing={{1}: (2, {})} | custom-call | flops 2097152 | bytes 8388608 | tf_op jit(solution)/shard_map/finish/pallas_call | solution.py:698
  (24 shorter events, 0.1 us)
Async XLA Ops:
  0.0 7.5 %copy-start = (s32[4,1024]{1,0:T(4,128)S(1)}, s32[4,1024]{1,0:T(4,128)}, u32[]{:S(2)}) copy-start(s32[4,1024]{1,0:T(4,128)} %node_out.3) | copy-start | bytes 49156
  0.0 7.5 %copy-start.2 = (s32[4,192]{1,0:T(4,128)S(1)}, s32[4,192]{1,0:T(4,128)}, u32[]{:S(2)}) copy-start(s32[4,192]{1,0:T(4,128)} %send_list.1) | copy-start | bytes 9220
  0.0 7.5 %copy-start.1 = (s32[4,1024]{1,0:T(4,128)S(1)}, s32[4,1024]{1,0:T(4,128)}, u32[]{:S(2)}) copy-start(s32[4,1024]{1,0:T(4,128)} %node_in.1) | copy-start | bytes 49156
  0.0 7.5 %copy-start.3 = (s32[4,192]{1,0:T(4,128)S(1)}, s32[4,192]{1,0:T(4,128)}, u32[]{:S(2)}) copy-start(s32[4,192]{1,0:T(4,128)} %rest_3_.1) | copy-start | bytes 9220
  0.0 10.4 %copy-start.4 = (f32[2048]{0:T(1024)S(1)}, f32[2048]{0:T(1024)}, u32[]{:S(2)}) copy-start(f32[2048]{0:T(1024)} %param.10) | copy-start | bytes 24580
  0.0 10.5 %copy-start.6 = (f32[2048]{0:T(1024)S(1)}, f32[2048]{0:T(1024)}, u32[]{:S(2)}) copy-start(f32[2048]{0:T(1024)} %param.12) | copy-start | bytes 24580
  0.0 10.5 %copy-start.5 = (f32[2048]{0:T(1024)S(1)}, f32[2048]{0:T(1024)}, u32[]{:S(2)}) copy-start(f32[2048]{0:T(1024)} %param.11) | copy-start | bytes 24580
  4.3 5.8 %collective-permute-start.2 = (f32[16,128]{1,0:T(8,128)S(1)}, f32[16,128]{1,0:T(8,128)S(1)}, u32[]{:S(2)}, u32[]{:S(2)}) collective-permute-start(f32[16,128]{1,0:T(8,128)S(1)} %get-tuple-element.42.after_ref), channel_id=1, source_target_pairs={{0,3},{1,2},{2,1},{3,0},{4,7},{5,6},{6,5},{7,4},{8,11},{9,10},{10,... | collective-permute-start | bytes 24584 | tf_op jit(solution)/shard_map/ppermute | solution.py:51
  6.8 3.7 %collective-permute-start.1 = (f32[16,128]{1,0:T(8,128)S(1)}, f32[16,128]{1,0:T(8,128)S(1)}, u32[]{:S(2)}, u32[]{:S(2)}) collective-permute-start(f32[16,128]{1,0:T(8,128)S(1)} %get-tuple-element.42.after_ref), channel_id=1, source_target_pairs={{0,2},{1,3},{2,0},{3,1},{4,6},{5,7},{6,4},{7,5},{8,10},{9,11},{10,... | collective-permute-start | bytes 24584 | tf_op jit(solution)/shard_map/ppermute | solution.py:51
  7.4 3.0 %collective-permute-start = (f32[16,128]{1,0:T(8,128)S(1)}, f32[16,128]{1,0:T(8,128)S(1)}, u32[]{:S(2)}, u32[]{:S(2)}) collective-permute-start(f32[16,128]{1,0:T(8,128)S(1)} %get-tuple-element.42.after_ref), channel_id=1, source_target_pairs={{0,1},{1,0},{2,3},{3,2},{4,5},{5,4},{6,7},{7,6},{8,9},{9,8},{10,11... | collective-permute-start | bytes 24584 | tf_op jit(solution)/shard_map/ppermute | solution.py:51
  10.5 6.4 %collective-permute-start.3 = (f32[16,128]{1,0:T(8,128)S(1)}, f32[16,128]{1,0:T(8,128)S(1)}, u32[]{:S(2)}, u32[]{:S(2)}) collective-permute-start(f32[16,128]{1,0:T(8,128)S(1)} %fusion.1.supply), channel_id=1, source_target_pairs={{0,4},{1,29},{2,10},{3,27},{4,8},{5,1},{6,14},{7,31},{8,12},{9,5},... | collective-permute-start | bytes 24584 | tf_op jit(solution)/shard_map/ppermute | solution.py:29
  14.2 26.0 %collective-permute-start.4 = (f32[1536,128]{1,0:T(8,128)S(1)}, f32[1536,128]{1,0:T(8,128)S(1)}, u32[]{:S(2)}, u32[]{:S(2)}) collective-permute-start(f32[1536,128]{1,0:T(8,128)S(1)} %send_ahead.1.sent_ref), channel_id=1, source_target_pairs={{24,0},{28,4},{0,8},{4,12},{8,16},{12,20},{16,24},{20,28},{25,1},{... | collective-permute-start | bytes 2359304 | tf_op jit(solution)/shard_map/ppermute | solution.py:45
  21.7 36.7 %collective-permute-start.9 = (f32[1536,128]{1,0:T(8,128)S(1)}, f32[1536,128]{1,0:T(8,128)S(1)}, u32[]{:S(2)}, u32[]{:S(2)}) collective-permute-start(f32[1536,128]{1,0:T(8,128)S(1)} %get-tuple-element.65), channel_id=1, source_target_pairs={{4,0},{8,4},{12,8},{16,12},{20,16},{24,20},{28,24},{0,28},{5,1},{9... | collective-permute-start | bytes 2359304 | tf_op jit(solution)/shard_map/ppermute | solution.py:45
  23.9 34.5 %collective-permute-start.8 = (f32[1536,128]{1,0:T(8,128)S(1)}, f32[1536,128]{1,0:T(8,128)S(1)}, u32[]{:S(2)}, u32[]{:S(2)}) collective-permute-start(f32[1536,128]{1,0:T(8,128)S(1)} %get-tuple-element.53.after_ref), channel_id=1, source_target_pairs={{28,0},{0,4},{4,8},{8,12},{12,16},{16,20},{20,24},{24,28},{29,1},{... | collective-permute-start | bytes 2359304 | tf_op jit(solution)/shard_map/ppermute | solution.py:45
  40.2 14.9 %collective-permute-start.7 = (f32[2,128]{1,0:T(2,128)S(1)}, f32[2,128]{1,0:T(2,128)S(1)}, u32[]{:S(2)}, u32[]{:S(2)}) collective-permute-start(f32[2,128]{1,0:T(2,128)S(1)} %get-tuple-element.75), channel_id=1, source_target_pairs={{0,8},{1,25},{2,10},{3,27},{4,12},{5,29},{6,14},{7,31},{8,16},{9,1... | collective-permute-start | bytes 3080 | tf_op jit(solution)/shard_map/ppermute | solution.py:39
  40.3 17.9 %collective-permute-start.6 = (f32[2,128]{1,0:T(2,128)S(1)}, f32[2,128]{1,0:T(2,128)S(1)}, u32[]{:S(2)}, u32[]{:S(2)}) collective-permute-start(f32[2,128]{1,0:T(2,128)S(1)} %get-tuple-element.76), channel_id=1, source_target_pairs={{0,4},{1,29},{2,6},{3,31},{4,8},{5,1},{6,10},{7,3},{8,12},{9,5},{1... | collective-permute-start | bytes 3080 | tf_op jit(solution)/shard_map/ppermute | solution.py:39
  43.5 26.8 %collective-permute-start.5 = (f32[1536,128]{1,0:T(8,128)S(1)}, f32[1536,128]{1,0:T(8,128)S(1)}, u32[]{:S(2)}, u32[]{:S(2)}) collective-permute-start(f32[1536,128]{1,0:T(8,128)S(1)} %send_scaled.1.sent_ref.after_ref), channel_id=1, source_target_pairs={{8,0},{12,4},{16,8},{20,12},{24,16},{28,20},{0,24},{4,28},{9,1},{1... | collective-permute-start | bytes 2359304 | tf_op jit(solution)/shard_map/ppermute | solution.py:45
  58.4 1.2 %collective-permute-start.10 = (f32[4,128]{1,0:T(4,128)S(1)}, f32[4,128]{1,0:T(4,128)S(1)}, u32[]{:S(2)}, u32[]{:S(2)}) collective-permute-start(f32[4,128]{1,0:T(4,128)S(1)} %pad_maximum_fusion.1), channel_id=1, source_target_pairs={{0,1},{1,0},{2,3},{3,2},{4,5},{5,4},{6,7},{7,6},{8,9},{9,8},{10,11... | collective-permute-start | bytes 6152 | tf_op jit(solution)/shard_map/ppermute | solution.py:684

commit v18 on v16

--- a/solution.py
+++ b/solution.py
@@ -215,13 +215,13 @@
         copy.wait()
 
         def body(step, carry, number=number):
-            for half in range(2):
-                first = number * chunk + step * 16 + half * 8
+            for part in range(4):
+                first = number * chunk + step * 32 + part * 8
                 total = rows_of_group(x, rows_ref, first, sub)
                 partial[pl.ds(pl.multiple_of(first, 8), 8), :] = total
             return carry
 
-        lax.fori_loop(0, chunk // 16, body, 0)
+        lax.fori_loop(0, chunk // 32, body, 0)
     sum_ref[...] = lane_sums(partial[...])
 
 
@@ -234,11 +234,11 @@
         copy.wait()
 
         def body(step, carry, number=number):
-            for half in range(2):
-                rows_of_group(x, rows_ref, number * chunk + step * 16 + half * 8, sub)
+            for part in range(4):
+                rows_of_group(x, rows_ref, number * chunk + step * 32 + part * 8, sub)
             return carry
 
-        lax.fori_loop(0, chunk // 16, body, 0)
+        lax.fori_loop(0, chunk // 32, body, 0)
 
 
 def gathered_flow(node, in_cell, scaled, sizes):
@@ -342,8 +342,8 @@
         return carry
 
     def measure(step, carry):
-        for half in range(2):
-            first = step * 16 + half * 8
+        for part in range(4):
+            first = step * 32 + part * 8
             totals = [jnp.zeros((8, LANES), F32)] * branches
             for q in range(sub):
                 at = pl.ds(first * sub + q, 8, stride=sub)
@@ -357,7 +357,7 @@
         return carry
 
     lax.fori_loop(0, nodes // 16, gather, 0)
-    lax.fori_loop(0, nodes // 16, measure, 0)
+    lax.fori_loop(0, nodes // 32, measure, 0)
     per_outlet = nodes // LANES
     for j in range(branches):
         demand[j * per_outlet : (j + 1) * per_outlet, :] = lane_sums(partial[j])
@@ -492,15 +492,15 @@
     for number in range(cells // chunk):
 
         def body(step, carry, number=number):
-            for half in range(2):
-                first = number * chunk + step * 16 + half * 8
+            for part in range(4):
+                first = number * chunk + step * 32 + part * 8
                 for q in range(sub):
                     staged[
                         pl.ds(pl.multiple_of(first, 8), 8), q * LANES : (q + 1) * LANES
                     ] = base[pl.ds(first * sub + q, 8, stride=sub), :]
             return carry
 
-        lax.fori_loop(0, chunk // 16, body, 0)
+        lax.fori_loop(0, chunk // 32, body, 0)
         at = pl.ds(number * chunk, chunk)
         copies.append(
             pltpu.make_async_copy(staged.at[at, :], out.at[at, :], sems.at[number])

time: 75 us -> 74.9 us (level)
  transfers between devices with their start and end apart: 11 -> 11, of which waited for: 6 -> 5; matrix products, arithmetic and copies ran while one was open for 0% -> 0% of each run, Pallas kernels for 45% -> 44%
where the time goes in v18:
time: 74.9 us; the launch traced here: 74.8 us
  Pallas kernels  42 us (56%)
  starting transfers between devices  14.1 us (19%)
  waiting for transfers between devices  12.3 us (16%)
  blocking collectives  6.08 us (8%)
    pallas_call x1, Pallas kernels, on_device(): pl.pallas_call(functools.partial(node_flow_kernel, sizes), in_specs=[SMEM...  8.75 us
    ppermute x4, waiting for transfers between devices, shifted(): return lax.ppermute(block, axis, route)  7.52 us
    ppermute x4, starting transfers between devices, shifted(): return lax.ppermute(block, axis, route)  6.94 us
    all_gather x1, blocking collectives, on_device(): shared = lax.all_gather(joined, 'dest', axis=0, tiled=True)  6.08 us
    pallas_call x1, Pallas kernels, on_device(): pl.pallas_call(functools.partial(home_kernel, sizes), in_specs=[SMEM_WHOL...  4.63 us
    pallas_call x1, Pallas kernels, on_device(): pl.pallas_call(functools.partial(finish_kernel, sizes, (3,), chunk), in_s...  4.46 us
    pallas_call x1, Pallas kernels, on_device(): pl.pallas_call(functools.partial(cell_sum_kernel, chunk, sub), in_specs=[...  4.28 us
    pallas_call x1, Pallas kernels, on_device(): pl.pallas_call(functools.partial(base_kernel, sizes), in_specs=[SMEM_WHOL...  3.85 us
  transfers between devices with their start and end apart: 11, of which 5 were waited for; matrix products, arithmetic and copies ran while one was open for 0% of the time, Pallas kernels for 44%

profile of v18, /device:TPU:0, one launch (start us, length us, event | category | flops | bytes accessed | tf_op | source)
XLA Modules:
  0.0 74.8 jit_solution(13366891226929176005)
XLA Ops:
  0.0 4.3 %cell_sum.1 = (f32[16,128]{1,0:T(8,128)S(1)}, f32[16392,128]{1,0:T(8,128)S(1)}) custom-call(f32[2048,1024]{1,0:T(8,128)} %x_hbm.2), custom_call_target="tpu_custom_call" | custom-call | flops 2097152 | bytes 8388608 | tf_op jit(solution)/shard_map/cell_sum/pallas_call | solution.py:530
  4.3 2.4 %collective-permute-start.2 = (f32[16,128]{1,0:T(8,128)S(1)}, f32[16,128]{1,0:T(8,128)S(1)}, u32[]{:S(2)}, u32[]{:S(2)}) collective-permute-start(f32[16,128]{1,0:T(8,128)S(1)} %get-tuple-element.41.after_ref), channel_id=1, source_target_pairs={{0,3},{1,2},{2,1},{3,0},{4,7},{5,6},{6,5},{7,4},{8,11},{9,10},{10,... | collective-permute-start | bytes 24584 | tf_op jit(solution)/shard_map/ppermute | solution.py:50
  6.8 0.6 collective-permute-start.1
  7.4 0.0 collective-permute-start
  7.5 2.6 %turn_rows.1 = (s32[8192,128]{1,0:T(8,128)S(1)}, s32[32,128]{1,0:T(8,128)S(1)}, s32[8,128]{1,0:T(8,128)S(1)}, s32[8,128]{1,0:T(8,128)S(1)}, s32[8,128]{1,0:T(8,1...) custom-call(s32[1024,1024]{1,0:T(8,128)} %x_hbm.3, ...), custom_call_target="tpu_custom_call" | custom-call | bytes 4194304 | tf_op jit(solution)/shard_map/turn_rows/pallas_call | solution.py:550
  10.1 0.3 collective-permute-done.1
  10.5 1.6 %collective-permute-start.3 = (f32[16,128]{1,0:T(8,128)S(1)}, f32[16,128]{1,0:T(8,128)S(1)}, u32[]{:S(2)}, u32[]{:S(2)}) collective-permute-start(f32[16,128]{1,0:T(8,128)S(1)} %fusion.1.supply), channel_id=1, source_target_pairs={{0,4},{1,29},{2,10},{3,27},{4,8},{5,1},{6,14},{7,31},{8,12},{9,5},... | collective-permute-start | bytes 24584 | tf_op jit(solution)/shard_map/ppermute | solution.py:28
  12.0 2.2 %send_ahead.1.sent_ref = f32[1536,128]{1,0:T(8,128)S(1)} custom-call(f32[2176]{0:T(1024)S(1)} %concatenate.13.fraction, s32[2048]{0:T(1024)S(1)} %bitcast.39, f32[16392,128]{1,0:T(8,128)S(1)} %get-tuple-element.46.rows, s32[8192,128]{1,0:T(8,128)S(1)} %get-tuple-element.48.turns), custom_call_target="tpu_custom_call" | custom-call | flops 1 | bytes 1 | tf_op jit(solution)/shard_map/send_ahead/pallas_call | solution.py:583
  14.3 1.6 %collective-permute-start.4 = (f32[1536,128]{1,0:T(8,128)S(1)}, f32[1536,128]{1,0:T(8,128)S(1)}, u32[]{:S(2)}, u32[]{:S(2)}) collective-permute-start(f32[1536,128]{1,0:T(8,128)S(1)} %send_ahead.1.sent_ref), channel_id=1, source_target_pairs={{24,0},{28,4},{0,8},{4,12},{8,16},{12,20},{16,24},{20,28},{25,1},{... | collective-permute-start | bytes 2359304 | tf_op jit(solution)/shard_map/ppermute | solution.py:44
  15.9 1.0 %collective-permute-done.3.supply_ref = f32[16,128]{1,0:T(8,128)S(1)} collective-permute-done((f32[16,128]{1,0:T(8,128)S(1)}, f32[16,128]{1,0:T(8,128)S(1)}, u32[]{:S(2)}, u32[]{:S(2)}) %collective-permute-start.3) | collective-permute-done | bytes 8224 | tf_op jit(solution)/shard_map/ppermute | solution.py:28
  16.9 2.5 %scale_rows.1.scaled = f32[16392,128]{1,0:T(8,128)S(1)} custom-call(f32[2048]{0:T(1024)S(1)} %bitcast.25, f32[16392,128]{1,0:T(8,128)S(1)} %get-tuple-element.46.rows, f32[1536,128]{1,0:T(8,128)S(1)} %send_ahead.1.sent_ref, f32[16,128]{1,0:T(8,128)S(1)} %collective-permute-done.3.supply_ref), custom_call_target="tpu_custom_call" | custom-call | flops 10000000000 | bytes 1 | tf_op jit(solution)/shard_map/scale_rows/pallas_call | solution.py:592
  19.4 3.3 %send_near.1 = (f32[1536,128]{1,0:T(8,128)S(1)}, f32[1536,128]{1,0:T(8,128)S(1)}) custom-call(s32[4096]{0:T(1024)S(1)} %bitcast.26, s32[1024]{0:T(1024)S(1)} %bitcast.28, s32[1024]{0:T(1024)S(1)} %bitcast.30, f32[16392,128]{1,0:T(8,128)S(1)} %scale_rows.1.scaled, s32[8192,128]{1,0:T(8,128)S(1)} %get-tuple-element.48.turns), custom_call_target="tpu_custom_call" | custom-call | flops 1 | bytes 1 | tf_op jit(solution)/shard_map/send_near/pallas_call | solution.py:601
  22.6 2.3 %collective-permute-start.9 = (f32[1536,128]{1,0:T(8,128)S(1)}, f32[1536,128]{1,0:T(8,128)S(1)}, u32[]{:S(2)}, u32[]{:S(2)}) collective-permute-start(f32[1536,128]{1,0:T(8,128)S(1)} %get-tuple-element.63), channel_id=1, source_target_pairs={{4,0},{8,4},{12,8},{16,12},{20,16},{24,20},{28,24},{0,28},{5,1},{9... | collective-permute-start | bytes 2359304 | tf_op jit(solution)/shard_map/ppermute | solution.py:44
  24.9 0.0 collective-permute-start.8
  24.9 8.8 %node_flow.1 = (f32[8192,128]{1,0:T(8,128)S(1)}, f32[32,128]{1,0:T(8,128)S(1)}) custom-call(s32[4096]{0:T(1024)S(1)} %bitcast.27, f32[16392,128]{1,0:T(8,128)S(1)} %scale_rows.1.scaled, s32[8192,128]{1,0:T(8,128)S(1)} %get-tuple-element.48.turns, f32[1536,128]{1,0:T(8,128)S(1)} %get-tuple-element.51.after_ref), custom_call_target="tpu_custom_call" | custom-call | flops 1 | bytes 1 | tf_op jit(solution)/shard_map/node_flow/pallas_call | solution.py:614
  33.7 6.1 %all_gather.3.shared = f32[192,128]{1,0:T(8,128)S(1)} all-gather(f32[48,128]{1,0:T(8,128)S(1)} %pad_maximum_fusion), channel_id=1, replica_groups=mesh['region'=8,'dest'=4] {'dest'}, dimensions={0}, use_global_device_ids=true | all-gather | bytes 122880 | tf_op jit(solution)/shard_map/all_gather | solution.py:629
  39.8 1.5 %theta.1 = (f32[8,128]{1,0:T(8,128)S(1)}, f32[4,128]{1,0:T(4,128)S(1)}) custom-call(f32[16,128]{1,0:T(8,128)S(1)} %fusion.1.supply, f32[192,128]{1,0:T(8,128)S(1)} %all_gather.3.shared, s32[4,1024]{1,0:T(4,128)S(1)} %copy-done, s32[4,192]{1,0:T(4,128)S(1)} %copy-done.2), custom_call_target="tpu_custom_call" | custom-call | flops 1 | bytes 1 | tf_op jit(solution)/shard_map/theta/pallas_call | solution.py:630
  41.2 0.0 collective-permute-done.4.arrived_ref.rest_2_
  41.3 0.1 collective-permute-start.7
  41.3 2.1 %collective-permute-start.6 = (f32[2,128]{1,0:T(2,128)S(1)}, f32[2,128]{1,0:T(2,128)S(1)}, u32[]{:S(2)}, u32[]{:S(2)}) collective-permute-start(f32[2,128]{1,0:T(2,128)S(1)} %get-tuple-element.74), channel_id=1, source_target_pairs={{0,4},{1,29},{2,6},{3,31},{4,8},{5,1},{6,10},{7,3},{8,12},{9,5},{1... | collective-permute-start | bytes 3080 | tf_op jit(solution)/shard_map/ppermute | solution.py:38
  43.4 1.2 %send_scaled.1.sent_ref.after_ref = f32[1536,128]{1,0:T(8,128)S(1)} custom-call(f32[1024]{0:T(1024)S(1)} %bitcast.32, s32[1024]{0:T(1024)S(1)} %bitcast.29, s32[1024]{0:T(1024)S(1)} %bitcast.31, f32[8192,128]{1,0:T(8,128)S(1)} %get-tuple-element.56.flow, s32[8192,128]{1,0:T(8,128)S(1)} %get-tuple-element.48.turns), custom_call_target="tpu_custom_call" | custom-call | flops 1 | bytes 1 | tf_op jit(solution)/shard_map/send_scaled/pallas_call | solution.py:646
  44.6 3.0 %collective-permute-start.5 = (f32[1536,128]{1,0:T(8,128)S(1)}, f32[1536,128]{1,0:T(8,128)S(1)}, u32[]{:S(2)}, u32[]{:S(2)}) collective-permute-start(f32[1536,128]{1,0:T(8,128)S(1)} %send_scaled.1.sent_ref.after_ref), channel_id=1, source_target_pairs={{8,0},{12,4},{16,8},{20,12},{24,16},{28,20},{0,24},{4,28},{9,1},{1... | collective-permute-start | bytes 2359304 | tf_op jit(solution)/shard_map/ppermute | solution.py:44
  47.6 4.6 %home_rows.1.home = f32[16392,128]{1,0:T(8,128)S(1)} custom-call(s32[2048]{0:T(1024)S(1)} %bitcast.35, s32[2048]{0:T(1024)S(1)} %bitcast.36, s32[8192,128]{1,0:T(8,128)S(1)} %get-tuple-element.48.turns, f32[8192,128]{1,0:T(8,128)S(1)} %get-tuple-element.56.flow, f32[1536,128]{1,0:T(8,128)S(1)} %send_scaled.1.sent_ref.after_ref), custom_call_target="tpu_custom_call" | custom-call | flops 4000000000 | bytes 1 | tf_op jit(solution)/shard_map/home_rows/pallas_call | solution.py:655
  52.2 0.7 keep.1
  52.9 3.8 %base_rows.1.rest_3_ = f32[16392,128]{1,0:T(8,128)S(1)} custom-call(f32[2048]{0:T(1024)S(1)} %bitcast.37, f32[2048]{0:T(1024)S(1)} %bitcast.38, f32[16392,128]{1,0:T(8,128)S(1)} %get-tuple-element.46.rows, f32[16392,128]{1,0:T(8,128)S(1)} %home_rows.1.home), custom_call_target="tpu_custom_call" | custom-call | flops 10000000 | bytes 1 | tf_op jit(solution)/shard_map/base_rows/pallas_call | solution.py:673
  56.8 2.6 %collective-permute-done.6 = f32[2,128]{1,0:T(2,128)S(1)} collective-permute-done((f32[2,128]{1,0:T(2,128)S(1)}, f32[2,128]{1,0:T(2,128)S(1)}, u32[]{:S(2)}, u32[]{:S(2)}) %collective-permute-start.6) | collective-permute-done | bytes 1056 | tf_op jit(solution)/shard_map/ppermute | solution.py:38
  59.4 0.0 collective-permute-done.9.rest_1_
  59.4 0.3 collective-permute-start.10
  59.8 0.9 %collective-permute-done.10 = f32[4,128]{1,0:T(4,128)S(1)} collective-permute-done((f32[4,128]{1,0:T(4,128)S(1)}, f32[4,128]{1,0:T(4,128)S(1)}, u32[]{:S(2)}, u32[]{:S(2)}) %collective-permute-start.10) | collective-permute-done | bytes 2080 | tf_op jit(solution)/shard_map/ppermute | solution.py:688
  60.6 2.2 %land_first.1.rest_1_ = f32[16392,128]{1,0:T(8,128)S(1)} custom-call(f32[1024]{0:T(1024)S(1)} %maximum_bitcast_fusion.scale, s32[1024]{0:T(1024)S(1)} %bitcast.33, f32[1536,128]{1,0:T(8,128)S(1)} %collective-permute-done.8.rest_0_, f32[1536,128]{1,0:T(8,128)S(1)} %collective-permute-done.9.rest_1_, ...), custom_call_target="tpu_custom_call", output_to_operand_aliasing={{}: (5, {})} | custom-call | flops 4000000000 | bytes 1 | tf_op jit(solution)/shard_map/land_first/pallas_call | solution.py:691
  62.8 7.5 %collective-permute-done.5.rest_0_ = f32[1536,128]{1,0:T(8,128)S(1)} collective-permute-done((f32[1536,128]{1,0:T(8,128)S(1)}, f32[1536,128]{1,0:T(8,128)S(1)}, u32[]{:S(2)}, u32[]{:S(2)}) %collective-permute-start.5) | collective-permute-done | bytes 786464 | tf_op jit(solution)/shard_map/ppermute | solution.py:44
  70.3 4.5 %finish.1 = (f32[2048,1024]{1,0:T(8,128)}, f32[16392,128]{1,0:T(8,128)S(1)}) custom-call(s32[1024]{0:T(1024)S(1)} %bitcast.34, f32[1536,128]{1,0:T(8,128)S(1)} %collective-permute-done.5.rest_0_, f32[16392,128]{1,0:T(8,128)S(1)} %land_first.1.rest_1_), custom_call_target="tpu_custom_call", output_to_operand_aliasing={{1}: (2, {})} | custom-call | flops 2097152 | bytes 8388608 | tf_op jit(solution)/shard_map/finish/pallas_call | solution.py:702
  (25 shorter events, 0.1 us)
Async XLA Ops:
  0.0 7.4 %copy-start = (s32[4,1024]{1,0:T(4,128)S(1)}, s32[4,1024]{1,0:T(4,128)}, u32[]{:S(2)}) copy-start(s32[4,1024]{1,0:T(4,128)} %node_out.3) | copy-start | bytes 49156
  0.0 7.4 %copy-start.2 = (s32[4,192]{1,0:T(4,128)S(1)}, s32[4,192]{1,0:T(4,128)}, u32[]{:S(2)}) copy-start(s32[4,192]{1,0:T(4,128)} %send_list.1) | copy-start | bytes 9220
  0.0 7.4 %copy-start.1 = (s32[4,1024]{1,0:T(4,128)S(1)}, s32[4,1024]{1,0:T(4,128)}, u32[]{:S(2)}) copy-start(s32[4,1024]{1,0:T(4,128)} %node_in.1) | copy-start | bytes 49156
  0.0 7.4 %copy-start.3 = (s32[4,192]{1,0:T(4,128)S(1)}, s32[4,192]{1,0:T(4,128)}, u32[]{:S(2)}) copy-start(s32[4,192]{1,0:T(4,128)} %rest_3_.1) | copy-start | bytes 9220
  0.0 10.4 %copy-start.4 = (f32[2048]{0:T(1024)S(1)}, f32[2048]{0:T(1024)}, u32[]{:S(2)}) copy-start(f32[2048]{0:T(1024)} %param.10) | copy-start | bytes 24580
  0.0 10.4 %copy-start.6 = (f32[2048]{0:T(1024)S(1)}, f32[2048]{0:T(1024)}, u32[]{:S(2)}) copy-start(f32[2048]{0:T(1024)} %param.12) | copy-start | bytes 24580
  0.0 10.4 %copy-start.5 = (f32[2048]{0:T(1024)S(1)}, f32[2048]{0:T(1024)}, u32[]{:S(2)}) copy-start(f32[2048]{0:T(1024)} %param.11) | copy-start | bytes 24580
  4.3 5.7 %collective-permute-start.2 = (f32[16,128]{1,0:T(8,128)S(1)}, f32[16,128]{1,0:T(8,128)S(1)}, u32[]{:S(2)}, u32[]{:S(2)}) collective-permute-start(f32[16,128]{1,0:T(8,128)S(1)} %get-tuple-element.41.after_ref), channel_id=1, source_target_pairs={{0,3},{1,2},{2,1},{3,0},{4,7},{5,6},{6,5},{7,4},{8,11},{9,10},{10,... | collective-permute-start | bytes 24584 | tf_op jit(solution)/shard_map/ppermute | solution.py:50
  6.8 3.7 %collective-permute-start.1 = (f32[16,128]{1,0:T(8,128)S(1)}, f32[16,128]{1,0:T(8,128)S(1)}, u32[]{:S(2)}, u32[]{:S(2)}) collective-permute-start(f32[16,128]{1,0:T(8,128)S(1)} %get-tuple-element.41.after_ref), channel_id=1, source_target_pairs={{0,2},{1,3},{2,0},{3,1},{4,6},{5,7},{6,4},{7,5},{8,10},{9,11},{10,... | collective-permute-start | bytes 24584 | tf_op jit(solution)/shard_map/ppermute | solution.py:50
  7.4 3.0 %collective-permute-start = (f32[16,128]{1,0:T(8,128)S(1)}, f32[16,128]{1,0:T(8,128)S(1)}, u32[]{:S(2)}, u32[]{:S(2)}) collective-permute-start(f32[16,128]{1,0:T(8,128)S(1)} %get-tuple-element.41.after_ref), channel_id=1, source_target_pairs={{0,1},{1,0},{2,3},{3,2},{4,5},{5,4},{6,7},{7,6},{8,9},{9,8},{10,11... | collective-permute-start | bytes 24584 | tf_op jit(solution)/shard_map/ppermute | solution.py:50
  10.5 6.4 %collective-permute-start.3 = (f32[16,128]{1,0:T(8,128)S(1)}, f32[16,128]{1,0:T(8,128)S(1)}, u32[]{:S(2)}, u32[]{:S(2)}) collective-permute-start(f32[16,128]{1,0:T(8,128)S(1)} %fusion.1.supply), channel_id=1, source_target_pairs={{0,4},{1,29},{2,10},{3,27},{4,8},{5,1},{6,14},{7,31},{8,12},{9,5},... | collective-permute-start | bytes 24584 | tf_op jit(solution)/shard_map/ppermute | solution.py:28
  14.3 27.0 %collective-permute-start.4 = (f32[1536,128]{1,0:T(8,128)S(1)}, f32[1536,128]{1,0:T(8,128)S(1)}, u32[]{:S(2)}, u32[]{:S(2)}) collective-permute-start(f32[1536,128]{1,0:T(8,128)S(1)} %send_ahead.1.sent_ref), channel_id=1, source_target_pairs={{24,0},{28,4},{0,8},{4,12},{8,16},{12,20},{16,24},{20,28},{25,1},{... | collective-permute-start | bytes 2359304 | tf_op jit(solution)/shard_map/ppermute | solution.py:44
  22.6 36.8 %collective-permute-start.9 = (f32[1536,128]{1,0:T(8,128)S(1)}, f32[1536,128]{1,0:T(8,128)S(1)}, u32[]{:S(2)}, u32[]{:S(2)}) collective-permute-start(f32[1536,128]{1,0:T(8,128)S(1)} %get-tuple-element.63), channel_id=1, source_target_pairs={{4,0},{8,4},{12,8},{16,12},{20,16},{24,20},{28,24},{0,28},{5,1},{9... | collective-permute-start | bytes 2359304 | tf_op jit(solution)/shard_map/ppermute | solution.py:44
  24.9 34.5 %collective-permute-start.8 = (f32[1536,128]{1,0:T(8,128)S(1)}, f32[1536,128]{1,0:T(8,128)S(1)}, u32[]{:S(2)}, u32[]{:S(2)}) collective-permute-start(f32[1536,128]{1,0:T(8,128)S(1)} %get-tuple-element.51.after_ref), channel_id=1, source_target_pairs={{28,0},{0,4},{4,8},{8,12},{12,16},{16,20},{20,24},{24,28},{29,1},{... | collective-permute-start | bytes 2359304 | tf_op jit(solution)/shard_map/ppermute | solution.py:44
  41.3 15.5 %collective-permute-start.7 = (f32[2,128]{1,0:T(2,128)S(1)}, f32[2,128]{1,0:T(2,128)S(1)}, u32[]{:S(2)}, u32[]{:S(2)}) collective-permute-start(f32[2,128]{1,0:T(2,128)S(1)} %get-tuple-element.73), channel_id=1, source_target_pairs={{0,8},{1,25},{2,10},{3,27},{4,12},{5,29},{6,14},{7,31},{8,16},{9,1... | collective-permute-start | bytes 3080 | tf_op jit(solution)/shard_map/ppermute | solution.py:38
  41.3 18.0 %collective-permute-start.6 = (f32[2,128]{1,0:T(2,128)S(1)}, f32[2,128]{1,0:T(2,128)S(1)}, u32[]{:S(2)}, u32[]{:S(2)}) collective-permute-start(f32[2,128]{1,0:T(2,128)S(1)} %get-tuple-element.74), channel_id=1, source_target_pairs={{0,4},{1,29},{2,6},{3,31},{4,8},{5,1},{6,10},{7,3},{8,12},{9,5},{1... | collective-permute-start | bytes 3080 | tf_op jit(solution)/shard_map/ppermute | solution.py:38
  44.6 25.7 %collective-permute-start.5 = (f32[1536,128]{1,0:T(8,128)S(1)}, f32[1536,128]{1,0:T(8,128)S(1)}, u32[]{:S(2)}, u32[]{:S(2)}) collective-permute-start(f32[1536,128]{1,0:T(8,128)S(1)} %send_scaled.1.sent_ref.after_ref), channel_id=1, source_target_pairs={{8,0},{12,4},{16,8},{20,12},{24,16},{28,20},{0,24},{4,28},{9,1},{1... | collective-permute-start | bytes 2359304 | tf_op jit(solution)/shard_map/ppermute | solution.py:44
  59.4 1.2 %collective-permute-start.10 = (f32[4,128]{1,0:T(4,128)S(1)}, f32[4,128]{1,0:T(4,128)S(1)}, u32[]{:S(2)}, u32[]{:S(2)}) collective-permute-start(f32[4,128]{1,0:T(4,128)S(1)} %pad_maximum_fusion.1), channel_id=1, source_target_pairs={{0,1},{1,0},{2,3},{3,2},{4,5},{5,4},{6,7},{7,6},{8,9},{9,8},{10,11... | collective-permute-start | bytes 6152 | tf_op jit(solution)/shard_map/ppermute | solution.py:688

commit v19 on v18

--- a/solution.py
+++ b/solution.py
@@ -522,7 +522,7 @@
     per_cell = (height, LANES)
     list_shape = (4 * padded(cap) // LANES, LANES)
     ahead_rows = -(-(branches + 2) * padded(cap) // LANES // 8) * 8
-    chunk = 128
+    chunk = 256
     row_bytes = width * 4
     occupancy = pltpu.with_memory_space_constraint(occupancy, pltpu.HBM)
     turn = pltpu.with_memory_space_constraint(turn, pltpu.HBM)

time: 74.9 us -> 75.1 us (level)
  no operation moved by 1% of the time
where the time goes in v19:
time: 75.1 us; the launch traced here: 74.9 us
  Pallas kernels  42.1 us (56%)
  starting transfers between devices  14.1 us (19%)
  waiting for transfers between devices  12.5 us (17%)
  blocking collectives  5.96 us (8%)
    pallas_call x1, Pallas kernels, on_device(): pl.pallas_call(functools.partial(node_flow_kernel, sizes), in_specs=[SMEM...  8.75 us
    ppermute x4, waiting for transfers between devices, shifted(): return lax.ppermute(block, axis, route)  7.5 us
    ppermute x4, starting transfers between devices, shifted(): return lax.ppermute(block, axis, route)  6.83 us
    all_gather x1, blocking collectives, on_device(): shared = lax.all_gather(joined, 'dest', axis=0, tiled=True)  5.96 us
    pallas_call x1, Pallas kernels, on_device(): pl.pallas_call(functools.partial(home_kernel, sizes), in_specs=[SMEM_WHOL...  4.63 us
    pallas_call x1, Pallas kernels, on_device(): pl.pallas_call(functools.partial(finish_kernel, sizes, (3,), chunk), in_s...  4.53 us
    pallas_call x1, Pallas kernels, on_device(): pl.pallas_call(functools.partial(cell_sum_kernel, chunk, sub), in_specs=[...  4.36 us
    pallas_call x1, Pallas kernels, on_device(): pl.pallas_call(functools.partial(base_kernel, sizes), in_specs=[SMEM_WHOL...  3.85 us
  transfers between devices with their start and end apart: 11, of which 5 were waited for; matrix products, arithmetic and copies ran while one was open for 0% of the time, Pallas kernels for 44%

profile of v19, /device:TPU:0, one launch (start us, length us, event | category | flops | bytes accessed | tf_op | source)
XLA Modules:
  0.0 74.9 jit_solution(13245028171297724251)
XLA Ops:
  0.0 4.4 %cell_sum.1 = (f32[16,128]{1,0:T(8,128)S(1)}, f32[16392,128]{1,0:T(8,128)S(1)}) custom-call(f32[2048,1024]{1,0:T(8,128)} %x_hbm.2), custom_call_target="tpu_custom_call" | custom-call | flops 2097152 | bytes 8388608 | tf_op jit(solution)/shard_map/cell_sum/pallas_call | solution.py:530
  4.4 2.4 %collective-permute-start.2 = (f32[16,128]{1,0:T(8,128)S(1)}, f32[16,128]{1,0:T(8,128)S(1)}, u32[]{:S(2)}, u32[]{:S(2)}) collective-permute-start(f32[16,128]{1,0:T(8,128)S(1)} %get-tuple-element.41.after_ref), channel_id=1, source_target_pairs={{0,3},{1,2},{2,1},{3,0},{4,7},{5,6},{6,5},{7,4},{8,11},{9,10},{10,... | collective-permute-start | bytes 24584 | tf_op jit(solution)/shard_map/ppermute | solution.py:50
  6.8 0.6 collective-permute-start.1
  7.5 0.0 collective-permute-start
  7.5 2.5 %turn_rows.1 = (s32[8192,128]{1,0:T(8,128)S(1)}, s32[32,128]{1,0:T(8,128)S(1)}, s32[8,128]{1,0:T(8,128)S(1)}, s32[8,128]{1,0:T(8,128)S(1)}, s32[8,128]{1,0:T(8,1...) custom-call(s32[1024,1024]{1,0:T(8,128)} %x_hbm.3, ...), custom_call_target="tpu_custom_call" | custom-call | bytes 4194304 | tf_op jit(solution)/shard_map/turn_rows/pallas_call | solution.py:550
  10.0 0.4 collective-permute-done.1
  10.5 1.6 %collective-permute-start.3 = (f32[16,128]{1,0:T(8,128)S(1)}, f32[16,128]{1,0:T(8,128)S(1)}, u32[]{:S(2)}, u32[]{:S(2)}) collective-permute-start(f32[16,128]{1,0:T(8,128)S(1)} %fusion.1.supply), channel_id=1, source_target_pairs={{0,4},{1,29},{2,10},{3,27},{4,8},{5,1},{6,14},{7,31},{8,12},{9,5},... | collective-permute-start | bytes 24584 | tf_op jit(solution)/shard_map/ppermute | solution.py:28
  12.1 2.2 %send_ahead.1.sent_ref = f32[1536,128]{1,0:T(8,128)S(1)} custom-call(f32[2176]{0:T(1024)S(1)} %concatenate.13.fraction, s32[2048]{0:T(1024)S(1)} %bitcast.39, f32[16392,128]{1,0:T(8,128)S(1)} %get-tuple-element.46.rows, s32[8192,128]{1,0:T(8,128)S(1)} %get-tuple-element.48.turns), custom_call_target="tpu_custom_call" | custom-call | flops 1 | bytes 1 | tf_op jit(solution)/shard_map/send_ahead/pallas_call | solution.py:583
  14.3 1.6 %collective-permute-start.4 = (f32[1536,128]{1,0:T(8,128)S(1)}, f32[1536,128]{1,0:T(8,128)S(1)}, u32[]{:S(2)}, u32[]{:S(2)}) collective-permute-start(f32[1536,128]{1,0:T(8,128)S(1)} %send_ahead.1.sent_ref), channel_id=1, source_target_pairs={{24,0},{28,4},{0,8},{4,12},{8,16},{12,20},{16,24},{20,28},{25,1},{... | collective-permute-start | bytes 2359304 | tf_op jit(solution)/shard_map/ppermute | solution.py:44
  16.0 1.0 %collective-permute-done.3.supply_ref = f32[16,128]{1,0:T(8,128)S(1)} collective-permute-done((f32[16,128]{1,0:T(8,128)S(1)}, f32[16,128]{1,0:T(8,128)S(1)}, u32[]{:S(2)}, u32[]{:S(2)}) %collective-permute-start.3) | collective-permute-done | bytes 8224 | tf_op jit(solution)/shard_map/ppermute | solution.py:28
  16.9 2.5 %scale_rows.1.scaled = f32[16392,128]{1,0:T(8,128)S(1)} custom-call(f32[2048]{0:T(1024)S(1)} %bitcast.25, f32[16392,128]{1,0:T(8,128)S(1)} %get-tuple-element.46.rows, f32[1536,128]{1,0:T(8,128)S(1)} %send_ahead.1.sent_ref, f32[16,128]{1,0:T(8,128)S(1)} %collective-permute-done.3.supply_ref), custom_call_target="tpu_custom_call" | custom-call | flops 10000000000 | bytes 1 | tf_op jit(solution)/shard_map/scale_rows/pallas_call | solution.py:592
  19.4 3.3 %send_near.1 = (f32[1536,128]{1,0:T(8,128)S(1)}, f32[1536,128]{1,0:T(8,128)S(1)}) custom-call(s32[4096]{0:T(1024)S(1)} %bitcast.26, s32[1024]{0:T(1024)S(1)} %bitcast.28, s32[1024]{0:T(1024)S(1)} %bitcast.30, f32[16392,128]{1,0:T(8,128)S(1)} %scale_rows.1.scaled, s32[8192,128]{1,0:T(8,128)S(1)} %get-tuple-element.48.turns), custom_call_target="tpu_custom_call" | custom-call | flops 1 | bytes 1 | tf_op jit(solution)/shard_map/send_near/pallas_call | solution.py:601
  22.7 2.3 %collective-permute-start.9 = (f32[1536,128]{1,0:T(8,128)S(1)}, f32[1536,128]{1,0:T(8,128)S(1)}, u32[]{:S(2)}, u32[]{:S(2)}) collective-permute-start(f32[1536,128]{1,0:T(8,128)S(1)} %get-tuple-element.63), channel_id=1, source_target_pairs={{4,0},{8,4},{12,8},{16,12},{20,16},{24,20},{28,24},{0,28},{5,1},{9... | collective-permute-start | bytes 2359304 | tf_op jit(solution)/shard_map/ppermute | solution.py:44
  25.0 0.0 collective-permute-start.8
  25.0 8.8 %node_flow.1 = (f32[8192,128]{1,0:T(8,128)S(1)}, f32[32,128]{1,0:T(8,128)S(1)}) custom-call(s32[4096]{0:T(1024)S(1)} %bitcast.27, f32[16392,128]{1,0:T(8,128)S(1)} %scale_rows.1.scaled, s32[8192,128]{1,0:T(8,128)S(1)} %get-tuple-element.48.turns, f32[1536,128]{1,0:T(8,128)S(1)} %get-tuple-element.51.after_ref), custom_call_target="tpu_custom_call" | custom-call | flops 1 | bytes 1 | tf_op jit(solution)/shard_map/node_flow/pallas_call | solution.py:614
  33.8 6.0 %all_gather.3.shared = f32[192,128]{1,0:T(8,128)S(1)} all-gather(f32[48,128]{1,0:T(8,128)S(1)} %pad_maximum_fusion), channel_id=1, replica_groups=mesh['region'=8,'dest'=4] {'dest'}, dimensions={0}, use_global_device_ids=true | all-gather | bytes 122880 | tf_op jit(solution)/shard_map/all_gather | solution.py:629
  39.7 1.5 %theta.1 = (f32[8,128]{1,0:T(8,128)S(1)}, f32[4,128]{1,0:T(4,128)S(1)}) custom-call(f32[16,128]{1,0:T(8,128)S(1)} %fusion.1.supply, f32[192,128]{1,0:T(8,128)S(1)} %all_gather.3.shared, s32[4,1024]{1,0:T(4,128)S(1)} %copy-done, s32[4,192]{1,0:T(4,128)S(1)} %copy-done.2), custom_call_target="tpu_custom_call" | custom-call | flops 1 | bytes 1 | tf_op jit(solution)/shard_map/theta/pallas_call | solution.py:630
  41.2 0.0 collective-permute-done.4.arrived_ref.rest_2_
  41.2 0.1 collective-permute-start.7
  41.3 2.2 %collective-permute-start.6 = (f32[2,128]{1,0:T(2,128)S(1)}, f32[2,128]{1,0:T(2,128)S(1)}, u32[]{:S(2)}, u32[]{:S(2)}) collective-permute-start(f32[2,128]{1,0:T(2,128)S(1)} %get-tuple-element.74), channel_id=1, source_target_pairs={{0,4},{1,29},{2,6},{3,31},{4,8},{5,1},{6,10},{7,3},{8,12},{9,5},{1... | collective-permute-start | bytes 3080 | tf_op jit(solution)/shard_map/ppermute | solution.py:38
  43.5 1.2 %send_scaled.1.sent_ref.after_ref = f32[1536,128]{1,0:T(8,128)S(1)} custom-call(f32[1024]{0:T(1024)S(1)} %bitcast.32, s32[1024]{0:T(1024)S(1)} %bitcast.29, s32[1024]{0:T(1024)S(1)} %bitcast.31, f32[8192,128]{1,0:T(8,128)S(1)} %get-tuple-element.56.flow, s32[8192,128]{1,0:T(8,128)S(1)} %get-tuple-element.48.turns), custom_call_target="tpu_custom_call" | custom-call | flops 1 | bytes 1 | tf_op jit(solution)/shard_map/send_scaled/pallas_call | solution.py:646
  44.6 2.9 %collective-permute-start.5 = (f32[1536,128]{1,0:T(8,128)S(1)}, f32[1536,128]{1,0:T(8,128)S(1)}, u32[]{:S(2)}, u32[]{:S(2)}) collective-permute-start(f32[1536,128]{1,0:T(8,128)S(1)} %send_scaled.1.sent_ref.after_ref), channel_id=1, source_target_pairs={{8,0},{12,4},{16,8},{20,12},{24,16},{28,20},{0,24},{4,28},{9,1},{1... | collective-permute-start | bytes 2359304 | tf_op jit(solution)/shard_map/ppermute | solution.py:44
  47.6 4.6 %home_rows.1.home = f32[16392,128]{1,0:T(8,128)S(1)} custom-call(s32[2048]{0:T(1024)S(1)} %bitcast.35, s32[2048]{0:T(1024)S(1)} %bitcast.36, s32[8192,128]{1,0:T(8,128)S(1)} %get-tuple-element.48.turns, f32[8192,128]{1,0:T(8,128)S(1)} %get-tuple-element.56.flow, f32[1536,128]{1,0:T(8,128)S(1)} %send_scaled.1.sent_ref.after_ref), custom_call_target="tpu_custom_call" | custom-call | flops 4000000000 | bytes 1 | tf_op jit(solution)/shard_map/home_rows/pallas_call | solution.py:655
  52.2 0.7 keep.1
  52.9 3.8 %base_rows.1.rest_3_ = f32[16392,128]{1,0:T(8,128)S(1)} custom-call(f32[2048]{0:T(1024)S(1)} %bitcast.37, f32[2048]{0:T(1024)S(1)} %bitcast.38, f32[16392,128]{1,0:T(8,128)S(1)} %get-tuple-element.46.rows, f32[16392,128]{1,0:T(8,128)S(1)} %home_rows.1.home), custom_call_target="tpu_custom_call" | custom-call | flops 10000000 | bytes 1 | tf_op jit(solution)/shard_map/base_rows/pallas_call | solution.py:673
  56.8 2.7 %collective-permute-done.6 = f32[2,128]{1,0:T(2,128)S(1)} collective-permute-done((f32[2,128]{1,0:T(2,128)S(1)}, f32[2,128]{1,0:T(2,128)S(1)}, u32[]{:S(2)}, u32[]{:S(2)}) %collective-permute-start.6) | collective-permute-done | bytes 1056 | tf_op jit(solution)/shard_map/ppermute | solution.py:38
  59.4 0.0 collective-permute-done.9.rest_1_
  59.5 0.4 collective-permute-start.10
  59.8 0.9 %collective-permute-done.10 = f32[4,128]{1,0:T(4,128)S(1)} collective-permute-done((f32[4,128]{1,0:T(4,128)S(1)}, f32[4,128]{1,0:T(4,128)S(1)}, u32[]{:S(2)}, u32[]{:S(2)}) %collective-permute-start.10) | collective-permute-done | bytes 2080 | tf_op jit(solution)/shard_map/ppermute | solution.py:688
  60.7 2.2 %land_first.1.rest_1_ = f32[16392,128]{1,0:T(8,128)S(1)} custom-call(f32[1024]{0:T(1024)S(1)} %maximum_bitcast_fusion.scale, s32[1024]{0:T(1024)S(1)} %bitcast.33, f32[1536,128]{1,0:T(8,128)S(1)} %collective-permute-done.8.rest_0_, f32[1536,128]{1,0:T(8,128)S(1)} %collective-permute-done.9.rest_1_, ...), custom_call_target="tpu_custom_call", output_to_operand_aliasing={{}: (5, {})} | custom-call | flops 4000000000 | bytes 1 | tf_op jit(solution)/shard_map/land_first/pallas_call | solution.py:691
  62.9 7.5 %collective-permute-done.5.rest_0_ = f32[1536,128]{1,0:T(8,128)S(1)} collective-permute-done((f32[1536,128]{1,0:T(8,128)S(1)}, f32[1536,128]{1,0:T(8,128)S(1)}, u32[]{:S(2)}, u32[]{:S(2)}) %collective-permute-start.5) | collective-permute-done | bytes 786464 | tf_op jit(solution)/shard_map/ppermute | solution.py:44
  70.4 4.5 %finish.1 = (f32[2048,1024]{1,0:T(8,128)}, f32[16392,128]{1,0:T(8,128)S(1)}) custom-call(s32[1024]{0:T(1024)S(1)} %bitcast.34, f32[1536,128]{1,0:T(8,128)S(1)} %collective-permute-done.5.rest_0_, f32[16392,128]{1,0:T(8,128)S(1)} %land_first.1.rest_1_), custom_call_target="tpu_custom_call", output_to_operand_aliasing={{1}: (2, {})} | custom-call | flops 2097152 | bytes 8388608 | tf_op jit(solution)/shard_map/finish/pallas_call | solution.py:702
  (25 shorter events, 0.1 us)
Async XLA Ops:
  0.0 7.5 %copy-start = (s32[4,1024]{1,0:T(4,128)S(1)}, s32[4,1024]{1,0:T(4,128)}, u32[]{:S(2)}) copy-start(s32[4,1024]{1,0:T(4,128)} %node_out.3) | copy-start | bytes 49156
  0.0 7.5 %copy-start.2 = (s32[4,192]{1,0:T(4,128)S(1)}, s32[4,192]{1,0:T(4,128)}, u32[]{:S(2)}) copy-start(s32[4,192]{1,0:T(4,128)} %send_list.1) | copy-start | bytes 9220
  0.0 7.5 %copy-start.1 = (s32[4,1024]{1,0:T(4,128)S(1)}, s32[4,1024]{1,0:T(4,128)}, u32[]{:S(2)}) copy-start(s32[4,1024]{1,0:T(4,128)} %node_in.1) | copy-start | bytes 49156
  0.0 7.5 %copy-start.3 = (s32[4,192]{1,0:T(4,128)S(1)}, s32[4,192]{1,0:T(4,128)}, u32[]{:S(2)}) copy-start(s32[4,192]{1,0:T(4,128)} %rest_3_.1) | copy-start | bytes 9220
  0.0 10.5 %copy-start.4 = (f32[2048]{0:T(1024)S(1)}, f32[2048]{0:T(1024)}, u32[]{:S(2)}) copy-start(f32[2048]{0:T(1024)} %param.10) | copy-start | bytes 24580
  0.0 10.5 %copy-start.6 = (f32[2048]{0:T(1024)S(1)}, f32[2048]{0:T(1024)}, u32[]{:S(2)}) copy-start(f32[2048]{0:T(1024)} %param.12) | copy-start | bytes 24580
  0.0 10.5 %copy-start.5 = (f32[2048]{0:T(1024)S(1)}, f32[2048]{0:T(1024)}, u32[]{:S(2)}) copy-start(f32[2048]{0:T(1024)} %param.11) | copy-start | bytes 24580
  4.4 5.6 %collective-permute-start.2 = (f32[16,128]{1,0:T(8,128)S(1)}, f32[16,128]{1,0:T(8,128)S(1)}, u32[]{:S(2)}, u32[]{:S(2)}) collective-permute-start(f32[16,128]{1,0:T(8,128)S(1)} %get-tuple-element.41.after_ref), channel_id=1, source_target_pairs={{0,3},{1,2},{2,1},{3,0},{4,7},{5,6},{6,5},{7,4},{8,11},{9,10},{10,... | collective-permute-start | bytes 24584 | tf_op jit(solution)/shard_map/ppermute | solution.py:50
  6.8 3.7 %collective-permute-start.1 = (f32[16,128]{1,0:T(8,128)S(1)}, f32[16,128]{1,0:T(8,128)S(1)}, u32[]{:S(2)}, u32[]{:S(2)}) collective-permute-start(f32[16,128]{1,0:T(8,128)S(1)} %get-tuple-element.41.after_ref), channel_id=1, source_target_pairs={{0,2},{1,3},{2,0},{3,1},{4,6},{5,7},{6,4},{7,5},{8,10},{9,11},{10,... | collective-permute-start | bytes 24584 | tf_op jit(solution)/shard_map/ppermute | solution.py:50
  7.5 3.0 %collective-permute-start = (f32[16,128]{1,0:T(8,128)S(1)}, f32[16,128]{1,0:T(8,128)S(1)}, u32[]{:S(2)}, u32[]{:S(2)}) collective-permute-start(f32[16,128]{1,0:T(8,128)S(1)} %get-tuple-element.41.after_ref), channel_id=1, source_target_pairs={{0,1},{1,0},{2,3},{3,2},{4,5},{5,4},{6,7},{7,6},{8,9},{9,8},{10,11... | collective-permute-start | bytes 24584 | tf_op jit(solution)/shard_map/ppermute | solution.py:50
  10.5 6.4 %collective-permute-start.3 = (f32[16,128]{1,0:T(8,128)S(1)}, f32[16,128]{1,0:T(8,128)S(1)}, u32[]{:S(2)}, u32[]{:S(2)}) collective-permute-start(f32[16,128]{1,0:T(8,128)S(1)} %fusion.1.supply), channel_id=1, source_target_pairs={{0,4},{1,29},{2,10},{3,27},{4,8},{5,1},{6,14},{7,31},{8,12},{9,5},... | collective-permute-start | bytes 24584 | tf_op jit(solution)/shard_map/ppermute | solution.py:28
  14.3 26.9 %collective-permute-start.4 = (f32[1536,128]{1,0:T(8,128)S(1)}, f32[1536,128]{1,0:T(8,128)S(1)}, u32[]{:S(2)}, u32[]{:S(2)}) collective-permute-start(f32[1536,128]{1,0:T(8,128)S(1)} %send_ahead.1.sent_ref), channel_id=1, source_target_pairs={{24,0},{28,4},{0,8},{4,12},{8,16},{12,20},{16,24},{20,28},{25,1},{... | collective-permute-start | bytes 2359304 | tf_op jit(solution)/shard_map/ppermute | solution.py:44
  22.7 36.7 %collective-permute-start.9 = (f32[1536,128]{1,0:T(8,128)S(1)}, f32[1536,128]{1,0:T(8,128)S(1)}, u32[]{:S(2)}, u32[]{:S(2)}) collective-permute-start(f32[1536,128]{1,0:T(8,128)S(1)} %get-tuple-element.63), channel_id=1, source_target_pairs={{4,0},{8,4},{12,8},{16,12},{20,16},{24,20},{28,24},{0,28},{5,1},{9... | collective-permute-start | bytes 2359304 | tf_op jit(solution)/shard_map/ppermute | solution.py:44
  25.0 34.5 %collective-permute-start.8 = (f32[1536,128]{1,0:T(8,128)S(1)}, f32[1536,128]{1,0:T(8,128)S(1)}, u32[]{:S(2)}, u32[]{:S(2)}) collective-permute-start(f32[1536,128]{1,0:T(8,128)S(1)} %get-tuple-element.51.after_ref), channel_id=1, source_target_pairs={{28,0},{0,4},{4,8},{8,12},{12,16},{16,20},{20,24},{24,28},{29,1},{... | collective-permute-start | bytes 2359304 | tf_op jit(solution)/shard_map/ppermute | solution.py:44
  41.2 15.5 %collective-permute-start.7 = (f32[2,128]{1,0:T(2,128)S(1)}, f32[2,128]{1,0:T(2,128)S(1)}, u32[]{:S(2)}, u32[]{:S(2)}) collective-permute-start(f32[2,128]{1,0:T(2,128)S(1)} %get-tuple-element.73), channel_id=1, source_target_pairs={{0,8},{1,25},{2,10},{3,27},{4,12},{5,29},{6,14},{7,31},{8,16},{9,1... | collective-permute-start | bytes 3080 | tf_op jit(solution)/shard_map/ppermute | solution.py:38
  41.3 18.2 %collective-permute-start.6 = (f32[2,128]{1,0:T(2,128)S(1)}, f32[2,128]{1,0:T(2,128)S(1)}, u32[]{:S(2)}, u32[]{:S(2)}) collective-permute-start(f32[2,128]{1,0:T(2,128)S(1)} %get-tuple-element.74), channel_id=1, source_target_pairs={{0,4},{1,29},{2,6},{3,31},{4,8},{5,1},{6,10},{7,3},{8,12},{9,5},{1... | collective-permute-start | bytes 3080 | tf_op jit(solution)/shard_map/ppermute | solution.py:38
  44.6 25.7 %collective-permute-start.5 = (f32[1536,128]{1,0:T(8,128)S(1)}, f32[1536,128]{1,0:T(8,128)S(1)}, u32[]{:S(2)}, u32[]{:S(2)}) collective-permute-start(f32[1536,128]{1,0:T(8,128)S(1)} %send_scaled.1.sent_ref.after_ref), channel_id=1, source_target_pairs={{8,0},{12,4},{16,8},{20,12},{24,16},{28,20},{0,24},{4,28},{9,1},{1... | collective-permute-start | bytes 2359304 | tf_op jit(solution)/shard_map/ppermute | solution.py:44
  59.5 1.2 %collective-permute-start.10 = (f32[4,128]{1,0:T(4,128)S(1)}, f32[4,128]{1,0:T(4,128)S(1)}, u32[]{:S(2)}, u32[]{:S(2)}) collective-permute-start(f32[4,128]{1,0:T(4,128)S(1)} %pad_maximum_fusion.1), channel_id=1, source_target_pairs={{0,1},{1,0},{2,3},{3,2},{4,5},{5,4},{6,7},{7,6},{8,9},{9,8},{10,11... | collective-permute-start | bytes 6152 | tf_op jit(solution)/shard_map/ppermute | solution.py:688
